TPU v7x, 32 devices: a whole 2x2x4 slice. The times are simulated.
32 devices in a mesh: gx: 4 (over y, x), gy: 8 (over z, core).
Axes of the slice: x: 2, y: 2, z: 4, core: 2. Of those that a mesh axis runs over, the one named last changes fastest.
Arguments:
- momentum_dist: float32 [19, 32, 128, 512], P(None, 'gx', 'gy'), may hold values from 0.2 to 0.8
- order_dist: float32 [19, 32, 128, 512], P(None, 'gx', 'gy'), may hold values from -0.25 to 0.25
- offsets: int32 [4], replicated, may hold values from 64 to 79, as said below
Outputs:
- next_momentum: float32 [19, 32, 128, 512], P(None, 'gx', 'gy')
- next_order: float32 [19, 32, 128, 512], P(None, 'gx', 'gy')
Inputs may be any that keep to these rules, and one draw needn't show every extreme that they name: Every offsets[k] lies from 64 to 79; offsets[0] is 64 and offsets[3] is 79.
All inputs are finite; a program needn't handle non-finite values.
Results may differ from a plain program's by a relative error of at most 0.00002.
Values sent between devices are 32-bit elements; how exact they have to be, the bound alone decides.
No kernel may reach another device: no remote copies, remote signals or barrier semaphores. Data moves between devices by JAX's collectives and lax.ppermute only.
A program may use at most 128 MiB of HBM per device.

v0:
```python
import jax
import jax.numpy as jnp
from jax import lax
from jax.sharding import PartitionSpec as P

lattice_velocity = [
    (0, 0, 0),
    (1, 0, 0),
    (-1, 0, 0),
    (0, 1, 0),
    (0, -1, 0),
    (0, 0, 1),
    (0, 0, -1),
    (1, 1, 0),
    (-1, -1, 0),
    (1, -1, 0),
    (-1, 1, 0),
    (1, 0, 1),
    (-1, 0, -1),
    (1, 0, -1),
    (-1, 0, 1),
    (0, 1, 1),
    (0, -1, -1),
    (0, 1, -1),
    (0, -1, 1),
]
lattice_weight = [1.0 / 3.0] + [1.0 / 18.0] * 6 + [1.0 / 36.0] * 12
relax_momentum = 0.8
relax_order = 0.9
bulk_quadratic = -0.0625
bulk_quartic = 0.0625
interface_kappa = 0.04
plane_speed = 0.04
rising = [1, 7, 9, 11, 13]
falling = [2, 8, 10, 12, 14]
sideways = [3, 4, 7, 8, 9, 10, 15, 16, 17, 18]


def extended(cells, sides, width):
    for axis, dim in sides:
        count = lax.axis_size(axis)
        head = lax.slice_in_dim(cells, 0, width, axis=dim)
        tail = lax.slice_in_dim(cells, cells.shape[dim] - width, cells.shape[dim], axis=dim)
        cells = jnp.concatenate(
            [
                lax.ppermute(tail, axis, [(i, (i + 1) % count) for i in range(count)]),
                cells,
                lax.ppermute(head, axis, [((i + 1) % count, i) for i in range(count)]),
            ],
            axis=dim,
        )
    return cells


def tables(chosen):
    weight = jnp.asarray([lattice_weight[c] for c in chosen], jnp.float32).reshape(-1, 1, 1, 1)
    directions = [
        jnp.asarray([float(lattice_velocity[c][axis_place]) for c in chosen], jnp.float32).reshape(
            -1, 1, 1, 1
        )
        for axis_place in range(3)
    ]
    return (weight, directions)


def equilibria(density, order_field, potential, velocity, weight, directions):
    projection = (
        directions[0] * velocity[0] + directions[1] * velocity[1] + directions[2] * velocity[2]
    )
    speed_square = velocity[0] * velocity[0] + velocity[1] * velocity[1] + velocity[2] * velocity[2]
    shape_term = 3.0 * projection + 4.5 * projection * projection - 1.5 * speed_square
    moment_eq = weight * density * (1.0 + shape_term)
    order_eq = weight * (3.0 * potential + order_field * shape_term)
    return (moment_eq, order_eq, projection)


def collide(momentum, order, order_field, potential, gradient_parts):
    weight, directions = tables(list(range(19)))
    density = jnp.sum(momentum, axis=0)
    force_parts = [potential * part_value for part_value in gradient_parts]
    velocity = [
        (jnp.sum(directions[axis_place] * momentum, axis=0) + 0.5 * force_parts[axis_place])
        / density
        for axis_place in range(3)
    ]
    moment_eq, order_eq, projection = equilibria(
        density, order_field, potential, velocity, weight, directions
    )
    order_eq = jnp.concatenate(
        [(order_field - jnp.sum(order_eq[1:], axis=0))[None], order_eq[1:]], 0
    )
    force_projection = (
        directions[0] * force_parts[0]
        + directions[1] * force_parts[1]
        + directions[2] * force_parts[2]
    )
    velocity_force = (
        velocity[0] * force_parts[0] + velocity[1] * force_parts[1] + velocity[2] * force_parts[2]
    )
    source = (
        (1.0 - 0.5 / relax_momentum)
        * weight
        * (3.0 * (force_projection - velocity_force) + 9.0 * projection * force_projection)
    )
    moment_post = momentum - (momentum - moment_eq) / relax_momentum + source
    order_post = order - (order - order_eq) / relax_order
    return (moment_post, order_post, moment_eq, order_eq, density, velocity)


def jump_terms(
    chosen, density, order_field, potential, velocity, velocity_jump, base_moment, base_order
):
    weight, directions = tables(chosen)
    shifted_velocity = [velocity[0], velocity[1] + velocity_jump, velocity[2]]
    moment_shift, order_shift, projection = equilibria(
        density, order_field, potential, shifted_velocity, weight, directions
    )
    return (moment_shift - base_moment, order_shift - base_order)


def gather_components(values, chosen):
    return jnp.stack([values[c] for c in chosen])


def plane_windows(low_piece, up_piece, low_shift, up_shift):
    row_count = low_piece.shape[1]
    count_y = lax.axis_size("gy")
    column_slab = lax.axis_index("gy")
    plane_length = row_count * count_y
    whole_low, whole_up = (
        lax.all_gather(low_piece, "gy", axis=1, tiled=True),
        lax.all_gather(up_piece, "gy", axis=1, tiled=True),
    )

    def window_of(whole, shift_value):
        doubled = jnp.concatenate([whole, whole[:, : row_count + 3]], 1)
        first_row = jnp.mod(column_slab * row_count - 1 + shift_value, plane_length)
        return lax.dynamic_slice_in_dim(doubled, first_row, row_count + 3, 1)

    return (window_of(whole_low, low_shift), window_of(whole_up, up_shift))


def on_device(momentum_dist, order_dist, offsets):
    rows_y = momentum_dist.shape[2]
    count_x = lax.axis_size("gx")
    slab_index = lax.axis_index("gx")
    per_plane = count_x // 4
    fractions = (2.0 * jnp.arange(4, dtype=jnp.float32) + 1.0) / 8.0
    upper_slab = (slab_index + 1) % count_x
    low_mask = slab_index % per_plane == 0
    low_plane = slab_index // per_plane % 4
    up_mask = upper_slab % per_plane == 0
    up_plane = upper_slab // per_plane % 4
    low_shift = jnp.where(low_mask, offsets[low_plane], 0)
    low_near = jnp.where(low_mask, 1.0 - fractions[low_plane], 1.0)
    low_far = jnp.where(low_mask, fractions[low_plane], 0.0)
    up_shift = jnp.where(up_mask, -offsets[up_plane] - 1, 0)
    up_near = jnp.where(up_mask, fractions[up_plane], 1.0)
    up_far = jnp.where(up_mask, 1.0 - fractions[up_plane], 0.0)
    order_field = jnp.sum(order_dist, axis=0)
    rimmed = extended(order_field, (("gx", 0), ("gy", 1)), 1)
    order_low_win, order_up_win = plane_windows(
        rimmed[0:1, 1:-1], rimmed[-1:, 1:-1], low_shift, up_shift
    )
    minus_row = (
        low_near * order_low_win[:, 1 : rows_y + 1] + low_far * order_low_win[:, 2 : rows_y + 2]
    )
    plus_row = up_near * order_up_win[:, 1 : rows_y + 1] + up_far * order_up_win[:, 2 : rows_y + 2]
    order_minus = jnp.concatenate([minus_row, order_field[:-1]], 0)
    order_plus = jnp.concatenate([order_field[1:], plus_row], 0)
    order_north = rimmed[1:-1, 2:]
    order_south = rimmed[1:-1, :-2]
    order_upper = jnp.roll(order_field, -1, 2)
    order_lower = jnp.roll(order_field, 1, 2)
    laplacian = (
        order_plus
        + order_minus
        + (order_north + order_south)
        + (order_upper + order_lower)
        - 6.0 * order_field
    )
    gradient_parts = [
        0.5 * (order_plus - order_minus),
        0.5 * (order_north - order_south),
        0.5 * (order_upper - order_lower),
    ]
    potential = (
        bulk_quadratic * order_field
        + bulk_quartic * order_field * order_field * order_field
        - interface_kappa * laplacian
    )
    moment_post, order_post, moment_eq, order_eq, density, velocity = collide(
        momentum_dist, order_dist, order_field, potential, gradient_parts
    )
    top_velocity = [part_value[-1:] for part_value in velocity]
    moment_delta, order_delta = jump_terms(
        rising,
        density[-1:],
        order_field[-1:],
        potential[-1:],
        top_velocity,
        -plane_speed,
        gather_components(moment_eq, rising)[:, -1:],
        gather_components(order_eq, rising)[:, -1:],
    )
    rise_f = gather_components(moment_post, rising)[:, -1:]
    rise_g = gather_components(order_post, rising)[:, -1:]
    rise_f = jnp.where(up_mask, rise_f + moment_delta, rise_f)
    rise_g = jnp.where(up_mask, rise_g + order_delta, rise_g)
    rise_rows = jnp.concatenate([rise_f, rise_g], 0)[:, 0]
    bottom_velocity = [part_value[:1] for part_value in velocity]
    moment_delta, order_delta = jump_terms(
        falling,
        density[:1],
        order_field[:1],
        potential[:1],
        bottom_velocity,
        plane_speed,
        gather_components(moment_eq, falling)[:, :1],
        gather_components(order_eq, falling)[:, :1],
    )
    fall_f = gather_components(moment_post, falling)[:, :1]
    fall_g = gather_components(order_post, falling)[:, :1]
    fall_f = jnp.where(low_mask, fall_f + moment_delta, fall_f)
    fall_g = jnp.where(low_mask, fall_g + order_delta, fall_g)
    fall_rows = jnp.concatenate([fall_f, fall_g], 0)[:, 0]
    rise_slots = rising + [19 + c for c in rising]
    fall_slots = falling + [19 + c for c in falling]
    top_row = jnp.concatenate([moment_post[:, -1], order_post[:, -1]], 0)
    bottom_row = jnp.concatenate([moment_post[:, 0], order_post[:, 0]], 0)
    top_row = top_row.at[jnp.asarray(rise_slots)].set(rise_rows)
    bottom_row = bottom_row.at[jnp.asarray(fall_slots)].set(fall_rows)
    edge_rows = jnp.stack([bottom_row, top_row], 1)
    bordered = extended(edge_rows, (("gx", 1),), 1)
    low_piece = gather_components(bordered[:, 0], rise_slots)
    up_piece = gather_components(bordered[:, 3], fall_slots)
    low_win, up_win = plane_windows(low_piece, up_piece, low_shift, up_shift)
    side_ext = extended(
        jnp.concatenate(
            [gather_components(moment_post, sideways), gather_components(order_post, sideways)], 0
        ),
        (("gy", 2),),
        1,
    )

    def stream(post, family):
        arrived_list = []
        for component in range(19):
            step_x, step_y, step_z = lattice_velocity[component]
            if step_y != 0:
                spread = side_ext[family * 10 + sideways.index(component)]
                shifted = spread[:, 1 - step_y : 1 - step_y + rows_y]
            else:
                shifted = post[component]
            if step_x == 1:
                window = low_win[family * 5 + rising.index(component)]
                arrival = (
                    low_near * window[1 - step_y : 1 - step_y + rows_y]
                    + low_far * window[2 - step_y : 2 - step_y + rows_y]
                )
                shifted = jnp.concatenate([arrival[None], shifted[:-1]], 0)
            elif step_x == -1:
                window = up_win[family * 5 + falling.index(component)]
                arrival = (
                    up_near * window[1 - step_y : 1 - step_y + rows_y]
                    + up_far * window[2 - step_y : 2 - step_y + rows_y]
                )
                shifted = jnp.concatenate([shifted[1:], arrival[None]], 0)
            arrived_list.append(jnp.roll(shifted, step_z, 2))
        return jnp.stack(arrived_list)

    return (stream(moment_post, 0), stream(order_post, 1))


def solution(mesh):
    return jax.shard_map(
        on_device,
        mesh=mesh,
        in_specs=(P(None, "gx", "gy", None), P(None, "gx", "gy", None), P()),
        out_specs=(P(None, "gx", "gy", None), P(None, "gx", "gy", None)),
        check_vma=False,
    )
```

profile of v0, /device:TPU:1, one launch (start us, length us, event | category | flops | bytes accessed | tf_op | source)
XLA Modules:
  0.0 252.9 jit_solution(16029746907188249961)
XLA Ops:
  7.2 2.9 %reduce_sum.56 = f32[8,16,512]{2,1,0:T(8,128)S(1)} reduce(f32[19,8,16,512]{3,2,1,0:T(8,128)} %param.18, f32[]{:T(128)} %constant.136.clone.1), dimensions={0}, to_apply=%region_2.3 | reduce | flops 1179648 | bytes 5242884 | tf_op jit(solution)/shard_map/reduce_sum | solution.py:160
  10.8 3.0 %collective-permute-start = (f32[1,16,512]{2,1,0:T(8,128)S(1)}, f32[1,16,512]{2,1,0:T(8,128)S(1)}, u32[]{:S(2)}, u32[]{:S(2)}) collective-permute-start(f32[1,16,512]{2,1,0:T(8,128)S(1)} %get-tuple-element.139), channel_id=1, source_target_pairs={{8,0},{16,8},{24,16},{0,24},{9,1},{17,9},{25,17},{1,25},{10,2},{18... | collective-permute-start | bytes 98312 | tf_op jit(solution)/shard_map/ppermute | solution.py:48
  14.1 2.9 %reduce_sum.54 = f32[8,16,512]{2,1,0:T(8,128)S(1)} reduce(f32[19,8,16,512]{3,2,1,0:T(8,128)} %param.17, f32[]{:T(128)} %constant.136.clone.1), dimensions={0}, to_apply=%region_0.1 | reduce | flops 1179648 | bytes 5242884 | tf_op jit(solution)/shard_map/reduce_sum | solution.py:79
  17.7 3.6 %multiply_reduce_fusion.2 = (f32[8,16,512]{2,1,0:T(8,128)S(1)}, f32[8,16,512]{2,1,0:T(8,128)S(1)}, f32[8,16,512]{2,1,0:T(8,128)S(1)}) fusion(f32[19,8,16,512]{3,2,1,0:T(8,128)} %param.17, f32[19]{0:T(128)S(1)} %copy-done.65, f32[19]{0:T(128)S(1)} %copy-done.67, f32[19]{0:T(128)S(1)} %copy-done.66), kind=kLoop, calls=%fused_computation.13 | loop fusion | flops 7274496 | bytes 5767396 | tf_op jit(solution)/shard_map/reduce_sum | solution.py:82
  25.2 15.2 %all_gather.12 = f32[1,128,512]{2,1,0:T(8,128)S(1)} all-gather(f32[1,16,512]{2,1,0:T(8,128)S(1)} %collective-permute-done), channel_id=1, replica_groups=mesh['gx'=4,'gy'=8] {'gy'}, dimensions={1}, use_global_device_ids=true | all-gather | bytes 294912 | tf_op jit(solution)/shard_map/all_gather | solution.py:132
  40.5 14.2 %all_gather.13 = f32[1,128,512]{2,1,0:T(8,128)S(1)} all-gather(f32[1,16,512]{2,1,0:T(8,128)S(1)} %collective-permute-done.1), channel_id=1, replica_groups=mesh['gx'=4,'gy'=8] {'gy'}, dimensions={1}, use_global_device_ids=true | all-gather | bytes 294912 | tf_op jit(solution)/shard_map/all_gather | solution.py:131
  54.9 1.6 collective-permute-start.3
  58.0 1.1 collective-permute-done.3
  60.0 1.3 slice-done.1
  61.3 6.9 %add_multiply_fusion.1 = (f32[19,8,16,512]{3,2,0,1:T(8,128)}, f32[19,8,16,512]{3,2,0,1:T(8,128)S(1)}, f32[19,8,16,512]{3,2,0,1:T(8,128)S(1)}) fusion(f32[8,16,512]{2,1,0:T(8,128)S(1)} %get-tuple-element.7, f32[8,16,512]{2,1,0:T(8,128)S(1)} %get-tuple-element.12, f32[19]{0:T(128)S(1)} %copy-done.67, f32[8,16,512]{2,1,0:T(8,128)S(1)} %get-tuple-element.10, ...), kind=kLoop, calls=%fused_computation.9 | loop fusion | flops 37355520 | bytes 22806908 | tf_op jit(solution)/shard_map/mul | solution.py:72
  69.1 2.9 %slice_reduce_fusion = (f32[8,16,512]{2,1,0:T(8,128)S(1)}, f32[18,8,16,512]{3,2,0,1:T(8,128)}) fusion(f32[19,8,16,512]{3,2,0,1:T(8,128)S(1)} %get-tuple-element.99), kind=kLoop, calls=%fused_computation.378 | loop fusion | flops 1114112 | bytes 9699328 | tf_op jit(solution)/shard_map/reduce_sum | solution.py:90
  74.2 3.8 %fusion.1 = f32[19,8,16,512]{3,2,0,1:T(8,128)S(1)} fusion(f32[18,8,16,512]{3,2,0,1:T(8,128)} %get-tuple-element.96, f32[1,8,16,512]{3,2,0,1:T(8,128)S(1)} %subtract_bitcast_fusion, f32[19,8,16,512]{3,2,1,0:T(8,128)S(1)} %bitcast.412), kind=kLoop, calls=%fused_computation.5 | loop fusion | flops 4980736 | bytes 14942208 | tf_op jit(solution)/shard_map/sub | solution.py:106
  78.5 1.8 copy-done.39
  80.3 1.2 copy-done.40
  82.5 1.2 slice_bitcast_fusion.24
  85.7 1.9 scatter_fusion.1
  87.6 2.6 %collective-permute-start.5 = (f32[38,1,16,512]{3,2,0,1:T(8,128)S(1)}, f32[38,1,16,512]{3,2,0,1:T(8,128)S(1)}, u32[]{:S(2)}, u32[]{:S(2)}) collective-permute-start(f32[38,1,16,512]{3,2,0,1:T(8,128)S(1)} %bitcast.416), channel_id=1, source_target_pairs={{8,0},{16,8},{24,16},{0,24},{9,1},{17,9},{25,17},{1,25},{10,2},{18... | collective-permute-start | bytes 3735560 | tf_op jit(solution)/shard_map/ppermute | solution.py:48
  90.2 22.3 %collective-permute-done.5 = f32[38,1,16,512]{3,2,0,1:T(8,128)S(1)} collective-permute-done((f32[38,1,16,512]{3,2,0,1:T(8,128)S(1)}, f32[38,1,16,512]{3,2,0,1:T(8,128)S(1)}, u32[]{:S(2)}, u32[]{:S(2)}) %collective-permute-start.5) | collective-permute-done | bytes 1245216 | tf_op jit(solution)/shard_map/ppermute | solution.py:48
  113.5 1.3 fusion.64
  114.9 1.0 scatter_fusion
  115.9 2.2 collective-permute-start.4
  118.1 23.5 %collective-permute-done.4 = f32[38,1,16,512]{3,2,1,0:T(8,128)S(1)} collective-permute-done((f32[38,1,16,512]{3,2,1,0:T(8,128)S(1)}, f32[38,1,16,512]{3,2,1,0:T(8,128)S(1)}, u32[]{:S(2)}, u32[]{:S(2)}) %collective-permute-start.4) | collective-permute-done | bytes 1245216 | tf_op jit(solution)/shard_map/ppermute | solution.py:46
  142.5 1.1 slice_dynamic-update-slice_fusion.5
  143.6 1.3 slice_dynamic-update-slice_fusion.3
  144.9 1.3 slice_dynamic-update-slice_fusion.2
  146.2 1.1 slice_dynamic-update-slice_fusion.4
  147.4 1.3 slice_dynamic-update-slice_fusion.1
  148.7 1.3 slice_dynamic-update-slice_fusion
  150.6 10.1 %collective-permute-start.6 = (f32[20,8,1,512]{3,2,0,1:T(1,128)S(1)}, f32[20,8,1,512]{3,2,0,1:T(1,128)S(1)}, u32[]{:S(2)}, u32[]{:S(2)}) collective-permute-start(f32[20,8,1,512]{3,2,0,1:T(1,128)S(1)} %get-tuple-element.33), channel_id=1, source_target_pairs={{0,1},{1,2},{2,3},{3,4},{4,5},{5,6},{6,7},{7,0},{8,9},{9,10},{10,1... | collective-permute-start | bytes 983048 | tf_op jit(solution)/shard_map/ppermute | solution.py:46
  160.8 1.7 fusion.21
  162.4 2.4 slice_bitcast_fusion.34
  164.8 1.7 fusion.36
  169.6 2.4 slice_bitcast_fusion.40
  172.1 12.4 %collective-permute-done.7 = f32[20,8,1,512]{3,2,0,1:T(1,128)S(1)} collective-permute-done((f32[20,8,1,512]{3,2,0,1:T(1,128)S(1)}, f32[20,8,1,512]{3,2,0,1:T(1,128)S(1)}, u32[]{:S(2)}, u32[]{:S(2)}) %collective-permute-start.7) | collective-permute-done | bytes 327712 | tf_op jit(solution)/shard_map/ppermute | solution.py:48
  184.5 1.7 pad_maximum_fusion
  186.2 2.1 slice_bitcast_fusion.4
  204.4 1.1 slice.1398
  205.5 1.3 fusion.2
  206.8 1.3 fusion.77
  208.1 1.4 fusion.67
  209.5 1.1 slice.1352
  210.6 1.3 fusion.3
  213.4 1.7 fusion.49
  215.1 1.7 fusion.50
  219.2 1.8 fusion.52
  221.0 1.7 fusion.53
  237.8 0.9 fusion.9
  241.9 0.9 fusion.24
  (310 shorter events, 58.4 us)
Async XLA Ops:
  7.2 197.2 %all-gather.5.cloned.1.call-start = ((), (), s32[]{:S(2)}) async-start(), calls=%async_computation.1 | async-start | bytes 2949120 | tf_op jit(solution)/shard_map/all_gather | solution.py:132
  10.8 14.4 %collective-permute-start = (f32[1,16,512]{2,1,0:T(8,128)S(1)}, f32[1,16,512]{2,1,0:T(8,128)S(1)}, u32[]{:S(2)}, u32[]{:S(2)}) collective-permute-start(f32[1,16,512]{2,1,0:T(8,128)S(1)} %get-tuple-element.139), channel_id=1, source_target_pairs={{8,0},{16,8},{24,16},{0,24},{9,1},{17,9},{25,17},{1,25},{10,2},{18... | collective-permute-start | bytes 98312 | tf_op jit(solution)/shard_map/ppermute | solution.py:48
  13.8 26.7 %collective-permute-start.1 = (f32[1,16,512]{2,1,0:T(8,128)S(1)}, f32[1,16,512]{2,1,0:T(8,128)S(1)}, u32[]{:S(2)}, u32[]{:S(2)}) collective-permute-start(f32[1,16,512]{2,1,0:T(8,128)S(1)} %get-tuple-element.138), channel_id=1, source_target_pairs={{0,8},{8,16},{16,24},{24,0},{1,9},{9,17},{17,25},{25,1},{2,10},{10... | collective-permute-start | bytes 98312 | tf_op jit(solution)/shard_map/ppermute | solution.py:46
  17.7 42.3 %slice-start = ((s8[4980736]{0:T(1024)(128)(4,1)}), s8[786432]{0:T(1024)(128)(4,1)S(1)}, s32[]{:S(2)}) async-start(s8[4980736]{0:T(1024)(128)(4,1)} %bitcast.409), calls=%async_computation.2 | async-start | bytes 1572864
  54.7 3.3 %collective-permute-start.2 = (f32[10,1,512]{2,1,0:T(1,128)S(1)}, f32[10,1,512]{2,1,0:T(1,128)S(1)}, u32[]{:S(2)}, u32[]{:S(2)}) collective-permute-start(f32[10,1,512]{2,1,0:T(1,128)S(1)} %get-tuple-element.122), channel_id=1, source_target_pairs={{1,0},{2,1},{3,2},{4,3},{5,4},{6,5},{7,6},{0,7},{9,8},{10,9},{11,1... | collective-permute-start | bytes 61448 | tf_op jit(solution)/shard_map/ppermute | solution.py:48
  54.9 4.1 %collective-permute-start.3 = (f32[10,1,512]{2,1,0:T(1,128)S(1)}, f32[10,1,512]{2,1,0:T(1,128)S(1)}, u32[]{:S(2)}, u32[]{:S(2)}) collective-permute-start(f32[10,1,512]{2,1,0:T(1,128)S(1)} %get-tuple-element.123), channel_id=1, source_target_pairs={{0,1},{1,2},{2,3},{3,4},{4,5},{5,6},{6,7},{7,0},{8,9},{9,10},{10,1... | collective-permute-start | bytes 61448 | tf_op jit(solution)/shard_map/ppermute | solution.py:46
  68.2 14.0 %copy-start = (f32[19,8,16,512]{3,2,0,1:T(8,128)}, f32[19,8,16,512]{3,2,0,1:T(8,128)S(1)}, u32[]{:S(2)}) copy-start(f32[19,8,16,512]{3,2,0,1:T(8,128)S(1)} %get-tuple-element.98) | copy-start | bytes 14942212
  83.7 29.8 %copy-start.44 = (f32[16,512]{1,0:T(8,128)S(1)}, f32[16,512]{1,0:T(8,128)}, u32[]{:S(2)}) copy-start(f32[16,512]{1,0:T(8,128)} %get-tuple-element.161) | copy-start | bytes 98308
  83.7 29.8 %copy-start.45 = (f32[16,512]{1,0:T(8,128)S(1)}, f32[16,512]{1,0:T(8,128)}, u32[]{:S(2)}) copy-start(f32[16,512]{1,0:T(8,128)} %get-tuple-element.165) | copy-start | bytes 98308
  83.7 29.8 %copy-start.46 = (f32[16,512]{1,0:T(8,128)S(1)}, f32[16,512]{1,0:T(8,128)}, u32[]{:S(2)}) copy-start(f32[16,512]{1,0:T(8,128)} %get-tuple-element.166) | copy-start | bytes 98308
  83.7 29.8 %copy-start.58 = (f32[16,512]{1,0:T(8,128)S(1)}, f32[16,512]{1,0:T(8,128)}, u32[]{:S(2)}) copy-start(f32[16,512]{1,0:T(8,128)} %get-tuple-element.137) | copy-start | bytes 98308
  83.7 29.8 %copy-start.59 = (f32[16,512]{1,0:T(8,128)S(1)}, f32[16,512]{1,0:T(8,128)}, u32[]{:S(2)}) copy-start(f32[16,512]{1,0:T(8,128)} %get-tuple-element.125) | copy-start | bytes 98308
  83.7 29.8 %copy-start.70 = (f32[5]{0:T(128)S(1)}, f32[5]{0:T(128)}, u32[]{:S(2)}) copy-start(f32[5]{0:T(128)} %constant.172.clone) | copy-start | bytes 64
  83.7 29.8 %copy-start.71 = (f32[5]{0:T(128)S(1)}, f32[5]{0:T(128)}, u32[]{:S(2)}) copy-start(f32[5]{0:T(128)} %constant.173.clone) | copy-start | bytes 64
  84.0 30.9 %copy-start.69 = (s32[10]{0:T(128)S(1)}, s32[10]{0:T(128)}, u32[]{:S(2)}) copy-start(s32[10]{0:T(128)} %constant.188) | copy-start | bytes 124
  87.6 25.0 %collective-permute-start.5 = (f32[38,1,16,512]{3,2,0,1:T(8,128)S(1)}, f32[38,1,16,512]{3,2,0,1:T(8,128)S(1)}, u32[]{:S(2)}, u32[]{:S(2)}) collective-permute-start(f32[38,1,16,512]{3,2,0,1:T(8,128)S(1)} %bitcast.416), channel_id=1, source_target_pairs={{8,0},{16,8},{24,16},{0,24},{9,1},{17,9},{25,17},{1,25},{10,2},{18... | collective-permute-start | bytes 3735560 | tf_op jit(solution)/shard_map/ppermute | solution.py:48
  113.4 96.0 %all-gather.3.cloned.1.call-start = ((), (), s32[]{:S(2)}) async-start(), calls=%async_computation | async-start | bytes 2949120 | tf_op jit(solution)/shard_map/all_gather | solution.py:131
  115.9 25.7 %collective-permute-start.4 = (f32[38,1,16,512]{3,2,1,0:T(8,128)S(1)}, f32[38,1,16,512]{3,2,1,0:T(8,128)S(1)}, u32[]{:S(2)}, u32[]{:S(2)}) collective-permute-start(f32[38,1,16,512]{3,2,1,0:T(8,128)S(1)} %bitcast.415), channel_id=1, source_target_pairs={{0,8},{8,16},{16,24},{24,0},{1,9},{9,17},{17,25},{25,1},{2,10},{10... | collective-permute-start | bytes 3735560 | tf_op jit(solution)/shard_map/ppermute | solution.py:46
  146.2 20.3 %copy-start.2 = (f32[8,16,512]{2,1,0:T(8,128)S(1)}, f32[8,16,512]{2,1,0:T(8,128)}, u32[]{:S(2)}) copy-start(f32[8,16,512]{2,1,0:T(8,128)} %get-tuple-element.41) | copy-start | bytes 786436
  150.6 21.4 %collective-permute-start.6 = (f32[20,8,1,512]{3,2,0,1:T(1,128)S(1)}, f32[20,8,1,512]{3,2,0,1:T(1,128)S(1)}, u32[]{:S(2)}, u32[]{:S(2)}) collective-permute-start(f32[20,8,1,512]{3,2,0,1:T(1,128)S(1)} %get-tuple-element.33), channel_id=1, source_target_pairs={{0,1},{1,2},{2,3},{3,4},{4,5},{5,6},{6,7},{7,0},{8,9},{9,10},{10,1... | collective-permute-start | bytes 983048 | tf_op jit(solution)/shard_map/ppermute | solution.py:46
  160.8 23.7 %collective-permute-start.7 = (f32[20,8,1,512]{3,2,0,1:T(1,128)S(1)}, f32[20,8,1,512]{3,2,0,1:T(1,128)S(1)}, u32[]{:S(2)}, u32[]{:S(2)}) collective-permute-start(f32[20,8,1,512]{3,2,0,1:T(1,128)S(1)} %get-tuple-element.34), channel_id=1, source_target_pairs={{1,0},{2,1},{3,2},{4,3},{5,4},{6,5},{7,6},{0,7},{9,8},{10,9},{11,1... | collective-permute-start | bytes 983048 | tf_op jit(solution)/shard_map/ppermute | solution.py:48
  209.5 13.3 %copy-start.20 = (f32[7,16,512]{2,1,0:T(8,128)S(1)}, f32[7,16,512]{2,1,0:T(8,128)}, u32[]{:S(2)}) copy-start(f32[7,16,512]{2,1,0:T(8,128)} %slice.1485) | copy-start | bytes 688132
  209.5 13.3 %copy-start.56 = (f32[1,16,512]{2,1,0:T(8,128)S(1)}, f32[1,16,512]{2,1,0:T(8,128)}, u32[]{:S(2)}) copy-start(f32[1,16,512]{2,1,0:T(8,128)} %get-tuple-element.103) | copy-start | bytes 98308
  209.5 14.0 %copy-start.19 = (f32[7,16,512]{2,1,0:T(8,128)S(1)}, f32[7,16,512]{2,1,0:T(8,128)}, u32[]{:S(2)}) copy-start(f32[7,16,512]{2,1,0:T(8,128)} %slice.1491) | copy-start | bytes 688132
  210.6 13.6 %copy-start.18 = (f32[7,16,512]{2,1,0:T(8,128)S(1)}, f32[7,16,512]{2,1,0:T(8,128)}, u32[]{:S(2)}) copy-start(f32[7,16,512]{2,1,0:T(8,128)} %slice.1493) | copy-start | bytes 688132
  210.6 13.6 %copy-start.55 = (f32[1,16,512]{2,1,0:T(8,128)S(1)}, f32[1,16,512]{2,1,0:T(8,128)}, u32[]{:S(2)}) copy-start(f32[1,16,512]{2,1,0:T(8,128)} %get-tuple-element.105) | copy-start | bytes 98308
  210.6 14.3 %copy-start.25 = (f32[7,16,512]{2,1,0:T(8,128)S(1)}, f32[7,16,512]{2,1,0:T(8,128)}, u32[]{:S(2)}) copy-start(f32[7,16,512]{2,1,0:T(8,128)} %get-tuple-element.38) | copy-start | bytes 688132
  212.0 15.6 %copy-start.26 = (f32[7,16,512]{2,1,0:T(8,128)S(1)}, f32[7,16,512]{2,1,0:T(8,128)}, u32[]{:S(2)}) copy-start(f32[7,16,512]{2,1,0:T(8,128)} %get-tuple-element.49) | copy-start | bytes 688132
  212.0 16.3 %copy-start.24 = (f32[7,16,512]{2,1,0:T(8,128)S(1)}, f32[7,16,512]{2,1,0:T(8,128)}, u32[]{:S(2)}) copy-start(f32[7,16,512]{2,1,0:T(8,128)} %get-tuple-element.48) | copy-start | bytes 688132
  212.0 16.3 %copy-start.63 = (f32[1,16,512]{2,1,0:T(8,128)S(1)}, f32[1,16,512]{2,1,0:T(8,128)}, u32[]{:S(2)}) copy-start(f32[1,16,512]{2,1,0:T(8,128)} %get-tuple-element.119) | copy-start | bytes 98308
  213.4 16.3 %copy-start.3 = (f32[8,18,512]{2,1,0:T(8,128)S(1)}, f32[8,18,512]{2,1,0:T(8,128)}, u32[]{:S(2)}) copy-start(f32[8,18,512]{2,1,0:T(8,128)} %get-tuple-element.32) | copy-start | bytes 884740
  216.8 13.8 %copy-start.37 = (f32[8,16,1]{2,1,0:T(8,128)S(1)}, f32[8,16,1]{2,1,0:T(8,128)}, u32[]{:S(2)}) copy-start(f32[8,16,1]{2,1,0:T(8,128)} %slice.1414) | copy-start | bytes 1540
  217.5 14.0 %copy-start.9 = (f32[8,16,511]{2,1,0:T(8,128)S(1)}, f32[8,16,511]{2,1,0:T(8,128)}, u32[]{:S(2)}) copy-start(f32[8,16,511]{2,1,0:T(8,128)} %slice.1417) | copy-start | bytes 784900
  217.5 14.0 %copy-start.32 = (f32[8,16,1]{2,1,0:T(8,128)S(1)}, f32[8,16,1]{2,1,0:T(8,128)}, u32[]{:S(2)}) copy-start(f32[8,16,1]{2,1,0:T(8,128)} %slice.1418) | copy-start | bytes 1540
  218.4 13.9 %copy-start.17 = (f32[7,16,512]{2,1,0:T(8,128)S(1)}, f32[7,16,512]{2,1,0:T(8,128)}, u32[]{:S(2)}) copy-start(f32[7,16,512]{2,1,0:T(8,128)} %slice.1422) | copy-start | bytes 688132
  219.2 13.8 %copy-start.16 = (f32[7,16,512]{2,1,0:T(8,128)S(1)}, f32[7,16,512]{2,1,0:T(8,128)}, u32[]{:S(2)}) copy-start(f32[7,16,512]{2,1,0:T(8,128)} %slice.1424) | copy-start | bytes 688132
  219.2 13.8 %copy-start.54 = (f32[1,16,512]{2,1,0:T(8,128)S(1)}, f32[1,16,512]{2,1,0:T(8,128)}, u32[]{:S(2)}) copy-start(f32[1,16,512]{2,1,0:T(8,128)} %get-tuple-element.108) | copy-start | bytes 98308
  219.2 14.5 %copy-start.15 = (f32[7,16,512]{2,1,0:T(8,128)S(1)}, f32[7,16,512]{2,1,0:T(8,128)}, u32[]{:S(2)}) copy-start(f32[7,16,512]{2,1,0:T(8,128)} %slice.1430) | copy-start | bytes 688132
  221.0 13.4 %copy-start.14 = (f32[7,16,512]{2,1,0:T(8,128)S(1)}, f32[7,16,512]{2,1,0:T(8,128)}, u32[]{:S(2)}) copy-start(f32[7,16,512]{2,1,0:T(8,128)} %slice.1432) | copy-start | bytes 688132
  221.0 13.4 %copy-start.53 = (f32[1,16,512]{2,1,0:T(8,128)S(1)}, f32[1,16,512]{2,1,0:T(8,128)}, u32[]{:S(2)}) copy-start(f32[1,16,512]{2,1,0:T(8,128)} %get-tuple-element.106) | copy-start | bytes 98308
  222.7 12.5 %copy-start.23 = (f32[7,16,512]{2,1,0:T(8,128)S(1)}, f32[7,16,512]{2,1,0:T(8,128)}, u32[]{:S(2)}) copy-start(f32[7,16,512]{2,1,0:T(8,128)} %get-tuple-element.47) | copy-start | bytes 688132
  229.7 12.2 %copy-start.62 = (f32[1,16,512]{2,1,0:T(8,128)S(1)}, f32[1,16,512]{2,1,0:T(8,128)}, u32[]{:S(2)}) copy-start(f32[1,16,512]{2,1,0:T(8,128)} %get-tuple-element.118) | copy-start | bytes 98308
  230.5 12.3 %copy-start.8 = (f32[8,16,511]{2,1,0:T(8,128)S(1)}, f32[8,16,511]{2,1,0:T(8,128)}, u32[]{:S(2)}) copy-start(f32[8,16,511]{2,1,0:T(8,128)} %slice.1453) | copy-start | bytes 784900
  230.5 12.3 %copy-start.31 = (f32[8,16,1]{2,1,0:T(8,128)S(1)}, f32[8,16,1]{2,1,0:T(8,128)}, u32[]{:S(2)}) copy-start(f32[8,16,1]{2,1,0:T(8,128)} %slice.1452) | copy-start | bytes 1540
  230.6 13.1 %copy-start.7 = (f32[8,16,511]{2,1,0:T(8,128)S(1)}, f32[8,16,511]{2,1,0:T(8,128)}, u32[]{:S(2)}) copy-start(f32[8,16,511]{2,1,0:T(8,128)} %slice.1455) | copy-start | bytes 784900
  230.6 13.0 %copy-start.30 = (f32[8,16,1]{2,1,0:T(8,128)S(1)}, f32[8,16,1]{2,1,0:T(8,128)}, u32[]{:S(2)}) copy-start(f32[8,16,1]{2,1,0:T(8,128)} %slice.1456) | copy-start | bytes 1540
  231.5 13.0 %copy-start.6 = (f32[8,16,511]{2,1,0:T(8,128)S(1)}, f32[8,16,511]{2,1,0:T(8,128)}, u32[]{:S(2)}) copy-start(f32[8,16,511]{2,1,0:T(8,128)} %slice.1458) | copy-start | bytes 784900
  231.5 13.0 %copy-start.29 = (f32[8,16,1]{2,1,0:T(8,128)S(1)}, f32[8,16,1]{2,1,0:T(8,128)}, u32[]{:S(2)}) copy-start(f32[8,16,1]{2,1,0:T(8,128)} %slice.1459) | copy-start | bytes 1540
  (45 other events, 263.9 us)
Sparse Core Ops, SparseCore 0:
  113.5 40.1 all-gather.4
  155.4 38.4 all-gather.2
where the time goes:
time: 255 us; the launch traced here: 253 us
  other arithmetic  66.6 us (26%)
  local copies, waits for them, and re-layouts  59.6 us (23%)
  waiting for transfers between devices  59.5 us (23%)
  blocking collectives  29.4 us (12%)
  starting transfers between devices  19.8 us (8%)
  between operations  18 us (7%)
    ppermute x4, waiting for transfers between devices, extended(): lax.ppermute(head, axis, [((i + 1) % count, i) for i in range(count)])  34.9 us
    unnamed x33, other arithmetic  27.3 us
    ppermute x4, waiting for transfers between devices, extended(): lax.ppermute(tail, axis, [(i, (i + 1) % count) for i in range(count)])  24.6 us
    unnamed x211, local copies, waits for them, and re-layouts  22 us
    all_gather x1, blocking collectives, plane_windows(): lax.all_gather(up_piece, 'gy', axis=1, tiled=True)  15.2 us
    all_gather x1, blocking collectives, plane_windows(): lax.all_gather(low_piece, 'gy', axis=1, tiled=True)  14.2 us
    ppermute x4, starting transfers between devices, extended(): lax.ppermute(tail, axis, [(i, (i + 1) % count) for i in range(count)])  13.9 us
    slice x22, local copies, waits for them, and re-layouts, stream(): arrived_list.append(jnp.roll(shifted, step_z, 2))  13.5 us
  transfers between devices with their start and end apart: 10, of which 5 were waited for; matrix products, arithmetic and copies ran while one was open for 22% of the time, Pallas kernels for 0%

commit v1 on v0

v1 whole, which is shorter than its diff:
```python
import jax
import jax.numpy as jnp
from jax import lax
from jax.experimental import pallas as pl
from jax.experimental.pallas import tpu as pltpu
from jax.sharding import PartitionSpec as P

lattice_velocity = [
    (0, 0, 0),
    (1, 0, 0),
    (-1, 0, 0),
    (0, 1, 0),
    (0, -1, 0),
    (0, 0, 1),
    (0, 0, -1),
    (1, 1, 0),
    (-1, -1, 0),
    (1, -1, 0),
    (-1, 1, 0),
    (1, 0, 1),
    (-1, 0, -1),
    (1, 0, -1),
    (-1, 0, 1),
    (0, 1, 1),
    (0, -1, -1),
    (0, 1, -1),
    (0, -1, 1),
]
lattice_weight = [1.0 / 3.0] + [1.0 / 18.0] * 6 + [1.0 / 36.0] * 12
plane_speed = 0.04
rising = [1, 7, 9, 11, 13]
falling = [2, 8, 10, 12, 14]
north_going = [i for i in range(19) if lattice_velocity[i][1] == 1]
south_going = [i for i in range(19) if lattice_velocity[i][1] == -1]
f32 = jnp.float32
VMEM = pltpu.VMEM
LANES = 128


def spec_of(space):
    return pl.BlockSpec(memory_space=space)


def params(limit):
    return pltpu.CompilerParams(vmem_limit_bytes=limit)


def along(parts, c):
    total = None
    for sign, part in zip(c, parts):
        if sign == 0:
            continue
        if total is None:
            total = part if sign > 0 else -part
        else:
            total = total + part if sign > 0 else total - part
    return total


def signed_sum(load, axis):
    ups = [i for i in range(19) if lattice_velocity[i][axis] == 1]
    downs = [i for i in range(19) if lattice_velocity[i][axis] == -1]
    total = load(ups[0]) - load(downs[0])
    for i, j in zip(ups[1:], downs[1:]):
        total = total + (load(i) - load(j))
    return total


class Site:
    def __init__(self, load, phi, minus, plus, south, north, lower, upper):
        rho = load(0)
        for i in range(1, 19):
            rho = rho + load(i)
        momentum = [signed_sum(load, axis) for axis in range(3)]
        lap = (plus + minus) + (north + south) + (upper + lower) - 6.0 * phi
        mu = phi * (0.0625 * (phi * phi) - 0.0625) - 0.04 * lap
        half_mu = 0.5 * mu
        force = [half_mu * (plus - minus), half_mu * (north - south), half_mu * (upper - lower)]
        inverse = 1.0 / rho
        u = [(j + 0.5 * k) * inverse for j, k in zip(momentum, force)]
        uu = u[0] * u[0] + u[1] * u[1] + u[2] * u[2]
        uf = u[0] * force[0] + u[1] * force[1] + u[2] * force[2]
        self.rho, self.phi, self.mu, self.u, self.force, self.uu = rho, phi, mu, u, force, uu
        self.r = 1.25 * rho
        self.k = self.r * (1.0 - 1.5 * uu) - 1.125 * uf
        self.g_scale = phi * (1.0 / 0.9)
        self.g_base = (3.0 / 0.9) * mu - 1.5 * (self.g_scale * uu)

    def pair_f(self, i):
        p, q = along(self.u, lattice_velocity[i]), along(self.force, lattice_velocity[i])
        w = lattice_weight[i]
        rp = self.r * p
        even = w * (self.k + p * (4.5 * rp + 3.375 * q))
        odd = (3.0 * w) * rp + (1.125 * w) * q
        return even, odd

    def pair_g(self, i):
        p = along(self.u, lattice_velocity[i])
        w = lattice_weight[i]
        gp = self.g_scale * p
        return w * (self.g_base + 4.5 * (gp * p)), (3.0 * w) * gp

    def jump(self, i, delta):
        cy = lattice_velocity[i][1]
        uy = self.u[1]
        if cy == 0:
            return delta * (-3.0 * uy) - (1.5 * delta * delta)
        p = along(self.u, lattice_velocity[i])
        return delta * (3.0 * cy + (9.0 * cy) * p - 3.0 * uy) + (3.0 * delta * delta)


def z_moved(value, step):
    if step == 0:
        return value
    return pltpu.roll(value, step % value.shape[-1], value.ndim - 1)


class Shear:
    def __init__(self, raw, wide, rows):
        self.raw, self.wide, self.rows = raw, wide, rows

    def clear(self):
        self.raw[...] = jnp.zeros_like(self.raw)
        self.wide[...] = jnp.zeros_like(self.wide)

    def put(self, value, up, near, far):
        n = self.rows
        for k in range(self.raw.shape[0]):
            self.raw[k, 8 : 8 + n] = value[:, LANES * k : LANES * k + LANES]
        for k in range(self.raw.shape[0]):
            if up:
                self.wide[k, n : n + n + 8] = (
                    near * self.raw[k, 0 : n + 8] + far * self.raw[k, 1 : n + 9]
                )
            else:
                self.wide[k, n + 8 : n + n + 16] = (
                    near * self.raw[k, 7 : n + 15] + far * self.raw[k, 8 : n + 16]
                )

    def take(self, up, block, rest, cy, store):
        n = self.rows
        if up:
            start = (n + 8 if block == 0 else 8) + rest - cy
        else:
            start = (n + 8 if block == 0 else n + n + 8) - rest - cy
        for k in range(self.raw.shape[0]):
            store(k, self.wide[k, pl.ds(start, n)])


def lane_store(ref, lead):
    def store(k, value):
        ref[(*lead, slice(None), slice(LANES * k, LANES * k + LANES))] = value

    return store


def shear_scratch(rows, cols):
    return [
        VMEM((cols // LANES, rows + 16, LANES), f32),
        VMEM((cols // LANES, 3 * rows + 16, LANES), f32),
    ]


def phi_kernel(
    ints, floats, g_ref, phi_ref, ra, rb, fa, fb, north, south, buf, sems, raw, wide
):
    layers, rows = buf.shape[1], buf.shape[2]
    order = [layers - 1, 0] + list(range(1, layers - 1))
    copies = {
        x: pltpu.make_async_copy(g_ref.at[:, pl.ds(x, 1)], buf.at[:, pl.ds(x, 1)], sems.at[x])
        for x in order
    }
    for x in order:
        copies[x].start()
    shear = Shear(raw, wide, rows)
    shear.clear()
    for x in order:
        copies[x].wait()
        total = buf[0, x]
        for i in range(1, 19):
            total = total + buf[i, x]
        phi_ref[x] = total
        north[x : x + 1] = total[rows - 1 : rows]
        south[x : x + 1] = total[0:1]
        if x == layers - 1:
            shear.put(total, True, floats[0], floats[1])
            shear.take(True, 0, ints[0], 0, lane_store(ra, ()))
            shear.take(True, 1, ints[0], 0, lane_store(rb, ()))
        if x == 0:
            shear.clear()
            shear.put(total, False, floats[2], floats[3])
            shear.take(False, 0, ints[1], 0, lane_store(fa, ()))
            shear.take(False, 1, ints[1], 0, lane_store(fb, ()))


def with_halo(ref, layer, below, above):
    rows = layer.shape[0]
    ref[8 : 8 + rows] = layer
    ref[7:8] = below
    ref[8 + rows : 9 + rows] = above


def face_kernel(
    ints,
    floats,
    f_ref,
    g_ref,
    phi_ref,
    ra,
    rb,
    fa,
    fb,
    from_south,
    from_north,
    mate,
    direct,
    across,
    joint,
    corner_near_up,
    corner_far_up,
    corner_near_low,
    corner_far_low,
    fbuf,
    gbuf,
    sems,
    halo,
    post,
    raw,
    wide,
):
    layers, rows, cols = phi_ref.shape
    faces = (layers - 1, 0)
    copies = []
    for s, x in enumerate(faces):
        copies.append(
            (
                pltpu.make_async_copy(f_ref.at[:, pl.ds(x, 1)], fbuf.at[:, pl.ds(s, 1)], sems.at[s, 0]),
                pltpu.make_async_copy(g_ref.at[:, pl.ds(x, 1)], gbuf.at[:, pl.ds(s, 1)], sems.at[s, 1]),
            )
        )
    for pair in copies:
        for copy in pair:
            copy.start()
    shear = Shear(raw, wide, rows)
    odd = ints[2] == 1
    for s, x in enumerate(faces):
        up = s == 0
        phi = phi_ref[x]
        with_halo(halo, phi, from_south[x : x + 1], from_north[x : x + 1])
        delta = floats[4] if up else floats[5]
        near, far = (floats[0], floats[1]) if up else (floats[2], floats[3])
        rest = ints[0] if up else ints[1]
        for copy in copies[s]:
            copy.wait()
        for h in range(0, rows, 8):
            span = slice(h, h + 8)
            phi_h = phi_ref[x, span]
            if up:
                minus, plus = phi_ref[x - 1, span], fa[span] + fb[span]
            else:
                minus, plus = ra[span] + rb[span], phi_ref[x + 1, span]
            site = Site(
                lambda i: fbuf[i, s, span],
                phi_h,
                minus,
                plus,
                halo[7 + h : 15 + h],
                halo[9 + h : 17 + h],
                z_moved(phi_h, 1),
                z_moved(phi_h, -1),
            )
            for j in range(5):
                i = rising[j] if up else falling[j]
                w = lattice_weight[i]
                change = w * site.jump(i, delta)
                even, odd_part = site.pair_f(i)
                value = even + odd_part - 0.25 * fbuf[i, s, span] + site.rho * change
                post[j, span] = z_moved(value, lattice_velocity[i][2])
                even, odd_part = site.pair_g(i)
                value = even + odd_part - (1.0 / 9.0) * gbuf[i, s, span] + phi_h * change
                post[5 + j, span] = z_moved(value, lattice_velocity[i][2])
        shear.clear()
        for j in range(10):
            i = (rising if up else falling)[j % 5]
            cy = lattice_velocity[i][1]
            shear.put(post[j], up, near, far)

            @pl.when(odd)
            def _():
                shear.take(up, 0, rest, cy, lane_store(direct if up else joint, (j,)))
                shear.take(up, 1, rest, cy, lane_store(mate if up else across, (j,)))

            @pl.when(jnp.logical_not(odd))
            def _():
                shear.take(up, 0, rest, cy, lane_store(joint if up else direct, (j,)))
                shear.take(up, 1, rest, cy, lane_store(across if up else mate, (j,)))

            slot = j // 5
            if cy == 1:
                gate = jnp.where(rest == (0 if up else rows - 1), near, 0.0)
                target = corner_near_up if up else corner_near_low
                target[slot : slot + 1] = gate * post[j, rows - 1 : rows]
            if cy == -1:
                gate = jnp.where(rest == (rows - 1 if up else 0), far, 0.0)
                target = corner_far_up if up else corner_far_low
                target[slot : slot + 1] = gate * post[j, 0:1]


def bulk_kernel(
    after,
    f_ref,
    g_ref,
    phi_ref,
    ra,
    rb,
    fa,
    fb,
    from_south,
    from_north,
    next_f,
    next_g,
    north,
    south,
    wide_phi,
    halo,
):
    layers, rows, cols = phi_ref.shape
    wide_phi[0] = ra[...] + rb[...]
    wide_phi[layers + 1] = fa[...] + fb[...]
    for x in range(layers):
        wide_phi[x + 1] = phi_ref[x]

    def layer(x, carry):
        with_halo(halo, phi_ref[x], from_south[pl.ds(x, 1)], from_north[pl.ds(x, 1)])
        beyond = lax.rem(x + 1, layers)
        before = lax.rem(x + layers - 1, layers)
        for h in range(0, rows, 8):
            span = slice(h, h + 8)
            phi_h = phi_ref[x, span]
            site = Site(
                lambda i: f_ref[i, x, span],
                phi_h,
                wide_phi[x, span],
                wide_phi[x + 2, span],
                halo[7 + h : 15 + h],
                halo[9 + h : 17 + h],
                z_moved(phi_h, 1),
                z_moved(phi_h, -1),
            )

            def emit(out, slot, i, value):
                cx, cy, cz = lattice_velocity[i]
                value = z_moved(value, cz)
                at = beyond if cx == 1 else before if cx == -1 else x
                if cy == 0:
                    out[i, at, span] = value
                elif cy == 1:
                    if h + 8 < rows:
                        out[i, at, h + 1 : h + 9] = value
                    else:
                        out[i, at, h + 1 : h + 8] = value[0:7]
                        north[slot * 5 + north_going.index(i), pl.ds(x, 1)] = value[7:8]
                else:
                    if h > 0:
                        out[i, at, h - 1 : h + 7] = value
                    else:
                        out[i, at, 0:7] = value[1:8]
                        south[slot * 5 + south_going.index(i), pl.ds(x, 1)] = value[0:1]

            emit(next_f, 0, 0, lattice_weight[0] * site.k - 0.25 * f_ref[0, x, span])
            rest_g = (phi_h - 2.0 * site.mu - 0.5 * (phi_h * site.uu)) * (1.0 / 0.9)
            emit(next_g, 1, 0, rest_g - (1.0 / 9.0) * g_ref[0, x, span])
            for i in range(1, 19, 2):
                even, odd = site.pair_f(i)
                emit(next_f, 0, i, (even + odd) - 0.25 * f_ref[i, x, span])
                emit(next_f, 0, i + 1, (even - odd) - 0.25 * f_ref[i + 1, x, span])
                even, odd = site.pair_g(i)
                emit(next_g, 1, i, (even + odd) - (1.0 / 9.0) * g_ref[i, x, span])
                emit(next_g, 1, i + 1, (even - odd) - (1.0 / 9.0) * g_ref[i + 1, x, span])
        return carry

    lax.fori_loop(0, layers, layer, 0)


def rim_kernel(from_south, from_north, f_in, g_in, f_out, g_out, buf, sems):
    layers, rows = f_out.shape[1], f_out.shape[2]
    jobs = []
    for side, (chosen, recv) in enumerate(((north_going, from_south), (south_going, from_north))):
        first = 0 if side == 0 else rows - 8
        for family, out in enumerate((f_out, g_out)):
            for j, i in enumerate(chosen):
                slot = side * 10 + family * 5 + j
                tile = out.at[i, :, pl.ds(first, 8)]
                jobs.append((slot, i, side, recv, family * 5 + j, tile))
    for slot, i, side, recv, row, tile in jobs:
        pltpu.make_async_copy(tile, buf.at[slot], sems.at[slot]).start()
    for slot, i, side, recv, row, tile in jobs:
        pltpu.make_async_copy(tile, buf.at[slot], sems.at[slot]).wait()
        cx = lattice_velocity[i][0]
        at = 0 if side == 0 else 7
        for x in range(layers):
            if 0 <= x + cx < layers:
                buf[slot, x + cx, at : at + 1] = recv[row, x : x + 1]
        pltpu.make_async_copy(buf.at[slot], tile, sems.at[slot]).start()
    for slot, i, side, recv, row, tile in jobs:
        pltpu.make_async_copy(buf.at[slot], tile, sems.at[slot]).wait()


def face_fill_kernel(
    ints,
    direct,
    across,
    joint,
    near_up,
    far_up,
    near_low,
    far_low,
    f_in,
    g_in,
    f_out,
    g_out,
    low,
    high,
    sems,
):
    layers, rows = f_out.shape[1], f_out.shape[2]
    odd = ints[2] == 1

    @pl.when(odd)
    def _():
        low[...] = direct[...] + across[...]
        high[...] = joint[...]

    @pl.when(jnp.logical_not(odd))
    def _():
        low[...] = joint[...]
        high[...] = direct[...] + across[...]

    copies = []
    for family, out in enumerate((f_out, g_out)):
        for j in range(5):
            slot = family * 5 + j
            for buf, chosen, near, far, x in (
                (low, rising, near_up, far_up, 0),
                (high, falling, near_low, far_low, layers - 1),
            ):
                cy = lattice_velocity[chosen[j]][1]
                if cy == 1:
                    buf[slot, 0:1] = buf[slot, 0:1] + near[family : family + 1]
                if cy == -1:
                    buf[slot, rows - 1 : rows] = buf[slot, rows - 1 : rows] + far[family : family + 1]
                copy = pltpu.make_async_copy(
                    buf.at[slot], out.at[chosen[j], x], sems.at[0 if x == 0 else 1, slot]
                )
                copy.start()
                copies.append(copy)
    for copy in copies:
        copy.wait()


def on_device(momentum_dist, order_dist, offsets):
    layers, rows, cols = momentum_dist.shape[1:]
    count_x, count_y = lax.axis_size("gx"), lax.axis_size("gy")
    per_plane = count_x // 4
    half = count_y // 2
    a, c = lax.axis_index("gx"), lax.axis_index("gy")

    def plane_of(column):
        is_plane = column % per_plane == 0
        plane = column // per_plane % 4
        rest = jnp.where(is_plane, jnp.clip(offsets[plane] - half * rows, 0, rows - 1), 0)
        return is_plane, (2.0 * plane.astype(f32) + 1.0) / 8.0, rest

    up_is, up_part, up_rest = plane_of((a + 1) % count_x)
    low_is, low_part, low_rest = plane_of(a)
    ints = jnp.stack([up_rest, low_rest, c % 2]).astype(jnp.int32)
    floats = jnp.stack(
        [
            jnp.where(up_is, 1.0 - up_part, 1.0),
            jnp.where(up_is, up_part, 0.0),
            jnp.where(low_is, low_part, 0.0),
            jnp.where(low_is, 1.0 - low_part, 1.0),
            jnp.where(up_is, -plane_speed, 0.0),
            jnp.where(low_is, plane_speed, 0.0),
        ]
    ).astype(f32)

    def hop(value, target):
        perm = []
        for x in range(count_x):
            for y in range(count_y):
                tx, ty = target(x, y)
                perm.append((x * count_y + y, tx % count_x * count_y + ty % count_y))
        return lax.ppermute(value, ("gx", "gy"), perm)

    def base_up(x):
        return half if (x + 1) % per_plane == 0 else 0

    def base_low(x):
        return half if x % per_plane == 0 else 0

    def hop_up(value, extra):
        return hop(value, lambda x, y: (x + 1, y - base_up(x) - extra))

    def hop_low(value, extra):
        return hop(value, lambda x, y: (x - 1, y + base_low(x) + extra))

    def hop_parity(value, odd_up, extra):
        def target(x, y):
            if (y % 2 == 1) == odd_up:
                return (x + 1, y - base_up(x) - extra)
            return (x - 1, y + base_low(x) + extra)

        return hop(value, target)

    def hop_y(value, step):
        return hop(value, lambda x, y: (x, y + step))

    smem, vmem, hbm = spec_of(pltpu.SMEM), spec_of(VMEM), spec_of(pl.ANY)
    plane = jax.ShapeDtypeStruct((rows, cols), f32)
    edge = jax.ShapeDtypeStruct((layers, cols), f32)
    phi, ra, rb, fa, fb, to_north, to_south = pl.pallas_call(
        phi_kernel,
        out_shape=[jax.ShapeDtypeStruct((layers, rows, cols), f32)] + [plane] * 4 + [edge] * 2,
        in_specs=[smem, smem, hbm],
        out_specs=[vmem] * 7,
        scratch_shapes=[
            VMEM((19, layers, rows, cols), f32),
            pltpu.SemaphoreType.DMA((layers,)),
            *shear_scratch(rows, cols),
        ],
        compiler_params=params(24 << 20),
        name="order_field",
    )(ints, floats, order_dist)

    ra, rb = hop_up(ra, 0), hop_up(rb, 1)
    fa, fb = hop_low(fa, 0), hop_low(fb, 1)
    phi_south, phi_north = hop_y(to_north, 1), hop_y(to_south, -1)
    field_parts = (phi, ra, rb, fa, fb, phi_south, phi_north)

    ten = jax.ShapeDtypeStruct((10, rows, cols), f32)
    two = jax.ShapeDtypeStruct((2, cols), f32)
    mate, direct, across, joint, near_up, far_up, near_low, far_low = pl.pallas_call(
        face_kernel,
        out_shape=[ten] * 4 + [two] * 4,
        in_specs=[smem, smem, hbm, hbm] + [vmem] * 7,
        out_specs=[vmem] * 8,
        scratch_shapes=[
            VMEM((19, 2, rows, cols), f32),
            VMEM((19, 2, rows, cols), f32),
            pltpu.SemaphoreType.DMA((2, 2)),
            VMEM((rows + 16, cols), f32),
            VMEM((10, rows, cols), f32),
            *shear_scratch(rows, cols),
        ],
        compiler_params=params(24 << 20),
        name="faces",
    )(ints, floats, momentum_dist, order_dist, *field_parts)

    mate = hop(mate, lambda x, y: (x, y ^ 1))
    direct = hop_parity(direct, True, 0)
    across = hop_parity(across, False, 1)
    near_up, far_up = hop_up(near_up, -1), hop_up(far_up, 2)
    near_low, far_low = hop_low(near_low, 2), hop_low(far_low, -1)
    joint = joint + mate
    after = joint
    joint = hop_parity(joint, False, 0)

    side = jax.ShapeDtypeStruct((10, layers, cols), f32)
    whole = jax.ShapeDtypeStruct(momentum_dist.shape, f32)
    next_f, next_g, to_north, to_south = pl.pallas_call(
        bulk_kernel,
        out_shape=[whole, whole, side, side],
        in_specs=[hbm] + [vmem] * 9,
        out_specs=[vmem] * 4,
        scratch_shapes=[
            VMEM((layers + 2, rows, cols), f32),
            VMEM((rows + 16, cols), f32),
        ],
        compiler_params=params(48 << 20),
        name="bulk",
    )(after, momentum_dist, order_dist, *field_parts)
    from_south, from_north = hop_y(to_north, 1), hop_y(to_south, -1)

    next_f, next_g = pl.pallas_call(
        rim_kernel,
        out_shape=[whole, whole],
        in_specs=[vmem, vmem, hbm, hbm],
        out_specs=[hbm, hbm],
        scratch_shapes=[VMEM((20, layers, 8, cols), f32), pltpu.SemaphoreType.DMA((20,))],
        input_output_aliases={2: 0, 3: 1},
        compiler_params=params(24 << 20),
        name="y_rims",
    )(from_south, from_north, next_f, next_g)

    return pl.pallas_call(
        face_fill_kernel,
        out_shape=[whole, whole],
        in_specs=[smem] + [vmem] * 7 + [hbm, hbm],
        out_specs=[hbm, hbm],
        scratch_shapes=[
            VMEM((10, rows, cols), f32),
            VMEM((10, rows, cols), f32),
            pltpu.SemaphoreType.DMA((2, 10)),
        ],
        input_output_aliases={8: 0, 9: 1},
        compiler_params=params(24 << 20),
        name="x_faces",
    )(ints, direct, across, joint, near_up, far_up, near_low, far_low, next_f, next_g)


def solution(mesh):
    return jax.shard_map(
        on_device,
        mesh=mesh,
        in_specs=(P(None, "gx", "gy", None), P(None, "gx", "gy", None), P()),
        out_specs=(P(None, "gx", "gy", None), P(None, "gx", "gy", None)),
        check_vma=False,
    )
```

time: 255 us -> 80.5 us (0.32)
  other arithmetic: 66.6 us -> 0.13 us
  local copies, waits for them, and re-layouts: 59.6 us -> 3.83 us
  waiting for transfers between devices: 59.5 us -> 24.3 us
  blocking collectives: 29.4 us -> 0 us
  Pallas kernels: 0 us -> 19 us
  between operations: 18 us -> 2.08 us
  starting transfers between devices: 19.8 us -> 30.9 us
    ppermute x8 -> x16, waiting for transfers between devices: 59.5 us -> 24.3 us  [hop(): return lax.ppermute(value, ('gx', 'gy'), perm)]
    all_gather x2 -> x0, blocking collectives: 29.4 us -> none  [the longest x1 15.2 us: plane_windows(): lax.all_gather(up_piece, 'gy', axis=1, tiled=True)]
    unnamed x33 -> x0, other arithmetic: 27.3 us -> none
    slice x40 -> x0, local copies, waits for them, and re-layouts: 27.1 us -> none  [the longest x22 13.5 us: stream(): arrived_list.append(jnp.roll(shifted, step_z, 2))]
    unnamed x211 -> x4, local copies, waits for them, and re-layouts: 22 us -> 2.42 us
    pallas_call x0 -> x5, Pallas kernels: none -> 19 us  [the longest x1 11.4 us: on_device(): pl.pallas_call(bulk_kernel, out_shape=[whole, whole, side, side], in_spec...]
    reduce_sum x4 -> x0, other arithmetic: 12.4 us -> none  [the longest x1 3.61 us: collide(): jnp.sum(directions[axis_place] * momentum, axis=0)]
    ppermute x8 -> x16, starting transfers between devices: 19.8 us -> 30.9 us  [hop(): return lax.ppermute(value, ('gx', 'gy'), perm)]
  transfers between devices with their start and end apart: 10 -> 16, of which waited for: 5 -> 4; matrix products, arithmetic and copies ran while one was open for 22% -> 0% of each run, Pallas kernels for 0% -> 17%
where the time goes in v1:
time: 80.5 us; the launch traced here: 80.3 us
  starting transfers between devices  30.9 us (38%)
  waiting for transfers between devices  24.3 us (30%)
  Pallas kernels  19 us (24%)
  local copies, waits for them, and re-layouts  3.83 us (5%)
  between operations  2.08 us (3%)
    ppermute x16, starting transfers between devices, hop(): return lax.ppermute(value, ('gx', 'gy'), perm)  30.9 us
    ppermute x16, waiting for transfers between devices, hop(): return lax.ppermute(value, ('gx', 'gy'), perm)  24.3 us
    pallas_call x1, Pallas kernels, on_device(): pl.pallas_call(bulk_kernel, out_shape=[whole, whole, side, side], in_spec...  11.4 us
    pallas_call x1, Pallas kernels, on_device(): pl.pallas_call(rim_kernel, out_shape=[whole, whole], in_specs=[vmem, vmem...  2.64 us
    unnamed x4, local copies, waits for them, and re-layouts  2.42 us
    pallas_call x1, Pallas kernels, on_device(): pl.pallas_call(face_kernel, out_shape=[ten] * 4 + [two] * 4, in_specs=[sm...  1.98 us
  transfers between devices with their start and end apart: 16, of which 4 were waited for; matrix products, arithmetic and copies ran while one was open for 0% of the time, Pallas kernels for 17%

profile of v1, /device:TPU:1, one launch (start us, length us, event | category | flops | bytes accessed | tf_op | source)
XLA Modules:
  0.0 80.3 jit_solution(11812146563672623760)
XLA Ops:
  0.7 1.3 %fusion = (s32[1]{0:T(128)}, s32[1]{0:T(128)}) fusion(s32[4]{0:T(128)} %param.5, s32[]{:T(128)S(6)} %select_n.45, s32[]{:T(128)S(6)} %select_n.47), kind=kLoop, calls=%fused_computation.1 | loop fusion | bytes 24 | tf_op jit(solution)/shard_map/dynamic_slice | solution.py:471
  3.3 0.1 pad_add_fusion.ints
  3.4 0.1 stack.31.floats
  3.5 0.0 copy-start
  3.5 2.4 %copy-done = f32[19,8,16,512]{3,2,1,0:T(8,128)S(1)} copy-done((f32[19,8,16,512]{3,2,1,0:T(8,128)S(1)}, f32[19,8,16,512]{3,2,1,0:T(8,128)}, u32[]{:S(2)}) %copy-start) | copy-done | bytes 4980760
  5.9 0.0 copy-start.1
  5.9 1.3 %order_field.1 = (f32[8,16,512]{2,1,0:T(8,128)S(1)}, f32[16,512]{1,0:T(8,128)S(1)}, f32[16,512]{1,0:T(8,128)S(1)}, f32[16,512]{1,0:T(8,128)S(1)}, f32[16,512]{1,...) custom-call(s32[3]{0:T(128)S(1)} %pad_add_fusion.ints, f32[6]{0:T(128)S(1)} %stack.31.floats, ...), custom_call_target="tpu_custom_call" | custom-call | tf_op jit(solution)/shard_map/order_field/pallas_call | solution.py:522
  7.2 2.7 %collective-permute-start.4 = (f32[8,512]{1,0:T(8,128)S(1)}, f32[8,512]{1,0:T(8,128)S(1)}, u32[]{:S(2)}, u32[]{:S(2)}) collective-permute-start(f32[8,512]{1,0:T(8,128)S(1)} %get-tuple-element.28), channel_id=1, source_target_pairs={{0,1},{1,2},{2,3},{3,4},{4,5},{5,6},{6,7},{7,0},{8,9},{9,10},{10,1... | collective-permute-start | bytes 49160 | tf_op jit(solution)/shard_map/ppermute | solution.py:494
  10.0 3.2 %collective-permute-start = (f32[16,512]{1,0:T(8,128)S(1)}, f32[16,512]{1,0:T(8,128)S(1)}, u32[]{:S(2)}, u32[]{:S(2)}) collective-permute-start(f32[16,512]{1,0:T(8,128)S(1)} %get-tuple-element.24), channel_id=1, source_target_pairs={{0,12},{1,13},{2,14},{3,15},{4,8},{5,9},{6,10},{7,11},{8,20},{9,21... | collective-permute-start | bytes 98312 | tf_op jit(solution)/shard_map/ppermute | solution.py:494
  13.2 0.0 collective-permute-start.1
  13.3 3.2 %collective-permute-start.2 = (f32[16,512]{1,0:T(8,128)S(1)}, f32[16,512]{1,0:T(8,128)S(1)}, u32[]{:S(2)}, u32[]{:S(2)}) collective-permute-start(f32[16,512]{1,0:T(8,128)S(1)} %get-tuple-element.26), channel_id=1, source_target_pairs={{0,28},{1,29},{2,30},{3,31},{4,24},{5,25},{6,26},{7,27},{8,4},{9,5... | collective-permute-start | bytes 98312 | tf_op jit(solution)/shard_map/ppermute | solution.py:494
  16.4 2.1 %collective-permute-start.3 = (f32[16,512]{1,0:T(8,128)S(1)}, f32[16,512]{1,0:T(8,128)S(1)}, u32[]{:S(2)}, u32[]{:S(2)}) collective-permute-start(f32[16,512]{1,0:T(8,128)S(1)} %get-tuple-element.27), channel_id=1, source_target_pairs={{0,29},{1,30},{2,31},{3,24},{4,25},{5,26},{6,27},{7,28},{8,5},{9,6... | collective-permute-start | bytes 98312 | tf_op jit(solution)/shard_map/ppermute | solution.py:494
  18.6 0.0 collective-permute-done.4.from_south
  18.6 0.0 collective-permute-start.5
  18.6 3.2 %collective-permute-done.5.from_north = f32[8,512]{1,0:T(8,128)S(1)} collective-permute-done((f32[8,512]{1,0:T(8,128)S(1)}, f32[8,512]{1,0:T(8,128)S(1)}, u32[]{:S(2)}, u32[]{:S(2)}) %collective-permute-start.5) | collective-permute-done | bytes 16416 | tf_op jit(solution)/shard_map/ppermute | solution.py:494
  21.7 0.0 collective-permute-done.ra
  21.7 0.0 collective-permute-done.1.rb
  21.7 0.0 collective-permute-done.2.fa
  21.7 0.0 collective-permute-done.3.fb
  21.8 0.0 copy-done.1
  21.8 2.0 %faces.1 = (f32[10,16,512]{2,1,0:T(8,128)S(1)}, f32[10,16,512]{2,1,0:T(8,128)S(1)}, f32[10,16,512]{2,1,0:T(8,128)S(1)}, f32[10,16,512]{2,1,0:T(8,128)S(1)}, f32[...) custom-call(s32[3]{0:T(128)S(1)} %pad_add_fusion.ints, ...), custom_call_target="tpu_custom_call" | custom-call | tf_op jit(solution)/shard_map/faces/pallas_call | solution.py:543
  23.8 0.1 collective-permute-start.8
  23.8 2.7 %collective-permute-start.6 = (f32[10,16,512]{2,1,0:T(8,128)S(1)}, f32[10,16,512]{2,1,0:T(8,128)S(1)}, u32[]{:S(2)}, u32[]{:S(2)}) collective-permute-start(f32[10,16,512]{2,1,0:T(8,128)S(1)} %get-tuple-element.30), channel_id=1, source_target_pairs={{0,28},{1,13},{2,30},{3,15},{4,24},{5,9},{6,26},{7,11},{8,4},{9,21... | collective-permute-start | bytes 983048 | tf_op jit(solution)/shard_map/ppermute | solution.py:494
  26.5 3.6 %collective-permute-start.7 = (f32[10,16,512]{2,1,0:T(8,128)S(1)}, f32[10,16,512]{2,1,0:T(8,128)S(1)}, u32[]{:S(2)}, u32[]{:S(2)}) collective-permute-start(f32[10,16,512]{2,1,0:T(8,128)S(1)} %get-tuple-element.31), channel_id=1, source_target_pairs={{0,11},{1,30},{2,13},{3,24},{4,15},{5,26},{6,9},{7,28},{8,19},{9,6... | collective-permute-start | bytes 983048 | tf_op jit(solution)/shard_map/ppermute | solution.py:494
  30.1 0.0 collective-permute-done.8
  30.1 1.3 %collective-permute-start.9 = (f32[10,16,512]{2,1,0:T(8,128)S(1)}, f32[10,16,512]{2,1,0:T(8,128)S(1)}, u32[]{:S(2)}, u32[]{:S(2)}) collective-permute-start(f32[10,16,512]{2,1,0:T(8,128)S(1)} %add.48.after), channel_id=1, source_target_pairs={{0,12},{1,29},{2,14},{3,31},{4,8},{5,25},{6,10},{7,27},{8,20},{9,5... | collective-permute-start | bytes 983048 | tf_op jit(solution)/shard_map/ppermute | solution.py:494
  31.4 1.2 %collective-permute-start.10 = (f32[2,512]{1,0:T(2,128)S(1)}, f32[2,512]{1,0:T(2,128)S(1)}, u32[]{:S(2)}, u32[]{:S(2)}) collective-permute-start(f32[2,512]{1,0:T(2,128)S(1)} %get-tuple-element.34), channel_id=1, source_target_pairs={{0,13},{1,14},{2,15},{3,8},{4,9},{5,10},{6,11},{7,12},{8,21},{9,22... | collective-permute-start | bytes 12296 | tf_op jit(solution)/shard_map/ppermute | solution.py:494
  32.6 1.4 %collective-permute-start.11 = (f32[2,512]{1,0:T(2,128)S(1)}, f32[2,512]{1,0:T(2,128)S(1)}, u32[]{:S(2)}, u32[]{:S(2)}) collective-permute-start(f32[2,512]{1,0:T(2,128)S(1)} %get-tuple-element.35), channel_id=1, source_target_pairs={{0,10},{1,11},{2,12},{3,13},{4,14},{5,15},{6,8},{7,9},{8,18},{9,19... | collective-permute-start | bytes 12296 | tf_op jit(solution)/shard_map/ppermute | solution.py:494
  34.0 11.4 %bulk.1 = (f32[19,8,16,512]{3,2,1,0:T(8,128)}, f32[19,8,16,512]{3,2,1,0:T(8,128)}, f32[10,8,512]{2,1,0:T(8,128)S(1)}, f32[10,8,512]{2,1,0:T(8,128)S(1)}) custom-call(f32[10,16,512]{2,1,0:T(8,128)S(1)} %add.48.after, f32[19,8,16,512]{3,2,1,0:T(8,128)S(1)} %copy-done.1, f32[19,8,16,512]{3,2,1,0:T(8,128)} %g_ref.5, ...), custom_call_target="tpu_custom_call" | custom-call | tf_op jit(solution)/shard_map/bulk/pallas_call | solution.py:571
  45.4 16.5 %collective-permute-done.10.near_up = f32[2,512]{1,0:T(2,128)S(1)} collective-permute-done((f32[2,512]{1,0:T(2,128)S(1)}, f32[2,512]{1,0:T(2,128)S(1)}, u32[]{:S(2)}, u32[]{:S(2)}) %collective-permute-start.10) | collective-permute-done | bytes 4128 | tf_op jit(solution)/shard_map/ppermute | solution.py:494
  62.0 3.2 %collective-permute-start.14 = (f32[10,8,512]{2,1,0:T(8,128)S(1)}, f32[10,8,512]{2,1,0:T(8,128)S(1)}, u32[]{:S(2)}, u32[]{:S(2)}) collective-permute-start(f32[10,8,512]{2,1,0:T(8,128)S(1)} %get-tuple-element.38), channel_id=1, source_target_pairs={{0,1},{1,2},{2,3},{3,4},{4,5},{5,6},{6,7},{7,0},{8,9},{9,10},{10,1... | collective-permute-start | bytes 491528 | tf_op jit(solution)/shard_map/ppermute | solution.py:494
  65.2 0.0 collective-permute-done.11.far_up
  65.2 0.0 collective-permute-start.15
  65.2 2.3 %collective-permute-done.14.from_south = f32[10,8,512]{2,1,0:T(8,128)S(1)} collective-permute-done((f32[10,8,512]{2,1,0:T(8,128)S(1)}, f32[10,8,512]{2,1,0:T(8,128)S(1)}, u32[]{:S(2)}, u32[]{:S(2)}) %collective-permute-start.14) | collective-permute-done | bytes 163872 | tf_op jit(solution)/shard_map/ppermute | solution.py:494
  67.5 5.5 %collective-permute-start.12 = (f32[2,512]{1,0:T(2,128)S(1)}, f32[2,512]{1,0:T(2,128)S(1)}, u32[]{:S(2)}, u32[]{:S(2)}) collective-permute-start(f32[2,512]{1,0:T(2,128)S(1)} %get-tuple-element.36), channel_id=1, source_target_pairs={{0,30},{1,31},{2,24},{3,25},{4,26},{5,27},{6,28},{7,29},{8,6},{9,7... | collective-permute-start | bytes 12296 | tf_op jit(solution)/shard_map/ppermute | solution.py:494
  72.9 0.0 collective-permute-done.15.from_north
  72.9 0.7 collective-permute-start.13
  73.6 2.6 %y_rims.1 = (f32[19,8,16,512]{3,2,1,0:T(8,128)}, f32[19,8,16,512]{3,2,1,0:T(8,128)}) custom-call(f32[10,8,512]{2,1,0:T(8,128)S(1)} %collective-permute-done.14.from_south, f32[10,8,512]{2,1,0:T(8,128)S(1)} %collective-permute-done.15.from_north, f32[19,8,16,512]{3,2,1,0:T(8,128)} %get-tuple-element.40.f_in, ...), custom_call_target="tpu_custom_call", output_to_operand_aliasing={{0}: (2, {}), {1}: (3, {})} | custom-call | tf_op jit(solution)/shard_map/y_rims/pallas_call | solution.py:585
  76.3 0.0 collective-permute-done.12.near_low
  76.3 2.4 %collective-permute-done.13.far_low = f32[2,512]{1,0:T(2,128)S(1)} collective-permute-done((f32[2,512]{1,0:T(2,128)S(1)}, f32[2,512]{1,0:T(2,128)S(1)}, u32[]{:S(2)}, u32[]{:S(2)}) %collective-permute-start.13) | collective-permute-done | bytes 4128 | tf_op jit(solution)/shard_map/ppermute | solution.py:494
  78.6 0.0 collective-permute-done.6.direct
  78.6 0.0 collective-permute-done.7.across
  78.6 0.0 collective-permute-done.9.joint
  78.7 1.6 %x_faces.1 = (f32[19,8,16,512]{3,2,1,0:T(8,128)}, f32[19,8,16,512]{3,2,1,0:T(8,128)}) custom-call(s32[3]{0:T(128)S(1)} %pad_add_fusion.ints, f32[10,16,512]{2,1,0:T(8,128)S(1)} %collective-permute-done.6.direct, f32[10,16,512]{2,1,0:T(8,128)S(1)} %collective-permute-done.7.across, ...), custom_call_target="tpu_custom_call", output_to_operand_aliasing={{0}: (8, {}), {1}: (9, {})} | custom-call | tf_op jit(solution)/shard_map/x_faces/pallas_call | solution.py:596
  (1 shorter events, 0.0 us)
Async XLA Ops:
  3.5 2.4 %copy-start = (f32[19,8,16,512]{3,2,1,0:T(8,128)S(1)}, f32[19,8,16,512]{3,2,1,0:T(8,128)}, u32[]{:S(2)}) copy-start(f32[19,8,16,512]{3,2,1,0:T(8,128)} %g_ref.5) | copy-start | bytes 14942212
  5.9 15.9 %copy-start.1 = (f32[19,8,16,512]{3,2,1,0:T(8,128)S(1)}, f32[19,8,16,512]{3,2,1,0:T(8,128)}, u32[]{:S(2)}) copy-start(f32[19,8,16,512]{3,2,1,0:T(8,128)} %f_ref.3) | copy-start | bytes 14942212
  7.2 11.3 %collective-permute-start.4 = (f32[8,512]{1,0:T(8,128)S(1)}, f32[8,512]{1,0:T(8,128)S(1)}, u32[]{:S(2)}, u32[]{:S(2)}) collective-permute-start(f32[8,512]{1,0:T(8,128)S(1)} %get-tuple-element.28), channel_id=1, source_target_pairs={{0,1},{1,2},{2,3},{3,4},{4,5},{5,6},{6,7},{7,0},{8,9},{9,10},{10,1... | collective-permute-start | bytes 49160 | tf_op jit(solution)/shard_map/ppermute | solution.py:494
  10.0 11.8 %collective-permute-start = (f32[16,512]{1,0:T(8,128)S(1)}, f32[16,512]{1,0:T(8,128)S(1)}, u32[]{:S(2)}, u32[]{:S(2)}) collective-permute-start(f32[16,512]{1,0:T(8,128)S(1)} %get-tuple-element.24), channel_id=1, source_target_pairs={{0,12},{1,13},{2,14},{3,15},{4,8},{5,9},{6,10},{7,11},{8,20},{9,21... | collective-permute-start | bytes 98312 | tf_op jit(solution)/shard_map/ppermute | solution.py:494
  13.2 8.5 %collective-permute-start.1 = (f32[16,512]{1,0:T(8,128)S(1)}, f32[16,512]{1,0:T(8,128)S(1)}, u32[]{:S(2)}, u32[]{:S(2)}) collective-permute-start(f32[16,512]{1,0:T(8,128)S(1)} %get-tuple-element.25), channel_id=1, source_target_pairs={{0,11},{1,12},{2,13},{3,14},{4,15},{5,8},{6,9},{7,10},{8,19},{9,20... | collective-permute-start | bytes 98312 | tf_op jit(solution)/shard_map/ppermute | solution.py:494
  13.3 8.5 %collective-permute-start.2 = (f32[16,512]{1,0:T(8,128)S(1)}, f32[16,512]{1,0:T(8,128)S(1)}, u32[]{:S(2)}, u32[]{:S(2)}) collective-permute-start(f32[16,512]{1,0:T(8,128)S(1)} %get-tuple-element.26), channel_id=1, source_target_pairs={{0,28},{1,29},{2,30},{3,31},{4,24},{5,25},{6,26},{7,27},{8,4},{9,5... | collective-permute-start | bytes 98312 | tf_op jit(solution)/shard_map/ppermute | solution.py:494
  16.4 5.3 %collective-permute-start.3 = (f32[16,512]{1,0:T(8,128)S(1)}, f32[16,512]{1,0:T(8,128)S(1)}, u32[]{:S(2)}, u32[]{:S(2)}) collective-permute-start(f32[16,512]{1,0:T(8,128)S(1)} %get-tuple-element.27), channel_id=1, source_target_pairs={{0,29},{1,30},{2,31},{3,24},{4,25},{5,26},{6,27},{7,28},{8,5},{9,6... | collective-permute-start | bytes 98312 | tf_op jit(solution)/shard_map/ppermute | solution.py:494
  18.6 3.2 %collective-permute-start.5 = (f32[8,512]{1,0:T(8,128)S(1)}, f32[8,512]{1,0:T(8,128)S(1)}, u32[]{:S(2)}, u32[]{:S(2)}) collective-permute-start(f32[8,512]{1,0:T(8,128)S(1)} %get-tuple-element.29), channel_id=1, source_target_pairs={{0,7},{1,0},{2,1},{3,2},{4,3},{5,4},{6,5},{7,6},{8,15},{9,8},{10,9... | collective-permute-start | bytes 49160 | tf_op jit(solution)/shard_map/ppermute | solution.py:494
  23.8 6.3 %collective-permute-start.8 = (f32[10,16,512]{2,1,0:T(8,128)S(1)}, f32[10,16,512]{2,1,0:T(8,128)S(1)}, u32[]{:S(2)}, u32[]{:S(2)}) collective-permute-start(f32[10,16,512]{2,1,0:T(8,128)S(1)} %get-tuple-element.33), channel_id=1, source_target_pairs={{0,1},{1,0},{2,3},{3,2},{4,5},{5,4},{6,7},{7,6},{8,9},{9,8},{10,11... | collective-permute-start | bytes 983048 | tf_op jit(solution)/shard_map/ppermute | solution.py:494
  23.8 54.8 %collective-permute-start.6 = (f32[10,16,512]{2,1,0:T(8,128)S(1)}, f32[10,16,512]{2,1,0:T(8,128)S(1)}, u32[]{:S(2)}, u32[]{:S(2)}) collective-permute-start(f32[10,16,512]{2,1,0:T(8,128)S(1)} %get-tuple-element.30), channel_id=1, source_target_pairs={{0,28},{1,13},{2,30},{3,15},{4,24},{5,9},{6,26},{7,11},{8,4},{9,21... | collective-permute-start | bytes 983048 | tf_op jit(solution)/shard_map/ppermute | solution.py:494
  26.5 52.1 %collective-permute-start.7 = (f32[10,16,512]{2,1,0:T(8,128)S(1)}, f32[10,16,512]{2,1,0:T(8,128)S(1)}, u32[]{:S(2)}, u32[]{:S(2)}) collective-permute-start(f32[10,16,512]{2,1,0:T(8,128)S(1)} %get-tuple-element.31), channel_id=1, source_target_pairs={{0,11},{1,30},{2,13},{3,24},{4,15},{5,26},{6,9},{7,28},{8,19},{9,6... | collective-permute-start | bytes 983048 | tf_op jit(solution)/shard_map/ppermute | solution.py:494
  30.1 48.5 %collective-permute-start.9 = (f32[10,16,512]{2,1,0:T(8,128)S(1)}, f32[10,16,512]{2,1,0:T(8,128)S(1)}, u32[]{:S(2)}, u32[]{:S(2)}) collective-permute-start(f32[10,16,512]{2,1,0:T(8,128)S(1)} %add.48.after), channel_id=1, source_target_pairs={{0,12},{1,29},{2,14},{3,31},{4,8},{5,25},{6,10},{7,27},{8,20},{9,5... | collective-permute-start | bytes 983048 | tf_op jit(solution)/shard_map/ppermute | solution.py:494
  31.4 30.5 %collective-permute-start.10 = (f32[2,512]{1,0:T(2,128)S(1)}, f32[2,512]{1,0:T(2,128)S(1)}, u32[]{:S(2)}, u32[]{:S(2)}) collective-permute-start(f32[2,512]{1,0:T(2,128)S(1)} %get-tuple-element.34), channel_id=1, source_target_pairs={{0,13},{1,14},{2,15},{3,8},{4,9},{5,10},{6,11},{7,12},{8,21},{9,22... | collective-permute-start | bytes 12296 | tf_op jit(solution)/shard_map/ppermute | solution.py:494
  32.6 32.6 %collective-permute-start.11 = (f32[2,512]{1,0:T(2,128)S(1)}, f32[2,512]{1,0:T(2,128)S(1)}, u32[]{:S(2)}, u32[]{:S(2)}) collective-permute-start(f32[2,512]{1,0:T(2,128)S(1)} %get-tuple-element.35), channel_id=1, source_target_pairs={{0,10},{1,11},{2,12},{3,13},{4,14},{5,15},{6,8},{7,9},{8,18},{9,19... | collective-permute-start | bytes 12296 | tf_op jit(solution)/shard_map/ppermute | solution.py:494
  62.0 5.5 %collective-permute-start.14 = (f32[10,8,512]{2,1,0:T(8,128)S(1)}, f32[10,8,512]{2,1,0:T(8,128)S(1)}, u32[]{:S(2)}, u32[]{:S(2)}) collective-permute-start(f32[10,8,512]{2,1,0:T(8,128)S(1)} %get-tuple-element.38), channel_id=1, source_target_pairs={{0,1},{1,2},{2,3},{3,4},{4,5},{5,6},{6,7},{7,0},{8,9},{9,10},{10,1... | collective-permute-start | bytes 491528 | tf_op jit(solution)/shard_map/ppermute | solution.py:494
  65.2 7.7 %collective-permute-start.15 = (f32[10,8,512]{2,1,0:T(8,128)S(1)}, f32[10,8,512]{2,1,0:T(8,128)S(1)}, u32[]{:S(2)}, u32[]{:S(2)}) collective-permute-start(f32[10,8,512]{2,1,0:T(8,128)S(1)} %get-tuple-element.39), channel_id=1, source_target_pairs={{0,7},{1,0},{2,1},{3,2},{4,3},{5,4},{6,5},{7,6},{8,15},{9,8},{10,9... | collective-permute-start | bytes 491528 | tf_op jit(solution)/shard_map/ppermute | solution.py:494
  67.5 8.8 %collective-permute-start.12 = (f32[2,512]{1,0:T(2,128)S(1)}, f32[2,512]{1,0:T(2,128)S(1)}, u32[]{:S(2)}, u32[]{:S(2)}) collective-permute-start(f32[2,512]{1,0:T(2,128)S(1)} %get-tuple-element.36), channel_id=1, source_target_pairs={{0,30},{1,31},{2,24},{3,25},{4,26},{5,27},{6,28},{7,29},{8,6},{9,7... | collective-permute-start | bytes 12296 | tf_op jit(solution)/shard_map/ppermute | solution.py:494
  72.9 5.7 %collective-permute-start.13 = (f32[2,512]{1,0:T(2,128)S(1)}, f32[2,512]{1,0:T(2,128)S(1)}, u32[]{:S(2)}, u32[]{:S(2)}) collective-permute-start(f32[2,512]{1,0:T(2,128)S(1)} %get-tuple-element.37), channel_id=1, source_target_pairs={{0,27},{1,28},{2,29},{3,30},{4,31},{5,24},{6,25},{7,26},{8,3},{9,4... | collective-permute-start | bytes 12296 | tf_op jit(solution)/shard_map/ppermute | solution.py:494

commit v2 on v1

v2 whole, which is shorter than its diff:
```python
import functools

import jax
import jax.numpy as jnp
from jax import lax
from jax.experimental import pallas as pl
from jax.experimental.pallas import tpu as pltpu
from jax.sharding import PartitionSpec as P

lattice_velocity = [
    (0, 0, 0),
    (1, 0, 0),
    (-1, 0, 0),
    (0, 1, 0),
    (0, -1, 0),
    (0, 0, 1),
    (0, 0, -1),
    (1, 1, 0),
    (-1, -1, 0),
    (1, -1, 0),
    (-1, 1, 0),
    (1, 0, 1),
    (-1, 0, -1),
    (1, 0, -1),
    (-1, 0, 1),
    (0, 1, 1),
    (0, -1, -1),
    (0, 1, -1),
    (0, -1, 1),
]
lattice_weight = [1.0 / 3.0] + [1.0 / 18.0] * 6 + [1.0 / 36.0] * 12
plane_speed = 0.04
rising = [1, 7, 9, 11, 13]
falling = [2, 8, 10, 12, 14]
north_going = [i for i in range(19) if lattice_velocity[i][1] == 1]
south_going = [i for i in range(19) if lattice_velocity[i][1] == -1]
f32 = jnp.float32
VMEM = pltpu.VMEM
LANES = 128


def z_moved(value, step):
    if step == 0:
        return value
    return pltpu.roll(value, step % value.shape[-1], value.ndim - 1)


def spec_of(space):
    return pl.BlockSpec(memory_space=space)


def params(limit):
    return pltpu.CompilerParams(vmem_limit_bytes=limit)


def along(parts, c):
    total = None
    for sign, part in zip(c, parts):
        if sign == 0:
            continue
        if total is None:
            total = part if sign > 0 else -part
        else:
            total = total + part if sign > 0 else total - part
    return total


def signed_sum(load, axis):
    ups = [i for i in range(19) if lattice_velocity[i][axis] == 1]
    downs = [i for i in range(19) if lattice_velocity[i][axis] == -1]
    total = load(ups[0]) - load(downs[0])
    for i, j in zip(ups[1:], downs[1:]):
        total = total + (load(i) - load(j))
    return total


def moments_of(load):
    rho = load(0)
    for i in range(1, 19):
        rho = rho + load(i)
    return [rho] + [signed_sum(load, axis) for axis in range(3)]


class Site:
    def __init__(self, moments, phi, minus, plus, south, north):
        rho, momentum = moments[0], moments[1:]
        lower, upper = z_moved(phi, 1), z_moved(phi, -1)
        lap = (plus + minus) + (north + south) + (upper + lower) - 6.0 * phi
        mu = phi * (0.0625 * (phi * phi) - 0.0625) - 0.04 * lap
        half_mu = 0.5 * mu
        force = [half_mu * (plus - minus), half_mu * (north - south), half_mu * (upper - lower)]
        inverse = 1.0 / rho
        u = [(j + 0.5 * k) * inverse for j, k in zip(momentum, force)]
        uu = u[0] * u[0] + u[1] * u[1] + u[2] * u[2]
        uf = u[0] * force[0] + u[1] * force[1] + u[2] * force[2]
        self.rho, self.phi, self.mu, self.u, self.force, self.uu = rho, phi, mu, u, force, uu
        self.r = 1.25 * rho
        self.k = self.r * (1.0 - 1.5 * uu) - 1.125 * uf
        self.g_scale = phi * (1.0 / 0.9)
        self.g_base = (3.0 / 0.9) * mu - 1.5 * (self.g_scale * uu)

    def pair_f(self, i):
        p, q = along(self.u, lattice_velocity[i]), along(self.force, lattice_velocity[i])
        w = lattice_weight[i]
        rp = self.r * p
        even = w * (self.k + p * (4.5 * rp + 3.375 * q))
        odd = (3.0 * w) * rp + (1.125 * w) * q
        return even, odd

    def pair_g(self, i):
        p = along(self.u, lattice_velocity[i])
        w = lattice_weight[i]
        gp = self.g_scale * p
        return w * (self.g_base + 4.5 * (gp * p)), (3.0 * w) * gp

    def jump(self, i, delta):
        cy = lattice_velocity[i][1]
        uy = self.u[1]
        if cy == 0:
            return delta * (-3.0 * uy) - (1.5 * delta * delta)
        p = along(self.u, lattice_velocity[i])
        return delta * (3.0 * cy + (9.0 * cy) * p - 3.0 * uy) + (3.0 * delta * delta)


class Shear:
    def __init__(self, raw, wide, rows):
        self.raw, self.wide, self.rows = raw, wide, rows

    def clear(self):
        self.raw[...] = jnp.zeros_like(self.raw)
        self.wide[...] = jnp.zeros_like(self.wide)

    def put(self, value, up, near, far):
        n = self.rows
        for k in range(self.raw.shape[0]):
            self.raw[k, 8 : 8 + n] = value[:, LANES * k : LANES * k + LANES]
        for k in range(self.raw.shape[0]):
            if up:
                self.wide[k, n : n + n + 8] = (
                    near * self.raw[k, 0 : n + 8] + far * self.raw[k, 1 : n + 9]
                )
            else:
                self.wide[k, n + 8 : n + n + 16] = (
                    near * self.raw[k, 7 : n + 15] + far * self.raw[k, 8 : n + 16]
                )

    def add_row(self, at, row):
        for k in range(self.raw.shape[0]):
            lanes = slice(LANES * k, LANES * k + LANES)
            self.wide[k, at : at + 1] = self.wide[k, at : at + 1] + row[:, lanes]

    def take(self, up, block, rest, cy, ref, j):
        n = self.rows
        if up:
            start = (n + 8 if block == 0 else 8) + rest - cy
        else:
            start = (n + 8 if block == 0 else n + n + 8) - rest - cy
        for k in range(self.raw.shape[0]):
            ref[j, :, LANES * k : LANES * k + LANES] = self.wide[k, pl.ds(start, n)]


class Planes:
    def __init__(self, offsets, rows, sizes):
        count_x, count_y = sizes
        per_plane, half = count_x // 4, count_y // 2
        a = lax.axis_index("gx")
        self.odd = lax.rem(lax.axis_index("gy"), 2) == 1

        def plane_of(column):
            is_plane = lax.rem(column, per_plane) == 0
            plane = lax.rem(lax.div(column, per_plane), 4)
            rest = jnp.where(is_plane, jnp.clip(offsets[plane] - half * rows, 0, rows - 1), 0)
            return is_plane, (2.0 * plane.astype(f32) + 1.0) * 0.125, rest

        up_is, up_part, self.up_rest = plane_of(lax.rem(a + 1, count_x))
        low_is, low_part, self.low_rest = plane_of(a)
        self.up_near = jnp.where(up_is, 1.0 - up_part, 1.0)
        self.up_far = jnp.where(up_is, up_part, 0.0)
        self.low_near = jnp.where(low_is, low_part, 0.0)
        self.low_far = jnp.where(low_is, 1.0 - low_part, 1.0)
        self.up_jump = jnp.where(up_is, -plane_speed, 0.0)
        self.low_jump = jnp.where(low_is, plane_speed, 0.0)


def order_sum(load):
    total = load(0)
    for i in range(1, 19):
        total = total + load(i)
    return total


def phi_faces_kernel(g_ref, top, bottom, buf, sems):
    layers = g_ref.shape[1]
    copies = [
        pltpu.make_async_copy(g_ref.at[:, x], buf.at[s], sems.at[s])
        for s, x in enumerate((layers - 1, 0))
    ]
    for copy in copies:
        copy.start()
    for s, (copy, out) in enumerate(zip(copies, (top, bottom))):
        copy.wait()
        out[...] = order_sum(lambda i: buf[s, i])


def phi_kernel(f_ref, g_ref, top, bottom, phi_ref, to_north, to_south, fbuf, sems):
    layers, rows = phi_ref.shape[0], phi_ref.shape[1]
    faces = (layers - 1, 0)
    copies = [
        pltpu.make_async_copy(f_ref.at[:, x], fbuf.at[:, s], sems.at[s])
        for s, x in enumerate(faces)
    ]
    for copy in copies:
        copy.start()
    phi_ref[layers - 1] = top[...]
    phi_ref[0] = bottom[...]
    for x in range(layers):
        if 0 < x < layers - 1:
            phi_ref[x] = order_sum(lambda i: g_ref[i, x])
        to_north[x : x + 1] = phi_ref[x, rows - 1 : rows]
        to_south[x : x + 1] = phi_ref[x, 0:1]
    for s, x in enumerate(faces):
        copies[s].wait()
        for out, edge, inner, chosen in (
            (to_north, rows - 1, rows - 2, (7, 10)),
            (to_south, 0, 1, (9, 8)),
        ):
            out[layers + s : layers + s + 1] = phi_ref[x, inner : inner + 1]
            at = layers + 2 + 6 * s
            i = chosen[s]
            out[at : at + 1] = fbuf[i, s, edge : edge + 1]
            out[at + 1 : at + 2] = g_ref[i, x, edge : edge + 1]
            for k, part in enumerate(moments_of(lambda i: fbuf[i, s, edge : edge + 1])):
                out[at + 2 + k : at + 3 + k] = part
    for out in (to_north, to_south):
        out[layers + 14 : layers + 16] = jnp.zeros((2, out.shape[1]), f32)


def with_halo(ref, layer, below, above):
    rows = layer.shape[0]
    ref[8 : 8 + rows] = layer
    ref[7:8] = below
    ref[8 + rows : 9 + rows] = above


def corner_values(cells, planes, phi_ref, south_msg, north_msg, minus_wide, plus_wide):
    layers, rows, cols = phi_ref.shape
    cells[...] = jnp.ones_like(cells)
    for row in range(4):
        msg = south_msg if row < 2 else north_msg
        x = layers - 1 if row % 2 == 0 else 0
        beside = rows + (layers - 2 if row % 2 == 0 else 1)
        wide_row = 7 if row < 2 else rows + 8
        at = rows + layers
        first = at + 2 + 6 * (row % 2)
        far_phi = msg[at + row % 2 : at + row % 2 + 1]
        own_phi = phi_ref[x, 0:1] if row < 2 else phi_ref[x, rows - 1 : rows]
        parts = [msg[first + k : first + k + 1] for k in range(6)]
        parts.append(msg[rows + x : rows + x + 1])
        if row % 2 == 0:
            parts += [msg[beside : beside + 1], plus_wide[wide_row : wide_row + 1]]
        else:
            parts += [minus_wide[wide_row : wide_row + 1], msg[beside : beside + 1]]
        parts += [far_phi, own_phi] if row < 2 else [own_phi, far_phi]
        for k, part in enumerate(parts):
            cells[k, row : row + 1] = part
    place = lax.broadcasted_iota(jnp.int32, (8, cols), 0)
    is_top = (place == 0) | (place == 2)
    sx = jnp.where(is_top, 1.0, -1.0)
    sy = jnp.where(place < 2, 1.0, -1.0)
    delta = jnp.where(is_top, planes.up_jump, planes.low_jump)
    site = Site([cells[k] for k in range(2, 6)], *[cells[k] for k in range(6, 11)])
    w = lattice_weight[7]
    p = sx * site.u[0] + sy * site.u[1]
    q = sx * site.force[0] + sy * site.force[1]
    change = delta * (3.0 * sy + 9.0 * (sy * p) - 3.0 * site.u[1]) + 3.0 * (delta * delta)
    rp, gp = site.r * p, site.g_scale * p
    f_post = w * (site.k + p * (4.5 * rp + 3.375 * q) + 3.0 * rp + 1.125 * q + site.rho * change)
    g_post = w * (site.g_base + 4.5 * (gp * p) + 3.0 * gp + site.phi * change)
    return f_post - 0.25 * cells[0], g_post - (1.0 / 9.0) * cells[1]


def face_kernel(
    sizes,
    offsets,
    f_ref,
    g_ref,
    phi_ref,
    rise,
    fall,
    south_msg,
    north_msg,
    mate,
    direct,
    across,
    joint,
    minus_out,
    plus_out,
    minus_wide,
    plus_wide,
    window,
    halo,
    post,
    cells,
    corners,
    raw,
    wide,
):
    layers, rows, cols = phi_ref.shape
    planes = Planes(offsets, rows, sizes)
    shear = Shear(raw, wide, rows)
    window[...] = jnp.zeros_like(window)
    for up in (True, False):
        if up:
            first, second = rise, north_msg
            near, far, start = planes.low_far, planes.low_near, planes.low_rest
        else:
            first, second = south_msg, fall
            near, far, start = planes.up_far, planes.up_near, rows - 1 - planes.up_rest
        target = minus_wide if up else plus_wide
        for k in range(window.shape[0]):
            lanes = slice(LANES * k, LANES * k + LANES)
            window[k, 8 : 8 + rows] = first[0:rows, lanes]
            window[k, 8 + rows : 8 + 2 * rows] = second[0:rows, lanes]
            target[:, lanes] = (
                near * window[k, pl.ds(start, rows + 16)]
                + far * window[k, pl.ds(start + 1, rows + 16)]
            )
    minus_out[...] = minus_wide[8 : 8 + rows]
    plus_out[...] = plus_wide[8 : 8 + rows]
    corners[0], corners[1] = corner_values(
        cells, planes, phi_ref, south_msg, north_msg, minus_wide, plus_wide
    )
    for up in (True, False):
        x = layers - 1 if up else 0
        with_halo(
            halo, phi_ref[x], south_msg[rows + x : rows + x + 1], north_msg[rows + x : rows + x + 1]
        )
        if up:
            near, far, rest, delta = planes.up_near, planes.up_far, planes.up_rest, planes.up_jump
        else:
            near, far, rest, delta = planes.low_near, planes.low_far, planes.low_rest, planes.low_jump
        for h in range(0, rows, 8):
            span = slice(h, h + 8)
            phi_h = phi_ref[x, span]
            if up:
                minus, plus = phi_ref[x - 1, span], plus_wide[8 + h : 16 + h]
            else:
                minus, plus = minus_wide[8 + h : 16 + h], phi_ref[x + 1, span]
            site = Site(
                moments_of(lambda i: f_ref[i, x, span]),
                phi_h,
                minus,
                plus,
                halo[7 + h : 15 + h],
                halo[9 + h : 17 + h],
            )
            for j in range(5):
                i = rising[j] if up else falling[j]
                cz = lattice_velocity[i][2]
                change = lattice_weight[i] * site.jump(i, delta)
                even, odd = site.pair_f(i)
                value = even + odd - 0.25 * f_ref[i, x, span] + site.rho * change
                post[j, span] = z_moved(value, cz)
                even, odd = site.pair_g(i)
                value = even + odd - (1.0 / 9.0) * g_ref[i, x, span] + phi_h * change
                post[5 + j, span] = z_moved(value, cz)
        shear.clear()
        for j in range(10):
            cy = lattice_velocity[(rising if up else falling)[j % 5]][1]
            shear.put(post[j], up, near, far)
            corner = (0 if up else 1) + (0 if cy == 1 else 2)
            if cy == 1:
                gate = jnp.where(rest == (0 if up else rows - 1), near, 0.0)
                at = rows + 7 if up else rows + 8
            if cy == -1:
                gate = jnp.where(rest == (rows - 1 if up else 0), far, 0.0)
                at = 2 * rows + 7 if up else 2 * rows + 8
            if cy != 0:
                shear.add_row(at, gate * corners[j // 5, corner : corner + 1])

            @pl.when(planes.odd)
            def _():
                shear.take(up, 0, rest, cy, direct if up else joint, j)
                shear.take(up, 1, rest, cy, mate if up else across, j)

            @pl.when(jnp.logical_not(planes.odd))
            def _():
                shear.take(up, 0, rest, cy, joint if up else direct, j)
                shear.take(up, 1, rest, cy, across if up else mate, j)


def rim_kernel(f_ref, g_ref, phi_ref, minus, plus, south_msg, north_msg, north, south, line):
    layers, rows, cols = phi_ref.shape
    for edge, out, chosen in ((rows - 1, north, north_going), (0, south, south_going)):
        phi = phi_ref[:, edge, :]
        with_halo(line, phi, minus[edge : edge + 1], plus[edge : edge + 1])
        if edge == 0:
            below, above = south_msg[rows : rows + layers], phi_ref[:, 1, :]
        else:
            below, above = phi_ref[:, rows - 2, :], north_msg[rows : rows + layers]
        site = Site(
            moments_of(lambda i: f_ref[i, :, edge, :]),
            phi,
            line[7 : 7 + layers],
            line[9 : 9 + layers],
            below,
            above,
        )
        for j, i in enumerate(chosen):
            cz = lattice_velocity[i][2]
            even, odd = site.pair_f(i)
            out[j] = z_moved(even + odd - 0.25 * f_ref[i, :, edge, :], cz)
            even, odd = site.pair_g(i)
            out[5 + j] = z_moved(even + odd - (1.0 / 9.0) * g_ref[i, :, edge, :], cz)


def bulk_kernel(
    after,
    f_ref,
    g_ref,
    phi_ref,
    minus,
    plus,
    south_msg,
    north_msg,
    south_rim,
    north_rim,
    next_f,
    next_g,
    wide_phi,
    halo,
):
    layers, rows, cols = phi_ref.shape
    wide_phi[0] = minus[...]
    wide_phi[layers + 1] = plus[...]
    for x in range(layers):
        wide_phi[x + 1] = phi_ref[x]

    def layer(x, carry):
        with_halo(halo, phi_ref[x], south_msg[pl.ds(rows + x, 1)], north_msg[pl.ds(rows + x, 1)])
        beyond = lax.rem(x + 1, layers)
        before = lax.rem(x + layers - 1, layers)
        for h in range(0, rows, 8):
            span = slice(h, h + 8)
            phi_h = phi_ref[x, span]
            site = Site(
                moments_of(lambda i: f_ref[i, x, span]),
                phi_h,
                wide_phi[x, span],
                wide_phi[x + 2, span],
                halo[7 + h : 15 + h],
                halo[9 + h : 17 + h],
            )

            def emit(out, slot, i, value):
                cx, cy, cz = lattice_velocity[i]
                value = z_moved(value, cz)
                at = beyond if cx == 1 else before if cx == -1 else x
                if cy == 0:
                    out[i, at, span] = value
                elif cy == 1:
                    if h == 0:
                        rim = slot * 5 + north_going.index(i)
                        out[i, at, 0:1] = south_rim[rim, pl.ds(x, 1)]
                    if h + 8 < rows:
                        out[i, at, h + 1 : h + 9] = value
                    else:
                        out[i, at, h + 1 : h + 8] = value[0:7]
                else:
                    if h + 8 == rows:
                        rim = slot * 5 + south_going.index(i)
                        out[i, at, rows - 1 : rows] = north_rim[rim, pl.ds(x, 1)]
                    if h > 0:
                        out[i, at, h - 1 : h + 7] = value
                    else:
                        out[i, at, 0:7] = value[1:8]

            emit(next_f, 0, 0, lattice_weight[0] * site.k - 0.25 * f_ref[0, x, span])
            rest_g = (phi_h - 2.0 * site.mu - 0.5 * (phi_h * site.uu)) * (1.0 / 0.9)
            emit(next_g, 1, 0, rest_g - (1.0 / 9.0) * g_ref[0, x, span])
            for i in range(1, 19, 2):
                even, odd = site.pair_f(i)
                emit(next_f, 0, i, (even + odd) - 0.25 * f_ref[i, x, span])
                emit(next_f, 0, i + 1, (even - odd) - 0.25 * f_ref[i + 1, x, span])
                even, odd = site.pair_g(i)
                emit(next_g, 1, i, (even + odd) - (1.0 / 9.0) * g_ref[i, x, span])
                emit(next_g, 1, i + 1, (even - odd) - (1.0 / 9.0) * g_ref[i + 1, x, span])
        return carry

    lax.fori_loop(0, layers, layer, 0)


def face_fill_kernel(direct, across, joint, f_in, g_in, f_out, g_out, low, high, sems):
    layers = f_out.shape[1]
    odd = lax.rem(lax.axis_index("gy"), 2) == 1

    @pl.when(odd)
    def _():
        low[...] = direct[...] + across[...]
        high[...] = joint[...]

    @pl.when(jnp.logical_not(odd))
    def _():
        low[...] = joint[...]
        high[...] = direct[...] + across[...]

    copies = []
    for family, out in enumerate((f_out, g_out)):
        for j in range(5):
            slot = family * 5 + j
            for side, buf, chosen, x in ((0, low, rising, 0), (1, high, falling, layers - 1)):
                copy = pltpu.make_async_copy(
                    buf.at[slot], out.at[chosen[j], x], sems.at[side, slot]
                )
                copy.start()
                copies.append(copy)
    for copy in copies:
        copy.wait()


def on_device(momentum_dist, order_dist, offsets):
    layers, rows, cols = momentum_dist.shape[1:]
    count_x, count_y = lax.axis_size("gx"), lax.axis_size("gy")
    per_plane = count_x // 4
    half = count_y // 2

    def hop(value, target):
        perm = []
        for x in range(count_x):
            for y in range(count_y):
                tx, ty = target(x, y)
                perm.append((x * count_y + y, tx % count_x * count_y + ty % count_y))
        return lax.ppermute(value, ("gx", "gy"), perm)

    def base_up(x):
        return half if (x + 1) % per_plane == 0 else 0

    def base_low(x):
        return half if x % per_plane == 0 else 0

    def hop_parity(value, odd_up, extra):
        def target(x, y):
            if (y % 2 == 1) == odd_up:
                return (x + 1, y - base_up(x) - extra)
            return (x - 1, y + base_low(x) + extra)

        return hop(value, target)

    def hop_y(value, step):
        return hop(value, lambda x, y: (x, y + step))

    smem, vmem, anywhere = spec_of(pltpu.SMEM), spec_of(VMEM), spec_of(pl.ANY)
    plane = jax.ShapeDtypeStruct((rows, cols), f32)
    top, bottom = pl.pallas_call(
        phi_faces_kernel,
        out_shape=[plane] * 2,
        in_specs=[anywhere],
        out_specs=[vmem] * 2,
        scratch_shapes=[VMEM((2, 19, rows, cols), f32), pltpu.SemaphoreType.DMA((2,))],
        compiler_params=params(60 << 20),
        name="phi_faces",
    )(order_dist)
    rise = hop(top, lambda x, y: (x + 1, y - base_up(x)))
    fall = hop(bottom, lambda x, y: (x - 1, y + base_low(x)))

    block = jax.ShapeDtypeStruct((layers + 16, cols), f32)
    phi, to_north, to_south = pl.pallas_call(
        phi_kernel,
        out_shape=[jax.ShapeDtypeStruct((layers, rows, cols), f32)] + [block] * 2,
        in_specs=[anywhere, vmem, vmem, vmem],
        out_specs=[vmem] * 3,
        scratch_shapes=[VMEM((19, 2, rows, cols), f32), pltpu.SemaphoreType.DMA((2,))],
        compiler_params=params(8 << 20),
        name="phi_all",
    )(momentum_dist, order_dist, top, bottom)
    south_msg = hop_y(jnp.concatenate([fall, to_north], 0), 1)
    north_msg = hop_y(jnp.concatenate([rise, to_south], 0), -1)

    ten = jax.ShapeDtypeStruct((10, rows, cols), f32)
    mate, direct, across, joint, minus, plus = pl.pallas_call(
        functools.partial(face_kernel, (count_x, count_y)),
        out_shape=[ten] * 4 + [plane] * 2,
        in_specs=[smem] + [vmem] * 7,
        out_specs=[vmem] * 6,
        scratch_shapes=[
            VMEM((rows + 16, cols), f32),
            VMEM((rows + 16, cols), f32),
            VMEM((cols // LANES, 2 * rows + 16, LANES), f32),
            VMEM((rows + 16, cols), f32),
            VMEM((10, rows, cols), f32),
            VMEM((11, 8, cols), f32),
            VMEM((2, 8, cols), f32),
            VMEM((cols // LANES, rows + 16, LANES), f32),
            VMEM((cols // LANES, 3 * rows + 16, LANES), f32),
        ],
        compiler_params=params(24 << 20),
        name="x_faces",
    )(offsets, momentum_dist, order_dist, phi, rise, fall, south_msg, north_msg)

    mate = hop(mate, lambda x, y: (x, y ^ 1))
    direct = hop_parity(direct, True, 0)

    side = jax.ShapeDtypeStruct((10, layers, cols), f32)
    around = (phi, minus, plus, south_msg, north_msg)
    to_north, to_south = pl.pallas_call(
        rim_kernel,
        out_shape=[side] * 2,
        in_specs=[vmem] * 7,
        out_specs=[vmem] * 2,
        scratch_shapes=[VMEM((layers + 16, cols), f32)],
        compiler_params=params(24 << 20),
        name="y_rims",
    )(momentum_dist, order_dist, *around)
    south_rim, north_rim = hop_y(to_north, 1), hop_y(to_south, -1)
    across = hop_parity(across, False, 1)
    joint = joint + mate
    after = joint
    joint = hop_parity(joint, False, 0)

    whole = jax.ShapeDtypeStruct(momentum_dist.shape, f32)
    next_f, next_g = pl.pallas_call(
        bulk_kernel,
        out_shape=[whole, whole],
        in_specs=[anywhere] + [vmem] * 9,
        out_specs=[vmem] * 2,
        scratch_shapes=[
            VMEM((layers + 2, rows, cols), f32),
            VMEM((rows + 16, cols), f32),
        ],
        compiler_params=params(48 << 20),
        name="bulk",
    )(after, momentum_dist, order_dist, *around, south_rim, north_rim)

    return pl.pallas_call(
        face_fill_kernel,
        out_shape=[whole, whole],
        in_specs=[vmem] * 3 + [anywhere, anywhere],
        out_specs=[anywhere, anywhere],
        scratch_shapes=[
            VMEM((10, rows, cols), f32),
            VMEM((10, rows, cols), f32),
            pltpu.SemaphoreType.DMA((2, 10)),
        ],
        input_output_aliases={3: 0, 4: 1},
        compiler_params=params(24 << 20),
        name="x_fill",
    )(direct, across, joint, next_f, next_g)


def solution(mesh):
    return jax.shard_map(
        on_device,
        mesh=mesh,
        in_specs=(P(None, "gx", "gy", None), P(None, "gx", "gy", None), P()),
        out_specs=(P(None, "gx", "gy", None), P(None, "gx", "gy", None)),
        check_vma=False,
    )
```

time: 80.5 us -> 74.7 us (0.928)
  the two profiles are of different devices: /device:TPU:1 before, /device:TPU:18 now
where the time goes in v2:
time: 74.7 us; the launch traced here: 74.4 us
  waiting for transfers between devices  34.9 us (47%)
  Pallas kernels  17.3 us (23%)
  starting transfers between devices  15 us (20%)
  local copies, waits for them, and re-layouts  6.35 us (9%)
    ppermute x10, waiting for transfers between devices, hop(): return lax.ppermute(value, ('gx', 'gy'), perm)  34.9 us
    ppermute x10, starting transfers between devices, hop(): return lax.ppermute(value, ('gx', 'gy'), perm)  15 us
    pallas_call x1, Pallas kernels, on_device(): pl.pallas_call(bulk_kernel, out_shape=[whole, whole], in_specs=[anywhere]...  11.3 us
    unnamed x14, local copies, waits for them, and re-layouts  6.35 us
    pallas_call x1, Pallas kernels, on_device(): pl.pallas_call(phi_faces_kernel, out_shape=[plane] * 2, in_specs=[anywher...  1.94 us
    pallas_call x1, Pallas kernels, on_device(): pl.pallas_call(functools.partial(face_kernel, (count_x, count_y)), out_sh...  1.84 us
  transfers between devices with their start and end apart: 10, of which 3 were waited for; matrix products, arithmetic and copies ran while one was open for 0% of the time, Pallas kernels for 17%

profile of v2, /device:TPU:18, one launch (start us, length us, event | category | flops | bytes accessed | tf_op | source)
XLA Modules:
  0.0 74.4 jit_solution(6751013905328244337)
XLA Ops:
  0.6 1.9 %phi_faces.1 = (f32[16,512]{1,0:T(8,128)}, f32[16,512]{1,0:T(8,128)}) custom-call(f32[19,8,16,512]{3,2,1,0:T(8,128)} %g_ref.9), custom_call_target="tpu_custom_call" | custom-call | tf_op jit(solution)/shard_map/phi_faces/pallas_call | solution.py:554
  2.6 1.3 %collective-permute-start = (f32[16,512]{1,0:T(8,128)}, f32[16,512]{1,0:T(8,128)S(1)}, u32[]{:S(2)}, u32[]{:S(2)}) collective-permute-start(f32[16,512]{1,0:T(8,128)} %get-tuple-element.17.top), channel_id=1, source_target_pairs={{0,12},{1,13},{2,14},{3,15},{4,8},{5,9},{6,10},{7,11},{8,20},{9,21... | collective-permute-start | bytes 98312 | tf_op jit(solution)/shard_map/ppermute | solution.py:533
  3.9 2.6 %collective-permute-start.1 = (f32[16,512]{1,0:T(8,128)}, f32[16,512]{1,0:T(8,128)S(1)}, u32[]{:S(2)}, u32[]{:S(2)}) collective-permute-start(f32[16,512]{1,0:T(8,128)} %get-tuple-element.18.bottom), channel_id=1, source_target_pairs={{0,28},{1,29},{2,30},{3,31},{4,24},{5,25},{6,26},{7,27},{8,4},{9,5... | collective-permute-start | bytes 98312 | tf_op jit(solution)/shard_map/ppermute | solution.py:533
  6.5 0.0 copy-start
  6.5 2.4 %copy-done = f32[19,8,16,512]{3,2,1,0:T(8,128)S(1)} copy-done((f32[19,8,16,512]{3,2,1,0:T(8,128)S(1)}, f32[19,8,16,512]{3,2,1,0:T(8,128)}, u32[]{:S(2)}) %copy-start) | copy-done | bytes 4980760
  8.9 0.0 copy-start.2
  8.9 2.4 %copy-done.2 = f32[19,8,16,512]{3,2,1,0:T(8,128)S(1)} copy-done((f32[19,8,16,512]{3,2,1,0:T(8,128)S(1)}, f32[19,8,16,512]{3,2,1,0:T(8,128)}, u32[]{:S(2)}) %copy-start.2) | copy-done | bytes 4980760
  11.3 0.0 copy-start.4
  11.3 0.8 %copy-done.4 = f32[16,512]{1,0:T(8,128)S(1)} copy-done((f32[16,512]{1,0:T(8,128)S(1)}, f32[16,512]{1,0:T(8,128)}, u32[]{:S(2)}) %copy-start.4) | copy-done | bytes 32792
  12.0 0.0 copy-start.5
  12.0 0.8 %copy-done.5 = f32[16,512]{1,0:T(8,128)S(1)} copy-done((f32[16,512]{1,0:T(8,128)S(1)}, f32[16,512]{1,0:T(8,128)}, u32[]{:S(2)}) %copy-start.5) | copy-done | bytes 32792
  12.8 0.0 copy-start.1
  12.8 0.0 copy-start.3
  12.8 0.0 copy-start.6
  12.8 0.3 phi_all.1
  13.2 0.0 collective-permute-done.rise
  13.2 0.1 collective-permute-start.3
  13.2 0.0 collective-permute-done.1.fall
  13.3 0.5 collective-permute-start.2
  13.8 1.5 %collective-permute-done.3.north_msg = f32[40,512]{1,0:T(8,128)S(1)} collective-permute-done((f32[40,512]{1,0:T(8,128)S(1)}, f32[40,512]{1,0:T(8,128)S(1)}, u32[]{:S(2)}, u32[]{:S(2)}) %collective-permute-start.3) | collective-permute-done | bytes 81952 | tf_op jit(solution)/shard_map/ppermute | solution.py:533
  15.3 1.9 %collective-permute-done.2.south_msg = f32[40,512]{1,0:T(8,128)S(1)} collective-permute-done((f32[40,512]{1,0:T(8,128)S(1)}, f32[40,512]{1,0:T(8,128)S(1)}, u32[]{:S(2)}, u32[]{:S(2)}) %collective-permute-start.2) | collective-permute-done | bytes 81952 | tf_op jit(solution)/shard_map/ppermute | solution.py:533
  17.2 0.0 copy-done.1
  17.2 0.0 copy-done.3
  17.2 0.0 copy-done.6
  17.2 1.8 %x_faces.1 = (f32[10,16,512]{2,1,0:T(8,128)S(1)}, f32[10,16,512]{2,1,0:T(8,128)S(1)}, f32[10,16,512]{2,1,0:T(8,128)S(1)}, f32[10,16,512]{2,1,0:T(8,128)S(1)}, f3...) custom-call(s32[4]{0:T(128)S(1)} %copy-done.6, f32[19,8,16,512]{3,2,1,0:T(8,128)S(1)} %copy-done.3, ...), custom_call_target="tpu_custom_call" | custom-call | tf_op jit(solution)/shard_map/x_faces/pallas_call | solution.py:580
  19.1 0.2 collective-permute-start.6
  19.2 5.4 %collective-permute-start.4 = (f32[10,16,512]{2,1,0:T(8,128)S(1)}, f32[10,16,512]{2,1,0:T(8,128)S(1)}, u32[]{:S(2)}, u32[]{:S(2)}) collective-permute-start(f32[10,16,512]{2,1,0:T(8,128)S(1)} %get-tuple-element.22), channel_id=1, source_target_pairs={{0,28},{1,13},{2,30},{3,15},{4,24},{5,9},{6,26},{7,11},{8,4},{9,21... | collective-permute-start | bytes 983048 | tf_op jit(solution)/shard_map/ppermute | solution.py:533
  24.6 0.0 collective-permute-start.5
  24.6 0.0 collective-permute-done.6
  24.7 2.6 %collective-permute-start.7 = (f32[10,16,512]{2,1,0:T(8,128)S(1)}, f32[10,16,512]{2,1,0:T(8,128)S(1)}, u32[]{:S(2)}, u32[]{:S(2)}) collective-permute-start(f32[10,16,512]{2,1,0:T(8,128)S(1)} %add.3.after), channel_id=1, source_target_pairs={{0,12},{1,29},{2,14},{3,31},{4,8},{5,25},{6,10},{7,27},{8,20},{9,5... | collective-permute-start | bytes 983048 | tf_op jit(solution)/shard_map/ppermute | solution.py:533
  27.3 0.8 %y_rims.1 = (f32[10,8,512]{2,1,0:T(8,128)S(1)}, f32[10,8,512]{2,1,0:T(8,128)S(1)}) custom-call(f32[19,8,16,512]{3,2,1,0:T(8,128)S(1)} %copy-done.3, f32[19,8,16,512]{3,2,1,0:T(8,128)S(1)} %copy-done.1, f32[8,16,512]{2,1,0:T(8,128)S(1)} %get-tuple-element.19.phi_ref, f32[16,512]{1,0:T(8,128)S(1)} %get-tuple-element.26.minus, ...), custom_call_target="tpu_custom_call" | custom-call | tf_op jit(solution)/shard_map/y_rims/pallas_call | solution.py:605
  28.1 0.1 collective-permute-start.8
  28.1 2.3 %collective-permute-start.9 = (f32[10,8,512]{2,1,0:T(8,128)S(1)}, f32[10,8,512]{2,1,0:T(8,128)S(1)}, u32[]{:S(2)}, u32[]{:S(2)}) collective-permute-start(f32[10,8,512]{2,1,0:T(8,128)S(1)} %get-tuple-element.29), channel_id=1, source_target_pairs={{0,7},{1,0},{2,1},{3,2},{4,3},{5,4},{6,5},{7,6},{8,15},{9,8},{10,9... | collective-permute-start | bytes 491528 | tf_op jit(solution)/shard_map/ppermute | solution.py:533
  30.5 31.5 %collective-permute-done.8.south_rim = f32[10,8,512]{2,1,0:T(8,128)S(1)} collective-permute-done((f32[10,8,512]{2,1,0:T(8,128)S(1)}, f32[10,8,512]{2,1,0:T(8,128)S(1)}, u32[]{:S(2)}, u32[]{:S(2)}) %collective-permute-start.8) | collective-permute-done | bytes 163872 | tf_op jit(solution)/shard_map/ppermute | solution.py:533
  62.0 0.0 collective-permute-done.9.north_rim
  62.0 11.3 %bulk.1 = (f32[19,8,16,512]{3,2,1,0:T(8,128)}, f32[19,8,16,512]{3,2,1,0:T(8,128)}) custom-call(f32[10,16,512]{2,1,0:T(8,128)S(1)} %add.3.after, f32[19,8,16,512]{3,2,1,0:T(8,128)S(1)} %copy-done.3, f32[19,8,16,512]{3,2,1,0:T(8,128)} %g_ref.9, f32[8,16,512]{2,1,0:T(8,128)S(1)} %get-tuple-element.19.phi_ref, f32[16,512]{1,0:T(8,128)S(1)} %get-tuple-element.26.minus, ...), custom_call_target="tpu_custom_call" | custom-call | tf_op jit(solution)/shard_map/bulk/pallas_call | solution.py:621
  73.3 0.0 collective-permute-done.4.direct
  73.3 0.0 collective-permute-done.5.across
  73.3 0.0 collective-permute-done.7.joint
  73.3 1.1 %x_fill.1 = (f32[19,8,16,512]{3,2,1,0:T(8,128)}, f32[19,8,16,512]{3,2,1,0:T(8,128)}) custom-call(f32[10,16,512]{2,1,0:T(8,128)S(1)} %collective-permute-done.4.direct, f32[10,16,512]{2,1,0:T(8,128)S(1)} %collective-permute-done.5.across, f32[10,16,512]{2,1,0:T(8,128)S(1)} %collective-permute-done.7.joint, ...), custom_call_target="tpu_custom_call", output_to_operand_aliasing={{0}: (3, {}), {1}: (4, {})} | custom-call | tf_op jit(solution)/shard_map/x_fill/pallas_call | solution.py:634
  (3 shorter events, 0.1 us)
Async XLA Ops:
  2.6 10.6 %collective-permute-start = (f32[16,512]{1,0:T(8,128)}, f32[16,512]{1,0:T(8,128)S(1)}, u32[]{:S(2)}, u32[]{:S(2)}) collective-permute-start(f32[16,512]{1,0:T(8,128)} %get-tuple-element.17.top), channel_id=1, source_target_pairs={{0,12},{1,13},{2,14},{3,15},{4,8},{5,9},{6,10},{7,11},{8,20},{9,21... | collective-permute-start | bytes 98312 | tf_op jit(solution)/shard_map/ppermute | solution.py:533
  3.9 9.4 %collective-permute-start.1 = (f32[16,512]{1,0:T(8,128)}, f32[16,512]{1,0:T(8,128)S(1)}, u32[]{:S(2)}, u32[]{:S(2)}) collective-permute-start(f32[16,512]{1,0:T(8,128)} %get-tuple-element.18.bottom), channel_id=1, source_target_pairs={{0,28},{1,29},{2,30},{3,31},{4,24},{5,25},{6,26},{7,27},{8,4},{9,5... | collective-permute-start | bytes 98312 | tf_op jit(solution)/shard_map/ppermute | solution.py:533
  6.5 2.4 %copy-start = (f32[19,8,16,512]{3,2,1,0:T(8,128)S(1)}, f32[19,8,16,512]{3,2,1,0:T(8,128)}, u32[]{:S(2)}) copy-start(f32[19,8,16,512]{3,2,1,0:T(8,128)} %g_ref.9) | copy-start | bytes 14942212
  8.9 2.4 %copy-start.2 = (f32[19,8,16,512]{3,2,1,0:T(8,128)S(1)}, f32[19,8,16,512]{3,2,1,0:T(8,128)}, u32[]{:S(2)}) copy-start(f32[19,8,16,512]{3,2,1,0:T(8,128)} %f_ref.7) | copy-start | bytes 14942212
  11.3 0.8 %copy-start.4 = (f32[16,512]{1,0:T(8,128)S(1)}, f32[16,512]{1,0:T(8,128)}, u32[]{:S(2)}) copy-start(f32[16,512]{1,0:T(8,128)} %get-tuple-element.18.bottom) | copy-start | bytes 98308
  12.0 0.8 %copy-start.5 = (f32[16,512]{1,0:T(8,128)S(1)}, f32[16,512]{1,0:T(8,128)}, u32[]{:S(2)}) copy-start(f32[16,512]{1,0:T(8,128)} %get-tuple-element.17.top) | copy-start | bytes 98308
  12.8 4.4 %copy-start.1 = (f32[19,8,16,512]{3,2,1,0:T(8,128)S(1)}, f32[19,8,16,512]{3,2,1,0:T(8,128)}, u32[]{:S(2)}) copy-start(f32[19,8,16,512]{3,2,1,0:T(8,128)} %g_ref.9) | copy-start | bytes 14942212
  12.8 4.4 %copy-start.3 = (f32[19,8,16,512]{3,2,1,0:T(8,128)S(1)}, f32[19,8,16,512]{3,2,1,0:T(8,128)}, u32[]{:S(2)}) copy-start(f32[19,8,16,512]{3,2,1,0:T(8,128)} %f_ref.7) | copy-start | bytes 14942212
  12.8 4.4 %copy-start.6 = (s32[4]{0:T(128)S(1)}, s32[4]{0:T(128)}, u32[]{:S(2)}) copy-start(s32[4]{0:T(128)} %offsets.1) | copy-start | bytes 52
  13.2 2.1 %collective-permute-start.3 = (f32[40,512]{1,0:T(8,128)S(1)}, f32[40,512]{1,0:T(8,128)S(1)}, u32[]{:S(2)}, u32[]{:S(2)}) collective-permute-start(f32[40,512]{1,0:T(8,128)S(1)} %pad_maximum_fusion.1), channel_id=1, source_target_pairs={{0,7},{1,0},{2,1},{3,2},{4,3},{5,4},{6,5},{7,6},{8,15},{9,8},{10,9... | collective-permute-start | bytes 245768 | tf_op jit(solution)/shard_map/ppermute | solution.py:533
  13.3 3.9 %collective-permute-start.2 = (f32[40,512]{1,0:T(8,128)S(1)}, f32[40,512]{1,0:T(8,128)S(1)}, u32[]{:S(2)}, u32[]{:S(2)}) collective-permute-start(f32[40,512]{1,0:T(8,128)S(1)} %pad_maximum_fusion), channel_id=1, source_target_pairs={{0,1},{1,2},{2,3},{3,4},{4,5},{5,6},{6,7},{7,0},{8,9},{9,10},{10,1... | collective-permute-start | bytes 245768 | tf_op jit(solution)/shard_map/ppermute | solution.py:533
  19.1 5.6 %collective-permute-start.6 = (f32[10,16,512]{2,1,0:T(8,128)S(1)}, f32[10,16,512]{2,1,0:T(8,128)S(1)}, u32[]{:S(2)}, u32[]{:S(2)}) collective-permute-start(f32[10,16,512]{2,1,0:T(8,128)S(1)} %get-tuple-element.25), channel_id=1, source_target_pairs={{0,1},{1,0},{2,3},{3,2},{4,5},{5,4},{6,7},{7,6},{8,9},{9,8},{10,11... | collective-permute-start | bytes 983048 | tf_op jit(solution)/shard_map/ppermute | solution.py:533
  19.2 54.0 %collective-permute-start.4 = (f32[10,16,512]{2,1,0:T(8,128)S(1)}, f32[10,16,512]{2,1,0:T(8,128)S(1)}, u32[]{:S(2)}, u32[]{:S(2)}) collective-permute-start(f32[10,16,512]{2,1,0:T(8,128)S(1)} %get-tuple-element.22), channel_id=1, source_target_pairs={{0,28},{1,13},{2,30},{3,15},{4,24},{5,9},{6,26},{7,11},{8,4},{9,21... | collective-permute-start | bytes 983048 | tf_op jit(solution)/shard_map/ppermute | solution.py:533
  24.6 48.6 %collective-permute-start.5 = (f32[10,16,512]{2,1,0:T(8,128)S(1)}, f32[10,16,512]{2,1,0:T(8,128)S(1)}, u32[]{:S(2)}, u32[]{:S(2)}) collective-permute-start(f32[10,16,512]{2,1,0:T(8,128)S(1)} %get-tuple-element.23), channel_id=1, source_target_pairs={{0,11},{1,30},{2,13},{3,24},{4,15},{5,26},{6,9},{7,28},{8,19},{9,6... | collective-permute-start | bytes 983048 | tf_op jit(solution)/shard_map/ppermute | solution.py:533
  24.7 48.6 %collective-permute-start.7 = (f32[10,16,512]{2,1,0:T(8,128)S(1)}, f32[10,16,512]{2,1,0:T(8,128)S(1)}, u32[]{:S(2)}, u32[]{:S(2)}) collective-permute-start(f32[10,16,512]{2,1,0:T(8,128)S(1)} %add.3.after), channel_id=1, source_target_pairs={{0,12},{1,29},{2,14},{3,31},{4,8},{5,25},{6,10},{7,27},{8,20},{9,5... | collective-permute-start | bytes 983048 | tf_op jit(solution)/shard_map/ppermute | solution.py:533
  28.1 33.9 %collective-permute-start.8 = (f32[10,8,512]{2,1,0:T(8,128)S(1)}, f32[10,8,512]{2,1,0:T(8,128)S(1)}, u32[]{:S(2)}, u32[]{:S(2)}) collective-permute-start(f32[10,8,512]{2,1,0:T(8,128)S(1)} %get-tuple-element.28), channel_id=1, source_target_pairs={{0,1},{1,2},{2,3},{3,4},{4,5},{5,6},{6,7},{7,0},{8,9},{9,10},{10,1... | collective-permute-start | bytes 491528 | tf_op jit(solution)/shard_map/ppermute | solution.py:533
  28.1 33.8 %collective-permute-start.9 = (f32[10,8,512]{2,1,0:T(8,128)S(1)}, f32[10,8,512]{2,1,0:T(8,128)S(1)}, u32[]{:S(2)}, u32[]{:S(2)}) collective-permute-start(f32[10,8,512]{2,1,0:T(8,128)S(1)} %get-tuple-element.29), channel_id=1, source_target_pairs={{0,7},{1,0},{2,1},{3,2},{4,3},{5,4},{6,5},{7,6},{8,15},{9,8},{10,9... | collective-permute-start | bytes 491528 | tf_op jit(solution)/shard_map/ppermute | solution.py:533

commit v3 on v2

--- a/solution.py
+++ b/solution.py
@@ -156,7 +156,7 @@
         else:
             start = (n + 8 if block == 0 else n + n + 8) - rest - cy
         for k in range(self.raw.shape[0]):
-            ref[j, :, LANES * k : LANES * k + LANES] = self.wide[k, pl.ds(start, n)]
+            ref[j, 0:n, LANES * k : LANES * k + LANES] = self.wide[k, pl.ds(start, n)]
 
 
 class Planes:
@@ -189,48 +189,39 @@
     return total
 
 
-def phi_faces_kernel(g_ref, top, bottom, buf, sems):
-    layers = g_ref.shape[1]
-    copies = [
-        pltpu.make_async_copy(g_ref.at[:, x], buf.at[s], sems.at[s])
-        for s, x in enumerate((layers - 1, 0))
-    ]
-    for copy in copies:
-        copy.start()
-    for s, (copy, out) in enumerate(zip(copies, (top, bottom))):
-        copy.wait()
-        out[...] = order_sum(lambda i: buf[s, i])
-
-
-def phi_kernel(f_ref, g_ref, top, bottom, phi_ref, to_north, to_south, fbuf, sems):
+def phi_kernel(f_ref, g_ref, top, bottom, phi_ref, to_north, to_south, fbuf, gbuf, sems):
     layers, rows = phi_ref.shape[0], phi_ref.shape[1]
     faces = (layers - 1, 0)
-    copies = [
-        pltpu.make_async_copy(f_ref.at[:, x], fbuf.at[:, s], sems.at[s])
+    f_copies = [
+        pltpu.make_async_copy(f_ref.at[:, x], fbuf.at[:, s], sems.at[layers + s])
         for s, x in enumerate(faces)
     ]
-    for copy in copies:
+    g_copies = [
+        pltpu.make_async_copy(g_ref.at[:, x], gbuf.at[:, x], sems.at[x]) for x in range(layers)
+    ]
+    for copy in f_copies + g_copies:
         copy.start()
     phi_ref[layers - 1] = top[...]
     phi_ref[0] = bottom[...]
+    edges = ((to_north, rows - 1, rows - 2, (7, 10)), (to_south, 0, 1, (9, 8)))
+    for s, x in enumerate(faces):
+        f_copies[s].wait()
+        for out, edge, inner, chosen in edges:
+            out[layers + s : layers + s + 1] = phi_ref[x, inner : inner + 1]
+            at = layers + 2 + 6 * s
+            out[at : at + 1] = fbuf[chosen[s], s, edge : edge + 1]
+            for k, part in enumerate(moments_of(lambda i: fbuf[i, s, edge : edge + 1])):
+                out[at + 2 + k : at + 3 + k] = part
     for x in range(layers):
+        g_copies[x].wait()
         if 0 < x < layers - 1:
-            phi_ref[x] = order_sum(lambda i: g_ref[i, x])
+            phi_ref[x] = order_sum(lambda i: gbuf[i, x])
         to_north[x : x + 1] = phi_ref[x, rows - 1 : rows]
         to_south[x : x + 1] = phi_ref[x, 0:1]
     for s, x in enumerate(faces):
-        copies[s].wait()
-        for out, edge, inner, chosen in (
-            (to_north, rows - 1, rows - 2, (7, 10)),
-            (to_south, 0, 1, (9, 8)),
-        ):
-            out[layers + s : layers + s + 1] = phi_ref[x, inner : inner + 1]
-            at = layers + 2 + 6 * s
-            i = chosen[s]
-            out[at : at + 1] = fbuf[i, s, edge : edge + 1]
-            out[at + 1 : at + 2] = g_ref[i, x, edge : edge + 1]
-            for k, part in enumerate(moments_of(lambda i: fbuf[i, s, edge : edge + 1])):
-                out[at + 2 + k : at + 3 + k] = part
+        for out, edge, inner, chosen in edges:
+            at = layers + 3 + 6 * s
+            out[at : at + 1] = gbuf[chosen[s], x, edge : edge + 1]
     for out in (to_north, to_south):
         out[layers + 14 : layers + 16] = jnp.zeros((2, out.shape[1]), f32)
 
@@ -279,6 +270,30 @@
     return f_post - 0.25 * cells[0], g_post - (1.0 / 9.0) * cells[1]
 
 
+def rim_values(f_ref, g_ref, phi_ref, minus, plus, south_msg, north_msg, line, edge, chosen, store):
+    layers, rows, cols = phi_ref.shape
+    phi = phi_ref[:, edge, :]
+    with_halo(line, phi, minus[edge : edge + 1], plus[edge : edge + 1])
+    if edge == 0:
+        below, above = south_msg[rows : rows + layers], phi_ref[:, 1, :]
+    else:
+        below, above = phi_ref[:, rows - 2, :], north_msg[rows : rows + layers]
+    site = Site(
+        moments_of(lambda i: f_ref[i, :, edge, :]),
+        phi,
+        line[7 : 7 + layers],
+        line[9 : 9 + layers],
+        below,
+        above,
+    )
+    for j, i in enumerate(chosen):
+        cz = lattice_velocity[i][2]
+        even, odd = site.pair_f(i)
+        store(j, z_moved(even + odd - 0.25 * f_ref[i, :, edge, :], cz))
+        even, odd = site.pair_g(i)
+        store(5 + j, z_moved(even + odd - (1.0 / 9.0) * g_ref[i, :, edge, :], cz))
+
+
 def face_kernel(
     sizes,
     offsets,
@@ -293,12 +308,14 @@
     direct,
     across,
     joint,
+    cross,
     minus_out,
     plus_out,
     minus_wide,
     plus_wide,
     window,
     halo,
+    line,
     post,
     cells,
     corners,
@@ -330,6 +347,31 @@
     corners[0], corners[1] = corner_values(
         cells, planes, phi_ref, south_msg, north_msg, minus_wide, plus_wide
     )
+    for edge, chosen in ((rows - 1, north_going), (0, south_going)):
+        to_mate = planes.odd if edge == 0 else jnp.logical_not(planes.odd)
+
+        def store(slot, value):
+            @pl.when(to_mate)
+            def _():
+                mate[slot, rows : rows + layers] = value
+
+            @pl.when(jnp.logical_not(to_mate))
+            def _():
+                cross[slot] = value
+
+        rim_values(
+            f_ref,
+            g_ref,
+            phi_ref,
+            minus_out,
+            plus_out,
+            south_msg,
+            north_msg,
+            line,
+            edge,
+            chosen,
+            store,
+        )
     for up in (True, False):
         x = layers - 1 if up else 0
         with_halo(
@@ -389,31 +431,6 @@
                 shear.take(up, 1, rest, cy, across if up else mate, j)
 
 
-def rim_kernel(f_ref, g_ref, phi_ref, minus, plus, south_msg, north_msg, north, south, line):
-    layers, rows, cols = phi_ref.shape
-    for edge, out, chosen in ((rows - 1, north, north_going), (0, south, south_going)):
-        phi = phi_ref[:, edge, :]
-        with_halo(line, phi, minus[edge : edge + 1], plus[edge : edge + 1])
-        if edge == 0:
-            below, above = south_msg[rows : rows + layers], phi_ref[:, 1, :]
-        else:
-            below, above = phi_ref[:, rows - 2, :], north_msg[rows : rows + layers]
-        site = Site(
-            moments_of(lambda i: f_ref[i, :, edge, :]),
-            phi,
-            line[7 : 7 + layers],
-            line[9 : 9 + layers],
-            below,
-            above,
-        )
-        for j, i in enumerate(chosen):
-            cz = lattice_velocity[i][2]
-            even, odd = site.pair_f(i)
-            out[j] = z_moved(even + odd - 0.25 * f_ref[i, :, edge, :], cz)
-            even, odd = site.pair_g(i)
-            out[5 + j] = z_moved(even + odd - (1.0 / 9.0) * g_ref[i, :, edge, :], cz)
-
-
 def bulk_kernel(
     after,
     f_ref,
@@ -423,14 +440,15 @@
     plus,
     south_msg,
     north_msg,
-    south_rim,
-    north_rim,
+    mate_rim,
+    cross_rim,
     next_f,
     next_g,
     wide_phi,
     halo,
 ):
     layers, rows, cols = phi_ref.shape
+    is_odd = lax.rem(lax.axis_index("gy"), 2) == 1
     wide_phi[0] = minus[...]
     wide_phi[layers + 1] = plus[...]
     for x in range(layers):
@@ -461,7 +479,9 @@
                 elif cy == 1:
                     if h == 0:
                         rim = slot * 5 + north_going.index(i)
-                        out[i, at, 0:1] = south_rim[rim, pl.ds(x, 1)]
+                        out[i, at, 0:1] = jnp.where(
+                            is_odd, mate_rim[rim, pl.ds(rows + x, 1)], cross_rim[rim, pl.ds(x, 1)]
+                        )
                     if h + 8 < rows:
                         out[i, at, h + 1 : h + 9] = value
                     else:
@@ -469,7 +489,9 @@
                 else:
                     if h + 8 == rows:
                         rim = slot * 5 + south_going.index(i)
-                        out[i, at, rows - 1 : rows] = north_rim[rim, pl.ds(x, 1)]
+                        out[i, at, rows - 1 : rows] = jnp.where(
+                            is_odd, cross_rim[rim, pl.ds(x, 1)], mate_rim[rim, pl.ds(rows + x, 1)]
+                        )
                     if h > 0:
                         out[i, at, h - 1 : h + 7] = value
                     else:
@@ -551,15 +573,7 @@
 
     smem, vmem, anywhere = spec_of(pltpu.SMEM), spec_of(VMEM), spec_of(pl.ANY)
     plane = jax.ShapeDtypeStruct((rows, cols), f32)
-    top, bottom = pl.pallas_call(
-        phi_faces_kernel,
-        out_shape=[plane] * 2,
-        in_specs=[anywhere],
-        out_specs=[vmem] * 2,
-        scratch_shapes=[VMEM((2, 19, rows, cols), f32), pltpu.SemaphoreType.DMA((2,))],
-        compiler_params=params(60 << 20),
-        name="phi_faces",
-    )(order_dist)
+    top, bottom = jnp.sum(order_dist[:, layers - 1], axis=0), jnp.sum(order_dist[:, 0], axis=0)
     rise = hop(top, lambda x, y: (x + 1, y - base_up(x)))
     fall = hop(bottom, lambda x, y: (x - 1, y + base_low(x)))
 
@@ -567,26 +581,33 @@
     phi, to_north, to_south = pl.pallas_call(
         phi_kernel,
         out_shape=[jax.ShapeDtypeStruct((layers, rows, cols), f32)] + [block] * 2,
-        in_specs=[anywhere, vmem, vmem, vmem],
+        in_specs=[anywhere, anywhere, vmem, vmem],
         out_specs=[vmem] * 3,
-        scratch_shapes=[VMEM((19, 2, rows, cols), f32), pltpu.SemaphoreType.DMA((2,))],
-        compiler_params=params(8 << 20),
+        scratch_shapes=[
+            VMEM((19, 2, rows, cols), f32),
+            VMEM((19, layers, rows, cols), f32),
+            pltpu.SemaphoreType.DMA((layers + 2,)),
+        ],
+        compiler_params=params(52 << 20),
         name="phi_all",
     )(momentum_dist, order_dist, top, bottom)
     south_msg = hop_y(jnp.concatenate([fall, to_north], 0), 1)
     north_msg = hop_y(jnp.concatenate([rise, to_south], 0), -1)
 
     ten = jax.ShapeDtypeStruct((10, rows, cols), f32)
-    mate, direct, across, joint, minus, plus = pl.pallas_call(
+    side = jax.ShapeDtypeStruct((10, layers, cols), f32)
+    ten_side = jax.ShapeDtypeStruct((10, rows + layers, cols), f32)
+    mate, direct, across, joint, cross, minus, plus = pl.pallas_call(
         functools.partial(face_kernel, (count_x, count_y)),
-        out_shape=[ten] * 4 + [plane] * 2,
+        out_shape=[ten_side] + [ten] * 3 + [side] + [plane] * 2,
         in_specs=[smem] + [vmem] * 7,
-        out_specs=[vmem] * 6,
+        out_specs=[vmem] * 7,
         scratch_shapes=[
             VMEM((rows + 16, cols), f32),
             VMEM((rows + 16, cols), f32),
             VMEM((cols // LANES, 2 * rows + 16, LANES), f32),
             VMEM((rows + 16, cols), f32),
+            VMEM((layers + 16, cols), f32),
             VMEM((10, rows, cols), f32),
             VMEM((11, 8, cols), f32),
             VMEM((2, 8, cols), f32),
@@ -594,28 +615,17 @@
             VMEM((cols // LANES, 3 * rows + 16, LANES), f32),
         ],
         compiler_params=params(24 << 20),
-        name="x_faces",
+        name="faces",
     )(offsets, momentum_dist, order_dist, phi, rise, fall, south_msg, north_msg)
 
     mate = hop(mate, lambda x, y: (x, y ^ 1))
+    cross = hop(cross, lambda x, y: (x, y + 1 if y % 2 == 1 else y - 1))
     direct = hop_parity(direct, True, 0)
-
-    side = jax.ShapeDtypeStruct((10, layers, cols), f32)
-    around = (phi, minus, plus, south_msg, north_msg)
-    to_north, to_south = pl.pallas_call(
-        rim_kernel,
-        out_shape=[side] * 2,
-        in_specs=[vmem] * 7,
-        out_specs=[vmem] * 2,
-        scratch_shapes=[VMEM((layers + 16, cols), f32)],
-        compiler_params=params(24 << 20),
-        name="y_rims",
-    )(momentum_dist, order_dist, *around)
-    south_rim, north_rim = hop_y(to_north, 1), hop_y(to_south, -1)
     across = hop_parity(across, False, 1)
-    joint = joint + mate
+    joint, cross = lax.optimization_barrier((joint + mate[:, :rows], cross))
     after = joint
     joint = hop_parity(joint, False, 0)
+    around = (phi, minus, plus, south_msg, north_msg)
 
     whole = jax.ShapeDtypeStruct(momentum_dist.shape, f32)
     next_f, next_g = pl.pallas_call(
@@ -629,7 +639,7 @@
         ],
         compiler_params=params(48 << 20),
         name="bulk",
-    )(after, momentum_dist, order_dist, *around, south_rim, north_rim)
+    )(after, momentum_dist, order_dist, *around, mate, cross)
 
     return pl.pallas_call(
         face_fill_kernel,

time: 74.7 us -> 66.1 us (0.88)
  the two profiles are of different devices: /device:TPU:18 before, /device:TPU:1 now
where the time goes in v3:
time: 66.1 us; the launch traced here: 65.9 us
  waiting for transfers between devices  25.4 us (38%)
  Pallas kernels  20.6 us (31%)
  starting transfers between devices  17.8 us (27%)
  other arithmetic  1.42 us (2%)
  between operations  0.7 us (1%)
    ppermute x9, waiting for transfers between devices, hop(): return lax.ppermute(value, ('gx', 'gy'), perm)  25.4 us
    ppermute x9, starting transfers between devices, hop(): return lax.ppermute(value, ('gx', 'gy'), perm)  17.8 us
    pallas_call x1, Pallas kernels, on_device(): pl.pallas_call(bulk_kernel, out_shape=[whole, whole], in_specs=[anywhere]...  12.8 us
    pallas_call x1, Pallas kernels, on_device(): pl.pallas_call(phi_kernel, out_shape=[jax.ShapeDtypeStruct((layers, rows,...  3.37 us
    pallas_call x1, Pallas kernels, on_device(): pl.pallas_call(functools.partial(face_kernel, (count_x, count_y)), out_sh...  3.34 us
    reduce_sum x1, other arithmetic, on_device(): jnp.sum(order_dist[:, 0], axis=0)  1.36 us
  transfers between devices with their start and end apart: 9, of which 5 were waited for; matrix products, arithmetic and copies ran while one was open for 0% of the time, Pallas kernels for 25%

profile of v3, /device:TPU:1, one launch (start us, length us, event | category | flops | bytes accessed | tf_op | source)
XLA Modules:
  0.0 65.9 jit_solution(3474956063911213237)
XLA Ops:
  0.6 1.4 %slice_reduce_fusion = (f32[16,512]{1,0:T(8,128)S(1)}, f32[16,512]{1,0:T(8,128)S(1)}) fusion(f32[19,8,16,512]{3,2,1,0:T(8,128)} %g_ref.5), kind=kLoop, calls=%fused_computation | loop fusion | flops 294912 | bytes 1310720 | tf_op jit(solution)/shard_map/reduce_sum | solution.py:576
  2.0 4.1 %collective-permute-start = (f32[16,512]{1,0:T(8,128)S(1)}, f32[16,512]{1,0:T(8,128)S(1)}, u32[]{:S(2)}, u32[]{:S(2)}) collective-permute-start(f32[16,512]{1,0:T(8,128)S(1)} %get-tuple-element.31.top), channel_id=1, source_target_pairs={{0,12},{1,13},{2,14},{3,15},{4,8},{5,9},{6,10},{7,11},{8,20},{9,21... | collective-permute-start | bytes 98312 | tf_op jit(solution)/shard_map/ppermute | solution.py:555
  6.1 0.0 slice-start
  6.1 0.0 slice-start.1
  6.1 0.0 copy-start
  6.1 0.0 copy-start.1
  6.1 1.1 %collective-permute-start.1 = (f32[16,512]{1,0:T(8,128)S(1)}, f32[16,512]{1,0:T(8,128)S(1)}, u32[]{:S(2)}, u32[]{:S(2)}) collective-permute-start(f32[16,512]{1,0:T(8,128)S(1)} %get-tuple-element.30.bottom), channel_id=1, source_target_pairs={{0,28},{1,29},{2,30},{3,31},{4,24},{5,25},{6,26},{7,27},{8,4},{9,5... | collective-permute-start | bytes 98312 | tf_op jit(solution)/shard_map/ppermute | solution.py:555
  7.2 3.4 %phi_all.1 = (f32[8,16,512]{2,1,0:T(8,128)S(1)}, f32[24,512]{1,0:T(8,128)S(1)}, f32[24,512]{1,0:T(8,128)S(1)}) custom-call(f32[19,8,16,512]{3,2,1,0:T(8,128)} %f_ref.5, f32[19,8,16,512]{3,2,1,0:T(8,128)} %g_ref.5, f32[16,512]{1,0:T(8,128)S(1)} %get-tuple-element.31.top, f32[16,512]{1,0:T(8,128)S(1)} %get-tuple-element.30.bottom), custom_call_target="tpu_custom_call" | custom-call | tf_op jit(solution)/shard_map/phi_all/pallas_call | solution.py:581
  10.6 0.0 collective-permute-done.rise
  10.6 1.0 %collective-permute-start.3 = (f32[40,512]{1,0:T(8,128)S(1)}, f32[40,512]{1,0:T(8,128)S(1)}, u32[]{:S(2)}, u32[]{:S(2)}) collective-permute-start(f32[40,512]{1,0:T(8,128)S(1)} %pad_maximum_fusion.1), channel_id=1, source_target_pairs={{0,7},{1,0},{2,1},{3,2},{4,3},{5,4},{6,5},{7,6},{8,15},{9,8},{10,9... | collective-permute-start | bytes 245768 | tf_op jit(solution)/shard_map/ppermute | solution.py:555
  11.6 0.0 collective-permute-done.1.fall
  11.6 2.4 %collective-permute-start.2 = (f32[40,512]{1,0:T(8,128)S(1)}, f32[40,512]{1,0:T(8,128)S(1)}, u32[]{:S(2)}, u32[]{:S(2)}) collective-permute-start(f32[40,512]{1,0:T(8,128)S(1)} %pad_maximum_fusion), channel_id=1, source_target_pairs={{0,1},{1,2},{2,3},{3,4},{4,5},{5,6},{6,7},{7,0},{8,9},{9,10},{10,1... | collective-permute-start | bytes 245768 | tf_op jit(solution)/shard_map/ppermute | solution.py:555
  14.0 1.2 %collective-permute-done.3.north_msg = f32[40,512]{1,0:T(8,128)S(1)} collective-permute-done((f32[40,512]{1,0:T(8,128)S(1)}, f32[40,512]{1,0:T(8,128)S(1)}, u32[]{:S(2)}, u32[]{:S(2)}) %collective-permute-start.3) | collective-permute-done | bytes 81952 | tf_op jit(solution)/shard_map/ppermute | solution.py:555
  15.2 1.1 %collective-permute-done.2.south_msg = f32[40,512]{1,0:T(8,128)S(1)} collective-permute-done((f32[40,512]{1,0:T(8,128)S(1)}, f32[40,512]{1,0:T(8,128)S(1)}, u32[]{:S(2)}, u32[]{:S(2)}) %collective-permute-start.2) | collective-permute-done | bytes 81952 | tf_op jit(solution)/shard_map/ppermute | solution.py:555
  16.3 0.0 slice-done
  16.3 0.0 slice-done.1
  16.3 0.0 copy-done
  16.3 0.0 copy-done.1
  16.3 3.3 %faces.1 = (f32[10,24,512]{2,1,0:T(8,128)S(1)}, f32[10,16,512]{2,1,0:T(8,128)S(1)}, f32[10,16,512]{2,1,0:T(8,128)S(1)}, f32[10,16,512]{2,1,0:T(8,128)S(1)}, f32[...) custom-call(s32[4]{0:T(128)S(1)} %copy-done.1, f32[19,8,16,512]{3,2,1,0:T(8,128)S(1)} %copy-done, ...), custom_call_target="tpu_custom_call" | custom-call | tf_op jit(solution)/shard_map/faces/pallas_call | solution.py:600
  19.7 3.3 %collective-permute-start.6 = (f32[10,24,512]{2,1,0:T(8,128)S(1)}, f32[10,24,512]{2,1,0:T(8,128)S(1)}, u32[]{:S(2)}, u32[]{:S(2)}) collective-permute-start(f32[10,24,512]{2,1,0:T(8,128)S(1)} %get-tuple-element.22), channel_id=1, source_target_pairs={{0,1},{1,0},{2,3},{3,2},{4,5},{5,4},{6,7},{7,6},{8,9},{9,8},{10,11... | collective-permute-start | bytes 1474568 | tf_op jit(solution)/shard_map/ppermute | solution.py:555
  22.9 0.0 collective-permute-start.7
  22.9 1.5 %collective-permute-start.4 = (f32[10,16,512]{2,1,0:T(8,128)S(1)}, f32[10,16,512]{2,1,0:T(8,128)S(1)}, u32[]{:S(2)}, u32[]{:S(2)}) collective-permute-start(f32[10,16,512]{2,1,0:T(8,128)S(1)} %get-tuple-element.19), channel_id=1, source_target_pairs={{0,28},{1,13},{2,30},{3,15},{4,24},{5,9},{6,26},{7,11},{8,4},{9,21... | collective-permute-start | bytes 983048 | tf_op jit(solution)/shard_map/ppermute | solution.py:555
  24.4 4.5 %collective-permute-start.5 = (f32[10,16,512]{2,1,0:T(8,128)S(1)}, f32[10,16,512]{2,1,0:T(8,128)S(1)}, u32[]{:S(2)}, u32[]{:S(2)}) collective-permute-start(f32[10,16,512]{2,1,0:T(8,128)S(1)} %get-tuple-element.20), channel_id=1, source_target_pairs={{0,11},{1,30},{2,13},{3,24},{4,15},{5,26},{6,9},{7,28},{8,19},{9,6... | collective-permute-start | bytes 983048 | tf_op jit(solution)/shard_map/ppermute | solution.py:555
  28.9 0.0 collective-permute-done.6.mate_rim
  29.0 1.3 %collective-permute-done.7.cross_rim = f32[10,8,512]{2,1,0:T(8,128)S(1)} collective-permute-done((f32[10,8,512]{2,1,0:T(8,128)S(1)}, f32[10,8,512]{2,1,0:T(8,128)S(1)}, u32[]{:S(2)}, u32[]{:S(2)}) %collective-permute-start.7) | collective-permute-done | bytes 163872 | tf_op jit(solution)/shard_map/ppermute | solution.py:555
  30.3 0.0 collective-permute-start.8
  30.3 12.8 %bulk.1 = (f32[19,8,16,512]{3,2,1,0:T(8,128)}, f32[19,8,16,512]{3,2,1,0:T(8,128)}) custom-call(f32[10,16,512]{2,1,0:T(8,128)S(1)} %slice_add_fusion.after, f32[19,8,16,512]{3,2,1,0:T(8,128)} %f_ref.5, f32[19,8,16,512]{3,2,1,0:T(8,128)} %g_ref.5, f32[8,16,512]{2,1,0:T(8,128)S(1)} %get-tuple-element.16.phi_ref, f32[16,512]{1,0:T(8,128)S(1)} %get-tuple-element.25.minus, ...), custom_call_target="tpu_custom_call" | custom-call | tf_op jit(solution)/shard_map/bulk/pallas_call | solution.py:631
  43.1 11.2 %collective-permute-done.4.direct = f32[10,16,512]{2,1,0:T(8,128)S(1)} collective-permute-done((f32[10,16,512]{2,1,0:T(8,128)S(1)}, f32[10,16,512]{2,1,0:T(8,128)S(1)}, u32[]{:S(2)}, u32[]{:S(2)}) %collective-permute-start.4) | collective-permute-done | bytes 327712 | tf_op jit(solution)/shard_map/ppermute | solution.py:555
  54.3 0.0 collective-permute-done.5.across
  54.3 10.6 %collective-permute-done.8.joint = f32[10,16,512]{2,1,0:T(8,128)S(1)} collective-permute-done((f32[10,16,512]{2,1,0:T(8,128)S(1)}, f32[10,16,512]{2,1,0:T(8,128)S(1)}, u32[]{:S(2)}, u32[]{:S(2)}) %collective-permute-start.8) | collective-permute-done | bytes 327712 | tf_op jit(solution)/shard_map/ppermute | solution.py:555
  64.9 1.0 %x_fill.1 = (f32[19,8,16,512]{3,2,1,0:T(8,128)}, f32[19,8,16,512]{3,2,1,0:T(8,128)}) custom-call(f32[10,16,512]{2,1,0:T(8,128)S(1)} %collective-permute-done.4.direct, f32[10,16,512]{2,1,0:T(8,128)S(1)} %collective-permute-done.5.across, f32[10,16,512]{2,1,0:T(8,128)S(1)} %collective-permute-done.8.joint, ...), custom_call_target="tpu_custom_call", output_to_operand_aliasing={{0}: (3, {}), {1}: (4, {})} | custom-call | tf_op jit(solution)/shard_map/x_fill/pallas_call | solution.py:644
  (4 shorter events, 0.1 us)
Async XLA Ops:
  2.0 8.6 %collective-permute-start = (f32[16,512]{1,0:T(8,128)S(1)}, f32[16,512]{1,0:T(8,128)S(1)}, u32[]{:S(2)}, u32[]{:S(2)}) collective-permute-start(f32[16,512]{1,0:T(8,128)S(1)} %get-tuple-element.31.top), channel_id=1, source_target_pairs={{0,12},{1,13},{2,14},{3,15},{4,8},{5,9},{6,10},{7,11},{8,20},{9,21... | collective-permute-start | bytes 98312 | tf_op jit(solution)/shard_map/ppermute | solution.py:555
  6.1 10.2 %slice-start = ((s8[4980736]{0:T(1024)(128)(4,1)}), s8[4194304]{0:T(1024)(128)(4,1)S(1)}, s32[]{:S(2)}) async-start(s8[4980736]{0:T(1024)(128)(4,1)} %bitcast), calls=%async_computation | async-start | bytes 8388608
  6.1 10.2 %slice-start.1 = ((s8[4980736]{0:T(1024)(128)(4,1)}), s8[786432]{0:T(1024)(128)(4,1)S(1)}, s32[]{:S(2)}) async-start(s8[4980736]{0:T(1024)(128)(4,1)} %bitcast), calls=%async_computation.1 | async-start | bytes 1572864
  6.1 10.2 %copy-start = (f32[19,8,16,512]{3,2,1,0:T(8,128)S(1)}, f32[19,8,16,512]{3,2,1,0:T(8,128)}, u32[]{:S(2)}) copy-start(f32[19,8,16,512]{3,2,1,0:T(8,128)} %f_ref.5) | copy-start | bytes 14942212
  6.1 10.2 %copy-start.1 = (s32[4]{0:T(128)S(1)}, s32[4]{0:T(128)}, u32[]{:S(2)}) copy-start(s32[4]{0:T(128)} %offsets.1) | copy-start | bytes 52
  6.1 5.5 %collective-permute-start.1 = (f32[16,512]{1,0:T(8,128)S(1)}, f32[16,512]{1,0:T(8,128)S(1)}, u32[]{:S(2)}, u32[]{:S(2)}) collective-permute-start(f32[16,512]{1,0:T(8,128)S(1)} %get-tuple-element.30.bottom), channel_id=1, source_target_pairs={{0,28},{1,29},{2,30},{3,31},{4,24},{5,25},{6,26},{7,27},{8,4},{9,5... | collective-permute-start | bytes 98312 | tf_op jit(solution)/shard_map/ppermute | solution.py:555
  10.6 4.6 %collective-permute-start.3 = (f32[40,512]{1,0:T(8,128)S(1)}, f32[40,512]{1,0:T(8,128)S(1)}, u32[]{:S(2)}, u32[]{:S(2)}) collective-permute-start(f32[40,512]{1,0:T(8,128)S(1)} %pad_maximum_fusion.1), channel_id=1, source_target_pairs={{0,7},{1,0},{2,1},{3,2},{4,3},{5,4},{6,5},{7,6},{8,15},{9,8},{10,9... | collective-permute-start | bytes 245768 | tf_op jit(solution)/shard_map/ppermute | solution.py:555
  11.6 4.7 %collective-permute-start.2 = (f32[40,512]{1,0:T(8,128)S(1)}, f32[40,512]{1,0:T(8,128)S(1)}, u32[]{:S(2)}, u32[]{:S(2)}) collective-permute-start(f32[40,512]{1,0:T(8,128)S(1)} %pad_maximum_fusion), channel_id=1, source_target_pairs={{0,1},{1,2},{2,3},{3,4},{4,5},{5,6},{6,7},{7,0},{8,9},{9,10},{10,1... | collective-permute-start | bytes 245768 | tf_op jit(solution)/shard_map/ppermute | solution.py:555
  19.7 9.2 %collective-permute-start.6 = (f32[10,24,512]{2,1,0:T(8,128)S(1)}, f32[10,24,512]{2,1,0:T(8,128)S(1)}, u32[]{:S(2)}, u32[]{:S(2)}) collective-permute-start(f32[10,24,512]{2,1,0:T(8,128)S(1)} %get-tuple-element.22), channel_id=1, source_target_pairs={{0,1},{1,0},{2,3},{3,2},{4,5},{5,4},{6,7},{7,6},{8,9},{9,8},{10,11... | collective-permute-start | bytes 1474568 | tf_op jit(solution)/shard_map/ppermute | solution.py:555
  22.9 7.3 %collective-permute-start.7 = (f32[10,8,512]{2,1,0:T(8,128)S(1)}, f32[10,8,512]{2,1,0:T(8,128)S(1)}, u32[]{:S(2)}, u32[]{:S(2)}) collective-permute-start(f32[10,8,512]{2,1,0:T(8,128)S(1)} %get-tuple-element.23), channel_id=1, source_target_pairs={{0,7},{1,2},{2,1},{3,4},{4,3},{5,6},{6,5},{7,0},{8,15},{9,10},{10,... | collective-permute-start | bytes 491528 | tf_op jit(solution)/shard_map/ppermute | solution.py:555
  22.9 31.3 %collective-permute-start.4 = (f32[10,16,512]{2,1,0:T(8,128)S(1)}, f32[10,16,512]{2,1,0:T(8,128)S(1)}, u32[]{:S(2)}, u32[]{:S(2)}) collective-permute-start(f32[10,16,512]{2,1,0:T(8,128)S(1)} %get-tuple-element.19), channel_id=1, source_target_pairs={{0,28},{1,13},{2,30},{3,15},{4,24},{5,9},{6,26},{7,11},{8,4},{9,21... | collective-permute-start | bytes 983048 | tf_op jit(solution)/shard_map/ppermute | solution.py:555
  24.4 29.9 %collective-permute-start.5 = (f32[10,16,512]{2,1,0:T(8,128)S(1)}, f32[10,16,512]{2,1,0:T(8,128)S(1)}, u32[]{:S(2)}, u32[]{:S(2)}) collective-permute-start(f32[10,16,512]{2,1,0:T(8,128)S(1)} %get-tuple-element.20), channel_id=1, source_target_pairs={{0,11},{1,30},{2,13},{3,24},{4,15},{5,26},{6,9},{7,28},{8,19},{9,6... | collective-permute-start | bytes 983048 | tf_op jit(solution)/shard_map/ppermute | solution.py:555
  30.3 34.6 %collective-permute-start.8 = (f32[10,16,512]{2,1,0:T(8,128)S(1)}, f32[10,16,512]{2,1,0:T(8,128)S(1)}, u32[]{:S(2)}, u32[]{:S(2)}) collective-permute-start(f32[10,16,512]{2,1,0:T(8,128)S(1)} %slice_add_fusion.after), channel_id=1, source_target_pairs={{0,12},{1,29},{2,14},{3,31},{4,8},{5,25},{6,10},{7,27},{8,20},{9,5... | collective-permute-start | bytes 983048 | tf_op jit(solution)/shard_map/ppermute | solution.py:555

commit v4 on v3

--- a/solution.py
+++ b/solution.py
@@ -270,7 +270,20 @@
     return f_post - 0.25 * cells[0], g_post - (1.0 / 9.0) * cells[1]
 
 
-def rim_values(f_ref, g_ref, phi_ref, minus, plus, south_msg, north_msg, line, edge, chosen, store):
+def moment_kernel(f_ref, g_ref, faces, rims):
+    layers, rows = f_ref.shape[1], f_ref.shape[2]
+    for s, x in enumerate((layers - 1, 0)):
+        for k, part in enumerate(moments_of(lambda i: f_ref[i, x])):
+            faces[s, k] = part
+    for s, (edge, chosen) in enumerate(((rows - 1, north_going), (0, south_going))):
+        for k, part in enumerate(moments_of(lambda i: f_ref[i, :, edge, :])):
+            rims[s, k] = part
+        for j, i in enumerate(chosen):
+            rims[s, 4 + j] = f_ref[i, :, edge, :]
+            rims[s, 9 + j] = g_ref[i, :, edge, :]
+
+
+def rim_values(rims, s, phi_ref, minus, plus, south_msg, north_msg, line, edge, chosen, store):
     layers, rows, cols = phi_ref.shape
     phi = phi_ref[:, edge, :]
     with_halo(line, phi, minus[edge : edge + 1], plus[edge : edge + 1])
@@ -279,7 +292,7 @@
     else:
         below, above = phi_ref[:, rows - 2, :], north_msg[rows : rows + layers]
     site = Site(
-        moments_of(lambda i: f_ref[i, :, edge, :]),
+        [rims[s, k] for k in range(4)],
         phi,
         line[7 : 7 + layers],
         line[9 : 9 + layers],
@@ -289,9 +302,9 @@
     for j, i in enumerate(chosen):
         cz = lattice_velocity[i][2]
         even, odd = site.pair_f(i)
-        store(j, z_moved(even + odd - 0.25 * f_ref[i, :, edge, :], cz))
+        store(j, z_moved(even + odd - 0.25 * rims[s, 4 + j], cz))
         even, odd = site.pair_g(i)
-        store(5 + j, z_moved(even + odd - (1.0 / 9.0) * g_ref[i, :, edge, :], cz))
+        store(5 + j, z_moved(even + odd - (1.0 / 9.0) * rims[s, 9 + j], cz))
 
 
 def face_kernel(
@@ -299,6 +312,8 @@
     offsets,
     f_ref,
     g_ref,
+    face_moments,
+    rims,
     phi_ref,
     rise,
     fall,
@@ -347,7 +362,7 @@
     corners[0], corners[1] = corner_values(
         cells, planes, phi_ref, south_msg, north_msg, minus_wide, plus_wide
     )
-    for edge, chosen in ((rows - 1, north_going), (0, south_going)):
+    for s, (edge, chosen) in enumerate(((rows - 1, north_going), (0, south_going))):
         to_mate = planes.odd if edge == 0 else jnp.logical_not(planes.odd)
 
         def store(slot, value):
@@ -360,8 +375,8 @@
                 cross[slot] = value
 
         rim_values(
-            f_ref,
-            g_ref,
+            rims,
+            s,
             phi_ref,
             minus_out,
             plus_out,
@@ -389,7 +404,7 @@
             else:
                 minus, plus = minus_wide[8 + h : 16 + h], phi_ref[x + 1, span]
             site = Site(
-                moments_of(lambda i: f_ref[i, x, span]),
+                [face_moments[0 if up else 1, k, span] for k in range(4)],
                 phi_h,
                 minus,
                 plus,
@@ -594,13 +609,25 @@
     south_msg = hop_y(jnp.concatenate([fall, to_north], 0), 1)
     north_msg = hop_y(jnp.concatenate([rise, to_south], 0), -1)
 
+    face_moments, rims = pl.pallas_call(
+        moment_kernel,
+        out_shape=[
+            jax.ShapeDtypeStruct((2, 4, rows, cols), f32),
+            jax.ShapeDtypeStruct((2, 14, layers, cols), f32),
+        ],
+        in_specs=[vmem] * 2,
+        out_specs=[vmem] * 2,
+        compiler_params=params(16 << 20),
+        name="moments",
+    )(momentum_dist, order_dist)
+
     ten = jax.ShapeDtypeStruct((10, rows, cols), f32)
     side = jax.ShapeDtypeStruct((10, layers, cols), f32)
     ten_side = jax.ShapeDtypeStruct((10, rows + layers, cols), f32)
     mate, direct, across, joint, cross, minus, plus = pl.pallas_call(
         functools.partial(face_kernel, (count_x, count_y)),
         out_shape=[ten_side] + [ten] * 3 + [side] + [plane] * 2,
-        in_specs=[smem] + [vmem] * 7,
+        in_specs=[smem] + [vmem] * 9,
         out_specs=[vmem] * 7,
         scratch_shapes=[
             VMEM((rows + 16, cols), f32),
@@ -616,7 +643,18 @@
         ],
         compiler_params=params(24 << 20),
         name="faces",
-    )(offsets, momentum_dist, order_dist, phi, rise, fall, south_msg, north_msg)
+    )(
+        offsets,
+        momentum_dist,
+        order_dist,
+        face_moments,
+        rims,
+        phi,
+        rise,
+        fall,
+        south_msg,
+        north_msg,
+    )
 
     mate = hop(mate, lambda x, y: (x, y ^ 1))
     cross = hop(cross, lambda x, y: (x, y + 1 if y % 2 == 1 else y - 1))

time: 66.1 us -> 65.7 us (level)
  no operation moved by 1% of the time
where the time goes in v4:
time: 65.7 us; the launch traced here: 65.5 us
  waiting for transfers between devices  24.9 us (38%)
  Pallas kernels  20.6 us (31%)
  starting transfers between devices  17.9 us (27%)
  other arithmetic  1.42 us (2%)
  between operations  0.7 us (1%)
    ppermute x9, waiting for transfers between devices, hop(): return lax.ppermute(value, ('gx', 'gy'), perm)  24.9 us
    ppermute x9, starting transfers between devices, hop(): return lax.ppermute(value, ('gx', 'gy'), perm)  17.9 us
    pallas_call x1, Pallas kernels, on_device(): pl.pallas_call(bulk_kernel, out_shape=[whole, whole], in_specs=[anywhere]...  12.8 us
    pallas_call x1, Pallas kernels, on_device(): pl.pallas_call(phi_kernel, out_shape=[jax.ShapeDtypeStruct((layers, rows,...  3.37 us
    pallas_call x1, Pallas kernels, on_device(): pl.pallas_call(functools.partial(face_kernel, (count_x, count_y)), out_sh...  2.96 us
    reduce_sum x1, other arithmetic, on_device(): jnp.sum(order_dist[:, 0], axis=0)  1.36 us
  transfers between devices with their start and end apart: 9, of which 5 were waited for; matrix products, arithmetic and copies ran while one was open for 0% of the time, Pallas kernels for 25%

profile of v4, /device:TPU:1, one launch (start us, length us, event | category | flops | bytes accessed | tf_op | source)
XLA Modules:
  0.0 65.5 jit_solution(17107091727482901370)
XLA Ops:
  0.6 1.4 %slice_reduce_fusion = (f32[16,512]{1,0:T(8,128)S(1)}, f32[16,512]{1,0:T(8,128)S(1)}) fusion(f32[19,8,16,512]{3,2,1,0:T(8,128)} %g_ref.7), kind=kLoop, calls=%fused_computation | loop fusion | flops 294912 | bytes 1310720 | tf_op jit(solution)/shard_map/reduce_sum | solution.py:591
  2.0 4.1 %collective-permute-start = (f32[16,512]{1,0:T(8,128)S(1)}, f32[16,512]{1,0:T(8,128)S(1)}, u32[]{:S(2)}, u32[]{:S(2)}) collective-permute-start(f32[16,512]{1,0:T(8,128)S(1)} %get-tuple-element.35.top), channel_id=1, source_target_pairs={{0,12},{1,13},{2,14},{3,15},{4,8},{5,9},{6,10},{7,11},{8,20},{9,21... | collective-permute-start | bytes 98312 | tf_op jit(solution)/shard_map/ppermute | solution.py:570
  6.1 0.0 slice-start
  6.1 0.0 slice-start.1
  6.1 0.0 copy-start
  6.1 1.1 %collective-permute-start.1 = (f32[16,512]{1,0:T(8,128)S(1)}, f32[16,512]{1,0:T(8,128)S(1)}, u32[]{:S(2)}, u32[]{:S(2)}) collective-permute-start(f32[16,512]{1,0:T(8,128)S(1)} %get-tuple-element.34.bottom), channel_id=1, source_target_pairs={{0,28},{1,29},{2,30},{3,31},{4,24},{5,25},{6,26},{7,27},{8,4},{9,5... | collective-permute-start | bytes 98312 | tf_op jit(solution)/shard_map/ppermute | solution.py:570
  7.2 3.4 %phi_all.1 = (f32[8,16,512]{2,1,0:T(8,128)S(1)}, f32[24,512]{1,0:T(8,128)S(1)}, f32[24,512]{1,0:T(8,128)S(1)}) custom-call(f32[19,8,16,512]{3,2,1,0:T(8,128)} %f_ref.7, f32[19,8,16,512]{3,2,1,0:T(8,128)} %g_ref.7, f32[16,512]{1,0:T(8,128)S(1)} %get-tuple-element.35.top, f32[16,512]{1,0:T(8,128)S(1)} %get-tuple-element.34.bottom), custom_call_target="tpu_custom_call" | custom-call | tf_op jit(solution)/shard_map/phi_all/pallas_call | solution.py:596
  10.5 0.0 collective-permute-done.rise
  10.6 1.0 %collective-permute-start.3 = (f32[40,512]{1,0:T(8,128)S(1)}, f32[40,512]{1,0:T(8,128)S(1)}, u32[]{:S(2)}, u32[]{:S(2)}) collective-permute-start(f32[40,512]{1,0:T(8,128)S(1)} %pad_maximum_fusion.1), channel_id=1, source_target_pairs={{0,7},{1,0},{2,1},{3,2},{4,3},{5,4},{6,5},{7,6},{8,15},{9,8},{10,9... | collective-permute-start | bytes 245768 | tf_op jit(solution)/shard_map/ppermute | solution.py:570
  11.6 0.0 collective-permute-done.1.fall
  11.6 0.0 copy-start.1
  11.6 2.4 %collective-permute-start.2 = (f32[40,512]{1,0:T(8,128)S(1)}, f32[40,512]{1,0:T(8,128)S(1)}, u32[]{:S(2)}, u32[]{:S(2)}) collective-permute-start(f32[40,512]{1,0:T(8,128)S(1)} %pad_maximum_fusion), channel_id=1, source_target_pairs={{0,1},{1,2},{2,3},{3,4},{4,5},{5,6},{6,7},{7,0},{8,9},{9,10},{10,1... | collective-permute-start | bytes 245768 | tf_op jit(solution)/shard_map/ppermute | solution.py:570
  14.0 0.0 slice-done
  14.0 0.0 slice-done.1
  14.0 0.0 copy-done
  14.0 0.4 moments.1
  14.5 0.6 collective-permute-done.3.north_msg
  15.1 1.1 %collective-permute-done.2.south_msg = f32[40,512]{1,0:T(8,128)S(1)} collective-permute-done((f32[40,512]{1,0:T(8,128)S(1)}, f32[40,512]{1,0:T(8,128)S(1)}, u32[]{:S(2)}, u32[]{:S(2)}) %collective-permute-start.2) | collective-permute-done | bytes 81952 | tf_op jit(solution)/shard_map/ppermute | solution.py:570
  16.2 0.0 copy-done.1
  16.2 3.0 %faces.1 = (f32[10,24,512]{2,1,0:T(8,128)S(1)}, f32[10,16,512]{2,1,0:T(8,128)S(1)}, f32[10,16,512]{2,1,0:T(8,128)S(1)}, f32[10,16,512]{2,1,0:T(8,128)S(1)}, f32[...) custom-call(s32[4]{0:T(128)S(1)} %copy-done.1, f32[19,8,16,512]{3,2,1,0:T(8,128)S(1)} %copy-done, ...), custom_call_target="tpu_custom_call" | custom-call | tf_op jit(solution)/shard_map/faces/pallas_call | solution.py:627
  19.2 3.4 %collective-permute-start.6 = (f32[10,24,512]{2,1,0:T(8,128)S(1)}, f32[10,24,512]{2,1,0:T(8,128)S(1)}, u32[]{:S(2)}, u32[]{:S(2)}) collective-permute-start(f32[10,24,512]{2,1,0:T(8,128)S(1)} %get-tuple-element.26), channel_id=1, source_target_pairs={{0,1},{1,0},{2,3},{3,2},{4,5},{5,4},{6,7},{7,6},{8,9},{9,8},{10,11... | collective-permute-start | bytes 1474568 | tf_op jit(solution)/shard_map/ppermute | solution.py:570
  22.5 0.0 collective-permute-start.7
  22.5 1.5 %collective-permute-start.4 = (f32[10,16,512]{2,1,0:T(8,128)S(1)}, f32[10,16,512]{2,1,0:T(8,128)S(1)}, u32[]{:S(2)}, u32[]{:S(2)}) collective-permute-start(f32[10,16,512]{2,1,0:T(8,128)S(1)} %get-tuple-element.23), channel_id=1, source_target_pairs={{0,28},{1,13},{2,30},{3,15},{4,24},{5,9},{6,26},{7,11},{8,4},{9,21... | collective-permute-start | bytes 983048 | tf_op jit(solution)/shard_map/ppermute | solution.py:570
  24.0 4.4 %collective-permute-start.5 = (f32[10,16,512]{2,1,0:T(8,128)S(1)}, f32[10,16,512]{2,1,0:T(8,128)S(1)}, u32[]{:S(2)}, u32[]{:S(2)}) collective-permute-start(f32[10,16,512]{2,1,0:T(8,128)S(1)} %get-tuple-element.24), channel_id=1, source_target_pairs={{0,11},{1,30},{2,13},{3,24},{4,15},{5,26},{6,9},{7,28},{8,19},{9,6... | collective-permute-start | bytes 983048 | tf_op jit(solution)/shard_map/ppermute | solution.py:570
  28.5 0.0 collective-permute-done.6.mate_rim
  28.5 1.3 %collective-permute-done.7.cross_rim = f32[10,8,512]{2,1,0:T(8,128)S(1)} collective-permute-done((f32[10,8,512]{2,1,0:T(8,128)S(1)}, f32[10,8,512]{2,1,0:T(8,128)S(1)}, u32[]{:S(2)}, u32[]{:S(2)}) %collective-permute-start.7) | collective-permute-done | bytes 163872 | tf_op jit(solution)/shard_map/ppermute | solution.py:570
  29.8 0.0 collective-permute-start.8
  29.8 12.8 %bulk.1 = (f32[19,8,16,512]{3,2,1,0:T(8,128)}, f32[19,8,16,512]{3,2,1,0:T(8,128)}) custom-call(f32[10,16,512]{2,1,0:T(8,128)S(1)} %slice_add_fusion.after, f32[19,8,16,512]{3,2,1,0:T(8,128)} %f_ref.7, f32[19,8,16,512]{3,2,1,0:T(8,128)} %g_ref.7, f32[8,16,512]{2,1,0:T(8,128)S(1)} %get-tuple-element.20.phi_ref, f32[16,512]{1,0:T(8,128)S(1)} %get-tuple-element.29.minus, ...), custom_call_target="tpu_custom_call" | custom-call | tf_op jit(solution)/shard_map/bulk/pallas_call | solution.py:669
  42.6 11.2 %collective-permute-done.4.direct = f32[10,16,512]{2,1,0:T(8,128)S(1)} collective-permute-done((f32[10,16,512]{2,1,0:T(8,128)S(1)}, f32[10,16,512]{2,1,0:T(8,128)S(1)}, u32[]{:S(2)}, u32[]{:S(2)}) %collective-permute-start.4) | collective-permute-done | bytes 327712 | tf_op jit(solution)/shard_map/ppermute | solution.py:570
  53.9 0.0 collective-permute-done.5.across
  53.9 10.6 %collective-permute-done.8.joint = f32[10,16,512]{2,1,0:T(8,128)S(1)} collective-permute-done((f32[10,16,512]{2,1,0:T(8,128)S(1)}, f32[10,16,512]{2,1,0:T(8,128)S(1)}, u32[]{:S(2)}, u32[]{:S(2)}) %collective-permute-start.8) | collective-permute-done | bytes 327712 | tf_op jit(solution)/shard_map/ppermute | solution.py:570
  64.5 1.0 %x_fill.1 = (f32[19,8,16,512]{3,2,1,0:T(8,128)}, f32[19,8,16,512]{3,2,1,0:T(8,128)}) custom-call(f32[10,16,512]{2,1,0:T(8,128)S(1)} %collective-permute-done.4.direct, f32[10,16,512]{2,1,0:T(8,128)S(1)} %collective-permute-done.5.across, f32[10,16,512]{2,1,0:T(8,128)S(1)} %collective-permute-done.8.joint, ...), custom_call_target="tpu_custom_call", output_to_operand_aliasing={{0}: (3, {}), {1}: (4, {})} | custom-call | tf_op jit(solution)/shard_map/x_fill/pallas_call | solution.py:682
  (4 shorter events, 0.1 us)
Async XLA Ops:
  2.0 8.6 %collective-permute-start = (f32[16,512]{1,0:T(8,128)S(1)}, f32[16,512]{1,0:T(8,128)S(1)}, u32[]{:S(2)}, u32[]{:S(2)}) collective-permute-start(f32[16,512]{1,0:T(8,128)S(1)} %get-tuple-element.35.top), channel_id=1, source_target_pairs={{0,12},{1,13},{2,14},{3,15},{4,8},{5,9},{6,10},{7,11},{8,20},{9,21... | collective-permute-start | bytes 98312 | tf_op jit(solution)/shard_map/ppermute | solution.py:570
  6.1 7.9 %slice-start = ((s8[4980736]{0:T(1024)(128)(4,1)}), s8[4194304]{0:T(1024)(128)(4,1)S(1)}, s32[]{:S(2)}) async-start(s8[4980736]{0:T(1024)(128)(4,1)} %bitcast), calls=%async_computation | async-start | bytes 8388608
  6.1 7.9 %slice-start.1 = ((s8[4980736]{0:T(1024)(128)(4,1)}), s8[786432]{0:T(1024)(128)(4,1)S(1)}, s32[]{:S(2)}) async-start(s8[4980736]{0:T(1024)(128)(4,1)} %bitcast), calls=%async_computation.1 | async-start | bytes 1572864
  6.1 7.9 %copy-start = (f32[19,8,16,512]{3,2,1,0:T(8,128)S(1)}, f32[19,8,16,512]{3,2,1,0:T(8,128)}, u32[]{:S(2)}) copy-start(f32[19,8,16,512]{3,2,1,0:T(8,128)} %f_ref.7) | copy-start | bytes 14942212
  6.1 5.5 %collective-permute-start.1 = (f32[16,512]{1,0:T(8,128)S(1)}, f32[16,512]{1,0:T(8,128)S(1)}, u32[]{:S(2)}, u32[]{:S(2)}) collective-permute-start(f32[16,512]{1,0:T(8,128)S(1)} %get-tuple-element.34.bottom), channel_id=1, source_target_pairs={{0,28},{1,29},{2,30},{3,31},{4,24},{5,25},{6,26},{7,27},{8,4},{9,5... | collective-permute-start | bytes 98312 | tf_op jit(solution)/shard_map/ppermute | solution.py:570
  10.6 4.5 %collective-permute-start.3 = (f32[40,512]{1,0:T(8,128)S(1)}, f32[40,512]{1,0:T(8,128)S(1)}, u32[]{:S(2)}, u32[]{:S(2)}) collective-permute-start(f32[40,512]{1,0:T(8,128)S(1)} %pad_maximum_fusion.1), channel_id=1, source_target_pairs={{0,7},{1,0},{2,1},{3,2},{4,3},{5,4},{6,5},{7,6},{8,15},{9,8},{10,9... | collective-permute-start | bytes 245768 | tf_op jit(solution)/shard_map/ppermute | solution.py:570
  11.6 4.6 %copy-start.1 = (s32[4]{0:T(128)S(1)}, s32[4]{0:T(128)}, u32[]{:S(2)}) copy-start(s32[4]{0:T(128)} %offsets.1) | copy-start | bytes 52
  11.6 4.6 %collective-permute-start.2 = (f32[40,512]{1,0:T(8,128)S(1)}, f32[40,512]{1,0:T(8,128)S(1)}, u32[]{:S(2)}, u32[]{:S(2)}) collective-permute-start(f32[40,512]{1,0:T(8,128)S(1)} %pad_maximum_fusion), channel_id=1, source_target_pairs={{0,1},{1,2},{2,3},{3,4},{4,5},{5,6},{6,7},{7,0},{8,9},{9,10},{10,1... | collective-permute-start | bytes 245768 | tf_op jit(solution)/shard_map/ppermute | solution.py:570
  19.2 9.3 %collective-permute-start.6 = (f32[10,24,512]{2,1,0:T(8,128)S(1)}, f32[10,24,512]{2,1,0:T(8,128)S(1)}, u32[]{:S(2)}, u32[]{:S(2)}) collective-permute-start(f32[10,24,512]{2,1,0:T(8,128)S(1)} %get-tuple-element.26), channel_id=1, source_target_pairs={{0,1},{1,0},{2,3},{3,2},{4,5},{5,4},{6,7},{7,6},{8,9},{9,8},{10,11... | collective-permute-start | bytes 1474568 | tf_op jit(solution)/shard_map/ppermute | solution.py:570
  22.5 7.3 %collective-permute-start.7 = (f32[10,8,512]{2,1,0:T(8,128)S(1)}, f32[10,8,512]{2,1,0:T(8,128)S(1)}, u32[]{:S(2)}, u32[]{:S(2)}) collective-permute-start(f32[10,8,512]{2,1,0:T(8,128)S(1)} %get-tuple-element.27), channel_id=1, source_target_pairs={{0,7},{1,2},{2,1},{3,4},{4,3},{5,6},{6,5},{7,0},{8,15},{9,10},{10,... | collective-permute-start | bytes 491528 | tf_op jit(solution)/shard_map/ppermute | solution.py:570
  22.5 31.3 %collective-permute-start.4 = (f32[10,16,512]{2,1,0:T(8,128)S(1)}, f32[10,16,512]{2,1,0:T(8,128)S(1)}, u32[]{:S(2)}, u32[]{:S(2)}) collective-permute-start(f32[10,16,512]{2,1,0:T(8,128)S(1)} %get-tuple-element.23), channel_id=1, source_target_pairs={{0,28},{1,13},{2,30},{3,15},{4,24},{5,9},{6,26},{7,11},{8,4},{9,21... | collective-permute-start | bytes 983048 | tf_op jit(solution)/shard_map/ppermute | solution.py:570
  24.0 29.8 %collective-permute-start.5 = (f32[10,16,512]{2,1,0:T(8,128)S(1)}, f32[10,16,512]{2,1,0:T(8,128)S(1)}, u32[]{:S(2)}, u32[]{:S(2)}) collective-permute-start(f32[10,16,512]{2,1,0:T(8,128)S(1)} %get-tuple-element.24), channel_id=1, source_target_pairs={{0,11},{1,30},{2,13},{3,24},{4,15},{5,26},{6,9},{7,28},{8,19},{9,6... | collective-permute-start | bytes 983048 | tf_op jit(solution)/shard_map/ppermute | solution.py:570
  29.8 34.7 %collective-permute-start.8 = (f32[10,16,512]{2,1,0:T(8,128)S(1)}, f32[10,16,512]{2,1,0:T(8,128)S(1)}, u32[]{:S(2)}, u32[]{:S(2)}) collective-permute-start(f32[10,16,512]{2,1,0:T(8,128)S(1)} %slice_add_fusion.after), channel_id=1, source_target_pairs={{0,12},{1,29},{2,14},{3,31},{4,8},{5,25},{6,10},{7,27},{8,20},{9,5... | collective-permute-start | bytes 983048 | tf_op jit(solution)/shard_map/ppermute | solution.py:570

commit v5 on v4

--- a/solution.py
+++ b/solution.py
@@ -283,6 +283,14 @@
             rims[s, 9 + j] = g_ref[i, :, edge, :]
 
 
+def half_rows(rows, first):
+    return slice(0, rows // 2) if first else slice(rows // 2, rows)
+
+
+def seam_rows(rows, up):
+    return slice(rows // 2 - 2, rows // 2) if up else slice(rows // 2, rows // 2 + 2)
+
+
 def rim_values(rims, s, phi_ref, minus, plus, south_msg, north_msg, line, edge, chosen, store):
     layers, rows, cols = phi_ref.shape
     phi = phi_ref[:, edge, :]
@@ -321,7 +329,9 @@
     north_msg,
     mate,
     direct,
+    direct_short,
     across,
+    across_short,
     joint,
     cross,
     minus_out,
@@ -445,6 +455,18 @@
                 shear.take(up, 0, rest, cy, joint if up else direct, j)
                 shear.take(up, 1, rest, cy, across if up else mate, j)
 
+    def shorten(direct_up, across_up):
+        for j in range(10):
+            direct_short[j] = direct[j, half_rows(rows, direct_up)]
+            across_short[part * j : part * j + part] = across[j, half_rows(rows, not across_up)]
+            across_short[seam + 2 * j : seam + 2 * j + 2] = across[j, seam_rows(rows, across_up)]
+
+    part = rows // 2
+    seam = 10 * part
+    across_short[seam + 20 : seam + 24] = jnp.zeros((4, cols), f32)
+    pl.when(planes.odd)(lambda: shorten(True, False))
+    pl.when(jnp.logical_not(planes.odd))(lambda: shorten(False, True))
+
 
 def bulk_kernel(
     after,
@@ -527,19 +549,54 @@
     lax.fori_loop(0, layers, layer, 0)
 
 
-def face_fill_kernel(direct, across, joint, f_in, g_in, f_out, g_out, low, high, sems):
-    layers = f_out.shape[1]
-    odd = lax.rem(lax.axis_index("gy"), 2) == 1
-
-    @pl.when(odd)
+def face_fill_kernel(
+    sizes,
+    offsets,
+    direct,
+    direct_short,
+    across,
+    across_short,
+    joint,
+    f_in,
+    g_in,
+    f_out,
+    g_out,
+    low,
+    high,
+    sems,
+):
+    layers, rows = f_out.shape[1], f_out.shape[2]
+    planes = Planes(offsets, rows, sizes)
+    part = rows // 2
+    seam = 10 * part
+
+    def merge(out, rest, up):
+        is_long = rest > part
+        near, other, between = half_rows(rows, up), half_rows(rows, not up), seam_rows(rows, up)
+
+        @pl.when(is_long)
+        def _():
+            out[...] = across[...]
+            for j in range(10):
+                out[j, near] = out[j, near] + direct_short[j]
+
+        @pl.when(jnp.logical_not(is_long))
+        def _():
+            out[...] = direct[...]
+            for j in range(10):
+                out[j, other] = out[j, other] + across_short[part * j : part * j + part]
+                at = seam + 2 * j
+                out[j, between] = out[j, between] + across_short[at : at + 2]
+
+    @pl.when(planes.odd)
     def _():
-        low[...] = direct[...] + across[...]
+        merge(low, planes.low_rest, True)
         high[...] = joint[...]
 
-    @pl.when(jnp.logical_not(odd))
+    @pl.when(jnp.logical_not(planes.odd))
     def _():
         low[...] = joint[...]
-        high[...] = direct[...] + across[...]
+        merge(high, planes.up_rest, False)
 
     copies = []
     for family, out in enumerate((f_out, g_out)):
@@ -621,14 +678,17 @@
         name="moments",
     )(momentum_dist, order_dist)
 
+    part = rows // 2
     ten = jax.ShapeDtypeStruct((10, rows, cols), f32)
+    ten_short = jax.ShapeDtypeStruct((10, part, cols), f32)
+    ten_seam = jax.ShapeDtypeStruct((10 * part + 24, cols), f32)
     side = jax.ShapeDtypeStruct((10, layers, cols), f32)
     ten_side = jax.ShapeDtypeStruct((10, rows + layers, cols), f32)
-    mate, direct, across, joint, cross, minus, plus = pl.pallas_call(
+    *outgoing, minus, plus = pl.pallas_call(
         functools.partial(face_kernel, (count_x, count_y)),
-        out_shape=[ten_side] + [ten] * 3 + [side] + [plane] * 2,
+        out_shape=[ten_side, ten, ten_short, ten, ten_seam, ten, side] + [plane] * 2,
         in_specs=[smem] + [vmem] * 9,
-        out_specs=[vmem] * 7,
+        out_specs=[vmem] * 9,
         scratch_shapes=[
             VMEM((rows + 16, cols), f32),
             VMEM((rows + 16, cols), f32),
@@ -655,44 +715,70 @@
         south_msg,
         north_msg,
     )
-
-    mate = hop(mate, lambda x, y: (x, y ^ 1))
-    cross = hop(cross, lambda x, y: (x, y + 1 if y % 2 == 1 else y - 1))
-    direct = hop_parity(direct, True, 0)
-    across = hop_parity(across, False, 1)
-    joint, cross = lax.optimization_barrier((joint + mate[:, :rows], cross))
-    after = joint
-    joint = hop_parity(joint, False, 0)
     around = (phi, minus, plus, south_msg, north_msg)
-
     whole = jax.ShapeDtypeStruct(momentum_dist.shape, f32)
-    next_f, next_g = pl.pallas_call(
-        bulk_kernel,
-        out_shape=[whole, whole],
-        in_specs=[anywhere] + [vmem] * 9,
-        out_specs=[vmem] * 2,
-        scratch_shapes=[
-            VMEM((layers + 2, rows, cols), f32),
-            VMEM((rows + 16, cols), f32),
-        ],
-        compiler_params=params(48 << 20),
-        name="bulk",
-    )(after, momentum_dist, order_dist, *around, mate, cross)
-
-    return pl.pallas_call(
-        face_fill_kernel,
-        out_shape=[whole, whole],
-        in_specs=[vmem] * 3 + [anywhere, anywhere],
-        out_specs=[anywhere, anywhere],
-        scratch_shapes=[
-            VMEM((10, rows, cols), f32),
-            VMEM((10, rows, cols), f32),
-            pltpu.SemaphoreType.DMA((2, 10)),
-        ],
-        input_output_aliases={3: 0, 4: 1},
-        compiler_params=params(24 << 20),
-        name="x_fill",
-    )(direct, across, joint, next_f, next_g)
+
+    def finish(long_planes, mate, direct, direct_short, across, across_short, joint, cross):
+
+        def is_long(x):
+            return x % per_plane == 0 and x // per_plane % 4 in long_planes
+
+        def hop_some(value, odd_up, extra, long):
+            pairs = []
+            for x in range(count_x):
+                for y in range(count_y):
+                    up = (y % 2 == 1) == odd_up
+                    tx = (x + 1 if up else x - 1) % count_x
+                    if is_long(tx if up else x) != long:
+                        continue
+                    ty = y - base_up(x) - extra if up else y + base_low(x) + extra
+                    pairs.append((x * count_y + y, tx * count_y + ty % count_y))
+            return lax.ppermute(value, ("gx", "gy"), pairs)
+
+        mate = hop(mate, lambda x, y: (x, y ^ 1))
+        cross = hop(cross, lambda x, y: (x, y + 1 if y % 2 == 1 else y - 1))
+        direct = hop_some(direct, True, 0, False)
+        direct_short = hop_some(direct_short, True, 0, True)
+        across = hop_some(across, False, 1, True)
+        across_short = hop_some(across_short, False, 1, False)
+        joint, cross = lax.optimization_barrier((joint + mate[:, :rows], cross))
+        after = joint
+        joint = hop_parity(joint, False, 0)
+
+        next_f, next_g = pl.pallas_call(
+            bulk_kernel,
+            out_shape=[whole, whole],
+            in_specs=[anywhere] + [vmem] * 9,
+            out_specs=[vmem] * 2,
+            scratch_shapes=[
+                VMEM((layers + 2, rows, cols), f32),
+                VMEM((rows + 16, cols), f32),
+            ],
+            compiler_params=params(48 << 20),
+            name="bulk",
+        )(after, momentum_dist, order_dist, *around, mate, cross)
+
+        return pl.pallas_call(
+            functools.partial(face_fill_kernel, (count_x, count_y)),
+            out_shape=[whole, whole],
+            in_specs=[smem] + [vmem] * 5 + [anywhere, anywhere],
+            out_specs=[anywhere, anywhere],
+            scratch_shapes=[
+                VMEM((10, rows, cols), f32),
+                VMEM((10, rows, cols), f32),
+                pltpu.SemaphoreType.DMA((2, 10)),
+            ],
+            input_output_aliases={6: 0, 7: 1},
+            compiler_params=params(24 << 20),
+            name="x_fill",
+        )(offsets, direct, direct_short, across, across_short, joint, next_f, next_g)
+
+    is_long = [(offsets[k] - half * rows > part).astype(jnp.int32) for k in (1, 2)]
+    branches = [
+        functools.partial(finish, {3} | ({1} if k & 2 else set()) | ({2} if k & 1 else set()))
+        for k in range(4)
+    ]
+    return lax.switch(2 * is_long[0] + is_long[1], branches, *outgoing)
 
 
 def solution(mesh):

time: 65.7 us -> 61.9 us (0.942)
  the two profiles are of different devices: /device:TPU:1 before, /device:TPU:5 now
where the time goes in v5:
time: 61.9 us; the launch traced here: 61.1 us
  starting transfers between devices  20.5 us (33%)
  waiting for transfers between devices  17.7 us (29%)
  Pallas kernels  17.2 us (28%)
  local copies, waits for them, and re-layouts  2.12 us (3%)
  between operations  2 us (3%)
  other arithmetic  1.42 us (2%)
    ppermute x4, waiting for transfers between devices, hop_some(): return lax.ppermute(value, ('gx', 'gy'), pairs)  15.8 us
    ppermute x7, starting transfers between devices, hop(): return lax.ppermute(value, ('gx', 'gy'), perm)  12.2 us
    pallas_call x1, Pallas kernels, finish(): pl.pallas_call(bulk_kernel, out_shape=[whole, whole], in_specs=[anywhere]...  8.9 us
    ppermute x4, starting transfers between devices, hop_some(): return lax.ppermute(value, ('gx', 'gy'), pairs)  8.3 us
    pallas_call x1, Pallas kernels, on_device(): pl.pallas_call(phi_kernel, out_shape=[jax.ShapeDtypeStruct((layers, rows,...  3.31 us
    pallas_call x1, Pallas kernels, on_device(): pl.pallas_call(functools.partial(face_kernel, (count_x, count_y)), out_sh...  2.98 us
    ppermute x7, waiting for transfers between devices, hop(): return lax.ppermute(value, ('gx', 'gy'), perm)  1.92 us
    pallas_call x1, Pallas kernels, finish(): pl.pallas_call(functools.partial(face_fill_kernel, (count_x, count_y)), o...  1.62 us
  transfers between devices with their start and end apart: 11, of which 3 were waited for; matrix products, arithmetic and copies ran while one was open for 1% of the time, Pallas kernels for 21%

profile of v5, /device:TPU:5, one launch (start us, length us, event | category | flops | bytes accessed | tf_op | source)
XLA Modules:
  0.0 61.1 jit_solution(3565157149949226848)
XLA Ops:
  0.6 1.4 %slice_reduce_fusion = (f32[16,512]{1,0:T(8,128)S(1)}, f32[16,512]{1,0:T(8,128)S(1)}) fusion(f32[19,8,16,512]{3,2,1,0:T(8,128)} %g_ref.5), kind=kLoop, calls=%fused_computation.4 | loop fusion | flops 294912 | bytes 1310720 | tf_op jit(solution)/shard_map/reduce_sum | solution.py:648
  2.0 3.3 %collective-permute-start.28 = (f32[16,512]{1,0:T(8,128)S(1)}, f32[16,512]{1,0:T(8,128)S(1)}, u32[]{:S(2)}, u32[]{:S(2)}) collective-permute-start(f32[16,512]{1,0:T(8,128)S(1)} %get-tuple-element.237.top), channel_id=1, source_target_pairs={{0,12},{1,13},{2,14},{3,15},{4,8},{5,9},{6,10},{7,11},{8,20},{9,21... | collective-permute-start | bytes 98312 | tf_op jit(solution)/shard_map/ppermute | solution.py:627
  5.3 0.0 slice-start
  5.3 0.0 slice-start.1
  5.3 0.0 copy-start
  5.3 0.9 %collective-permute-start.29 = (f32[16,512]{1,0:T(8,128)S(1)}, f32[16,512]{1,0:T(8,128)S(1)}, u32[]{:S(2)}, u32[]{:S(2)}) collective-permute-start(f32[16,512]{1,0:T(8,128)S(1)} %get-tuple-element.236.bottom), channel_id=1, source_target_pairs={{0,28},{1,29},{2,30},{3,31},{4,24},{5,25},{6,26},{7,27},{8,4},{9,5... | collective-permute-start | bytes 98312 | tf_op jit(solution)/shard_map/ppermute | solution.py:627
  6.2 3.3 %phi_all.1 = (f32[8,16,512]{2,1,0:T(8,128)S(1)}, f32[24,512]{1,0:T(8,128)S(1)}, f32[24,512]{1,0:T(8,128)S(1)}) custom-call(f32[19,8,16,512]{3,2,1,0:T(8,128)} %f_ref.5, f32[19,8,16,512]{3,2,1,0:T(8,128)} %g_ref.5, f32[16,512]{1,0:T(8,128)S(1)} %get-tuple-element.237.top, f32[16,512]{1,0:T(8,128)S(1)} %get-tuple-element.236.bottom), custom_call_target="tpu_custom_call" | custom-call | tf_op jit(solution)/shard_map/phi_all/pallas_call | solution.py:653
  9.5 0.0 slice-done
  9.5 0.0 slice-done.1
  9.6 1.5 %copy-done = f32[19,8,16,512]{3,2,1,0:T(8,128)S(1)} copy-done((f32[19,8,16,512]{3,2,1,0:T(8,128)S(1)}, f32[19,8,16,512]{3,2,1,0:T(8,128)}, u32[]{:S(2)}) %copy-start) | copy-done | bytes 4980760
  11.1 0.0 copy-start.1
  11.1 0.4 moments.1
  11.5 0.0 collective-permute-done.28.rise
  11.5 1.0 %collective-permute-start.31 = (f32[40,512]{1,0:T(8,128)S(1)}, f32[40,512]{1,0:T(8,128)S(1)}, u32[]{:S(2)}, u32[]{:S(2)}) collective-permute-start(f32[40,512]{1,0:T(8,128)S(1)} %pad_maximum_fusion.1), channel_id=1, source_target_pairs={{0,7},{1,0},{2,1},{3,2},{4,3},{5,4},{6,5},{7,6},{8,15},{9,8},{10,9... | collective-permute-start | bytes 245768 | tf_op jit(solution)/shard_map/ppermute | solution.py:627
  12.5 0.0 collective-permute-done.29.fall
  12.5 1.3 %collective-permute-start.30 = (f32[40,512]{1,0:T(8,128)S(1)}, f32[40,512]{1,0:T(8,128)S(1)}, u32[]{:S(2)}, u32[]{:S(2)}) collective-permute-start(f32[40,512]{1,0:T(8,128)S(1)} %pad_maximum_fusion), channel_id=1, source_target_pairs={{0,1},{1,2},{2,3},{3,4},{4,5},{5,6},{6,7},{7,0},{8,9},{9,10},{10,1... | collective-permute-start | bytes 245768 | tf_op jit(solution)/shard_map/ppermute | solution.py:627
  13.8 0.0 copy-done.1
  13.8 0.6 fusion
  15.7 0.1 collective-permute-done.31.north_msg
  15.8 0.0 collective-permute-done.30.south_msg
  15.8 3.0 %faces.1 = (f32[10,24,512]{2,1,0:T(8,128)S(1)}, f32[10,16,512]{2,1,0:T(8,128)S(1)}, f32[10,8,512]{2,1,0:T(8,128)S(1)}, f32[10,16,512]{2,1,0:T(8,128)S(1)}, f32[1...) custom-call(s32[4]{0:T(128)S(1)} %copy-done.1, ...), custom_call_target="tpu_custom_call" | custom-call | tf_op jit(solution)/shard_map/faces/pallas_call | solution.py:687
  18.8 42.2 %conditional.1 = ((f32[19,8,16,512]{3,2,1,0:T(8,128)}, f32[19,8,16,512]{3,2,1,0:T(8,128)})) conditional(s32[]{:T(128)} %bitcast, (f32[10,16,512]{2,1,0:T(8,128)S(1)}, f32[10,8,512]{2,1,0:T(8,128)S(1)}, f32[10,16,512]{2,1,0:T(8,128)S(1)}, f32[104,512]{1,0:T(8,128)S(1)}, f32[10,24,512]{2,1,0:T(8,128)S(1)}, ...), branch_computations={%region_2.0_spmd, %region_3.0_spmd, %region_4.0_spmd, %region_5.0_... | conditional | flops 81920 | bytes 9044256 | solution.py:781
  18.9 3.3 %collective-permute-start.25 = (f32[10,24,512]{2,1,0:T(8,128)S(1)}, f32[10,24,512]{2,1,0:T(8,128)S(1)}, u32[]{:S(2)}, u32[]{:S(2)}) collective-permute-start(f32[10,24,512]{2,1,0:T(8,128)S(1)} %get-tuple-element.183), channel_id=1, source_target_pairs={{0,1},{1,0},{2,3},{3,2},{4,5},{5,4},{6,7},{7,6},{8,9},{9,8},{10,11... | collective-permute-start | bytes 1474568 | tf_op jit(solution)/shard_map/cond/branch_3_fun/ppermute | solution.py:627
  22.2 0.0 collective-permute-start.26
  22.2 0.7 %collective-permute-start.21 = (f32[10,16,512]{2,1,0:T(8,128)S(1)}, f32[10,16,512]{2,1,0:T(8,128)S(1)}, u32[]{:S(2)}, u32[]{:S(2)}) collective-permute-start(f32[10,16,512]{2,1,0:T(8,128)S(1)} %get-tuple-element.178), channel_id=1, source_target_pairs={{0,28},{2,30},{4,24},{6,26},{25,5},{27,7},{29,1},{31,3}} | collective-permute-start | bytes 983048 | tf_op jit(solution)/shard_map/cond/branch_3_fun/ppermute | solution.py:736
  22.9 4.2 %collective-permute-start.23 = (f32[10,16,512]{2,1,0:T(8,128)S(1)}, f32[10,16,512]{2,1,0:T(8,128)S(1)}, u32[]{:S(2)}, u32[]{:S(2)}) collective-permute-start(f32[10,16,512]{2,1,0:T(8,128)S(1)} %get-tuple-element.180), channel_id=1, source_target_pairs={{0,11},{2,13},{4,15},{6,9},{8,19},{9,6},{10,21},{11,0},{12,23},{13... | collective-permute-start | bytes 983048 | tf_op jit(solution)/shard_map/cond/branch_3_fun/ppermute | solution.py:736
  27.0 0.0 collective-permute-done.25.mate_rim
  27.1 1.8 %collective-permute-done.26.cross_rim = f32[10,8,512]{2,1,0:T(8,128)S(1)} collective-permute-done((f32[10,8,512]{2,1,0:T(8,128)S(1)}, f32[10,8,512]{2,1,0:T(8,128)S(1)}, u32[]{:S(2)}, u32[]{:S(2)}) %collective-permute-start.26) | collective-permute-done | bytes 163872 | tf_op jit(solution)/shard_map/cond/branch_3_fun/ppermute | solution.py:627
  28.9 2.4 %collective-permute-start.27 = (f32[10,16,512]{2,1,0:T(8,128)S(1)}, f32[10,16,512]{2,1,0:T(8,128)S(1)}, u32[]{:S(2)}, u32[]{:S(2)}) collective-permute-start(f32[10,16,512]{2,1,0:T(8,128)S(1)} %slice_add_fusion.3.after), channel_id=1, source_target_pairs={{0,12},{1,29},{2,14},{3,31},{4,8},{5,25},{6,10},{7,27},{8,20},{9,5... | collective-permute-start | bytes 983048 | tf_op jit(solution)/shard_map/cond/branch_3_fun/ppermute | solution.py:627
  31.3 0.7 %collective-permute-start.24 = (f32[104,512]{1,0:T(8,128)S(1)}, f32[104,512]{1,0:T(8,128)S(1)}, u32[]{:S(2)}, u32[]{:S(2)}) collective-permute-start(f32[104,512]{1,0:T(8,128)S(1)} %get-tuple-element.181), channel_id=1, source_target_pairs={{1,30},{3,24},{5,26},{7,28},{24,3},{26,5},{28,7},{30,1}} | collective-permute-start | bytes 638984 | tf_op jit(solution)/shard_map/cond/branch_3_fun/ppermute | solution.py:736
  31.9 2.8 %collective-permute-start.22 = (f32[10,8,512]{2,1,0:T(8,128)S(1)}, f32[10,8,512]{2,1,0:T(8,128)S(1)}, u32[]{:S(2)}, u32[]{:S(2)}) collective-permute-start(f32[10,8,512]{2,1,0:T(8,128)S(1)} %get-tuple-element.179), channel_id=1, source_target_pairs={{1,13},{3,15},{5,9},{7,11},{8,4},{9,21},{10,6},{11,23},{12,0},{13,... | collective-permute-start | bytes 491528 | tf_op jit(solution)/shard_map/cond/branch_3_fun/ppermute | solution.py:736
  34.7 8.9 %bulk.7 = (f32[19,8,16,512]{3,2,1,0:T(8,128)}, f32[19,8,16,512]{3,2,1,0:T(8,128)}) custom-call(f32[10,16,512]{2,1,0:T(8,128)S(1)} %slice_add_fusion.3.after, f32[19,8,16,512]{3,2,1,0:T(8,128)S(1)} %get-tuple-element.186.f_ref, f32[19,8,16,512]{3,2,1,0:T(8,128)S(1)} %get-tuple-element.187.g_ref, f32[8,16,512]{2,1,0:T(8,128)S(1)} %get-tuple-element.188.phi_ref, ...), custom_call_target="tpu_custom_call" | custom-call | tf_op jit(solution)/shard_map/cond/branch_3_fun/bulk/pallas_call | solution.py:748
  43.6 15.8 %collective-permute-done.22.direct_short = f32[10,8,512]{2,1,0:T(8,128)S(1)} collective-permute-done((f32[10,8,512]{2,1,0:T(8,128)S(1)}, f32[10,8,512]{2,1,0:T(8,128)S(1)}, u32[]{:S(2)}, u32[]{:S(2)}) %collective-permute-start.22) | collective-permute-done | bytes 163872 | tf_op jit(solution)/shard_map/cond/branch_3_fun/ppermute | solution.py:736
  59.4 0.0 collective-permute-done.24.across_short
  59.4 0.0 collective-permute-done.21.direct
  59.4 0.0 collective-permute-done.23.across
  59.4 0.0 collective-permute-done.27.joint
  59.5 1.6 %x_fill.7 = (f32[19,8,16,512]{3,2,1,0:T(8,128)}, f32[19,8,16,512]{3,2,1,0:T(8,128)}) custom-call(s32[4]{0:T(128)S(1)} %get-tuple-element.177.offsets, f32[10,16,512]{2,1,0:T(8,128)S(1)} %collective-permute-done.21.direct, f32[10,8,512]{2,1,0:T(8,128)S(1)} %collective-permute-done.22.direct_short, ...), custom_call_target="tpu_custom_call", output_to_operand_aliasing={{0}: (6, {}), {1}: (7, {})} | custom-call | tf_op jit(solution)/shard_map/cond/branch_3_fun/x_fill/pallas_call | solution.py:761
  (4 shorter events, 0.1 us)
Async XLA Ops:
  2.0 9.5 %collective-permute-start.28 = (f32[16,512]{1,0:T(8,128)S(1)}, f32[16,512]{1,0:T(8,128)S(1)}, u32[]{:S(2)}, u32[]{:S(2)}) collective-permute-start(f32[16,512]{1,0:T(8,128)S(1)} %get-tuple-element.237.top), channel_id=1, source_target_pairs={{0,12},{1,13},{2,14},{3,15},{4,8},{5,9},{6,10},{7,11},{8,20},{9,21... | collective-permute-start | bytes 98312 | tf_op jit(solution)/shard_map/ppermute | solution.py:627
  5.3 4.3 %slice-start = ((s8[4980736]{0:T(1024)(128)(4,1)}), s8[4194304]{0:T(1024)(128)(4,1)S(1)}, s32[]{:S(2)}) async-start(s8[4980736]{0:T(1024)(128)(4,1)} %bitcast.1), calls=%async_computation | async-start | bytes 8388608
  5.3 4.3 %slice-start.1 = ((s8[4980736]{0:T(1024)(128)(4,1)}), s8[786432]{0:T(1024)(128)(4,1)S(1)}, s32[]{:S(2)}) async-start(s8[4980736]{0:T(1024)(128)(4,1)} %bitcast.1), calls=%async_computation.1 | async-start | bytes 1572864
  5.3 5.8 %copy-start = (f32[19,8,16,512]{3,2,1,0:T(8,128)S(1)}, f32[19,8,16,512]{3,2,1,0:T(8,128)}, u32[]{:S(2)}) copy-start(f32[19,8,16,512]{3,2,1,0:T(8,128)} %f_ref.5) | copy-start | bytes 14942212
  5.3 7.3 %collective-permute-start.29 = (f32[16,512]{1,0:T(8,128)S(1)}, f32[16,512]{1,0:T(8,128)S(1)}, u32[]{:S(2)}, u32[]{:S(2)}) collective-permute-start(f32[16,512]{1,0:T(8,128)S(1)} %get-tuple-element.236.bottom), channel_id=1, source_target_pairs={{0,28},{1,29},{2,30},{3,31},{4,24},{5,25},{6,26},{7,27},{8,4},{9,5... | collective-permute-start | bytes 98312 | tf_op jit(solution)/shard_map/ppermute | solution.py:627
  11.1 2.7 %copy-start.1 = (s32[4]{0:T(128)S(1)}, s32[4]{0:T(128)}, u32[]{:S(2)}) copy-start(s32[4]{0:T(128)} %offsets.1) | copy-start | bytes 52
  11.5 4.3 %collective-permute-start.31 = (f32[40,512]{1,0:T(8,128)S(1)}, f32[40,512]{1,0:T(8,128)S(1)}, u32[]{:S(2)}, u32[]{:S(2)}) collective-permute-start(f32[40,512]{1,0:T(8,128)S(1)} %pad_maximum_fusion.1), channel_id=1, source_target_pairs={{0,7},{1,0},{2,1},{3,2},{4,3},{5,4},{6,5},{7,6},{8,15},{9,8},{10,9... | collective-permute-start | bytes 245768 | tf_op jit(solution)/shard_map/ppermute | solution.py:627
  12.5 3.3 %collective-permute-start.30 = (f32[40,512]{1,0:T(8,128)S(1)}, f32[40,512]{1,0:T(8,128)S(1)}, u32[]{:S(2)}, u32[]{:S(2)}) collective-permute-start(f32[40,512]{1,0:T(8,128)S(1)} %pad_maximum_fusion), channel_id=1, source_target_pairs={{0,1},{1,2},{2,3},{3,4},{4,5},{5,6},{6,7},{7,0},{8,9},{9,10},{10,1... | collective-permute-start | bytes 245768 | tf_op jit(solution)/shard_map/ppermute | solution.py:627
  18.9 8.2 %collective-permute-start.25 = (f32[10,24,512]{2,1,0:T(8,128)S(1)}, f32[10,24,512]{2,1,0:T(8,128)S(1)}, u32[]{:S(2)}, u32[]{:S(2)}) collective-permute-start(f32[10,24,512]{2,1,0:T(8,128)S(1)} %get-tuple-element.183), channel_id=1, source_target_pairs={{0,1},{1,0},{2,3},{3,2},{4,5},{5,4},{6,7},{7,6},{8,9},{9,8},{10,11... | collective-permute-start | bytes 1474568 | tf_op jit(solution)/shard_map/cond/branch_3_fun/ppermute | solution.py:627
  22.2 6.7 %collective-permute-start.26 = (f32[10,8,512]{2,1,0:T(8,128)S(1)}, f32[10,8,512]{2,1,0:T(8,128)S(1)}, u32[]{:S(2)}, u32[]{:S(2)}) collective-permute-start(f32[10,8,512]{2,1,0:T(8,128)S(1)} %get-tuple-element.184), channel_id=1, source_target_pairs={{0,7},{1,2},{2,1},{3,4},{4,3},{5,6},{6,5},{7,0},{8,15},{9,10},{10,... | collective-permute-start | bytes 491528 | tf_op jit(solution)/shard_map/cond/branch_3_fun/ppermute | solution.py:627
  22.2 37.3 %collective-permute-start.21 = (f32[10,16,512]{2,1,0:T(8,128)S(1)}, f32[10,16,512]{2,1,0:T(8,128)S(1)}, u32[]{:S(2)}, u32[]{:S(2)}) collective-permute-start(f32[10,16,512]{2,1,0:T(8,128)S(1)} %get-tuple-element.178), channel_id=1, source_target_pairs={{0,28},{2,30},{4,24},{6,26},{25,5},{27,7},{29,1},{31,3}} | collective-permute-start | bytes 983048 | tf_op jit(solution)/shard_map/cond/branch_3_fun/ppermute | solution.py:736
  22.9 36.6 %collective-permute-start.23 = (f32[10,16,512]{2,1,0:T(8,128)S(1)}, f32[10,16,512]{2,1,0:T(8,128)S(1)}, u32[]{:S(2)}, u32[]{:S(2)}) collective-permute-start(f32[10,16,512]{2,1,0:T(8,128)S(1)} %get-tuple-element.180), channel_id=1, source_target_pairs={{0,11},{2,13},{4,15},{6,9},{8,19},{9,6},{10,21},{11,0},{12,23},{13... | collective-permute-start | bytes 983048 | tf_op jit(solution)/shard_map/cond/branch_3_fun/ppermute | solution.py:736
  28.9 30.6 %collective-permute-start.27 = (f32[10,16,512]{2,1,0:T(8,128)S(1)}, f32[10,16,512]{2,1,0:T(8,128)S(1)}, u32[]{:S(2)}, u32[]{:S(2)}) collective-permute-start(f32[10,16,512]{2,1,0:T(8,128)S(1)} %slice_add_fusion.3.after), channel_id=1, source_target_pairs={{0,12},{1,29},{2,14},{3,31},{4,8},{5,25},{6,10},{7,27},{8,20},{9,5... | collective-permute-start | bytes 983048 | tf_op jit(solution)/shard_map/cond/branch_3_fun/ppermute | solution.py:627
  31.3 28.2 %collective-permute-start.24 = (f32[104,512]{1,0:T(8,128)S(1)}, f32[104,512]{1,0:T(8,128)S(1)}, u32[]{:S(2)}, u32[]{:S(2)}) collective-permute-start(f32[104,512]{1,0:T(8,128)S(1)} %get-tuple-element.181), channel_id=1, source_target_pairs={{1,30},{3,24},{5,26},{7,28},{24,3},{26,5},{28,7},{30,1}} | collective-permute-start | bytes 638984 | tf_op jit(solution)/shard_map/cond/branch_3_fun/ppermute | solution.py:736
  31.9 27.5 %collective-permute-start.22 = (f32[10,8,512]{2,1,0:T(8,128)S(1)}, f32[10,8,512]{2,1,0:T(8,128)S(1)}, u32[]{:S(2)}, u32[]{:S(2)}) collective-permute-start(f32[10,8,512]{2,1,0:T(8,128)S(1)} %get-tuple-element.179), channel_id=1, source_target_pairs={{1,13},{3,15},{5,9},{7,11},{8,4},{9,21},{10,6},{11,23},{12,0},{13,... | collective-permute-start | bytes 491528 | tf_op jit(solution)/shard_map/cond/branch_3_fun/ppermute | solution.py:736

commit v6 on v5

--- a/solution.py
+++ b/solution.py
@@ -189,7 +189,7 @@
     return total
 
 
-def phi_kernel(f_ref, g_ref, top, bottom, phi_ref, to_north, to_south, fbuf, gbuf, sems):
+def phi_kernel(f_ref, g_ref, top, bottom, phi_ref, to_north, to_south, gbuf, fbuf, sems):
     layers, rows = phi_ref.shape[0], phi_ref.shape[1]
     faces = (layers - 1, 0)
     f_copies = [
@@ -270,7 +270,7 @@
     return f_post - 0.25 * cells[0], g_post - (1.0 / 9.0) * cells[1]
 
 
-def moment_kernel(f_ref, g_ref, faces, rims):
+def moment_kernel(after_north, after_south, f_ref, g_ref, faces, rims):
     layers, rows = f_ref.shape[1], f_ref.shape[2]
     for s, x in enumerate((layers - 1, 0)):
         for k, part in enumerate(moments_of(lambda i: f_ref[i, x])):
@@ -291,7 +291,7 @@
     return slice(rows // 2 - 2, rows // 2) if up else slice(rows // 2, rows // 2 + 2)
 
 
-def rim_values(rims, s, phi_ref, minus, plus, south_msg, north_msg, line, edge, chosen, store):
+def rim_values(rims, s, phi_ref, minus, plus, south_msg, north_msg, line, edge, chosen, out):
     layers, rows, cols = phi_ref.shape
     phi = phi_ref[:, edge, :]
     with_halo(line, phi, minus[edge : edge + 1], plus[edge : edge + 1])
@@ -310,9 +310,9 @@
     for j, i in enumerate(chosen):
         cz = lattice_velocity[i][2]
         even, odd = site.pair_f(i)
-        store(j, z_moved(even + odd - 0.25 * rims[s, 4 + j], cz))
+        out[s, j] = z_moved(even + odd - 0.25 * rims[s, 4 + j], cz)
         even, odd = site.pair_g(i)
-        store(5 + j, z_moved(even + odd - (1.0 / 9.0) * rims[s, 9 + j], cz))
+        out[s, 5 + j] = z_moved(even + odd - (1.0 / 9.0) * rims[s, 9 + j], cz)
 
 
 def face_kernel(
@@ -341,6 +341,7 @@
     window,
     halo,
     line,
+    rim_post,
     post,
     cells,
     corners,
@@ -373,17 +374,6 @@
         cells, planes, phi_ref, south_msg, north_msg, minus_wide, plus_wide
     )
     for s, (edge, chosen) in enumerate(((rows - 1, north_going), (0, south_going))):
-        to_mate = planes.odd if edge == 0 else jnp.logical_not(planes.odd)
-
-        def store(slot, value):
-            @pl.when(to_mate)
-            def _():
-                mate[slot, rows : rows + layers] = value
-
-            @pl.when(jnp.logical_not(to_mate))
-            def _():
-                cross[slot] = value
-
         rim_values(
             rims,
             s,
@@ -395,17 +385,14 @@
             line,
             edge,
             chosen,
-            store,
+            rim_post,
         )
-    for up in (True, False):
+    for side, up in enumerate((True, False)):
         x = layers - 1 if up else 0
+        delta = planes.up_jump if up else planes.low_jump
         with_halo(
             halo, phi_ref[x], south_msg[rows + x : rows + x + 1], north_msg[rows + x : rows + x + 1]
         )
-        if up:
-            near, far, rest, delta = planes.up_near, planes.up_far, planes.up_rest, planes.up_jump
-        else:
-            near, far, rest, delta = planes.low_near, planes.low_far, planes.low_rest, planes.low_jump
         for h in range(0, rows, 8):
             span = slice(h, h + 8)
             phi_h = phi_ref[x, span]
@@ -414,58 +401,58 @@
             else:
                 minus, plus = minus_wide[8 + h : 16 + h], phi_ref[x + 1, span]
             site = Site(
-                [face_moments[0 if up else 1, k, span] for k in range(4)],
+                [face_moments[side, k, span] for k in range(4)],
                 phi_h,
                 minus,
                 plus,
                 halo[7 + h : 15 + h],
                 halo[9 + h : 17 + h],
             )
-            for j in range(5):
-                i = rising[j] if up else falling[j]
+            for j, i in enumerate(rising if up else falling):
                 cz = lattice_velocity[i][2]
                 change = lattice_weight[i] * site.jump(i, delta)
                 even, odd = site.pair_f(i)
                 value = even + odd - 0.25 * f_ref[i, x, span] + site.rho * change
-                post[j, span] = z_moved(value, cz)
+                post[side, j, span] = z_moved(value, cz)
                 even, odd = site.pair_g(i)
                 value = even + odd - (1.0 / 9.0) * g_ref[i, x, span] + phi_h * change
-                post[5 + j, span] = z_moved(value, cz)
-        shear.clear()
-        for j in range(10):
-            cy = lattice_velocity[(rising if up else falling)[j % 5]][1]
-            shear.put(post[j], up, near, far)
-            corner = (0 if up else 1) + (0 if cy == 1 else 2)
-            if cy == 1:
-                gate = jnp.where(rest == (0 if up else rows - 1), near, 0.0)
-                at = rows + 7 if up else rows + 8
-            if cy == -1:
-                gate = jnp.where(rest == (rows - 1 if up else 0), far, 0.0)
-                at = 2 * rows + 7 if up else 2 * rows + 8
-            if cy != 0:
-                shear.add_row(at, gate * corners[j // 5, corner : corner + 1])
-
-            @pl.when(planes.odd)
-            def _():
-                shear.take(up, 0, rest, cy, direct if up else joint, j)
-                shear.take(up, 1, rest, cy, mate if up else across, j)
-
-            @pl.when(jnp.logical_not(planes.odd))
-            def _():
-                shear.take(up, 0, rest, cy, joint if up else direct, j)
-                shear.take(up, 1, rest, cy, across if up else mate, j)
-
-    def shorten(direct_up, across_up):
-        for j in range(10):
-            direct_short[j] = direct[j, half_rows(rows, direct_up)]
-            across_short[part * j : part * j + part] = across[j, half_rows(rows, not across_up)]
-            across_short[seam + 2 * j : seam + 2 * j + 2] = across[j, seam_rows(rows, across_up)]
+                post[side, 5 + j, span] = z_moved(value, cz)
 
     part = rows // 2
     seam = 10 * part
-    across_short[seam + 20 : seam + 24] = jnp.zeros((4, cols), f32)
-    pl.when(planes.odd)(lambda: shorten(True, False))
-    pl.when(jnp.logical_not(planes.odd))(lambda: shorten(False, True))
+
+    def hand_out(is_odd):
+        for side, up in enumerate((True, False)):
+            if up:
+                near, far, rest = planes.up_near, planes.up_far, planes.up_rest
+            else:
+                near, far, rest = planes.low_near, planes.low_far, planes.low_rest
+            first, second = (direct, mate) if up == is_odd else (joint, across)
+            shear.clear()
+            for j in range(10):
+                cy = lattice_velocity[(rising if up else falling)[j % 5]][1]
+                shear.put(post[side, j], up, near, far)
+                corner = side + (0 if cy == 1 else 2)
+                if cy == 1:
+                    gate = jnp.where(rest == (0 if up else rows - 1), near, 0.0)
+                    at = rows + 7 if up else rows + 8
+                if cy == -1:
+                    gate = jnp.where(rest == (rows - 1 if up else 0), far, 0.0)
+                    at = 2 * rows + 7 if up else 2 * rows + 8
+                if cy != 0:
+                    shear.add_row(at, gate * corners[j // 5, corner : corner + 1])
+                shear.take(up, 0, rest, cy, first, j)
+                shear.take(up, 1, rest, cy, second, j)
+        for j in range(10):
+            mate[j, rows : rows + layers] = rim_post[1 if is_odd else 0, j]
+            cross[j] = rim_post[0 if is_odd else 1, j]
+            direct_short[j] = direct[j, half_rows(rows, is_odd)]
+            across_short[part * j : part * j + part] = across[j, half_rows(rows, is_odd)]
+            across_short[seam + 2 * j : seam + 2 * j + 2] = across[j, seam_rows(rows, not is_odd)]
+        across_short[seam + 20 : seam + 24] = jnp.zeros((4, cols), f32)
+
+    pl.when(planes.odd)(lambda: hand_out(True))
+    pl.when(jnp.logical_not(planes.odd))(lambda: hand_out(False))
 
 
 def bulk_kernel(
@@ -549,20 +536,30 @@
     lax.fori_loop(0, layers, layer, 0)
 
 
-def face_fill_kernel(
+def put_faces(buf, out_f, out_g, chosen, x, sems):
+    copies = [
+        pltpu.make_async_copy(buf.at[5 * family + j], out.at[i, x], sems.at[5 * family + j])
+        for family, out in enumerate((out_f, out_g))
+        for j, i in enumerate(chosen)
+    ]
+    for copy in copies:
+        copy.start()
+    for copy in copies:
+        copy.wait()
+
+
+def merge_fill_kernel(
     sizes,
     offsets,
     direct,
     direct_short,
     across,
     across_short,
-    joint,
     f_in,
     g_in,
     f_out,
     g_out,
-    low,
-    high,
+    buf,
     sems,
 ):
     layers, rows = f_out.shape[1], f_out.shape[2]
@@ -570,46 +567,38 @@
     part = rows // 2
     seam = 10 * part
 
-    def merge(out, rest, up):
+    def merge(rest, up):
         is_long = rest > part
         near, other, between = half_rows(rows, up), half_rows(rows, not up), seam_rows(rows, up)
 
         @pl.when(is_long)
         def _():
-            out[...] = across[...]
+            buf[...] = across[...]
             for j in range(10):
-                out[j, near] = out[j, near] + direct_short[j]
+                buf[j, near] = buf[j, near] + direct_short[j]
 
         @pl.when(jnp.logical_not(is_long))
         def _():
-            out[...] = direct[...]
+            buf[...] = direct[...]
             for j in range(10):
-                out[j, other] = out[j, other] + across_short[part * j : part * j + part]
+                buf[j, other] = buf[j, other] + across_short[part * j : part * j + part]
                 at = seam + 2 * j
-                out[j, between] = out[j, between] + across_short[at : at + 2]
-
-    @pl.when(planes.odd)
-    def _():
-        merge(low, planes.low_rest, True)
-        high[...] = joint[...]
-
-    @pl.when(jnp.logical_not(planes.odd))
-    def _():
-        low[...] = joint[...]
-        merge(high, planes.up_rest, False)
-
-    copies = []
-    for family, out in enumerate((f_out, g_out)):
-        for j in range(5):
-            slot = family * 5 + j
-            for side, buf, chosen, x in ((0, low, rising, 0), (1, high, falling, layers - 1)):
-                copy = pltpu.make_async_copy(
-                    buf.at[slot], out.at[chosen[j], x], sems.at[side, slot]
-                )
-                copy.start()
-                copies.append(copy)
-    for copy in copies:
-        copy.wait()
+                buf[j, between] = buf[j, between] + across_short[at : at + 2]
+
+        if up:
+            put_faces(buf, f_out, g_out, rising, 0, sems)
+        else:
+            put_faces(buf, f_out, g_out, falling, layers - 1, sems)
+
+    pl.when(planes.odd)(lambda: merge(planes.low_rest, True))
+    pl.when(jnp.logical_not(planes.odd))(lambda: merge(planes.up_rest, False))
+
+
+def joint_fill_kernel(joint, f_in, g_in, f_out, g_out, sems):
+    odd = lax.rem(lax.axis_index("gy"), 2) == 1
+    layers = f_out.shape[1]
+    pl.when(odd)(lambda: put_faces(joint, f_out, g_out, falling, layers - 1, sems))
+    pl.when(jnp.logical_not(odd))(lambda: put_faces(joint, f_out, g_out, rising, 0, sems))
 
 
 def on_device(momentum_dist, order_dist, offsets):
@@ -650,21 +639,23 @@
     fall = hop(bottom, lambda x, y: (x - 1, y + base_low(x)))
 
     block = jax.ShapeDtypeStruct((layers + 16, cols), f32)
-    phi, to_north, to_south = pl.pallas_call(
+    phi, to_north, to_south, order_near = pl.pallas_call(
         phi_kernel,
-        out_shape=[jax.ShapeDtypeStruct((layers, rows, cols), f32)] + [block] * 2,
+        out_shape=[jax.ShapeDtypeStruct((layers, rows, cols), f32)]
+        + [block] * 2
+        + [jax.ShapeDtypeStruct(order_dist.shape, f32)],
         in_specs=[anywhere, anywhere, vmem, vmem],
-        out_specs=[vmem] * 3,
+        out_specs=[vmem] * 4,
         scratch_shapes=[
             VMEM((19, 2, rows, cols), f32),
-            VMEM((19, layers, rows, cols), f32),
             pltpu.SemaphoreType.DMA((layers + 2,)),
         ],
         compiler_params=params(52 << 20),
         name="phi_all",
     )(momentum_dist, order_dist, top, bottom)
-    south_msg = hop_y(jnp.concatenate([fall, to_north], 0), 1)
-    north_msg = hop_y(jnp.concatenate([rise, to_south], 0), -1)
+    to_north = jnp.concatenate([fall, to_north], 0)
+    to_south = jnp.concatenate([rise, to_south], 0)
+    south_msg, north_msg = hop_y(to_north, 1), hop_y(to_south, -1)
 
     face_moments, rims = pl.pallas_call(
         moment_kernel,
@@ -672,11 +663,11 @@
             jax.ShapeDtypeStruct((2, 4, rows, cols), f32),
             jax.ShapeDtypeStruct((2, 14, layers, cols), f32),
         ],
-        in_specs=[vmem] * 2,
+        in_specs=[anywhere, anywhere, vmem, vmem],
         out_specs=[vmem] * 2,
         compiler_params=params(16 << 20),
         name="moments",
-    )(momentum_dist, order_dist)
+    )(to_north, to_south, momentum_dist, order_near)
 
     part = rows // 2
     ten = jax.ShapeDtypeStruct((10, rows, cols), f32)
@@ -695,7 +686,8 @@
             VMEM((cols // LANES, 2 * rows + 16, LANES), f32),
             VMEM((rows + 16, cols), f32),
             VMEM((layers + 16, cols), f32),
-            VMEM((10, rows, cols), f32),
+            VMEM((2, 10, layers, cols), f32),
+            VMEM((2, 10, rows, cols), f32),
             VMEM((11, 8, cols), f32),
             VMEM((2, 8, cols), f32),
             VMEM((cols // LANES, rows + 16, LANES), f32),
@@ -706,7 +698,7 @@
     )(
         offsets,
         momentum_dist,
-        order_dist,
+        order_near,
         face_moments,
         rims,
         phi,
@@ -735,13 +727,13 @@
                     pairs.append((x * count_y + y, tx * count_y + ty % count_y))
             return lax.ppermute(value, ("gx", "gy"), pairs)
 
+        cross = hop(cross, lambda x, y: (x, y + 1 if y % 2 == 1 else y - 1))
         mate = hop(mate, lambda x, y: (x, y ^ 1))
-        cross = hop(cross, lambda x, y: (x, y + 1 if y % 2 == 1 else y - 1))
         direct = hop_some(direct, True, 0, False)
         direct_short = hop_some(direct_short, True, 0, True)
         across = hop_some(across, False, 1, True)
         across_short = hop_some(across_short, False, 1, False)
-        joint, cross = lax.optimization_barrier((joint + mate[:, :rows], cross))
+        joint = joint + mate[:, :rows]
         after = joint
         joint = hop_parity(joint, False, 0)
 
@@ -756,22 +748,29 @@
             ],
             compiler_params=params(48 << 20),
             name="bulk",
-        )(after, momentum_dist, order_dist, *around, mate, cross)
+        )(after, momentum_dist, order_near, *around, mate, cross)
+
+        next_f, next_g = pl.pallas_call(
+            functools.partial(merge_fill_kernel, (count_x, count_y)),
+            out_shape=[whole, whole],
+            in_specs=[smem] + [vmem] * 4 + [anywhere, anywhere],
+            out_specs=[anywhere, anywhere],
+            scratch_shapes=[VMEM((10, rows, cols), f32), pltpu.SemaphoreType.DMA((10,))],
+            input_output_aliases={5: 0, 6: 1},
+            compiler_params=params(24 << 20),
+            name="merge_fill",
+        )(offsets, direct, direct_short, across, across_short, next_f, next_g)
 
         return pl.pallas_call(
-            functools.partial(face_fill_kernel, (count_x, count_y)),
+            joint_fill_kernel,
             out_shape=[whole, whole],
-            in_specs=[smem] + [vmem] * 5 + [anywhere, anywhere],
+            in_specs=[vmem, anywhere, anywhere],
             out_specs=[anywhere, anywhere],
-            scratch_shapes=[
-                VMEM((10, rows, cols), f32),
-                VMEM((10, rows, cols), f32),
-                pltpu.SemaphoreType.DMA((2, 10)),
-            ],
-            input_output_aliases={6: 0, 7: 1},
+            scratch_shapes=[pltpu.SemaphoreType.DMA((10,))],
+            input_output_aliases={1: 0, 2: 1},
             compiler_params=params(24 << 20),
-            name="x_fill",
-        )(offsets, direct, direct_short, across, across_short, joint, next_f, next_g)
+            name="joint_fill",
+        )(joint, next_f, next_g)
 
     is_long = [(offsets[k] - half * rows > part).astype(jnp.int32) for k in (1, 2)]
     branches = [

time: 61.9 us -> 61.4 us (level)
  the two profiles are of different devices: /device:TPU:5 before, /device:TPU:14 now
where the time goes in v6:
time: 61.4 us; the launch traced here: 60.7 us
  waiting for transfers between devices  21.4 us (35%)
  starting transfers between devices  18.4 us (30%)
  Pallas kernels  16.6 us (27%)
  between operations  2.05 us (3%)
  other arithmetic  1.4 us (2%)
  local copies, waits for them, and re-layouts  0.62 us (1%)
    ppermute x4, waiting for transfers between devices, hop_some(): return lax.ppermute(value, ('gx', 'gy'), pairs)  17.8 us
    ppermute x7, starting transfers between devices, hop(): return lax.ppermute(value, ('gx', 'gy'), perm)  12 us
    pallas_call x1, Pallas kernels, finish(): pl.pallas_call(bulk_kernel, out_shape=[whole, whole], in_specs=[anywhere]...  8.9 us
    ppermute x4, starting transfers between devices, hop_some(): return lax.ppermute(value, ('gx', 'gy'), pairs)  6.48 us
    ppermute x7, waiting for transfers between devices, hop(): return lax.ppermute(value, ('gx', 'gy'), perm)  3.63 us
    pallas_call x1, Pallas kernels, on_device(): pl.pallas_call(phi_kernel, out_shape=[jax.ShapeDtypeStruct((layers, rows,...  3.04 us
    pallas_call x1, Pallas kernels, on_device(): pl.pallas_call(functools.partial(face_kernel, (count_x, count_y)), out_sh...  2.04 us
    pallas_call x1, Pallas kernels, finish(): pl.pallas_call(functools.partial(merge_fill_kernel, (count_x, count_y)),...  1.42 us
  transfers between devices with their start and end apart: 11, of which 4 were waited for; matrix products, arithmetic and copies ran while one was open for 1% of the time, Pallas kernels for 23%

profile of v6, /device:TPU:14, one launch (start us, length us, event | category | flops | bytes accessed | tf_op | source)
XLA Modules:
  0.0 60.7 jit_solution(7006293090417411417)
XLA Ops:
  0.6 1.4 %slice_reduce_fusion = (f32[16,512]{1,0:T(8,128)S(1)}, f32[16,512]{1,0:T(8,128)S(1)}) fusion(f32[19,8,16,512]{3,2,1,0:T(8,128)} %g_ref.1), kind=kLoop, calls=%fused_computation.4 | loop fusion | flops 294912 | bytes 1310720 | tf_op jit(solution)/shard_map/reduce_sum | solution.py:637
  2.0 2.6 %collective-permute-start.29 = (f32[16,512]{1,0:T(8,128)S(1)}, f32[16,512]{1,0:T(8,128)S(1)}, u32[]{:S(2)}, u32[]{:S(2)}) collective-permute-start(f32[16,512]{1,0:T(8,128)S(1)} %get-tuple-element.239.top), channel_id=1, source_target_pairs={{0,12},{1,13},{2,14},{3,15},{4,8},{5,9},{6,10},{7,11},{8,20},{9,21... | collective-permute-start | bytes 98312 | tf_op jit(solution)/shard_map/ppermute | solution.py:616
  4.5 0.0 slice-start
  4.5 0.0 copy-start
  4.5 0.0 slice-start.1
  4.6 1.3 %collective-permute-start.28 = (f32[16,512]{1,0:T(8,128)S(1)}, f32[16,512]{1,0:T(8,128)S(1)}, u32[]{:S(2)}, u32[]{:S(2)}) collective-permute-start(f32[16,512]{1,0:T(8,128)S(1)} %get-tuple-element.238.bottom), channel_id=1, source_target_pairs={{0,28},{1,29},{2,30},{3,31},{4,24},{5,25},{6,26},{7,27},{8,4},{9,5... | collective-permute-start | bytes 98312 | tf_op jit(solution)/shard_map/ppermute | solution.py:616
  5.9 3.0 %phi_all.1 = (f32[8,16,512]{2,1,0:T(8,128)S(1)}, f32[24,512]{1,0:T(8,128)S(1)}, f32[24,512]{1,0:T(8,128)S(1)}, f32[19,8,16,512]{3,2,1,0:T(8,128)S(1)}) custom-call(f32[19,8,16,512]{3,2,1,0:T(8,128)} %f_ref.5, f32[19,8,16,512]{3,2,1,0:T(8,128)} %g_ref.1, f32[16,512]{1,0:T(8,128)S(1)} %get-tuple-element.239.top, f32[16,512]{1,0:T(8,128)S(1)} %get-tuple-element.238.bottom), custom_call_target="tpu_custom_call" | custom-call | tf_op jit(solution)/shard_map/phi_all/pallas_call | solution.py:642
  8.9 0.0 collective-permute-done.29.rise
  9.0 0.1 collective-permute-start.31
  9.0 2.1 %collective-permute-done.28.fall = f32[16,512]{1,0:T(8,128)S(1)} collective-permute-done((f32[16,512]{1,0:T(8,128)S(1)}, f32[16,512]{1,0:T(8,128)S(1)}, u32[]{:S(2)}, u32[]{:S(2)}) %collective-permute-start.28) | collective-permute-done | bytes 32800 | tf_op jit(solution)/shard_map/ppermute | solution.py:616
  11.2 0.1 collective-permute-start.30
  11.2 0.0 copy-done
  11.3 0.6 fusion
  13.1 0.0 slice-done
  13.2 0.0 slice-done.1
  13.2 0.4 moments.1
  13.6 0.0 collective-permute-done.31.north_msg
  13.6 1.5 %collective-permute-done.30.south_msg = f32[40,512]{1,0:T(8,128)S(1)} collective-permute-done((f32[40,512]{1,0:T(8,128)S(1)}, f32[40,512]{1,0:T(8,128)S(1)}, u32[]{:S(2)}, u32[]{:S(2)}) %collective-permute-start.30) | collective-permute-done | bytes 81952 | tf_op jit(solution)/shard_map/ppermute | solution.py:616
  15.1 2.0 %faces.1 = (f32[10,24,512]{2,1,0:T(8,128)S(1)}, f32[10,16,512]{2,1,0:T(8,128)S(1)}, f32[10,8,512]{2,1,0:T(8,128)S(1)}, f32[10,16,512]{2,1,0:T(8,128)S(1)}, f32[1...) custom-call(s32[4]{0:T(128)S(1)} %copy-done, ...), custom_call_target="tpu_custom_call" | custom-call | tf_op jit(solution)/shard_map/faces/pallas_call | solution.py:678
  17.1 43.6 %conditional.1 = ((f32[19,8,16,512]{3,2,1,0:T(8,128)}, f32[19,8,16,512]{3,2,1,0:T(8,128)})) conditional(s32[]{:T(128)} %bitcast, (f32[10,24,512]{2,1,0:T(8,128)S(1)}, f32[10,16,512]{2,1,0:T(8,128)S(1)}, f32[10,16,512]{2,1,0:T(8,128)S(1)}, f32[10,8,512]{2,1,0:T(8,128)S(1)}, f32[10,16,512]{2,1,0:T(8,128)S(1)}, ...), branch_computations={%region_2.0_spmd, %region_3.0_spmd, %region_4.0_spmd, %region_5.0_... | conditional | flops 81920 | bytes 9044256 | solution.py:780
  17.2 0.1 collective-permute-start.7
  17.2 2.5 %collective-permute-start.13 = (f32[10,8,512]{2,1,0:T(8,128)S(1)}, f32[10,8,512]{2,1,0:T(8,128)S(1)}, u32[]{:S(2)}, u32[]{:S(2)}) collective-permute-start(f32[10,8,512]{2,1,0:T(8,128)S(1)} %get-tuple-element.153), channel_id=1, source_target_pairs={{0,7},{1,2},{2,1},{3,4},{4,3},{5,6},{6,5},{7,0},{8,15},{9,10},{10,... | collective-permute-start | bytes 491528 | tf_op jit(solution)/shard_map/cond/branch_1_fun/ppermute | solution.py:616
  19.7 1.3 %collective-permute-start.9 = (f32[10,16,512]{2,1,0:T(8,128)S(1)}, f32[10,16,512]{2,1,0:T(8,128)S(1)}, u32[]{:S(2)}, u32[]{:S(2)}) collective-permute-start(f32[10,16,512]{2,1,0:T(8,128)S(1)} %get-tuple-element.142), channel_id=1, source_target_pairs={{0,28},{1,13},{2,30},{3,15},{4,24},{5,9},{6,26},{7,11},{8,4},{10,6... | collective-permute-start | bytes 983048 | tf_op jit(solution)/shard_map/cond/branch_1_fun/ppermute | solution.py:728
  21.0 0.7 %collective-permute-start.11 = (f32[10,16,512]{2,1,0:T(8,128)S(1)}, f32[10,16,512]{2,1,0:T(8,128)S(1)}, u32[]{:S(2)}, u32[]{:S(2)}) collective-permute-start(f32[10,16,512]{2,1,0:T(8,128)S(1)} %get-tuple-element.144), channel_id=1, source_target_pairs={{8,19},{10,21},{12,23},{14,17},{16,27},{17,14},{18,29},{19,8},{20,... | collective-permute-start | bytes 983048 | tf_op jit(solution)/shard_map/cond/branch_1_fun/ppermute | solution.py:728
  21.7 0.0 collective-permute-done.7.mate_rim
  21.8 5.4 %collective-permute-start.8 = (f32[10,16,512]{2,1,0:T(8,128)S(1)}, f32[10,16,512]{2,1,0:T(8,128)S(1)}, u32[]{:S(2)}, u32[]{:S(2)}) collective-permute-start(f32[10,16,512]{2,1,0:T(8,128)S(1)} %slice_add_fusion.1.after), channel_id=1, source_target_pairs={{0,12},{1,29},{2,14},{3,31},{4,8},{5,25},{6,10},{7,27},{8,20},{9,5... | collective-permute-start | bytes 983048 | tf_op jit(solution)/shard_map/cond/branch_1_fun/ppermute | solution.py:616
  27.2 3.2 %collective-permute-start.12 = (f32[104,512]{1,0:T(8,128)S(1)}, f32[104,512]{1,0:T(8,128)S(1)}, u32[]{:S(2)}, u32[]{:S(2)}) collective-permute-start(f32[104,512]{1,0:T(8,128)S(1)} %get-tuple-element.145), channel_id=1, source_target_pairs={{0,11},{1,30},{2,13},{3,24},{4,15},{5,26},{6,9},{7,28},{9,6},{11,0... | collective-permute-start | bytes 638984 | tf_op jit(solution)/shard_map/cond/branch_1_fun/ppermute | solution.py:728
  30.4 0.0 collective-permute-done.13.cross_rim
  30.4 1.3 %collective-permute-start.10 = (f32[10,8,512]{2,1,0:T(8,128)S(1)}, f32[10,8,512]{2,1,0:T(8,128)S(1)}, u32[]{:S(2)}, u32[]{:S(2)}) collective-permute-start(f32[10,8,512]{2,1,0:T(8,128)S(1)} %get-tuple-element.143), channel_id=1, source_target_pairs={{9,21},{11,23},{13,17},{15,19},{16,12},{17,29},{18,14},{19,31},{20... | collective-permute-start | bytes 491528 | tf_op jit(solution)/shard_map/cond/branch_1_fun/ppermute | solution.py:728
  31.7 8.9 %bulk.5 = (f32[19,8,16,512]{3,2,1,0:T(8,128)}, f32[19,8,16,512]{3,2,1,0:T(8,128)}) custom-call(f32[10,16,512]{2,1,0:T(8,128)S(1)} %slice_add_fusion.1.after, f32[19,8,16,512]{3,2,1,0:T(8,128)S(1)} %get-tuple-element.146.f_ref, f32[19,8,16,512]{3,2,1,0:T(8,128)S(1)} %get-tuple-element.147.g_ref, f32[8,16,512]{2,1,0:T(8,128)S(1)} %get-tuple-element.148.phi_ref, ...), custom_call_target="tpu_custom_call" | custom-call | tf_op jit(solution)/shard_map/cond/branch_1_fun/bulk/pallas_call | solution.py:740
  40.6 13.4 %collective-permute-done.10.direct_short = f32[10,8,512]{2,1,0:T(8,128)S(1)} collective-permute-done((f32[10,8,512]{2,1,0:T(8,128)S(1)}, f32[10,8,512]{2,1,0:T(8,128)S(1)}, u32[]{:S(2)}, u32[]{:S(2)}) %collective-permute-start.10) | collective-permute-done | bytes 163872 | tf_op jit(solution)/shard_map/cond/branch_1_fun/ppermute | solution.py:728
  54.0 4.4 %collective-permute-done.12.across_short = f32[104,512]{1,0:T(8,128)S(1)} collective-permute-done((f32[104,512]{1,0:T(8,128)S(1)}, f32[104,512]{1,0:T(8,128)S(1)}, u32[]{:S(2)}, u32[]{:S(2)}) %collective-permute-start.12) | collective-permute-done | bytes 213024 | tf_op jit(solution)/shard_map/cond/branch_1_fun/ppermute | solution.py:728
  58.4 0.0 collective-permute-done.9.direct
  58.4 0.0 collective-permute-done.11.across
  58.4 1.4 %merge_fill.5 = (f32[19,8,16,512]{3,2,1,0:T(8,128)}, f32[19,8,16,512]{3,2,1,0:T(8,128)}) custom-call(s32[4]{0:T(128)S(1)} %get-tuple-element.141.offsets, f32[10,16,512]{2,1,0:T(8,128)S(1)} %collective-permute-done.9.direct, f32[10,8,512]{2,1,0:T(8,128)S(1)} %collective-permute-done.10.direct_short, ...), custom_call_target="tpu_custom_call", output_to_operand_aliasing={{0}: (5, {}), {1}: (6, {})} | custom-call | tf_op jit(solution)/shard_map/cond/branch_1_fun/merge_fill/pallas_call | solution.py:753
  59.8 0.0 collective-permute-done.8.joint
  59.9 0.8 %joint_fill.5 = (f32[19,8,16,512]{3,2,1,0:T(8,128)}, f32[19,8,16,512]{3,2,1,0:T(8,128)}) custom-call(f32[10,16,512]{2,1,0:T(8,128)S(1)} %collective-permute-done.8.joint, f32[19,8,16,512]{3,2,1,0:T(8,128)} %get-tuple-element.156.f_in, f32[19,8,16,512]{3,2,1,0:T(8,128)} %get-tuple-element.157.g_in), custom_call_target="tpu_custom_call", output_to_operand_aliasing={{0}: (1, {}), {1}: (2, {})} | custom-call | tf_op jit(solution)/shard_map/cond/branch_1_fun/joint_fill/pallas_call | solution.py:764
  (6 shorter events, 0.1 us)
Async XLA Ops:
  2.0 6.9 %collective-permute-start.29 = (f32[16,512]{1,0:T(8,128)S(1)}, f32[16,512]{1,0:T(8,128)S(1)}, u32[]{:S(2)}, u32[]{:S(2)}) collective-permute-start(f32[16,512]{1,0:T(8,128)S(1)} %get-tuple-element.239.top), channel_id=1, source_target_pairs={{0,12},{1,13},{2,14},{3,15},{4,8},{5,9},{6,10},{7,11},{8,20},{9,21... | collective-permute-start | bytes 98312 | tf_op jit(solution)/shard_map/ppermute | solution.py:616
  4.5 8.6 %slice-start = ((s8[4980736]{0:T(1024)(128)(4,1)}), s8[4194304]{0:T(1024)(128)(4,1)S(1)}, s32[]{:S(2)}) async-start(s8[4980736]{0:T(1024)(128)(4,1)} %bitcast.1), calls=%async_computation | async-start | bytes 8388608
  4.5 6.7 %copy-start = (s32[4]{0:T(128)S(1)}, s32[4]{0:T(128)}, u32[]{:S(2)}) copy-start(s32[4]{0:T(128)} %offsets.1) | copy-start | bytes 52
  4.5 8.6 %slice-start.1 = ((s8[4980736]{0:T(1024)(128)(4,1)}), s8[786432]{0:T(1024)(128)(4,1)S(1)}, s32[]{:S(2)}) async-start(s8[4980736]{0:T(1024)(128)(4,1)} %bitcast.1), calls=%async_computation.1 | async-start | bytes 1572864
  4.6 6.6 %collective-permute-start.28 = (f32[16,512]{1,0:T(8,128)S(1)}, f32[16,512]{1,0:T(8,128)S(1)}, u32[]{:S(2)}, u32[]{:S(2)}) collective-permute-start(f32[16,512]{1,0:T(8,128)S(1)} %get-tuple-element.238.bottom), channel_id=1, source_target_pairs={{0,28},{1,29},{2,30},{3,31},{4,24},{5,25},{6,26},{7,27},{8,4},{9,5... | collective-permute-start | bytes 98312 | tf_op jit(solution)/shard_map/ppermute | solution.py:616
  9.0 4.6 %collective-permute-start.31 = (f32[40,512]{1,0:T(8,128)S(1)}, f32[40,512]{1,0:T(8,128)S(1)}, u32[]{:S(2)}, u32[]{:S(2)}) collective-permute-start(f32[40,512]{1,0:T(8,128)S(1)} %constant_dynamic-update-slice_fusion.2.after_south), channel_id=1, source_target_pairs={{0,7},{1,0},{2,1},{3,2},{4,3},{5,4},{6,5},{7,6},{8,15},{9,8},{10,9... | collective-permute-start | bytes 245768 | tf_op jit(solution)/shard_map/ppermute | solution.py:616
  11.2 3.9 %collective-permute-start.30 = (f32[40,512]{1,0:T(8,128)S(1)}, f32[40,512]{1,0:T(8,128)S(1)}, u32[]{:S(2)}, u32[]{:S(2)}) collective-permute-start(f32[40,512]{1,0:T(8,128)S(1)} %constant_dynamic-update-slice_fusion.after_north), channel_id=1, source_target_pairs={{0,1},{1,2},{2,3},{3,4},{4,5},{5,6},{6,7},{7,0},{8,9},{9,10},{10,1... | collective-permute-start | bytes 245768 | tf_op jit(solution)/shard_map/ppermute | solution.py:616
  17.2 4.6 %collective-permute-start.7 = (f32[10,24,512]{2,1,0:T(8,128)S(1)}, f32[10,24,512]{2,1,0:T(8,128)S(1)}, u32[]{:S(2)}, u32[]{:S(2)}) collective-permute-start(f32[10,24,512]{2,1,0:T(8,128)S(1)} %get-tuple-element.140), channel_id=1, source_target_pairs={{0,1},{1,0},{2,3},{3,2},{4,5},{5,4},{6,7},{7,6},{8,9},{9,8},{10,11... | collective-permute-start | bytes 1474568 | tf_op jit(solution)/shard_map/cond/branch_1_fun/ppermute | solution.py:616
  17.2 13.2 %collective-permute-start.13 = (f32[10,8,512]{2,1,0:T(8,128)S(1)}, f32[10,8,512]{2,1,0:T(8,128)S(1)}, u32[]{:S(2)}, u32[]{:S(2)}) collective-permute-start(f32[10,8,512]{2,1,0:T(8,128)S(1)} %get-tuple-element.153), channel_id=1, source_target_pairs={{0,7},{1,2},{2,1},{3,4},{4,3},{5,6},{6,5},{7,0},{8,15},{9,10},{10,... | collective-permute-start | bytes 491528 | tf_op jit(solution)/shard_map/cond/branch_1_fun/ppermute | solution.py:616
  19.7 38.7 %collective-permute-start.9 = (f32[10,16,512]{2,1,0:T(8,128)S(1)}, f32[10,16,512]{2,1,0:T(8,128)S(1)}, u32[]{:S(2)}, u32[]{:S(2)}) collective-permute-start(f32[10,16,512]{2,1,0:T(8,128)S(1)} %get-tuple-element.142), channel_id=1, source_target_pairs={{0,28},{1,13},{2,30},{3,15},{4,24},{5,9},{6,26},{7,11},{8,4},{10,6... | collective-permute-start | bytes 983048 | tf_op jit(solution)/shard_map/cond/branch_1_fun/ppermute | solution.py:728
  21.0 37.4 %collective-permute-start.11 = (f32[10,16,512]{2,1,0:T(8,128)S(1)}, f32[10,16,512]{2,1,0:T(8,128)S(1)}, u32[]{:S(2)}, u32[]{:S(2)}) collective-permute-start(f32[10,16,512]{2,1,0:T(8,128)S(1)} %get-tuple-element.144), channel_id=1, source_target_pairs={{8,19},{10,21},{12,23},{14,17},{16,27},{17,14},{18,29},{19,8},{20,... | collective-permute-start | bytes 983048 | tf_op jit(solution)/shard_map/cond/branch_1_fun/ppermute | solution.py:728
  21.8 38.1 %collective-permute-start.8 = (f32[10,16,512]{2,1,0:T(8,128)S(1)}, f32[10,16,512]{2,1,0:T(8,128)S(1)}, u32[]{:S(2)}, u32[]{:S(2)}) collective-permute-start(f32[10,16,512]{2,1,0:T(8,128)S(1)} %slice_add_fusion.1.after), channel_id=1, source_target_pairs={{0,12},{1,29},{2,14},{3,31},{4,8},{5,25},{6,10},{7,27},{8,20},{9,5... | collective-permute-start | bytes 983048 | tf_op jit(solution)/shard_map/cond/branch_1_fun/ppermute | solution.py:616
  27.2 31.2 %collective-permute-start.12 = (f32[104,512]{1,0:T(8,128)S(1)}, f32[104,512]{1,0:T(8,128)S(1)}, u32[]{:S(2)}, u32[]{:S(2)}) collective-permute-start(f32[104,512]{1,0:T(8,128)S(1)} %get-tuple-element.145), channel_id=1, source_target_pairs={{0,11},{1,30},{2,13},{3,24},{4,15},{5,26},{6,9},{7,28},{9,6},{11,0... | collective-permute-start | bytes 638984 | tf_op jit(solution)/shard_map/cond/branch_1_fun/ppermute | solution.py:728
  30.4 23.6 %collective-permute-start.10 = (f32[10,8,512]{2,1,0:T(8,128)S(1)}, f32[10,8,512]{2,1,0:T(8,128)S(1)}, u32[]{:S(2)}, u32[]{:S(2)}) collective-permute-start(f32[10,8,512]{2,1,0:T(8,128)S(1)} %get-tuple-element.143), channel_id=1, source_target_pairs={{9,21},{11,23},{13,17},{15,19},{16,12},{17,29},{18,14},{19,31},{20... | collective-permute-start | bytes 491528 | tf_op jit(solution)/shard_map/cond/branch_1_fun/ppermute | solution.py:728

commit v7 on v6

--- a/solution.py
+++ b/solution.py
@@ -270,17 +270,34 @@
     return f_post - 0.25 * cells[0], g_post - (1.0 / 9.0) * cells[1]
 
 
-def moment_kernel(after_north, after_south, f_ref, g_ref, faces, rims):
+def moment_kernel(
+    base,
+    after_north,
+    after_south,
+    offsets,
+    f_ref,
+    g_ref,
+    phi_ref,
+    faces,
+    raw_north,
+    raw_south,
+    index,
+):
     layers, rows = f_ref.shape[1], f_ref.shape[2]
+    is_long = [(offsets[k] - base > rows // 2).astype(jnp.int32) for k in (1, 2)]
+    index[0] = 2 * is_long[0] + is_long[1]
     for s, x in enumerate((layers - 1, 0)):
         for k, part in enumerate(moments_of(lambda i: f_ref[i, x])):
             faces[s, k] = part
-    for s, (edge, chosen) in enumerate(((rows - 1, north_going), (0, south_going))):
-        for k, part in enumerate(moments_of(lambda i: f_ref[i, :, edge, :])):
-            rims[s, k] = part
-        for j, i in enumerate(chosen):
-            rims[s, 4 + j] = f_ref[i, :, edge, :]
-            rims[s, 9 + j] = g_ref[i, :, edge, :]
+    for out, edge, inner, chosen in (
+        (raw_north, rows - 1, rows - 2, north_going),
+        (raw_south, 0, 1, south_going),
+    ):
+        parts = moments_of(lambda i: f_ref[i, :, edge, :])
+        parts += [f_ref[i, :, edge, :] for i in chosen] + [g_ref[i, :, edge, :] for i in chosen]
+        parts.append(phi_ref[:, inner, :])
+        for k, part in enumerate(parts):
+            out[layers * k : layers * k + layers] = part
 
 
 def half_rows(rows, first):
@@ -291,28 +308,43 @@
     return slice(rows // 2 - 2, rows // 2) if up else slice(rows // 2, rows // 2 + 2)
 
 
-def rim_values(rims, s, phi_ref, minus, plus, south_msg, north_msg, line, edge, chosen, out):
+def rim_values(planes, raw, msg, phi_ref, minus_wide, plus_wide, line, south, out):
     layers, rows, cols = phi_ref.shape
-    phi = phi_ref[:, edge, :]
-    with_halo(line, phi, minus[edge : edge + 1], plus[edge : edge + 1])
-    if edge == 0:
-        below, above = south_msg[rows : rows + layers], phi_ref[:, 1, :]
+
+    def piece(k):
+        return raw[layers * k : layers * k + layers]
+
+    extra = 15 * layers
+    beside, relayed = raw[extra : extra + 1], raw[extra + 1 : extra + 2]
+    row = 7 if south else rows + 8
+    minus, plus = minus_wide[row : row + 1], plus_wide[row : row + 1]
+    low_rest, up_rest = planes.low_rest, planes.up_rest
+    if south:
+        minus = minus + jnp.where(low_rest == 0, planes.low_far, 0.0) * beside
+        plus = plus + jnp.where(up_rest == rows - 1, planes.up_far, 0.0) * relayed
     else:
-        below, above = phi_ref[:, rows - 2, :], north_msg[rows : rows + layers]
+        minus = minus + jnp.where(low_rest == rows - 1, planes.low_near, 0.0) * relayed
+        plus = plus + jnp.where(up_rest == 0, planes.up_near, 0.0) * beside
+    phi = msg[rows : rows + layers]
+    with_halo(line, phi, minus, plus)
+    if south:
+        below, above = piece(14), phi_ref[:, 0, :]
+    else:
+        below, above = phi_ref[:, rows - 1, :], piece(14)
     site = Site(
-        [rims[s, k] for k in range(4)],
+        [piece(k) for k in range(4)],
         phi,
         line[7 : 7 + layers],
         line[9 : 9 + layers],
         below,
         above,
     )
-    for j, i in enumerate(chosen):
+    for j, i in enumerate(north_going if south else south_going):
         cz = lattice_velocity[i][2]
         even, odd = site.pair_f(i)
-        out[s, j] = z_moved(even + odd - 0.25 * rims[s, 4 + j], cz)
+        out[j] = z_moved(even + odd - 0.25 * piece(4 + j), cz)
         even, odd = site.pair_g(i)
-        out[s, 5 + j] = z_moved(even + odd - (1.0 / 9.0) * rims[s, 9 + j], cz)
+        out[5 + j] = z_moved(even + odd - (1.0 / 9.0) * piece(9 + j), cz)
 
 
 def face_kernel(
@@ -321,7 +353,6 @@
     f_ref,
     g_ref,
     face_moments,
-    rims,
     phi_ref,
     rise,
     fall,
@@ -333,15 +364,10 @@
     across,
     across_short,
     joint,
-    cross,
-    minus_out,
-    plus_out,
     minus_wide,
     plus_wide,
     window,
     halo,
-    line,
-    rim_post,
     post,
     cells,
     corners,
@@ -368,25 +394,9 @@
                 near * window[k, pl.ds(start, rows + 16)]
                 + far * window[k, pl.ds(start + 1, rows + 16)]
             )
-    minus_out[...] = minus_wide[8 : 8 + rows]
-    plus_out[...] = plus_wide[8 : 8 + rows]
     corners[0], corners[1] = corner_values(
         cells, planes, phi_ref, south_msg, north_msg, minus_wide, plus_wide
     )
-    for s, (edge, chosen) in enumerate(((rows - 1, north_going), (0, south_going))):
-        rim_values(
-            rims,
-            s,
-            phi_ref,
-            minus_out,
-            plus_out,
-            south_msg,
-            north_msg,
-            line,
-            edge,
-            chosen,
-            rim_post,
-        )
     for side, up in enumerate((True, False)):
         x = layers - 1 if up else 0
         delta = planes.up_jump if up else planes.low_jump
@@ -444,8 +454,6 @@
                 shear.take(up, 0, rest, cy, first, j)
                 shear.take(up, 1, rest, cy, second, j)
         for j in range(10):
-            mate[j, rows : rows + layers] = rim_post[1 if is_odd else 0, j]
-            cross[j] = rim_post[0 if is_odd else 1, j]
             direct_short[j] = direct[j, half_rows(rows, is_odd)]
             across_short[part * j : part * j + part] = across[j, half_rows(rows, is_odd)]
             across_short[seam + 2 * j : seam + 2 * j + 2] = across[j, seam_rows(rows, not is_odd)]
@@ -456,7 +464,9 @@
 
 
 def bulk_kernel(
+    sizes,
     after,
+    offsets,
     f_ref,
     g_ref,
     phi_ref,
@@ -464,17 +474,22 @@
     plus,
     south_msg,
     north_msg,
-    mate_rim,
-    cross_rim,
+    south_raw,
+    north_raw,
     next_f,
     next_g,
     wide_phi,
     halo,
+    line,
+    south_rim,
+    north_rim,
 ):
     layers, rows, cols = phi_ref.shape
-    is_odd = lax.rem(lax.axis_index("gy"), 2) == 1
-    wide_phi[0] = minus[...]
-    wide_phi[layers + 1] = plus[...]
+    planes = Planes(offsets, rows, sizes)
+    rim_values(planes, south_raw, south_msg, phi_ref, minus, plus, line, True, south_rim)
+    rim_values(planes, north_raw, north_msg, phi_ref, minus, plus, line, False, north_rim)
+    wide_phi[0] = minus[8 : 8 + rows]
+    wide_phi[layers + 1] = plus[8 : 8 + rows]
     for x in range(layers):
         wide_phi[x + 1] = phi_ref[x]
 
@@ -503,9 +518,7 @@
                 elif cy == 1:
                     if h == 0:
                         rim = slot * 5 + north_going.index(i)
-                        out[i, at, 0:1] = jnp.where(
-                            is_odd, mate_rim[rim, pl.ds(rows + x, 1)], cross_rim[rim, pl.ds(x, 1)]
-                        )
+                        out[i, at, 0:1] = south_rim[rim, pl.ds(x, 1)]
                     if h + 8 < rows:
                         out[i, at, h + 1 : h + 9] = value
                     else:
@@ -513,9 +526,7 @@
                 else:
                     if h + 8 == rows:
                         rim = slot * 5 + south_going.index(i)
-                        out[i, at, rows - 1 : rows] = jnp.where(
-                            is_odd, cross_rim[rim, pl.ds(x, 1)], mate_rim[rim, pl.ds(rows + x, 1)]
-                        )
+                        out[i, at, rows - 1 : rows] = north_rim[rim, pl.ds(x, 1)]
                     if h > 0:
                         out[i, at, h - 1 : h + 7] = value
                     else:
@@ -638,6 +649,7 @@
     rise = hop(top, lambda x, y: (x + 1, y - base_up(x)))
     fall = hop(bottom, lambda x, y: (x - 1, y + base_low(x)))
 
+    part = rows // 2
     block = jax.ShapeDtypeStruct((layers + 16, cols), f32)
     phi, to_north, to_south, order_near = pl.pallas_call(
         phi_kernel,
@@ -657,60 +669,31 @@
     to_south = jnp.concatenate([rise, to_south], 0)
     south_msg, north_msg = hop_y(to_north, 1), hop_y(to_south, -1)
 
-    face_moments, rims = pl.pallas_call(
-        moment_kernel,
+    raw = jax.ShapeDtypeStruct((15 * layers, cols), f32)
+    face_moments, raw_north, raw_south, index = pl.pallas_call(
+        functools.partial(moment_kernel, half * rows),
         out_shape=[
             jax.ShapeDtypeStruct((2, 4, rows, cols), f32),
-            jax.ShapeDtypeStruct((2, 14, layers, cols), f32),
+            raw,
+            raw,
+            jax.ShapeDtypeStruct((1,), jnp.int32),
         ],
-        in_specs=[anywhere, anywhere, vmem, vmem],
-        out_specs=[vmem] * 2,
+        in_specs=[anywhere, anywhere, smem] + [vmem] * 3,
+        out_specs=[vmem] * 3 + [smem],
         compiler_params=params(16 << 20),
         name="moments",
-    )(to_north, to_south, momentum_dist, order_near)
-
-    part = rows // 2
+    )(to_north, to_south, offsets, momentum_dist, order_near, phi)
+    blank = jnp.zeros((6, cols), f32)
+    raw_north = jnp.concatenate([raw_north, rise[rows - 1 :], south_msg[rows - 1 : rows], blank], 0)
+    raw_south = jnp.concatenate([raw_south, fall[:1], north_msg[:1], blank], 0)
+
     ten = jax.ShapeDtypeStruct((10, rows, cols), f32)
     ten_short = jax.ShapeDtypeStruct((10, part, cols), f32)
     ten_seam = jax.ShapeDtypeStruct((10 * part + 24, cols), f32)
-    side = jax.ShapeDtypeStruct((10, layers, cols), f32)
-    ten_side = jax.ShapeDtypeStruct((10, rows + layers, cols), f32)
-    *outgoing, minus, plus = pl.pallas_call(
-        functools.partial(face_kernel, (count_x, count_y)),
-        out_shape=[ten_side, ten, ten_short, ten, ten_seam, ten, side] + [plane] * 2,
-        in_specs=[smem] + [vmem] * 9,
-        out_specs=[vmem] * 9,
-        scratch_shapes=[
-            VMEM((rows + 16, cols), f32),
-            VMEM((rows + 16, cols), f32),
-            VMEM((cols // LANES, 2 * rows + 16, LANES), f32),
-            VMEM((rows + 16, cols), f32),
-            VMEM((layers + 16, cols), f32),
-            VMEM((2, 10, layers, cols), f32),
-            VMEM((2, 10, rows, cols), f32),
-            VMEM((11, 8, cols), f32),
-            VMEM((2, 8, cols), f32),
-            VMEM((cols // LANES, rows + 16, LANES), f32),
-            VMEM((cols // LANES, 3 * rows + 16, LANES), f32),
-        ],
-        compiler_params=params(24 << 20),
-        name="faces",
-    )(
-        offsets,
-        momentum_dist,
-        order_near,
-        face_moments,
-        rims,
-        phi,
-        rise,
-        fall,
-        south_msg,
-        north_msg,
-    )
-    around = (phi, minus, plus, south_msg, north_msg)
+    wide = jax.ShapeDtypeStruct((rows + 16, cols), f32)
     whole = jax.ShapeDtypeStruct(momentum_dist.shape, f32)
 
-    def finish(long_planes, mate, direct, direct_short, across, across_short, joint, cross):
+    def finish(long_planes):
 
         def is_long(x):
             return x % per_plane == 0 and x // per_plane % 4 in long_planes
@@ -727,28 +710,59 @@
                     pairs.append((x * count_y + y, tx * count_y + ty % count_y))
             return lax.ppermute(value, ("gx", "gy"), pairs)
 
-        cross = hop(cross, lambda x, y: (x, y + 1 if y % 2 == 1 else y - 1))
+        south_raw, north_raw = hop_y(raw_north, 1), hop_y(raw_south, -1)
+        mate, direct, direct_short, across, across_short, joint, minus, plus = pl.pallas_call(
+            functools.partial(face_kernel, (count_x, count_y)),
+            out_shape=[ten, ten, ten_short, ten, ten_seam, ten] + [wide] * 2,
+            in_specs=[smem] + [vmem] * 8,
+            out_specs=[vmem] * 8,
+            scratch_shapes=[
+                VMEM((cols // LANES, 2 * rows + 16, LANES), f32),
+                VMEM((rows + 16, cols), f32),
+                VMEM((2, 10, rows, cols), f32),
+                VMEM((11, 8, cols), f32),
+                VMEM((2, 8, cols), f32),
+                VMEM((cols // LANES, rows + 16, LANES), f32),
+                VMEM((cols // LANES, 3 * rows + 16, LANES), f32),
+            ],
+            compiler_params=params(24 << 20),
+            name="faces",
+        )(
+            offsets,
+            momentum_dist,
+            order_near,
+            face_moments,
+            phi,
+            rise,
+            fall,
+            south_msg,
+            north_msg,
+        )
+        around = (phi, minus, plus, south_msg, north_msg)
         mate = hop(mate, lambda x, y: (x, y ^ 1))
         direct = hop_some(direct, True, 0, False)
         direct_short = hop_some(direct_short, True, 0, True)
         across = hop_some(across, False, 1, True)
         across_short = hop_some(across_short, False, 1, False)
-        joint = joint + mate[:, :rows]
+        joint = joint + mate
         after = joint
         joint = hop_parity(joint, False, 0)
 
         next_f, next_g = pl.pallas_call(
-            bulk_kernel,
+            functools.partial(bulk_kernel, (count_x, count_y)),
             out_shape=[whole, whole],
-            in_specs=[anywhere] + [vmem] * 9,
+            in_specs=[anywhere, smem] + [vmem] * 9,
             out_specs=[vmem] * 2,
             scratch_shapes=[
                 VMEM((layers + 2, rows, cols), f32),
                 VMEM((rows + 16, cols), f32),
+                VMEM((layers + 16, cols), f32),
+                VMEM((10, layers, cols), f32),
+                VMEM((10, layers, cols), f32),
             ],
             compiler_params=params(48 << 20),
             name="bulk",
-        )(after, momentum_dist, order_near, *around, mate, cross)
+        )(after, offsets, momentum_dist, order_near, *around, south_raw, north_raw)
 
         next_f, next_g = pl.pallas_call(
             functools.partial(merge_fill_kernel, (count_x, count_y)),
@@ -772,12 +786,11 @@
             name="joint_fill",
         )(joint, next_f, next_g)
 
-    is_long = [(offsets[k] - half * rows > part).astype(jnp.int32) for k in (1, 2)]
     branches = [
         functools.partial(finish, {3} | ({1} if k & 2 else set()) | ({2} if k & 1 else set()))
         for k in range(4)
     ]
-    return lax.switch(2 * is_long[0] + is_long[1], branches, *outgoing)
+    return lax.switch(index[0], branches)
 
 
 def solution(mesh):

time: 61.4 us -> 63.9 us (1.041)
  the two profiles are of different devices: /device:TPU:14 before, /device:TPU:1 now
where the time goes in v7:
time: 63.9 us; the launch traced here: 62.7 us
  starting transfers between devices  28.4 us (44%)
  Pallas kernels  18 us (28%)
  waiting for transfers between devices  12.5 us (20%)
  between operations  1.56 us (2%)
  other arithmetic  1.51 us (2%)
    ppermute x8, starting transfers between devices, hop(): return lax.ppermute(value, ('gx', 'gy'), perm)  20.3 us
    ppermute x8, waiting for transfers between devices, hop(): return lax.ppermute(value, ('gx', 'gy'), perm)  12.5 us
    pallas_call x1, Pallas kernels, finish(): pl.pallas_call(functools.partial(bulk_kernel, (count_x, count_y)), out_sh...  9.75 us
    ppermute x4, starting transfers between devices, hop_some(): return lax.ppermute(value, ('gx', 'gy'), pairs)  8.14 us
    pallas_call x1, Pallas kernels, on_device(): pl.pallas_call(phi_kernel, out_shape=[jax.ShapeDtypeStruct((layers, rows,...  3.31 us
    pallas_call x1, Pallas kernels, finish(): pl.pallas_call(functools.partial(face_kernel, (count_x, count_y)), out_sh...  1.7 us
    pallas_call x1, Pallas kernels, finish(): pl.pallas_call(functools.partial(merge_fill_kernel, (count_x, count_y)),...  1.42 us
    reduce_sum x1, other arithmetic, on_device(): jnp.sum(order_dist[:, layers - 1], axis=0)  1.36 us
  transfers between devices with their start and end apart: 12, of which 2 were waited for; matrix products, arithmetic and copies ran while one was open for 0% of the time, Pallas kernels for 25%

profile of v7, /device:TPU:1, one launch (start us, length us, event | category | flops | bytes accessed | tf_op | source)
XLA Modules:
  0.0 62.7 jit_solution(3648730239514087285)
XLA Ops:
  0.6 1.4 %slice_reduce_fusion = (f32[16,512]{1,0:T(8,128)S(1)}, f32[16,512]{1,0:T(8,128)S(1)}) fusion(f32[19,8,16,512]{3,2,1,0:T(8,128)} %g_ref.1), kind=kLoop, calls=%fused_computation | loop fusion | flops 294912 | bytes 1310720 | tf_op jit(solution)/shard_map/reduce_sum | solution.py:648
  2.0 4.1 %collective-permute-start.33 = (f32[16,512]{1,0:T(8,128)S(1)}, f32[16,512]{1,0:T(8,128)S(1)}, u32[]{:S(2)}, u32[]{:S(2)}) collective-permute-start(f32[16,512]{1,0:T(8,128)S(1)} %get-tuple-element.208.top), channel_id=1, source_target_pairs={{0,12},{1,13},{2,14},{3,15},{4,8},{5,9},{6,10},{7,11},{8,20},{9,21... | collective-permute-start | bytes 98312 | tf_op jit(solution)/shard_map/ppermute | solution.py:627
  6.1 0.0 slice-start
  6.1 0.0 slice-start.1
  6.1 0.0 copy-start
  6.1 1.1 %collective-permute-start.32 = (f32[16,512]{1,0:T(8,128)S(1)}, f32[16,512]{1,0:T(8,128)S(1)}, u32[]{:S(2)}, u32[]{:S(2)}) collective-permute-start(f32[16,512]{1,0:T(8,128)S(1)} %get-tuple-element.209.bottom), channel_id=1, source_target_pairs={{0,28},{1,29},{2,30},{3,31},{4,24},{5,25},{6,26},{7,27},{8,4},{9,5... | collective-permute-start | bytes 98312 | tf_op jit(solution)/shard_map/ppermute | solution.py:627
  7.2 3.3 %phi_all.1 = (f32[8,16,512]{2,1,0:T(8,128)S(1)}, f32[24,512]{1,0:T(8,128)S(1)}, f32[24,512]{1,0:T(8,128)S(1)}, f32[19,8,16,512]{3,2,1,0:T(8,128)S(1)}) custom-call(f32[19,8,16,512]{3,2,1,0:T(8,128)} %f_ref.3, f32[19,8,16,512]{3,2,1,0:T(8,128)} %g_ref.1, f32[16,512]{1,0:T(8,128)S(1)} %get-tuple-element.208.top, f32[16,512]{1,0:T(8,128)S(1)} %get-tuple-element.209.bottom), custom_call_target="tpu_custom_call" | custom-call | tf_op jit(solution)/shard_map/phi_all/pallas_call | solution.py:654
  10.5 0.0 collective-permute-done.33
  10.5 1.0 %collective-permute-start.35 = (f32[40,512]{1,0:T(8,128)S(1)}, f32[40,512]{1,0:T(8,128)S(1)}, u32[]{:S(2)}, u32[]{:S(2)}) collective-permute-start(f32[40,512]{1,0:T(8,128)S(1)} %constant_dynamic-update-slice_fusion.2.after_south), channel_id=1, source_target_pairs={{0,7},{1,0},{2,1},{3,2},{4,3},{5,4},{6,5},{7,6},{8,15},{9,8},{10,9... | collective-permute-start | bytes 245768 | tf_op jit(solution)/shard_map/ppermute | solution.py:627
  11.5 0.0 collective-permute-done.32
  11.5 2.5 %collective-permute-start.34 = (f32[40,512]{1,0:T(8,128)S(1)}, f32[40,512]{1,0:T(8,128)S(1)}, u32[]{:S(2)}, u32[]{:S(2)}) collective-permute-start(f32[40,512]{1,0:T(8,128)S(1)} %constant_dynamic-update-slice_fusion.after_north), channel_id=1, source_target_pairs={{0,1},{1,2},{2,3},{3,4},{4,5},{5,6},{6,7},{7,0},{8,9},{9,10},{10,1... | collective-permute-start | bytes 245768 | tf_op jit(solution)/shard_map/ppermute | solution.py:627
  14.0 0.1 pad.7.clone
  14.1 0.0 slice-done
  14.1 0.0 slice-done.1
  14.1 0.0 copy-done
  14.1 1.1 %moments.1 = (f32[2,4,16,512]{3,2,1,0:T(8,128)S(1)}, f32[120,512]{1,0:T(8,128)S(1)}, f32[120,512]{1,0:T(8,128)S(1)}, s32[1]{0:T(128)}) custom-call(f32[40,512]{1,0:T(8,128)S(1)} %constant_dynamic-update-slice_fusion.after_north, f32[40,512]{1,0:T(8,128)S(1)} %constant_dynamic-update-slice_fusion.2.after_south, s32[4]{0:T(128)S(1)} %copy-done, ...), custom_call_target="tpu_custom_call" | custom-call | tf_op jit(solution)/shard_map/moments/pallas_call | solution.py:673
  15.9 0.0 collective-permute-done.35
  15.9 0.4 collective-permute-done.34
  16.3 0.1 maximum_maximum_fusion.1
  16.4 46.1 %conditional.1 = ((f32[19,8,16,512]{3,2,1,0:T(8,128)}, f32[19,8,16,512]{3,2,1,0:T(8,128)})) conditional(s32[]{:T(128)} %bitcast, (s32[4]{0:T(128)S(1)}, f32[19,8,16,512]{3,2,1,0:T(8,128)S(1)}, f32[19,8,16,512]{3,2,1,0:T(8,128)S(1)}, f32[2,4,16,512]{3,2,1,0:T(8,128)S(1)}, f32[8,16,512]{2,1,0:T(8,128)S(1)}, ...), branch_computations={%region_2.0_spmd, %region_3.0_spmd, %region_4.0_spmd, %region_5.0_... | conditional | flops 81920 | bytes 9830728 | solution.py:793
  16.4 1.7 %faces.6 = (f32[10,16,512]{2,1,0:T(8,128)S(1)}, f32[10,16,512]{2,1,0:T(8,128)S(1)}, f32[10,8,512]{2,1,0:T(8,128)S(1)}, f32[10,16,512]{2,1,0:T(8,128)S(1)}, f32[1...) custom-call(s32[4]{0:T(128)S(1)} %get-tuple-element.134.offsets, ...), custom_call_target="tpu_custom_call" | custom-call | tf_op jit(solution)/shard_map/cond/branch_2_fun/faces/pallas_call | solution.py:714
  18.1 3.3 %collective-permute-start.16 = (f32[10,16,512]{2,1,0:T(8,128)S(1)}, f32[10,16,512]{2,1,0:T(8,128)S(1)}, u32[]{:S(2)}, u32[]{:S(2)}) collective-permute-start(f32[10,16,512]{2,1,0:T(8,128)S(1)} %get-tuple-element.144), channel_id=1, source_target_pairs={{0,1},{1,0},{2,3},{3,2},{4,5},{5,4},{6,7},{7,6},{8,9},{9,8},{10,11... | collective-permute-start | bytes 983048 | tf_op jit(solution)/shard_map/cond/branch_2_fun/ppermute | solution.py:627
  21.4 0.0 collective-permute-start.22
  21.4 0.5 collective-permute-start.23
  21.9 1.3 %collective-permute-start.18 = (f32[10,16,512]{2,1,0:T(8,128)S(1)}, f32[10,16,512]{2,1,0:T(8,128)S(1)}, u32[]{:S(2)}, u32[]{:S(2)}) collective-permute-start(f32[10,16,512]{2,1,0:T(8,128)S(1)} %get-tuple-element.145), channel_id=1, source_target_pairs={{0,28},{2,30},{4,24},{6,26},{9,21},{11,23},{13,17},{15,19},{16,12}... | collective-permute-start | bytes 983048 | tf_op jit(solution)/shard_map/cond/branch_2_fun/ppermute | solution.py:711
  23.2 0.7 %collective-permute-start.20 = (f32[10,16,512]{2,1,0:T(8,128)S(1)}, f32[10,16,512]{2,1,0:T(8,128)S(1)}, u32[]{:S(2)}, u32[]{:S(2)}) collective-permute-start(f32[10,16,512]{2,1,0:T(8,128)S(1)} %get-tuple-element.147), channel_id=1, source_target_pairs={{0,11},{2,13},{4,15},{6,9},{9,6},{11,0},{13,2},{15,4},{16,27},{18,... | collective-permute-start | bytes 983048 | tf_op jit(solution)/shard_map/cond/branch_2_fun/ppermute | solution.py:711
  23.8 0.0 collective-permute-done.16
  23.9 7.9 %collective-permute-start.17 = (f32[10,16,512]{2,1,0:T(8,128)S(1)}, f32[10,16,512]{2,1,0:T(8,128)S(1)}, u32[]{:S(2)}, u32[]{:S(2)}) collective-permute-start(f32[10,16,512]{2,1,0:T(8,128)S(1)} %add.10.after), channel_id=1, source_target_pairs={{0,12},{1,29},{2,14},{3,31},{4,8},{5,25},{6,10},{7,27},{8,20},{9,5... | collective-permute-start | bytes 983048 | tf_op jit(solution)/shard_map/cond/branch_2_fun/ppermute | solution.py:627
  31.8 0.0 collective-permute-done.22.south_raw
  31.8 4.9 %collective-permute-start.21 = (f32[104,512]{1,0:T(8,128)S(1)}, f32[104,512]{1,0:T(8,128)S(1)}, u32[]{:S(2)}, u32[]{:S(2)}) collective-permute-start(f32[104,512]{1,0:T(8,128)S(1)} %get-tuple-element.148), channel_id=1, source_target_pairs={{1,30},{3,24},{5,26},{7,28},{8,19},{10,21},{12,23},{14,17},{17,14}... | collective-permute-start | bytes 638984 | tf_op jit(solution)/shard_map/cond/branch_2_fun/ppermute | solution.py:711
  36.7 0.0 collective-permute-done.23.north_raw
  36.7 1.3 %collective-permute-start.19 = (f32[10,8,512]{2,1,0:T(8,128)S(1)}, f32[10,8,512]{2,1,0:T(8,128)S(1)}, u32[]{:S(2)}, u32[]{:S(2)}) collective-permute-start(f32[10,8,512]{2,1,0:T(8,128)S(1)} %get-tuple-element.146), channel_id=1, source_target_pairs={{1,13},{3,15},{5,9},{7,11},{8,4},{10,6},{12,0},{14,2},{17,29},{19,... | collective-permute-start | bytes 491528 | tf_op jit(solution)/shard_map/cond/branch_2_fun/ppermute | solution.py:711
  38.0 9.8 %bulk.6 = (f32[19,8,16,512]{3,2,1,0:T(8,128)}, f32[19,8,16,512]{3,2,1,0:T(8,128)}) custom-call(f32[10,16,512]{2,1,0:T(8,128)S(1)} %add.10.after, s32[4]{0:T(128)S(1)} %get-tuple-element.134.offsets, f32[19,8,16,512]{3,2,1,0:T(8,128)S(1)} %get-tuple-element.135.f_ref, f32[19,8,16,512]{3,2,1,0:T(8,128)S(1)} %get-tuple-element.136.g_ref, ...), custom_call_target="tpu_custom_call" | custom-call | tf_op jit(solution)/shard_map/cond/branch_2_fun/bulk/pallas_call | solution.py:751
  47.7 0.0 collective-permute-done.19.direct_short
  47.7 0.0 collective-permute-done.21.across_short
  47.7 0.0 collective-permute-done.18.direct
  47.8 0.0 collective-permute-done.20.across
  47.8 1.4 %merge_fill.6 = (f32[19,8,16,512]{3,2,1,0:T(8,128)}, f32[19,8,16,512]{3,2,1,0:T(8,128)}) custom-call(s32[4]{0:T(128)S(1)} %get-tuple-element.134.offsets, f32[10,16,512]{2,1,0:T(8,128)S(1)} %collective-permute-done.18.direct, f32[10,8,512]{2,1,0:T(8,128)S(1)} %collective-permute-done.19.direct_short, ...), custom_call_target="tpu_custom_call", output_to_operand_aliasing={{0}: (5, {}), {1}: (6, {})} | custom-call | tf_op jit(solution)/shard_map/cond/branch_2_fun/merge_fill/pallas_call | solution.py:767
  49.2 12.1 %collective-permute-done.17.joint = f32[10,16,512]{2,1,0:T(8,128)S(1)} collective-permute-done((f32[10,16,512]{2,1,0:T(8,128)S(1)}, f32[10,16,512]{2,1,0:T(8,128)S(1)}, u32[]{:S(2)}, u32[]{:S(2)}) %collective-permute-start.17) | collective-permute-done | bytes 327712 | tf_op jit(solution)/shard_map/cond/branch_2_fun/ppermute | solution.py:627
  61.3 0.8 %joint_fill.6 = (f32[19,8,16,512]{3,2,1,0:T(8,128)}, f32[19,8,16,512]{3,2,1,0:T(8,128)}) custom-call(f32[10,16,512]{2,1,0:T(8,128)S(1)} %collective-permute-done.17.joint, f32[19,8,16,512]{3,2,1,0:T(8,128)} %get-tuple-element.155.f_in, f32[19,8,16,512]{3,2,1,0:T(8,128)} %get-tuple-element.156.g_in), custom_call_target="tpu_custom_call", output_to_operand_aliasing={{0}: (1, {}), {1}: (2, {})} | custom-call | tf_op jit(solution)/shard_map/cond/branch_2_fun/joint_fill/pallas_call | solution.py:778
  (11 shorter events, 0.1 us)
Async XLA Ops:
  2.0 8.5 %collective-permute-start.33 = (f32[16,512]{1,0:T(8,128)S(1)}, f32[16,512]{1,0:T(8,128)S(1)}, u32[]{:S(2)}, u32[]{:S(2)}) collective-permute-start(f32[16,512]{1,0:T(8,128)S(1)} %get-tuple-element.208.top), channel_id=1, source_target_pairs={{0,12},{1,13},{2,14},{3,15},{4,8},{5,9},{6,10},{7,11},{8,20},{9,21... | collective-permute-start | bytes 98312 | tf_op jit(solution)/shard_map/ppermute | solution.py:627
  6.1 8.0 %slice-start = ((s8[4980736]{0:T(1024)(128)(4,1)}), s8[4194304]{0:T(1024)(128)(4,1)S(1)}, s32[]{:S(2)}) async-start(s8[4980736]{0:T(1024)(128)(4,1)} %bitcast.1), calls=%async_computation | async-start | bytes 8388608
  6.1 8.0 %slice-start.1 = ((s8[4980736]{0:T(1024)(128)(4,1)}), s8[786432]{0:T(1024)(128)(4,1)S(1)}, s32[]{:S(2)}) async-start(s8[4980736]{0:T(1024)(128)(4,1)} %bitcast.1), calls=%async_computation.1 | async-start | bytes 1572864
  6.1 8.0 %copy-start = (s32[4]{0:T(128)S(1)}, s32[4]{0:T(128)}, u32[]{:S(2)}) copy-start(s32[4]{0:T(128)} %offsets.1) | copy-start | bytes 52
  6.1 5.4 %collective-permute-start.32 = (f32[16,512]{1,0:T(8,128)S(1)}, f32[16,512]{1,0:T(8,128)S(1)}, u32[]{:S(2)}, u32[]{:S(2)}) collective-permute-start(f32[16,512]{1,0:T(8,128)S(1)} %get-tuple-element.209.bottom), channel_id=1, source_target_pairs={{0,28},{1,29},{2,30},{3,31},{4,24},{5,25},{6,26},{7,27},{8,4},{9,5... | collective-permute-start | bytes 98312 | tf_op jit(solution)/shard_map/ppermute | solution.py:627
  10.5 5.3 %collective-permute-start.35 = (f32[40,512]{1,0:T(8,128)S(1)}, f32[40,512]{1,0:T(8,128)S(1)}, u32[]{:S(2)}, u32[]{:S(2)}) collective-permute-start(f32[40,512]{1,0:T(8,128)S(1)} %constant_dynamic-update-slice_fusion.2.after_south), channel_id=1, source_target_pairs={{0,7},{1,0},{2,1},{3,2},{4,3},{5,4},{6,5},{7,6},{8,15},{9,8},{10,9... | collective-permute-start | bytes 245768 | tf_op jit(solution)/shard_map/ppermute | solution.py:627
  11.5 4.7 %collective-permute-start.34 = (f32[40,512]{1,0:T(8,128)S(1)}, f32[40,512]{1,0:T(8,128)S(1)}, u32[]{:S(2)}, u32[]{:S(2)}) collective-permute-start(f32[40,512]{1,0:T(8,128)S(1)} %constant_dynamic-update-slice_fusion.after_north), channel_id=1, source_target_pairs={{0,1},{1,2},{2,3},{3,4},{4,5},{5,6},{6,7},{7,0},{8,9},{9,10},{10,1... | collective-permute-start | bytes 245768 | tf_op jit(solution)/shard_map/ppermute | solution.py:627
  18.1 5.7 %collective-permute-start.16 = (f32[10,16,512]{2,1,0:T(8,128)S(1)}, f32[10,16,512]{2,1,0:T(8,128)S(1)}, u32[]{:S(2)}, u32[]{:S(2)}) collective-permute-start(f32[10,16,512]{2,1,0:T(8,128)S(1)} %get-tuple-element.144), channel_id=1, source_target_pairs={{0,1},{1,0},{2,3},{3,2},{4,5},{5,4},{6,7},{7,6},{8,9},{9,8},{10,11... | collective-permute-start | bytes 983048 | tf_op jit(solution)/shard_map/cond/branch_2_fun/ppermute | solution.py:627
  21.4 10.4 %collective-permute-start.22 = (f32[128,512]{1,0:T(8,128)S(1)}, f32[128,512]{1,0:T(8,128)S(1)}, u32[]{:S(2)}, u32[]{:S(2)}) collective-permute-start(f32[128,512]{1,0:T(8,128)S(1)} %get-tuple-element.151), channel_id=1, source_target_pairs={{0,1},{1,2},{2,3},{3,4},{4,5},{5,6},{6,7},{7,0},{8,9},{9,10},{10,1... | collective-permute-start | bytes 786440 | tf_op jit(solution)/shard_map/cond/branch_2_fun/ppermute | solution.py:627
  21.4 15.3 %collective-permute-start.23 = (f32[128,512]{1,0:T(8,128)S(1)}, f32[128,512]{1,0:T(8,128)S(1)}, u32[]{:S(2)}, u32[]{:S(2)}) collective-permute-start(f32[128,512]{1,0:T(8,128)S(1)} %get-tuple-element.152), channel_id=1, source_target_pairs={{0,7},{1,0},{2,1},{3,2},{4,3},{5,4},{6,5},{7,6},{8,15},{9,8},{10,9... | collective-permute-start | bytes 786440 | tf_op jit(solution)/shard_map/cond/branch_2_fun/ppermute | solution.py:627
  21.9 25.9 %collective-permute-start.18 = (f32[10,16,512]{2,1,0:T(8,128)S(1)}, f32[10,16,512]{2,1,0:T(8,128)S(1)}, u32[]{:S(2)}, u32[]{:S(2)}) collective-permute-start(f32[10,16,512]{2,1,0:T(8,128)S(1)} %get-tuple-element.145), channel_id=1, source_target_pairs={{0,28},{2,30},{4,24},{6,26},{9,21},{11,23},{13,17},{15,19},{16,12}... | collective-permute-start | bytes 983048 | tf_op jit(solution)/shard_map/cond/branch_2_fun/ppermute | solution.py:711
  23.2 24.6 %collective-permute-start.20 = (f32[10,16,512]{2,1,0:T(8,128)S(1)}, f32[10,16,512]{2,1,0:T(8,128)S(1)}, u32[]{:S(2)}, u32[]{:S(2)}) collective-permute-start(f32[10,16,512]{2,1,0:T(8,128)S(1)} %get-tuple-element.147), channel_id=1, source_target_pairs={{0,11},{2,13},{4,15},{6,9},{9,6},{11,0},{13,2},{15,4},{16,27},{18,... | collective-permute-start | bytes 983048 | tf_op jit(solution)/shard_map/cond/branch_2_fun/ppermute | solution.py:711
  23.9 37.4 %collective-permute-start.17 = (f32[10,16,512]{2,1,0:T(8,128)S(1)}, f32[10,16,512]{2,1,0:T(8,128)S(1)}, u32[]{:S(2)}, u32[]{:S(2)}) collective-permute-start(f32[10,16,512]{2,1,0:T(8,128)S(1)} %add.10.after), channel_id=1, source_target_pairs={{0,12},{1,29},{2,14},{3,31},{4,8},{5,25},{6,10},{7,27},{8,20},{9,5... | collective-permute-start | bytes 983048 | tf_op jit(solution)/shard_map/cond/branch_2_fun/ppermute | solution.py:627
  31.8 16.0 %collective-permute-start.21 = (f32[104,512]{1,0:T(8,128)S(1)}, f32[104,512]{1,0:T(8,128)S(1)}, u32[]{:S(2)}, u32[]{:S(2)}) collective-permute-start(f32[104,512]{1,0:T(8,128)S(1)} %get-tuple-element.148), channel_id=1, source_target_pairs={{1,30},{3,24},{5,26},{7,28},{8,19},{10,21},{12,23},{14,17},{17,14}... | collective-permute-start | bytes 638984 | tf_op jit(solution)/shard_map/cond/branch_2_fun/ppermute | solution.py:711
  36.7 11.1 %collective-permute-start.19 = (f32[10,8,512]{2,1,0:T(8,128)S(1)}, f32[10,8,512]{2,1,0:T(8,128)S(1)}, u32[]{:S(2)}, u32[]{:S(2)}) collective-permute-start(f32[10,8,512]{2,1,0:T(8,128)S(1)} %get-tuple-element.146), channel_id=1, source_target_pairs={{1,13},{3,15},{5,9},{7,11},{8,4},{10,6},{12,0},{14,2},{17,29},{19,... | collective-permute-start | bytes 491528 | tf_op jit(solution)/shard_map/cond/branch_2_fun/ppermute | solution.py:711

commit v8 on v7

--- a/solution.py
+++ b/solution.py
@@ -739,6 +739,7 @@
             north_msg,
         )
         around = (phi, minus, plus, south_msg, north_msg)
+        mate, south_raw, north_raw = lax.optimization_barrier((mate, south_raw, north_raw))
         mate = hop(mate, lambda x, y: (x, y ^ 1))
         direct = hop_some(direct, True, 0, False)
         direct_short = hop_some(direct_short, True, 0, True)

time: 63.9 us -> 67.9 us (1.063)
  the two profiles are of different devices: /device:TPU:1 before, /device:TPU:8 now
where the time goes in v8:
time: 67.9 us; the launch traced here: 67.6 us
  waiting for transfers between devices  26.6 us (39%)
  starting transfers between devices  19.5 us (29%)
  Pallas kernels  17.9 us (26%)
  between operations  1.58 us (2%)
  other arithmetic  1.51 us (2%)
    ppermute x4, waiting for transfers between devices, hop_some(): return lax.ppermute(value, ('gx', 'gy'), pairs)  19.8 us
    ppermute x4, starting transfers between devices, hop_some(): return lax.ppermute(value, ('gx', 'gy'), pairs)  12.8 us
    pallas_call x1, Pallas kernels, finish(): pl.pallas_call(functools.partial(bulk_kernel, (count_x, count_y)), out_sh...  9.75 us
    ppermute x8, waiting for transfers between devices, hop(): return lax.ppermute(value, ('gx', 'gy'), perm)  6.86 us
    ppermute x8, starting transfers between devices, hop(): return lax.ppermute(value, ('gx', 'gy'), perm)  6.74 us
    pallas_call x1, Pallas kernels, on_device(): pl.pallas_call(phi_kernel, out_shape=[jax.ShapeDtypeStruct((layers, rows,...  3.16 us
    pallas_call x1, Pallas kernels, finish(): pl.pallas_call(functools.partial(face_kernel, (count_x, count_y)), out_sh...  1.68 us
    pallas_call x1, Pallas kernels, finish(): pl.pallas_call(functools.partial(merge_fill_kernel, (count_x, count_y)),...  1.42 us
  transfers between devices with their start and end apart: 12, of which 5 were waited for; matrix products, arithmetic and copies ran while one was open for 0% of the time, Pallas kernels for 25%

profile of v8, /device:TPU:8, one launch (start us, length us, event | category | flops | bytes accessed | tf_op | source)
XLA Modules:
  0.0 67.6 jit_solution(11641196879858140222)
XLA Ops:
  0.6 1.4 %slice_reduce_fusion = (f32[16,512]{1,0:T(8,128)S(1)}, f32[16,512]{1,0:T(8,128)S(1)}) fusion(f32[19,8,16,512]{3,2,1,0:T(8,128)} %g_ref.1), kind=kLoop, calls=%fused_computation | loop fusion | flops 294912 | bytes 1310720 | tf_op jit(solution)/shard_map/reduce_sum | solution.py:648
  2.0 3.6 %collective-permute-start.33 = (f32[16,512]{1,0:T(8,128)S(1)}, f32[16,512]{1,0:T(8,128)S(1)}, u32[]{:S(2)}, u32[]{:S(2)}) collective-permute-start(f32[16,512]{1,0:T(8,128)S(1)} %get-tuple-element.220.top), channel_id=1, source_target_pairs={{0,12},{1,13},{2,14},{3,15},{4,8},{5,9},{6,10},{7,11},{8,20},{9,21... | collective-permute-start | bytes 98312 | tf_op jit(solution)/shard_map/ppermute | solution.py:627
  5.6 0.0 slice-start
  5.6 0.0 slice-start.1
  5.6 0.0 copy-start
  5.6 1.2 %collective-permute-start.32 = (f32[16,512]{1,0:T(8,128)S(1)}, f32[16,512]{1,0:T(8,128)S(1)}, u32[]{:S(2)}, u32[]{:S(2)}) collective-permute-start(f32[16,512]{1,0:T(8,128)S(1)} %get-tuple-element.221.bottom), channel_id=1, source_target_pairs={{0,28},{1,29},{2,30},{3,31},{4,24},{5,25},{6,26},{7,27},{8,4},{9,5... | collective-permute-start | bytes 98312 | tf_op jit(solution)/shard_map/ppermute | solution.py:627
  6.8 3.2 %phi_all.1 = (f32[8,16,512]{2,1,0:T(8,128)S(1)}, f32[24,512]{1,0:T(8,128)S(1)}, f32[24,512]{1,0:T(8,128)S(1)}, f32[19,8,16,512]{3,2,1,0:T(8,128)S(1)}) custom-call(f32[19,8,16,512]{3,2,1,0:T(8,128)} %f_ref.3, f32[19,8,16,512]{3,2,1,0:T(8,128)} %g_ref.1, f32[16,512]{1,0:T(8,128)S(1)} %get-tuple-element.220.top, f32[16,512]{1,0:T(8,128)S(1)} %get-tuple-element.221.bottom), custom_call_target="tpu_custom_call" | custom-call | tf_op jit(solution)/shard_map/phi_all/pallas_call | solution.py:654
  9.9 0.0 collective-permute-done.33
  10.0 0.1 collective-permute-start.35
  10.0 1.2 %collective-permute-done.32 = f32[16,512]{1,0:T(8,128)S(1)} collective-permute-done((f32[16,512]{1,0:T(8,128)S(1)}, f32[16,512]{1,0:T(8,128)S(1)}, u32[]{:S(2)}, u32[]{:S(2)}) %collective-permute-start.32) | collective-permute-done | bytes 32800 | tf_op jit(solution)/shard_map/ppermute | solution.py:627
  11.3 0.1 collective-permute-start.34
  11.4 0.1 pad.7.clone
  11.4 0.0 slice-done
  11.4 0.0 slice-done.1
  11.4 0.0 copy-done
  11.5 1.1 %moments.1 = (f32[2,4,16,512]{3,2,1,0:T(8,128)S(1)}, f32[120,512]{1,0:T(8,128)S(1)}, f32[120,512]{1,0:T(8,128)S(1)}, s32[1]{0:T(128)}) custom-call(f32[40,512]{1,0:T(8,128)S(1)} %constant_dynamic-update-slice_fusion.after_north, f32[40,512]{1,0:T(8,128)S(1)} %constant_dynamic-update-slice_fusion.2.after_south, s32[4]{0:T(128)S(1)} %copy-done, ...), custom_call_target="tpu_custom_call" | custom-call | tf_op jit(solution)/shard_map/moments/pallas_call | solution.py:673
  13.2 0.0 collective-permute-done.35
  13.2 2.7 %collective-permute-done.34 = f32[40,512]{1,0:T(8,128)S(1)} collective-permute-done((f32[40,512]{1,0:T(8,128)S(1)}, f32[40,512]{1,0:T(8,128)S(1)}, u32[]{:S(2)}, u32[]{:S(2)}) %collective-permute-start.34) | collective-permute-done | bytes 81952 | tf_op jit(solution)/shard_map/ppermute | solution.py:627
  16.0 0.1 maximum_maximum_fusion.1
  16.1 51.4 %conditional.1 = ((f32[19,8,16,512]{3,2,1,0:T(8,128)}, f32[19,8,16,512]{3,2,1,0:T(8,128)})) conditional(s32[]{:T(128)} %bitcast, (s32[4]{0:T(128)S(1)}, f32[19,8,16,512]{3,2,1,0:T(8,128)S(1)}, f32[19,8,16,512]{3,2,1,0:T(8,128)S(1)}, f32[2,4,16,512]{3,2,1,0:T(8,128)S(1)}, f32[8,16,512]{2,1,0:T(8,128)S(1)}, ...), branch_computations={%region_2.0_spmd, %region_3.0_spmd, %region_4.0_spmd, %region_5.0_... | conditional | flops 81920 | bytes 9830728 | solution.py:794
  16.1 0.1 collective-permute-start
  16.2 1.7 %collective-permute-start.1 = (f32[128,512]{1,0:T(8,128)S(1)}, f32[128,512]{1,0:T(8,128)S(1)}, u32[]{:S(2)}, u32[]{:S(2)}) collective-permute-start(f32[128,512]{1,0:T(8,128)S(1)} %get-tuple-element.100), channel_id=1, source_target_pairs={{0,7},{1,0},{2,1},{3,2},{4,3},{5,4},{6,5},{7,6},{8,15},{9,8},{10,9... | collective-permute-start | bytes 786440 | tf_op jit(solution)/shard_map/cond/branch_0_fun/ppermute | solution.py:627
  17.9 1.7 %faces.4 = (f32[10,16,512]{2,1,0:T(8,128)S(1)}, f32[10,16,512]{2,1,0:T(8,128)S(1)}, f32[10,8,512]{2,1,0:T(8,128)S(1)}, f32[10,16,512]{2,1,0:T(8,128)S(1)}, f32[1...) custom-call(s32[4]{0:T(128)S(1)} %get-tuple-element.88.offsets, ...), custom_call_target="tpu_custom_call" | custom-call | tf_op jit(solution)/shard_map/cond/branch_0_fun/faces/pallas_call | solution.py:714
  19.6 2.4 %collective-permute-done.south_raw = f32[128,512]{1,0:T(8,128)S(1)} collective-permute-done((f32[128,512]{1,0:T(8,128)S(1)}, f32[128,512]{1,0:T(8,128)S(1)}, u32[]{:S(2)}, u32[]{:S(2)}) %collective-permute-start) | collective-permute-done | bytes 262176 | tf_op jit(solution)/shard_map/cond/branch_0_fun/ppermute | solution.py:627
  21.9 0.5 collective-permute-done.1.north_raw
  22.5 0.0 collective-permute-start.2
  22.5 9.1 %collective-permute-start.4 = (f32[10,16,512]{2,1,0:T(8,128)S(1)}, f32[10,16,512]{2,1,0:T(8,128)S(1)}, u32[]{:S(2)}, u32[]{:S(2)}) collective-permute-start(f32[10,16,512]{2,1,0:T(8,128)S(1)} %get-tuple-element.102), channel_id=1, source_target_pairs={{0,28},{1,13},{2,30},{3,15},{4,24},{5,9},{6,26},{7,11},{8,4},{9,21... | collective-permute-start | bytes 983048 | tf_op jit(solution)/shard_map/cond/branch_0_fun/ppermute | solution.py:711
  31.5 0.7 %collective-permute-start.6 = (f32[10,16,512]{2,1,0:T(8,128)S(1)}, f32[10,16,512]{2,1,0:T(8,128)S(1)}, u32[]{:S(2)}, u32[]{:S(2)}) collective-permute-start(f32[10,16,512]{2,1,0:T(8,128)S(1)} %get-tuple-element.104), channel_id=1, source_target_pairs={{16,27},{18,29},{20,31},{22,25},{25,22},{27,16},{29,18},{31,20}} | collective-permute-start | bytes 983048 | tf_op jit(solution)/shard_map/cond/branch_0_fun/ppermute | solution.py:711
  32.2 0.0 collective-permute-done.2
  32.3 0.1 collective-permute-start.3
  32.4 2.4 %collective-permute-start.7 = (f32[104,512]{1,0:T(8,128)S(1)}, f32[104,512]{1,0:T(8,128)S(1)}, u32[]{:S(2)}, u32[]{:S(2)}) collective-permute-start(f32[104,512]{1,0:T(8,128)S(1)} %get-tuple-element.105), channel_id=1, source_target_pairs={{0,11},{1,30},{2,13},{3,24},{4,15},{5,26},{6,9},{7,28},{8,19},{9,6... | collective-permute-start | bytes 638984 | tf_op jit(solution)/shard_map/cond/branch_0_fun/ppermute | solution.py:711
  34.7 0.7 collective-permute-start.5
  35.4 9.8 %bulk.4 = (f32[19,8,16,512]{3,2,1,0:T(8,128)}, f32[19,8,16,512]{3,2,1,0:T(8,128)}) custom-call(f32[10,16,512]{2,1,0:T(8,128)S(1)} %add.8.after, s32[4]{0:T(128)S(1)} %get-tuple-element.88.offsets, f32[19,8,16,512]{3,2,1,0:T(8,128)S(1)} %get-tuple-element.89.f_ref, f32[19,8,16,512]{3,2,1,0:T(8,128)S(1)} %get-tuple-element.90.g_ref, ...), custom_call_target="tpu_custom_call" | custom-call | tf_op jit(solution)/shard_map/cond/branch_0_fun/bulk/pallas_call | solution.py:752
  45.2 0.0 collective-permute-done.5.direct_short
  45.2 19.8 %collective-permute-done.7.across_short = f32[104,512]{1,0:T(8,128)S(1)} collective-permute-done((f32[104,512]{1,0:T(8,128)S(1)}, f32[104,512]{1,0:T(8,128)S(1)}, u32[]{:S(2)}, u32[]{:S(2)}) %collective-permute-start.7) | collective-permute-done | bytes 213024 | tf_op jit(solution)/shard_map/cond/branch_0_fun/ppermute | solution.py:711
  64.9 0.0 collective-permute-done.4.direct
  64.9 0.0 collective-permute-done.6.across
  64.9 1.4 %merge_fill.4 = (f32[19,8,16,512]{3,2,1,0:T(8,128)}, f32[19,8,16,512]{3,2,1,0:T(8,128)}) custom-call(s32[4]{0:T(128)S(1)} %get-tuple-element.88.offsets, f32[10,16,512]{2,1,0:T(8,128)S(1)} %collective-permute-done.4.direct, f32[10,8,512]{2,1,0:T(8,128)S(1)} %collective-permute-done.5.direct_short, ...), custom_call_target="tpu_custom_call", output_to_operand_aliasing={{0}: (5, {}), {1}: (6, {})} | custom-call | tf_op jit(solution)/shard_map/cond/branch_0_fun/merge_fill/pallas_call | solution.py:768
  66.4 0.0 collective-permute-done.3.joint
  66.4 0.8 %joint_fill.4 = (f32[19,8,16,512]{3,2,1,0:T(8,128)}, f32[19,8,16,512]{3,2,1,0:T(8,128)}) custom-call(f32[10,16,512]{2,1,0:T(8,128)S(1)} %collective-permute-done.3.joint, f32[19,8,16,512]{3,2,1,0:T(8,128)} %get-tuple-element.112.f_in, f32[19,8,16,512]{3,2,1,0:T(8,128)} %get-tuple-element.113.g_in), custom_call_target="tpu_custom_call", output_to_operand_aliasing={{0}: (1, {}), {1}: (2, {})} | custom-call | tf_op jit(solution)/shard_map/cond/branch_0_fun/joint_fill/pallas_call | solution.py:779
  (11 shorter events, 0.1 us)
Async XLA Ops:
  2.0 8.0 %collective-permute-start.33 = (f32[16,512]{1,0:T(8,128)S(1)}, f32[16,512]{1,0:T(8,128)S(1)}, u32[]{:S(2)}, u32[]{:S(2)}) collective-permute-start(f32[16,512]{1,0:T(8,128)S(1)} %get-tuple-element.220.top), channel_id=1, source_target_pairs={{0,12},{1,13},{2,14},{3,15},{4,8},{5,9},{6,10},{7,11},{8,20},{9,21... | collective-permute-start | bytes 98312 | tf_op jit(solution)/shard_map/ppermute | solution.py:627
  5.6 5.9 %slice-start = ((s8[4980736]{0:T(1024)(128)(4,1)}), s8[4194304]{0:T(1024)(128)(4,1)S(1)}, s32[]{:S(2)}) async-start(s8[4980736]{0:T(1024)(128)(4,1)} %bitcast.1), calls=%async_computation | async-start | bytes 8388608
  5.6 5.9 %slice-start.1 = ((s8[4980736]{0:T(1024)(128)(4,1)}), s8[786432]{0:T(1024)(128)(4,1)S(1)}, s32[]{:S(2)}) async-start(s8[4980736]{0:T(1024)(128)(4,1)} %bitcast.1), calls=%async_computation.1 | async-start | bytes 1572864
  5.6 5.9 %copy-start = (s32[4]{0:T(128)S(1)}, s32[4]{0:T(128)}, u32[]{:S(2)}) copy-start(s32[4]{0:T(128)} %offsets.1) | copy-start | bytes 52
  5.6 5.7 %collective-permute-start.32 = (f32[16,512]{1,0:T(8,128)S(1)}, f32[16,512]{1,0:T(8,128)S(1)}, u32[]{:S(2)}, u32[]{:S(2)}) collective-permute-start(f32[16,512]{1,0:T(8,128)S(1)} %get-tuple-element.221.bottom), channel_id=1, source_target_pairs={{0,28},{1,29},{2,30},{3,31},{4,24},{5,25},{6,26},{7,27},{8,4},{9,5... | collective-permute-start | bytes 98312 | tf_op jit(solution)/shard_map/ppermute | solution.py:627
  10.0 3.2 %collective-permute-start.35 = (f32[40,512]{1,0:T(8,128)S(1)}, f32[40,512]{1,0:T(8,128)S(1)}, u32[]{:S(2)}, u32[]{:S(2)}) collective-permute-start(f32[40,512]{1,0:T(8,128)S(1)} %constant_dynamic-update-slice_fusion.2.after_south), channel_id=1, source_target_pairs={{0,7},{1,0},{2,1},{3,2},{4,3},{5,4},{6,5},{7,6},{8,15},{9,8},{10,9... | collective-permute-start | bytes 245768 | tf_op jit(solution)/shard_map/ppermute | solution.py:627
  11.3 4.7 %collective-permute-start.34 = (f32[40,512]{1,0:T(8,128)S(1)}, f32[40,512]{1,0:T(8,128)S(1)}, u32[]{:S(2)}, u32[]{:S(2)}) collective-permute-start(f32[40,512]{1,0:T(8,128)S(1)} %constant_dynamic-update-slice_fusion.after_north), channel_id=1, source_target_pairs={{0,1},{1,2},{2,3},{3,4},{4,5},{5,6},{6,7},{7,0},{8,9},{9,10},{10,1... | collective-permute-start | bytes 245768 | tf_op jit(solution)/shard_map/ppermute | solution.py:627
  16.1 5.8 %collective-permute-start = (f32[128,512]{1,0:T(8,128)S(1)}, f32[128,512]{1,0:T(8,128)S(1)}, u32[]{:S(2)}, u32[]{:S(2)}) collective-permute-start(f32[128,512]{1,0:T(8,128)S(1)} %get-tuple-element.99), channel_id=1, source_target_pairs={{0,1},{1,2},{2,3},{3,4},{4,5},{5,6},{6,7},{7,0},{8,9},{9,10},{10,1... | collective-permute-start | bytes 786440 | tf_op jit(solution)/shard_map/cond/branch_0_fun/ppermute | solution.py:627
  16.2 6.3 %collective-permute-start.1 = (f32[128,512]{1,0:T(8,128)S(1)}, f32[128,512]{1,0:T(8,128)S(1)}, u32[]{:S(2)}, u32[]{:S(2)}) collective-permute-start(f32[128,512]{1,0:T(8,128)S(1)} %get-tuple-element.100), channel_id=1, source_target_pairs={{0,7},{1,0},{2,1},{3,2},{4,3},{5,4},{6,5},{7,6},{8,15},{9,8},{10,9... | collective-permute-start | bytes 786440 | tf_op jit(solution)/shard_map/cond/branch_0_fun/ppermute | solution.py:627
  22.5 9.8 %collective-permute-start.2 = (f32[10,16,512]{2,1,0:T(8,128)S(1)}, f32[10,16,512]{2,1,0:T(8,128)S(1)}, u32[]{:S(2)}, u32[]{:S(2)}) collective-permute-start(f32[10,16,512]{2,1,0:T(8,128)S(1)} %get-tuple-element.101), channel_id=1, source_target_pairs={{0,1},{1,0},{2,3},{3,2},{4,5},{5,4},{6,7},{7,6},{8,9},{9,8},{10,11... | collective-permute-start | bytes 983048 | tf_op jit(solution)/shard_map/cond/branch_0_fun/ppermute | solution.py:627
  22.5 42.5 %collective-permute-start.4 = (f32[10,16,512]{2,1,0:T(8,128)S(1)}, f32[10,16,512]{2,1,0:T(8,128)S(1)}, u32[]{:S(2)}, u32[]{:S(2)}) collective-permute-start(f32[10,16,512]{2,1,0:T(8,128)S(1)} %get-tuple-element.102), channel_id=1, source_target_pairs={{0,28},{1,13},{2,30},{3,15},{4,24},{5,9},{6,26},{7,11},{8,4},{9,21... | collective-permute-start | bytes 983048 | tf_op jit(solution)/shard_map/cond/branch_0_fun/ppermute | solution.py:711
  31.5 33.4 %collective-permute-start.6 = (f32[10,16,512]{2,1,0:T(8,128)S(1)}, f32[10,16,512]{2,1,0:T(8,128)S(1)}, u32[]{:S(2)}, u32[]{:S(2)}) collective-permute-start(f32[10,16,512]{2,1,0:T(8,128)S(1)} %get-tuple-element.104), channel_id=1, source_target_pairs={{16,27},{18,29},{20,31},{22,25},{25,22},{27,16},{29,18},{31,20}} | collective-permute-start | bytes 983048 | tf_op jit(solution)/shard_map/cond/branch_0_fun/ppermute | solution.py:711
  32.3 34.1 %collective-permute-start.3 = (f32[10,16,512]{2,1,0:T(8,128)S(1)}, f32[10,16,512]{2,1,0:T(8,128)S(1)}, u32[]{:S(2)}, u32[]{:S(2)}) collective-permute-start(f32[10,16,512]{2,1,0:T(8,128)S(1)} %add.8.after), channel_id=1, source_target_pairs={{0,12},{1,29},{2,14},{3,31},{4,8},{5,25},{6,10},{7,27},{8,20},{9,5... | collective-permute-start | bytes 983048 | tf_op jit(solution)/shard_map/cond/branch_0_fun/ppermute | solution.py:627
  32.4 32.6 %collective-permute-start.7 = (f32[104,512]{1,0:T(8,128)S(1)}, f32[104,512]{1,0:T(8,128)S(1)}, u32[]{:S(2)}, u32[]{:S(2)}) collective-permute-start(f32[104,512]{1,0:T(8,128)S(1)} %get-tuple-element.105), channel_id=1, source_target_pairs={{0,11},{1,30},{2,13},{3,24},{4,15},{5,26},{6,9},{7,28},{8,19},{9,6... | collective-permute-start | bytes 638984 | tf_op jit(solution)/shard_map/cond/branch_0_fun/ppermute | solution.py:711
  34.7 10.4 %collective-permute-start.5 = (f32[10,8,512]{2,1,0:T(8,128)S(1)}, f32[10,8,512]{2,1,0:T(8,128)S(1)}, u32[]{:S(2)}, u32[]{:S(2)}) collective-permute-start(f32[10,8,512]{2,1,0:T(8,128)S(1)} %get-tuple-element.103), channel_id=1, source_target_pairs={{17,29},{19,31},{21,25},{23,27},{24,20},{26,22},{28,16},{30,18}} | collective-permute-start | bytes 491528 | tf_op jit(solution)/shard_map/cond/branch_0_fun/ppermute | solution.py:711

commit v9 on v6

--- a/solution.py
+++ b/solution.py
@@ -189,39 +189,39 @@
     return total
 
 
-def phi_kernel(f_ref, g_ref, top, bottom, phi_ref, to_north, to_south, gbuf, fbuf, sems):
+def branch_kernel(part, base, g_ref, offsets, index):
+    first, second = offsets[1] - base > part, offsets[2] - base > part
+    index[0] = 2 * first.astype(jnp.int32) + second.astype(jnp.int32)
+
+
+def phi_kernel(index, f_ref, g_ref, top, bottom, phi_ref, to_north, to_south, fbuf, sems):
     layers, rows = phi_ref.shape[0], phi_ref.shape[1]
     faces = (layers - 1, 0)
-    f_copies = [
-        pltpu.make_async_copy(f_ref.at[:, x], fbuf.at[:, s], sems.at[layers + s])
+    copies = [
+        pltpu.make_async_copy(f_ref.at[:, x], fbuf.at[:, s], sems.at[s])
         for s, x in enumerate(faces)
     ]
-    g_copies = [
-        pltpu.make_async_copy(g_ref.at[:, x], gbuf.at[:, x], sems.at[x]) for x in range(layers)
-    ]
-    for copy in f_copies + g_copies:
+    for copy in copies:
         copy.start()
     phi_ref[layers - 1] = top[...]
     phi_ref[0] = bottom[...]
-    edges = ((to_north, rows - 1, rows - 2, (7, 10)), (to_south, 0, 1, (9, 8)))
+    for x in range(layers):
+        if 0 < x < layers - 1:
+            phi_ref[x] = order_sum(lambda i: g_ref[i, x])
+        to_north[x : x + 1] = phi_ref[x, rows - 1 : rows]
+        to_south[x : x + 1] = phi_ref[x, 0:1]
     for s, x in enumerate(faces):
-        f_copies[s].wait()
-        for out, edge, inner, chosen in edges:
+        copies[s].wait()
+        for out, edge, inner, chosen in (
+            (to_north, rows - 1, rows - 2, (7, 10)),
+            (to_south, 0, 1, (9, 8)),
+        ):
             out[layers + s : layers + s + 1] = phi_ref[x, inner : inner + 1]
             at = layers + 2 + 6 * s
             out[at : at + 1] = fbuf[chosen[s], s, edge : edge + 1]
+            out[at + 1 : at + 2] = g_ref[chosen[s], x, edge : edge + 1]
             for k, part in enumerate(moments_of(lambda i: fbuf[i, s, edge : edge + 1])):
                 out[at + 2 + k : at + 3 + k] = part
-    for x in range(layers):
-        g_copies[x].wait()
-        if 0 < x < layers - 1:
-            phi_ref[x] = order_sum(lambda i: gbuf[i, x])
-        to_north[x : x + 1] = phi_ref[x, rows - 1 : rows]
-        to_south[x : x + 1] = phi_ref[x, 0:1]
-    for s, x in enumerate(faces):
-        for out, edge, inner, chosen in edges:
-            at = layers + 3 + 6 * s
-            out[at : at + 1] = gbuf[chosen[s], x, edge : edge + 1]
     for out in (to_north, to_south):
         out[layers + 14 : layers + 16] = jnp.zeros((2, out.shape[1]), f32)
 
@@ -639,20 +639,24 @@
     fall = hop(bottom, lambda x, y: (x - 1, y + base_low(x)))
 
     block = jax.ShapeDtypeStruct((layers + 16, cols), f32)
-    phi, to_north, to_south, order_near = pl.pallas_call(
+    part = rows // 2
+    index = pl.pallas_call(
+        functools.partial(branch_kernel, part, half * rows),
+        out_shape=jax.ShapeDtypeStruct((1,), jnp.int32),
+        in_specs=[anywhere, smem],
+        out_specs=smem,
+        compiler_params=params(50 << 20),
+        name="branch",
+    )(order_dist, offsets)
+    phi, to_north, to_south = pl.pallas_call(
         phi_kernel,
-        out_shape=[jax.ShapeDtypeStruct((layers, rows, cols), f32)]
-        + [block] * 2
-        + [jax.ShapeDtypeStruct(order_dist.shape, f32)],
-        in_specs=[anywhere, anywhere, vmem, vmem],
-        out_specs=[vmem] * 4,
-        scratch_shapes=[
-            VMEM((19, 2, rows, cols), f32),
-            pltpu.SemaphoreType.DMA((layers + 2,)),
-        ],
-        compiler_params=params(52 << 20),
+        out_shape=[jax.ShapeDtypeStruct((layers, rows, cols), f32)] + [block] * 2,
+        in_specs=[smem, anywhere, vmem, vmem, vmem],
+        out_specs=[vmem] * 3,
+        scratch_shapes=[VMEM((19, 2, rows, cols), f32), pltpu.SemaphoreType.DMA((2,))],
+        compiler_params=params(8 << 20),
         name="phi_all",
-    )(momentum_dist, order_dist, top, bottom)
+    )(index, momentum_dist, order_dist, top, bottom)
     to_north = jnp.concatenate([fall, to_north], 0)
     to_south = jnp.concatenate([rise, to_south], 0)
     south_msg, north_msg = hop_y(to_north, 1), hop_y(to_south, -1)
@@ -667,9 +671,8 @@
         out_specs=[vmem] * 2,
         compiler_params=params(16 << 20),
         name="moments",
-    )(to_north, to_south, momentum_dist, order_near)
-
-    part = rows // 2
+    )(to_north, to_south, momentum_dist, order_dist)
+
     ten = jax.ShapeDtypeStruct((10, rows, cols), f32)
     ten_short = jax.ShapeDtypeStruct((10, part, cols), f32)
     ten_seam = jax.ShapeDtypeStruct((10 * part + 24, cols), f32)
@@ -698,7 +701,7 @@
     )(
         offsets,
         momentum_dist,
-        order_near,
+        order_dist,
         face_moments,
         rims,
         phi,
@@ -748,7 +751,7 @@
             ],
             compiler_params=params(48 << 20),
             name="bulk",
-        )(after, momentum_dist, order_near, *around, mate, cross)
+        )(after, momentum_dist, order_dist, *around, mate, cross)
 
         next_f, next_g = pl.pallas_call(
             functools.partial(merge_fill_kernel, (count_x, count_y)),
@@ -772,12 +775,11 @@
             name="joint_fill",
         )(joint, next_f, next_g)
 
-    is_long = [(offsets[k] - half * rows > part).astype(jnp.int32) for k in (1, 2)]
     branches = [
         functools.partial(finish, {3} | ({1} if k & 2 else set()) | ({2} if k & 1 else set()))
         for k in range(4)
     ]
-    return lax.switch(2 * is_long[0] + is_long[1], branches, *outgoing)
+    return lax.switch(index[0], branches, *outgoing)
 
 
 def solution(mesh):

time: 61.4 us -> 61.8 us (level)
  the two profiles are of different devices: /device:TPU:14 before, /device:TPU:7 now
where the time goes in v9:
time: 61.8 us; the launch traced here: 60.8 us
  starting transfers between devices  22.1 us (36%)
  waiting for transfers between devices  18.6 us (30%)
  Pallas kernels  16.9 us (27%)
  other arithmetic  1.56 us (3%)
  between operations  1.41 us (2%)
    ppermute x4, waiting for transfers between devices, hop_some(): return lax.ppermute(value, ('gx', 'gy'), pairs)  17.8 us
    ppermute x4, starting transfers between devices, hop_some(): return lax.ppermute(value, ('gx', 'gy'), pairs)  11.1 us
    ppermute x7, starting transfers between devices, hop(): return lax.ppermute(value, ('gx', 'gy'), perm)  11.1 us
    pallas_call x1, Pallas kernels, finish(): pl.pallas_call(bulk_kernel, out_shape=[whole, whole], in_specs=[anywhere]...  8.9 us
    pallas_call x1, Pallas kernels, on_device(): pl.pallas_call(functools.partial(face_kernel, (count_x, count_y)), out_sh...  2.04 us
    pallas_call x1, Pallas kernels, on_device(): pl.pallas_call(phi_kernel, out_shape=[jax.ShapeDtypeStruct((layers, rows,...  2.03 us
    reduce_sum x1, other arithmetic, on_device(): jnp.sum(order_dist[:, layers - 1], axis=0)  1.51 us
    pallas_call x1, Pallas kernels, finish(): pl.pallas_call(functools.partial(merge_fill_kernel, (count_x, count_y)),...  1.4 us
  transfers between devices with their start and end apart: 11, of which 2 were waited for; matrix products, arithmetic and copies ran while one was open for 0% of the time, Pallas kernels for 23%

profile of v9, /device:TPU:7, one launch (start us, length us, event | category | flops | bytes accessed | tf_op | source)
XLA Modules:
  0.0 60.8 jit_solution(6674660228947310585)
XLA Ops:
  0.6 0.0 copy-start
  0.6 1.5 %slice_reduce_fusion = (f32[16,512]{1,0:T(8,128)S(1)}, f32[16,512]{1,0:T(8,128)S(1)}) fusion(f32[19,8,16,512]{3,2,1,0:T(8,128)} %g_ref.7), kind=kLoop, calls=%fused_computation.4 | loop fusion | flops 294912 | bytes 1310720 | tf_op jit(solution)/shard_map/reduce_sum | solution.py:637
  2.2 2.3 %collective-permute-start.29 = (f32[16,512]{1,0:T(8,128)S(1)}, f32[16,512]{1,0:T(8,128)S(1)}, u32[]{:S(2)}, u32[]{:S(2)}) collective-permute-start(f32[16,512]{1,0:T(8,128)S(1)} %get-tuple-element.236.top), channel_id=1, source_target_pairs={{0,12},{1,13},{2,14},{3,15},{4,8},{5,9},{6,10},{7,11},{8,20},{9,21... | collective-permute-start | bytes 98312 | tf_op jit(solution)/shard_map/ppermute | solution.py:616
  4.4 1.0 %collective-permute-start.28 = (f32[16,512]{1,0:T(8,128)S(1)}, f32[16,512]{1,0:T(8,128)S(1)}, u32[]{:S(2)}, u32[]{:S(2)}) collective-permute-start(f32[16,512]{1,0:T(8,128)S(1)} %get-tuple-element.237.bottom), channel_id=1, source_target_pairs={{0,28},{1,29},{2,30},{3,31},{4,24},{5,25},{6,26},{7,27},{8,4},{9,5... | collective-permute-start | bytes 98312 | tf_op jit(solution)/shard_map/ppermute | solution.py:616
  5.5 0.0 slice-start
  5.5 1.3 %branch.1.index = s32[1]{0:T(128)} custom-call(f32[19,8,16,512]{3,2,1,0:T(8,128)} %g_ref.7, s32[4]{0:T(128)} %offsets.3), custom_call_target="tpu_custom_call" | custom-call | tf_op jit(solution)/shard_map/branch/pallas_call | solution.py:643
  6.8 0.0 copy-done
  6.8 0.0 slice-start.1
  6.8 2.0 %phi_all.1 = (f32[8,16,512]{2,1,0:T(8,128)S(1)}, f32[24,512]{1,0:T(8,128)S(1)}, f32[24,512]{1,0:T(8,128)S(1)}) custom-call(s32[1]{0:T(128)} %branch.1.index, f32[19,8,16,512]{3,2,1,0:T(8,128)} %f_ref.5, f32[19,8,16,512]{3,2,1,0:T(8,128)S(1)} %copy-done, f32[16,512]{1,0:T(8,128)S(1)} %get-tuple-element.236.top, f32[16,512]{1,0:T(8,128)S(1)} %get-tuple-element.237.bottom), custom_call_target="tpu_custom_call" | custom-call | tf_op jit(solution)/shard_map/phi_all/pallas_call | solution.py:651
  8.9 0.0 collective-permute-done.29.rise
  8.9 1.3 %collective-permute-start.31 = (f32[40,512]{1,0:T(8,128)S(1)}, f32[40,512]{1,0:T(8,128)S(1)}, u32[]{:S(2)}, u32[]{:S(2)}) collective-permute-start(f32[40,512]{1,0:T(8,128)S(1)} %constant_dynamic-update-slice_fusion.2.after_south), channel_id=1, source_target_pairs={{0,7},{1,0},{2,1},{3,2},{4,3},{5,4},{6,5},{7,6},{8,15},{9,8},{10,9... | collective-permute-start | bytes 245768 | tf_op jit(solution)/shard_map/ppermute | solution.py:616
  10.2 0.0 collective-permute-done.28.fall
  10.2 3.0 %collective-permute-start.30 = (f32[40,512]{1,0:T(8,128)S(1)}, f32[40,512]{1,0:T(8,128)S(1)}, u32[]{:S(2)}, u32[]{:S(2)}) collective-permute-start(f32[40,512]{1,0:T(8,128)S(1)} %constant_dynamic-update-slice_fusion.after_north), channel_id=1, source_target_pairs={{0,1},{1,2},{2,3},{3,4},{4,5},{5,6},{6,7},{7,0},{8,9},{9,10},{10,1... | collective-permute-start | bytes 245768 | tf_op jit(solution)/shard_map/ppermute | solution.py:616
  13.9 0.0 slice-done
  13.9 0.0 slice-done.1
  13.9 0.0 copy-start.1
  13.9 0.4 moments.1
  14.4 0.0 collective-permute-done.31.north_msg
  14.4 0.7 %collective-permute-done.30.south_msg = f32[40,512]{1,0:T(8,128)S(1)} collective-permute-done((f32[40,512]{1,0:T(8,128)S(1)}, f32[40,512]{1,0:T(8,128)S(1)}, u32[]{:S(2)}, u32[]{:S(2)}) %collective-permute-start.30) | collective-permute-done | bytes 81952 | tf_op jit(solution)/shard_map/ppermute | solution.py:616
  15.1 0.0 copy-done.1
  15.1 2.0 %faces.1 = (f32[10,24,512]{2,1,0:T(8,128)S(1)}, f32[10,16,512]{2,1,0:T(8,128)S(1)}, f32[10,8,512]{2,1,0:T(8,128)S(1)}, f32[10,16,512]{2,1,0:T(8,128)S(1)}, f32[1...) custom-call(s32[4]{0:T(128)S(1)} %copy-done.1, ...), custom_call_target="tpu_custom_call" | custom-call | tf_op jit(solution)/shard_map/faces/pallas_call | solution.py:681
  17.2 43.6 %conditional.1 = ((f32[19,8,16,512]{3,2,1,0:T(8,128)}, f32[19,8,16,512]{3,2,1,0:T(8,128)})) conditional(s32[]{:T(128)} %bitcast, (f32[10,24,512]{2,1,0:T(8,128)S(1)}, f32[10,16,512]{2,1,0:T(8,128)S(1)}, f32[10,16,512]{2,1,0:T(8,128)S(1)}, f32[10,8,512]{2,1,0:T(8,128)S(1)}, f32[10,16,512]{2,1,0:T(8,128)S(1)}, ...), branch_computations={%region_2.0_spmd, %region_3.0_spmd, %region_4.0_spmd, %region_5.0_... | conditional | flops 81920 | bytes 9044256 | solution.py:782
  17.2 3.3 %collective-permute-start = (f32[10,24,512]{2,1,0:T(8,128)S(1)}, f32[10,24,512]{2,1,0:T(8,128)S(1)}, u32[]{:S(2)}, u32[]{:S(2)}) collective-permute-start(f32[10,24,512]{2,1,0:T(8,128)S(1)} %get-tuple-element.121), channel_id=1, source_target_pairs={{0,1},{1,0},{2,3},{3,2},{4,5},{5,4},{6,7},{7,6},{8,9},{9,8},{10,11... | collective-permute-start | bytes 1474568 | tf_op jit(solution)/shard_map/cond/branch_0_fun/ppermute | solution.py:616
  20.5 0.0 collective-permute-start.6
  20.5 3.5 %collective-permute-start.2 = (f32[10,16,512]{2,1,0:T(8,128)S(1)}, f32[10,16,512]{2,1,0:T(8,128)S(1)}, u32[]{:S(2)}, u32[]{:S(2)}) collective-permute-start(f32[10,16,512]{2,1,0:T(8,128)S(1)} %get-tuple-element.123), channel_id=1, source_target_pairs={{0,28},{1,13},{2,30},{3,15},{4,24},{5,9},{6,26},{7,11},{8,4},{9,21... | collective-permute-start | bytes 983048 | tf_op jit(solution)/shard_map/cond/branch_0_fun/ppermute | solution.py:731
  24.0 5.7 %collective-permute-start.4 = (f32[10,16,512]{2,1,0:T(8,128)S(1)}, f32[10,16,512]{2,1,0:T(8,128)S(1)}, u32[]{:S(2)}, u32[]{:S(2)}) collective-permute-start(f32[10,16,512]{2,1,0:T(8,128)S(1)} %get-tuple-element.125), channel_id=1, source_target_pairs={{16,27},{18,29},{20,31},{22,25},{25,22},{27,16},{29,18},{31,20}} | collective-permute-start | bytes 983048 | tf_op jit(solution)/shard_map/cond/branch_0_fun/ppermute | solution.py:731
  29.7 0.0 collective-permute-done.mate_rim
  29.7 0.1 collective-permute-start.1
  29.8 0.7 %collective-permute-start.5 = (f32[104,512]{1,0:T(8,128)S(1)}, f32[104,512]{1,0:T(8,128)S(1)}, u32[]{:S(2)}, u32[]{:S(2)}) collective-permute-start(f32[104,512]{1,0:T(8,128)S(1)} %get-tuple-element.126), channel_id=1, source_target_pairs={{0,11},{1,30},{2,13},{3,24},{4,15},{5,26},{6,9},{7,28},{8,19},{9,6... | collective-permute-start | bytes 638984 | tf_op jit(solution)/shard_map/cond/branch_0_fun/ppermute | solution.py:731
  30.5 0.0 collective-permute-done.6.cross_rim
  30.5 1.3 %collective-permute-start.3 = (f32[10,8,512]{2,1,0:T(8,128)S(1)}, f32[10,8,512]{2,1,0:T(8,128)S(1)}, u32[]{:S(2)}, u32[]{:S(2)}) collective-permute-start(f32[10,8,512]{2,1,0:T(8,128)S(1)} %get-tuple-element.124), channel_id=1, source_target_pairs={{17,29},{19,31},{21,25},{23,27},{24,20},{26,22},{28,16},{30,18}} | collective-permute-start | bytes 491528 | tf_op jit(solution)/shard_map/cond/branch_0_fun/ppermute | solution.py:731
  31.8 8.9 %bulk.4 = (f32[19,8,16,512]{3,2,1,0:T(8,128)}, f32[19,8,16,512]{3,2,1,0:T(8,128)}) custom-call(f32[10,16,512]{2,1,0:T(8,128)S(1)} %slice_add_fusion.after, f32[19,8,16,512]{3,2,1,0:T(8,128)S(1)} %get-tuple-element.127.f_ref, f32[19,8,16,512]{3,2,1,0:T(8,128)S(1)} %get-tuple-element.128.g_ref, f32[8,16,512]{2,1,0:T(8,128)S(1)} %get-tuple-element.129.phi_ref, ...), custom_call_target="tpu_custom_call" | custom-call | tf_op jit(solution)/shard_map/cond/branch_0_fun/bulk/pallas_call | solution.py:743
  40.7 17.8 %collective-permute-done.3.direct_short = f32[10,8,512]{2,1,0:T(8,128)S(1)} collective-permute-done((f32[10,8,512]{2,1,0:T(8,128)S(1)}, f32[10,8,512]{2,1,0:T(8,128)S(1)}, u32[]{:S(2)}, u32[]{:S(2)}) %collective-permute-start.3) | collective-permute-done | bytes 163872 | tf_op jit(solution)/shard_map/cond/branch_0_fun/ppermute | solution.py:731
  58.5 0.0 collective-permute-done.5.across_short
  58.5 0.0 collective-permute-done.2.direct
  58.5 0.0 collective-permute-done.4.across
  58.5 1.4 %merge_fill.4 = (f32[19,8,16,512]{3,2,1,0:T(8,128)}, f32[19,8,16,512]{3,2,1,0:T(8,128)}) custom-call(s32[4]{0:T(128)S(1)} %get-tuple-element.122.offsets, f32[10,16,512]{2,1,0:T(8,128)S(1)} %collective-permute-done.2.direct, f32[10,8,512]{2,1,0:T(8,128)S(1)} %collective-permute-done.3.direct_short, ...), custom_call_target="tpu_custom_call", output_to_operand_aliasing={{0}: (5, {}), {1}: (6, {})} | custom-call | tf_op jit(solution)/shard_map/cond/branch_0_fun/merge_fill/pallas_call | solution.py:756
  60.0 0.0 collective-permute-done.1.joint
  60.0 0.8 %joint_fill.4 = (f32[19,8,16,512]{3,2,1,0:T(8,128)}, f32[19,8,16,512]{3,2,1,0:T(8,128)}) custom-call(f32[10,16,512]{2,1,0:T(8,128)S(1)} %collective-permute-done.1.joint, f32[19,8,16,512]{3,2,1,0:T(8,128)} %get-tuple-element.137.f_in, f32[19,8,16,512]{3,2,1,0:T(8,128)} %get-tuple-element.138.g_in), custom_call_target="tpu_custom_call", output_to_operand_aliasing={{0}: (1, {}), {1}: (2, {})} | custom-call | tf_op jit(solution)/shard_map/cond/branch_0_fun/joint_fill/pallas_call | solution.py:767
  (6 shorter events, 0.1 us)
Async XLA Ops:
  0.6 6.2 %copy-start = (f32[19,8,16,512]{3,2,1,0:T(8,128)S(1)}, f32[19,8,16,512]{3,2,1,0:T(8,128)}, u32[]{:S(2)}) copy-start(f32[19,8,16,512]{3,2,1,0:T(8,128)} %g_ref.7) | copy-start | bytes 14942212
  2.2 6.7 %collective-permute-start.29 = (f32[16,512]{1,0:T(8,128)S(1)}, f32[16,512]{1,0:T(8,128)S(1)}, u32[]{:S(2)}, u32[]{:S(2)}) collective-permute-start(f32[16,512]{1,0:T(8,128)S(1)} %get-tuple-element.236.top), channel_id=1, source_target_pairs={{0,12},{1,13},{2,14},{3,15},{4,8},{5,9},{6,10},{7,11},{8,20},{9,21... | collective-permute-start | bytes 98312 | tf_op jit(solution)/shard_map/ppermute | solution.py:616
  4.4 5.8 %collective-permute-start.28 = (f32[16,512]{1,0:T(8,128)S(1)}, f32[16,512]{1,0:T(8,128)S(1)}, u32[]{:S(2)}, u32[]{:S(2)}) collective-permute-start(f32[16,512]{1,0:T(8,128)S(1)} %get-tuple-element.237.bottom), channel_id=1, source_target_pairs={{0,28},{1,29},{2,30},{3,31},{4,24},{5,25},{6,26},{7,27},{8,4},{9,5... | collective-permute-start | bytes 98312 | tf_op jit(solution)/shard_map/ppermute | solution.py:616
  5.5 8.4 %slice-start = ((s8[4980736]{0:T(1024)(128)(4,1)}), s8[4194304]{0:T(1024)(128)(4,1)S(1)}, s32[]{:S(2)}) async-start(s8[4980736]{0:T(1024)(128)(4,1)} %bitcast.1), calls=%async_computation | async-start | bytes 8388608
  6.8 7.1 %slice-start.1 = ((s8[4980736]{0:T(1024)(128)(4,1)}), s8[786432]{0:T(1024)(128)(4,1)S(1)}, s32[]{:S(2)}) async-start(s8[4980736]{0:T(1024)(128)(4,1)} %bitcast.1), calls=%async_computation.1 | async-start | bytes 1572864
  8.9 5.5 %collective-permute-start.31 = (f32[40,512]{1,0:T(8,128)S(1)}, f32[40,512]{1,0:T(8,128)S(1)}, u32[]{:S(2)}, u32[]{:S(2)}) collective-permute-start(f32[40,512]{1,0:T(8,128)S(1)} %constant_dynamic-update-slice_fusion.2.after_south), channel_id=1, source_target_pairs={{0,7},{1,0},{2,1},{3,2},{4,3},{5,4},{6,5},{7,6},{8,15},{9,8},{10,9... | collective-permute-start | bytes 245768 | tf_op jit(solution)/shard_map/ppermute | solution.py:616
  10.2 4.9 %collective-permute-start.30 = (f32[40,512]{1,0:T(8,128)S(1)}, f32[40,512]{1,0:T(8,128)S(1)}, u32[]{:S(2)}, u32[]{:S(2)}) collective-permute-start(f32[40,512]{1,0:T(8,128)S(1)} %constant_dynamic-update-slice_fusion.after_north), channel_id=1, source_target_pairs={{0,1},{1,2},{2,3},{3,4},{4,5},{5,6},{6,7},{7,0},{8,9},{9,10},{10,1... | collective-permute-start | bytes 245768 | tf_op jit(solution)/shard_map/ppermute | solution.py:616
  13.9 1.2 %copy-start.1 = (s32[4]{0:T(128)S(1)}, s32[4]{0:T(128)}, u32[]{:S(2)}) copy-start(s32[4]{0:T(128)} %offsets.3) | copy-start | bytes 52
  17.2 12.5 %collective-permute-start = (f32[10,24,512]{2,1,0:T(8,128)S(1)}, f32[10,24,512]{2,1,0:T(8,128)S(1)}, u32[]{:S(2)}, u32[]{:S(2)}) collective-permute-start(f32[10,24,512]{2,1,0:T(8,128)S(1)} %get-tuple-element.121), channel_id=1, source_target_pairs={{0,1},{1,0},{2,3},{3,2},{4,5},{5,4},{6,7},{7,6},{8,9},{9,8},{10,11... | collective-permute-start | bytes 1474568 | tf_op jit(solution)/shard_map/cond/branch_0_fun/ppermute | solution.py:616
  20.5 10.0 %collective-permute-start.6 = (f32[10,8,512]{2,1,0:T(8,128)S(1)}, f32[10,8,512]{2,1,0:T(8,128)S(1)}, u32[]{:S(2)}, u32[]{:S(2)}) collective-permute-start(f32[10,8,512]{2,1,0:T(8,128)S(1)} %get-tuple-element.134), channel_id=1, source_target_pairs={{0,7},{1,2},{2,1},{3,4},{4,3},{5,6},{6,5},{7,0},{8,15},{9,10},{10,... | collective-permute-start | bytes 491528 | tf_op jit(solution)/shard_map/cond/branch_0_fun/ppermute | solution.py:616
  20.5 38.0 %collective-permute-start.2 = (f32[10,16,512]{2,1,0:T(8,128)S(1)}, f32[10,16,512]{2,1,0:T(8,128)S(1)}, u32[]{:S(2)}, u32[]{:S(2)}) collective-permute-start(f32[10,16,512]{2,1,0:T(8,128)S(1)} %get-tuple-element.123), channel_id=1, source_target_pairs={{0,28},{1,13},{2,30},{3,15},{4,24},{5,9},{6,26},{7,11},{8,4},{9,21... | collective-permute-start | bytes 983048 | tf_op jit(solution)/shard_map/cond/branch_0_fun/ppermute | solution.py:731
  24.0 34.5 %collective-permute-start.4 = (f32[10,16,512]{2,1,0:T(8,128)S(1)}, f32[10,16,512]{2,1,0:T(8,128)S(1)}, u32[]{:S(2)}, u32[]{:S(2)}) collective-permute-start(f32[10,16,512]{2,1,0:T(8,128)S(1)} %get-tuple-element.125), channel_id=1, source_target_pairs={{16,27},{18,29},{20,31},{22,25},{25,22},{27,16},{29,18},{31,20}} | collective-permute-start | bytes 983048 | tf_op jit(solution)/shard_map/cond/branch_0_fun/ppermute | solution.py:731
  29.7 30.2 %collective-permute-start.1 = (f32[10,16,512]{2,1,0:T(8,128)S(1)}, f32[10,16,512]{2,1,0:T(8,128)S(1)}, u32[]{:S(2)}, u32[]{:S(2)}) collective-permute-start(f32[10,16,512]{2,1,0:T(8,128)S(1)} %slice_add_fusion.after), channel_id=1, source_target_pairs={{0,12},{1,29},{2,14},{3,31},{4,8},{5,25},{6,10},{7,27},{8,20},{9,5... | collective-permute-start | bytes 983048 | tf_op jit(solution)/shard_map/cond/branch_0_fun/ppermute | solution.py:616
  29.8 28.7 %collective-permute-start.5 = (f32[104,512]{1,0:T(8,128)S(1)}, f32[104,512]{1,0:T(8,128)S(1)}, u32[]{:S(2)}, u32[]{:S(2)}) collective-permute-start(f32[104,512]{1,0:T(8,128)S(1)} %get-tuple-element.126), channel_id=1, source_target_pairs={{0,11},{1,30},{2,13},{3,24},{4,15},{5,26},{6,9},{7,28},{8,19},{9,6... | collective-permute-start | bytes 638984 | tf_op jit(solution)/shard_map/cond/branch_0_fun/ppermute | solution.py:731
  30.5 28.0 %collective-permute-start.3 = (f32[10,8,512]{2,1,0:T(8,128)S(1)}, f32[10,8,512]{2,1,0:T(8,128)S(1)}, u32[]{:S(2)}, u32[]{:S(2)}) collective-permute-start(f32[10,8,512]{2,1,0:T(8,128)S(1)} %get-tuple-element.124), channel_id=1, source_target_pairs={{17,29},{19,31},{21,25},{23,27},{24,20},{26,22},{28,16},{30,18}} | collective-permute-start | bytes 491528 | tf_op jit(solution)/shard_map/cond/branch_0_fun/ppermute | solution.py:731

commit v10 on v6

--- a/solution.py
+++ b/solution.py
@@ -729,6 +729,9 @@
 
         cross = hop(cross, lambda x, y: (x, y + 1 if y % 2 == 1 else y - 1))
         mate = hop(mate, lambda x, y: (x, y ^ 1))
+        direct, direct_short, across, across_short, cross = lax.optimization_barrier(
+            (direct, direct_short, across, across_short, cross)
+        )
         direct = hop_some(direct, True, 0, False)
         direct_short = hop_some(direct_short, True, 0, True)
         across = hop_some(across, False, 1, True)
@@ -751,6 +754,17 @@
         )(after, momentum_dist, order_near, *around, mate, cross)
 
         next_f, next_g = pl.pallas_call(
+            joint_fill_kernel,
+            out_shape=[whole, whole],
+            in_specs=[vmem, anywhere, anywhere],
+            out_specs=[anywhere, anywhere],
+            scratch_shapes=[pltpu.SemaphoreType.DMA((10,))],
+            input_output_aliases={1: 0, 2: 1},
+            compiler_params=params(24 << 20),
+            name="joint_fill",
+        )(joint, next_f, next_g)
+
+        return pl.pallas_call(
             functools.partial(merge_fill_kernel, (count_x, count_y)),
             out_shape=[whole, whole],
             in_specs=[smem] + [vmem] * 4 + [anywhere, anywhere],
@@ -761,17 +775,6 @@
             name="merge_fill",
         )(offsets, direct, direct_short, across, across_short, next_f, next_g)
 
-        return pl.pallas_call(
-            joint_fill_kernel,
-            out_shape=[whole, whole],
-            in_specs=[vmem, anywhere, anywhere],
-            out_specs=[anywhere, anywhere],
-            scratch_shapes=[pltpu.SemaphoreType.DMA((10,))],
-            input_output_aliases={1: 0, 2: 1},
-            compiler_params=params(24 << 20),
-            name="joint_fill",
-        )(joint, next_f, next_g)
-
     is_long = [(offsets[k] - half * rows > part).astype(jnp.int32) for k in (1, 2)]
     branches = [
         functools.partial(finish, {3} | ({1} if k & 2 else set()) | ({2} if k & 1 else set()))

time: 61.4 us -> 61.2 us (level)
  the two profiles are of different devices: /device:TPU:14 before, /device:TPU:0 now
where the time goes in v10:
time: 61.2 us; the launch traced here: 61 us
  waiting for transfers between devices  20.6 us (34%)
  starting transfers between devices  19.3 us (32%)
  Pallas kernels  16.9 us (28%)
  between operations  2.03 us (3%)
  other arithmetic  1.4 us (2%)
  local copies, waits for them, and re-layouts  0.62 us (1%)
    ppermute x7, waiting for transfers between devices, hop(): return lax.ppermute(value, ('gx', 'gy'), perm)  12.7 us
    ppermute x4, starting transfers between devices, hop_some(): return lax.ppermute(value, ('gx', 'gy'), pairs)  9.72 us
    ppermute x7, starting transfers between devices, hop(): return lax.ppermute(value, ('gx', 'gy'), perm)  9.61 us
    pallas_call x1, Pallas kernels, finish(): pl.pallas_call(bulk_kernel, out_shape=[whole, whole], in_specs=[anywhere]...  8.9 us
    ppermute x4, waiting for transfers between devices, hop_some(): return lax.ppermute(value, ('gx', 'gy'), pairs)  7.84 us
    pallas_call x1, Pallas kernels, on_device(): pl.pallas_call(phi_kernel, out_shape=[jax.ShapeDtypeStruct((layers, rows,...  3.31 us
    pallas_call x1, Pallas kernels, on_device(): pl.pallas_call(functools.partial(face_kernel, (count_x, count_y)), out_sh...  2.05 us
    pallas_call x1, Pallas kernels, finish(): pl.pallas_call(functools.partial(merge_fill_kernel, (count_x, count_y)),...  1.42 us
  transfers between devices with their start and end apart: 11, of which 6 were waited for; matrix products, arithmetic and copies ran while one was open for 1% of the time, Pallas kernels for 22%

profile of v10, /device:TPU:0, one launch (start us, length us, event | category | flops | bytes accessed | tf_op | source)
XLA Modules:
  0.0 61.0 jit_solution(4343234143914350767)
XLA Ops:
  0.6 1.4 %slice_reduce_fusion = (f32[16,512]{1,0:T(8,128)S(1)}, f32[16,512]{1,0:T(8,128)S(1)}) fusion(f32[19,8,16,512]{3,2,1,0:T(8,128)} %g_ref.1), kind=kLoop, calls=%fused_computation.4 | loop fusion | flops 294912 | bytes 1310720 | tf_op jit(solution)/shard_map/reduce_sum | solution.py:637
  2.0 5.0 %collective-permute-start.29 = (f32[16,512]{1,0:T(8,128)S(1)}, f32[16,512]{1,0:T(8,128)S(1)}, u32[]{:S(2)}, u32[]{:S(2)}) collective-permute-start(f32[16,512]{1,0:T(8,128)S(1)} %get-tuple-element.259.top), channel_id=1, source_target_pairs={{0,12},{1,13},{2,14},{3,15},{4,8},{5,9},{6,10},{7,11},{8,20},{9,21... | collective-permute-start | bytes 98312 | tf_op jit(solution)/shard_map/ppermute | solution.py:616
  7.0 0.0 slice-start
  7.0 0.0 copy-start
  7.0 0.0 slice-start.1
  7.0 1.1 %collective-permute-start.28 = (f32[16,512]{1,0:T(8,128)S(1)}, f32[16,512]{1,0:T(8,128)S(1)}, u32[]{:S(2)}, u32[]{:S(2)}) collective-permute-start(f32[16,512]{1,0:T(8,128)S(1)} %get-tuple-element.258.bottom), channel_id=1, source_target_pairs={{0,28},{1,29},{2,30},{3,31},{4,24},{5,25},{6,26},{7,27},{8,4},{9,5... | collective-permute-start | bytes 98312 | tf_op jit(solution)/shard_map/ppermute | solution.py:616
  8.1 3.3 %phi_all.1 = (f32[8,16,512]{2,1,0:T(8,128)S(1)}, f32[24,512]{1,0:T(8,128)S(1)}, f32[24,512]{1,0:T(8,128)S(1)}, f32[19,8,16,512]{3,2,1,0:T(8,128)S(1)}) custom-call(f32[19,8,16,512]{3,2,1,0:T(8,128)} %f_ref.5, f32[19,8,16,512]{3,2,1,0:T(8,128)} %g_ref.1, f32[16,512]{1,0:T(8,128)S(1)} %get-tuple-element.259.top, f32[16,512]{1,0:T(8,128)S(1)} %get-tuple-element.258.bottom), custom_call_target="tpu_custom_call" | custom-call | tf_op jit(solution)/shard_map/phi_all/pallas_call | solution.py:642
  11.4 0.0 collective-permute-done.29.rise
  11.4 2.2 %collective-permute-start.31 = (f32[40,512]{1,0:T(8,128)S(1)}, f32[40,512]{1,0:T(8,128)S(1)}, u32[]{:S(2)}, u32[]{:S(2)}) collective-permute-start(f32[40,512]{1,0:T(8,128)S(1)} %constant_dynamic-update-slice_fusion.2.after_south), channel_id=1, source_target_pairs={{0,7},{1,0},{2,1},{3,2},{4,3},{5,4},{6,5},{7,6},{8,15},{9,8},{10,9... | collective-permute-start | bytes 245768 | tf_op jit(solution)/shard_map/ppermute | solution.py:616
  13.7 0.0 collective-permute-done.28.fall
  13.7 0.1 collective-permute-start.30
  13.7 0.0 copy-done
  13.8 0.6 fusion
  15.6 0.0 slice-done
  15.7 0.0 slice-done.1
  15.7 0.4 moments.1
  16.1 0.3 collective-permute-done.31.north_msg
  16.4 3.0 %collective-permute-done.30.south_msg = f32[40,512]{1,0:T(8,128)S(1)} collective-permute-done((f32[40,512]{1,0:T(8,128)S(1)}, f32[40,512]{1,0:T(8,128)S(1)}, u32[]{:S(2)}, u32[]{:S(2)}) %collective-permute-start.30) | collective-permute-done | bytes 81952 | tf_op jit(solution)/shard_map/ppermute | solution.py:616
  19.4 2.1 %faces.1 = (f32[10,24,512]{2,1,0:T(8,128)S(1)}, f32[10,16,512]{2,1,0:T(8,128)S(1)}, f32[10,8,512]{2,1,0:T(8,128)S(1)}, f32[10,16,512]{2,1,0:T(8,128)S(1)}, f32[1...) custom-call(s32[4]{0:T(128)S(1)} %copy-done, ...), custom_call_target="tpu_custom_call" | custom-call | tf_op jit(solution)/shard_map/faces/pallas_call | solution.py:678
  21.5 39.5 %conditional.1 = ((f32[19,8,16,512]{3,2,1,0:T(8,128)}, f32[19,8,16,512]{3,2,1,0:T(8,128)})) conditional(s32[]{:T(128)} %bitcast, (f32[10,8,512]{2,1,0:T(8,128)S(1)}, f32[10,16,512]{2,1,0:T(8,128)S(1)}, f32[10,8,512]{2,1,0:T(8,128)S(1)}, f32[10,16,512]{2,1,0:T(8,128)S(1)}, f32[104,512]{1,0:T(8,128)S(1)}, ...), branch_computations={%region_2.0_spmd, %region_3.0_spmd, %region_4.0_spmd, %region_5.0_... | conditional | flops 81920 | bytes 9044256 | solution.py:783
  21.5 0.1 collective-permute-start.5
  21.5 0.8 %collective-permute-start = (f32[10,8,512]{2,1,0:T(8,128)S(1)}, f32[10,8,512]{2,1,0:T(8,128)S(1)}, u32[]{:S(2)}, u32[]{:S(2)}) collective-permute-start(f32[10,8,512]{2,1,0:T(8,128)S(1)} %get-tuple-element.125), channel_id=1, source_target_pairs={{0,7},{1,2},{2,1},{3,4},{4,3},{5,6},{6,5},{7,0},{8,15},{9,10},{10,... | collective-permute-start | bytes 491528 | tf_op jit(solution)/shard_map/cond/branch_0_fun/ppermute | solution.py:616
  22.3 1.1 %collective-permute-done.5.mate_rim = f32[10,24,512]{2,1,0:T(8,128)S(1)} collective-permute-done((f32[10,24,512]{2,1,0:T(8,128)S(1)}, f32[10,24,512]{2,1,0:T(8,128)S(1)}, u32[]{:S(2)}, u32[]{:S(2)}) %collective-permute-start.5) | collective-permute-done | bytes 491552 | tf_op jit(solution)/shard_map/cond/branch_0_fun/ppermute | solution.py:616
  23.4 0.4 collective-permute-start.6
  23.9 4.4 %collective-permute-done.cross_rim = f32[10,8,512]{2,1,0:T(8,128)S(1)} collective-permute-done((f32[10,8,512]{2,1,0:T(8,128)S(1)}, f32[10,8,512]{2,1,0:T(8,128)S(1)}, u32[]{:S(2)}, u32[]{:S(2)}) %collective-permute-start) | collective-permute-done | bytes 163872 | tf_op jit(solution)/shard_map/cond/branch_0_fun/ppermute | solution.py:616
  28.3 1.9 %collective-permute-start.1 = (f32[10,16,512]{2,1,0:T(8,128)S(1)}, f32[10,16,512]{2,1,0:T(8,128)S(1)}, u32[]{:S(2)}, u32[]{:S(2)}) collective-permute-start(f32[10,16,512]{2,1,0:T(8,128)S(1)} %get-tuple-element.126), channel_id=1, source_target_pairs={{0,28},{1,13},{2,30},{3,15},{4,24},{5,9},{6,26},{7,11},{8,4},{9,21... | collective-permute-start | bytes 983048 | tf_op jit(solution)/shard_map/cond/branch_0_fun/ppermute | solution.py:728
  30.2 0.7 %collective-permute-start.3 = (f32[10,16,512]{2,1,0:T(8,128)S(1)}, f32[10,16,512]{2,1,0:T(8,128)S(1)}, u32[]{:S(2)}, u32[]{:S(2)}) collective-permute-start(f32[10,16,512]{2,1,0:T(8,128)S(1)} %get-tuple-element.128), channel_id=1, source_target_pairs={{16,27},{18,29},{20,31},{22,25},{25,22},{27,16},{29,18},{31,20}} | collective-permute-start | bytes 983048 | tf_op jit(solution)/shard_map/cond/branch_0_fun/ppermute | solution.py:728
  30.9 6.5 %collective-permute-start.4 = (f32[104,512]{1,0:T(8,128)S(1)}, f32[104,512]{1,0:T(8,128)S(1)}, u32[]{:S(2)}, u32[]{:S(2)}) collective-permute-start(f32[104,512]{1,0:T(8,128)S(1)} %get-tuple-element.129), channel_id=1, source_target_pairs={{0,11},{1,30},{2,13},{3,24},{4,15},{5,26},{6,9},{7,28},{8,19},{9,6... | collective-permute-start | bytes 638984 | tf_op jit(solution)/shard_map/cond/branch_0_fun/ppermute | solution.py:728
  37.3 0.7 %collective-permute-start.2 = (f32[10,8,512]{2,1,0:T(8,128)S(1)}, f32[10,8,512]{2,1,0:T(8,128)S(1)}, u32[]{:S(2)}, u32[]{:S(2)}) collective-permute-start(f32[10,8,512]{2,1,0:T(8,128)S(1)} %get-tuple-element.127), channel_id=1, source_target_pairs={{17,29},{19,31},{21,25},{23,27},{24,20},{26,22},{28,16},{30,18}} | collective-permute-start | bytes 491528 | tf_op jit(solution)/shard_map/cond/branch_0_fun/ppermute | solution.py:728
  38.0 8.9 %bulk.4 = (f32[19,8,16,512]{3,2,1,0:T(8,128)}, f32[19,8,16,512]{3,2,1,0:T(8,128)}) custom-call(f32[10,16,512]{2,1,0:T(8,128)S(1)} %slice_add_fusion.after, f32[19,8,16,512]{3,2,1,0:T(8,128)S(1)} %get-tuple-element.132.f_ref, f32[19,8,16,512]{3,2,1,0:T(8,128)S(1)} %get-tuple-element.133.g_ref, f32[8,16,512]{2,1,0:T(8,128)S(1)} %get-tuple-element.134.phi_ref, ...), custom_call_target="tpu_custom_call" | custom-call | tf_op jit(solution)/shard_map/cond/branch_0_fun/bulk/pallas_call | solution.py:743
  46.9 4.0 %collective-permute-done.6.joint = f32[10,16,512]{2,1,0:T(8,128)S(1)} collective-permute-done((f32[10,16,512]{2,1,0:T(8,128)S(1)}, f32[10,16,512]{2,1,0:T(8,128)S(1)}, u32[]{:S(2)}, u32[]{:S(2)}) %collective-permute-start.6) | collective-permute-done | bytes 327712 | tf_op jit(solution)/shard_map/cond/branch_0_fun/ppermute | solution.py:616
  50.9 0.8 %joint_fill.4 = (f32[19,8,16,512]{3,2,1,0:T(8,128)}, f32[19,8,16,512]{3,2,1,0:T(8,128)}) custom-call(f32[10,16,512]{2,1,0:T(8,128)S(1)} %collective-permute-done.6.joint, f32[19,8,16,512]{3,2,1,0:T(8,128)} %get-tuple-element.140.f_in, f32[19,8,16,512]{3,2,1,0:T(8,128)} %get-tuple-element.141.g_in), custom_call_target="tpu_custom_call", output_to_operand_aliasing={{0}: (1, {}), {1}: (2, {})} | custom-call | tf_op jit(solution)/shard_map/cond/branch_0_fun/joint_fill/pallas_call | solution.py:756
  51.7 0.0 collective-permute-done.2.direct_short
  51.7 0.0 collective-permute-done.4.across_short
  51.7 7.8 %collective-permute-done.1.direct = f32[10,16,512]{2,1,0:T(8,128)S(1)} collective-permute-done((f32[10,16,512]{2,1,0:T(8,128)S(1)}, f32[10,16,512]{2,1,0:T(8,128)S(1)}, u32[]{:S(2)}, u32[]{:S(2)}) %collective-permute-start.1) | collective-permute-done | bytes 327712 | tf_op jit(solution)/shard_map/cond/branch_0_fun/ppermute | solution.py:728
  59.5 0.0 collective-permute-done.3.across
  59.5 1.4 %merge_fill.4 = (f32[19,8,16,512]{3,2,1,0:T(8,128)}, f32[19,8,16,512]{3,2,1,0:T(8,128)}) custom-call(s32[4]{0:T(128)S(1)} %get-tuple-element.120.offsets, f32[10,16,512]{2,1,0:T(8,128)S(1)} %collective-permute-done.1.direct, f32[10,8,512]{2,1,0:T(8,128)S(1)} %collective-permute-done.2.direct_short, ...), custom_call_target="tpu_custom_call", output_to_operand_aliasing={{0}: (5, {}), {1}: (6, {})} | custom-call | tf_op jit(solution)/shard_map/cond/branch_0_fun/merge_fill/pallas_call | solution.py:767
  (6 shorter events, 0.1 us)
Async XLA Ops:
  2.0 9.4 %collective-permute-start.29 = (f32[16,512]{1,0:T(8,128)S(1)}, f32[16,512]{1,0:T(8,128)S(1)}, u32[]{:S(2)}, u32[]{:S(2)}) collective-permute-start(f32[16,512]{1,0:T(8,128)S(1)} %get-tuple-element.259.top), channel_id=1, source_target_pairs={{0,12},{1,13},{2,14},{3,15},{4,8},{5,9},{6,10},{7,11},{8,20},{9,21... | collective-permute-start | bytes 98312 | tf_op jit(solution)/shard_map/ppermute | solution.py:616
  7.0 8.6 %slice-start = ((s8[4980736]{0:T(1024)(128)(4,1)}), s8[4194304]{0:T(1024)(128)(4,1)S(1)}, s32[]{:S(2)}) async-start(s8[4980736]{0:T(1024)(128)(4,1)} %bitcast.1), calls=%async_computation | async-start | bytes 8388608
  7.0 6.7 %copy-start = (s32[4]{0:T(128)S(1)}, s32[4]{0:T(128)}, u32[]{:S(2)}) copy-start(s32[4]{0:T(128)} %offsets.1) | copy-start | bytes 52
  7.0 8.7 %slice-start.1 = ((s8[4980736]{0:T(1024)(128)(4,1)}), s8[786432]{0:T(1024)(128)(4,1)S(1)}, s32[]{:S(2)}) async-start(s8[4980736]{0:T(1024)(128)(4,1)} %bitcast.1), calls=%async_computation.1 | async-start | bytes 1572864
  7.0 6.7 %collective-permute-start.28 = (f32[16,512]{1,0:T(8,128)S(1)}, f32[16,512]{1,0:T(8,128)S(1)}, u32[]{:S(2)}, u32[]{:S(2)}) collective-permute-start(f32[16,512]{1,0:T(8,128)S(1)} %get-tuple-element.258.bottom), channel_id=1, source_target_pairs={{0,28},{1,29},{2,30},{3,31},{4,24},{5,25},{6,26},{7,27},{8,4},{9,5... | collective-permute-start | bytes 98312 | tf_op jit(solution)/shard_map/ppermute | solution.py:616
  11.4 4.9 %collective-permute-start.31 = (f32[40,512]{1,0:T(8,128)S(1)}, f32[40,512]{1,0:T(8,128)S(1)}, u32[]{:S(2)}, u32[]{:S(2)}) collective-permute-start(f32[40,512]{1,0:T(8,128)S(1)} %constant_dynamic-update-slice_fusion.2.after_south), channel_id=1, source_target_pairs={{0,7},{1,0},{2,1},{3,2},{4,3},{5,4},{6,5},{7,6},{8,15},{9,8},{10,9... | collective-permute-start | bytes 245768 | tf_op jit(solution)/shard_map/ppermute | solution.py:616
  13.7 5.7 %collective-permute-start.30 = (f32[40,512]{1,0:T(8,128)S(1)}, f32[40,512]{1,0:T(8,128)S(1)}, u32[]{:S(2)}, u32[]{:S(2)}) collective-permute-start(f32[40,512]{1,0:T(8,128)S(1)} %constant_dynamic-update-slice_fusion.after_north), channel_id=1, source_target_pairs={{0,1},{1,2},{2,3},{3,4},{4,5},{5,6},{6,7},{7,0},{8,9},{9,10},{10,1... | collective-permute-start | bytes 245768 | tf_op jit(solution)/shard_map/ppermute | solution.py:616
  21.5 1.9 %collective-permute-start.5 = (f32[10,24,512]{2,1,0:T(8,128)S(1)}, f32[10,24,512]{2,1,0:T(8,128)S(1)}, u32[]{:S(2)}, u32[]{:S(2)}) collective-permute-start(f32[10,24,512]{2,1,0:T(8,128)S(1)} %get-tuple-element.131), channel_id=1, source_target_pairs={{0,1},{1,0},{2,3},{3,2},{4,5},{5,4},{6,7},{7,6},{8,9},{9,8},{10,11... | collective-permute-start | bytes 1474568 | tf_op jit(solution)/shard_map/cond/branch_0_fun/ppermute | solution.py:616
  21.5 6.7 %collective-permute-start = (f32[10,8,512]{2,1,0:T(8,128)S(1)}, f32[10,8,512]{2,1,0:T(8,128)S(1)}, u32[]{:S(2)}, u32[]{:S(2)}) collective-permute-start(f32[10,8,512]{2,1,0:T(8,128)S(1)} %get-tuple-element.125), channel_id=1, source_target_pairs={{0,7},{1,2},{2,1},{3,4},{4,3},{5,6},{6,5},{7,0},{8,15},{9,10},{10,... | collective-permute-start | bytes 491528 | tf_op jit(solution)/shard_map/cond/branch_0_fun/ppermute | solution.py:616
  23.4 27.4 %collective-permute-start.6 = (f32[10,16,512]{2,1,0:T(8,128)S(1)}, f32[10,16,512]{2,1,0:T(8,128)S(1)}, u32[]{:S(2)}, u32[]{:S(2)}) collective-permute-start(f32[10,16,512]{2,1,0:T(8,128)S(1)} %slice_add_fusion.after), channel_id=1, source_target_pairs={{0,12},{1,29},{2,14},{3,31},{4,8},{5,25},{6,10},{7,27},{8,20},{9,5... | collective-permute-start | bytes 983048 | tf_op jit(solution)/shard_map/cond/branch_0_fun/ppermute | solution.py:616
  28.3 31.3 %collective-permute-start.1 = (f32[10,16,512]{2,1,0:T(8,128)S(1)}, f32[10,16,512]{2,1,0:T(8,128)S(1)}, u32[]{:S(2)}, u32[]{:S(2)}) collective-permute-start(f32[10,16,512]{2,1,0:T(8,128)S(1)} %get-tuple-element.126), channel_id=1, source_target_pairs={{0,28},{1,13},{2,30},{3,15},{4,24},{5,9},{6,26},{7,11},{8,4},{9,21... | collective-permute-start | bytes 983048 | tf_op jit(solution)/shard_map/cond/branch_0_fun/ppermute | solution.py:728
  30.2 29.4 %collective-permute-start.3 = (f32[10,16,512]{2,1,0:T(8,128)S(1)}, f32[10,16,512]{2,1,0:T(8,128)S(1)}, u32[]{:S(2)}, u32[]{:S(2)}) collective-permute-start(f32[10,16,512]{2,1,0:T(8,128)S(1)} %get-tuple-element.128), channel_id=1, source_target_pairs={{16,27},{18,29},{20,31},{22,25},{25,22},{27,16},{29,18},{31,20}} | collective-permute-start | bytes 983048 | tf_op jit(solution)/shard_map/cond/branch_0_fun/ppermute | solution.py:728
  30.9 20.8 %collective-permute-start.4 = (f32[104,512]{1,0:T(8,128)S(1)}, f32[104,512]{1,0:T(8,128)S(1)}, u32[]{:S(2)}, u32[]{:S(2)}) collective-permute-start(f32[104,512]{1,0:T(8,128)S(1)} %get-tuple-element.129), channel_id=1, source_target_pairs={{0,11},{1,30},{2,13},{3,24},{4,15},{5,26},{6,9},{7,28},{8,19},{9,6... | collective-permute-start | bytes 638984 | tf_op jit(solution)/shard_map/cond/branch_0_fun/ppermute | solution.py:728
  37.3 14.4 %collective-permute-start.2 = (f32[10,8,512]{2,1,0:T(8,128)S(1)}, f32[10,8,512]{2,1,0:T(8,128)S(1)}, u32[]{:S(2)}, u32[]{:S(2)}) collective-permute-start(f32[10,8,512]{2,1,0:T(8,128)S(1)} %get-tuple-element.127), channel_id=1, source_target_pairs={{17,29},{19,31},{21,25},{23,27},{24,20},{26,22},{28,16},{30,18}} | collective-permute-start | bytes 491528 | tf_op jit(solution)/shard_map/cond/branch_0_fun/ppermute | solution.py:728

commit v11 on v9

--- a/solution.py
+++ b/solution.py
@@ -189,20 +189,24 @@
     return total
 
 
-def branch_kernel(part, base, g_ref, offsets, index):
-    first, second = offsets[1] - base > part, offsets[2] - base > part
-    index[0] = 2 * first.astype(jnp.int32) + second.astype(jnp.int32)
-
-
-def phi_kernel(index, f_ref, g_ref, top, bottom, phi_ref, to_north, to_south, fbuf, sems):
-    layers, rows = phi_ref.shape[0], phi_ref.shape[1]
-    faces = (layers - 1, 0)
+def phi_faces_kernel(part, base, f_ref, g_ref, offsets, top, bottom, index, buf, sems):
+    layers = g_ref.shape[1]
     copies = [
-        pltpu.make_async_copy(f_ref.at[:, x], fbuf.at[:, s], sems.at[s])
-        for s, x in enumerate(faces)
+        pltpu.make_async_copy(g_ref.at[:, x], buf.at[s], sems.at[s])
+        for s, x in enumerate((layers - 1, 0))
     ]
     for copy in copies:
         copy.start()
+    first, second = offsets[1] - base > part, offsets[2] - base > part
+    index[0] = 2 * first.astype(jnp.int32) + second.astype(jnp.int32)
+    for s, (copy, out) in enumerate(zip(copies, (top, bottom))):
+        copy.wait()
+        out[...] = order_sum(lambda i: buf[s, i])
+
+
+def phi_kernel(f_ref, g_ref, top, bottom, phi_ref, to_north, to_south):
+    layers, rows = phi_ref.shape[0], phi_ref.shape[1]
+    faces = (layers - 1, 0)
     phi_ref[layers - 1] = top[...]
     phi_ref[0] = bottom[...]
     for x in range(layers):
@@ -211,16 +215,15 @@
         to_north[x : x + 1] = phi_ref[x, rows - 1 : rows]
         to_south[x : x + 1] = phi_ref[x, 0:1]
     for s, x in enumerate(faces):
-        copies[s].wait()
         for out, edge, inner, chosen in (
             (to_north, rows - 1, rows - 2, (7, 10)),
             (to_south, 0, 1, (9, 8)),
         ):
             out[layers + s : layers + s + 1] = phi_ref[x, inner : inner + 1]
             at = layers + 2 + 6 * s
-            out[at : at + 1] = fbuf[chosen[s], s, edge : edge + 1]
+            out[at : at + 1] = f_ref[chosen[s], x, edge : edge + 1]
             out[at + 1 : at + 2] = g_ref[chosen[s], x, edge : edge + 1]
-            for k, part in enumerate(moments_of(lambda i: fbuf[i, s, edge : edge + 1])):
+            for k, part in enumerate(moments_of(lambda i: f_ref[i, x, edge : edge + 1])):
                 out[at + 2 + k : at + 3 + k] = part
     for out in (to_north, to_south):
         out[layers + 14 : layers + 16] = jnp.zeros((2, out.shape[1]), f32)
@@ -634,29 +637,28 @@
 
     smem, vmem, anywhere = spec_of(pltpu.SMEM), spec_of(VMEM), spec_of(pl.ANY)
     plane = jax.ShapeDtypeStruct((rows, cols), f32)
-    top, bottom = jnp.sum(order_dist[:, layers - 1], axis=0), jnp.sum(order_dist[:, 0], axis=0)
+    part = rows // 2
+    top, bottom, index = pl.pallas_call(
+        functools.partial(phi_faces_kernel, part, half * rows),
+        out_shape=[plane] * 2 + [jax.ShapeDtypeStruct((1,), jnp.int32)],
+        in_specs=[anywhere, anywhere, smem],
+        out_specs=[vmem] * 2 + [smem],
+        scratch_shapes=[VMEM((2, 19, rows, cols), f32), pltpu.SemaphoreType.DMA((2,))],
+        compiler_params=params(46 << 20),
+        name="phi_faces",
+    )(momentum_dist, order_dist, offsets)
     rise = hop(top, lambda x, y: (x + 1, y - base_up(x)))
     fall = hop(bottom, lambda x, y: (x - 1, y + base_low(x)))
 
     block = jax.ShapeDtypeStruct((layers + 16, cols), f32)
-    part = rows // 2
-    index = pl.pallas_call(
-        functools.partial(branch_kernel, part, half * rows),
-        out_shape=jax.ShapeDtypeStruct((1,), jnp.int32),
-        in_specs=[anywhere, smem],
-        out_specs=smem,
-        compiler_params=params(50 << 20),
-        name="branch",
-    )(order_dist, offsets)
     phi, to_north, to_south = pl.pallas_call(
         phi_kernel,
         out_shape=[jax.ShapeDtypeStruct((layers, rows, cols), f32)] + [block] * 2,
-        in_specs=[smem, anywhere, vmem, vmem, vmem],
+        in_specs=[vmem] * 4,
         out_specs=[vmem] * 3,
-        scratch_shapes=[VMEM((19, 2, rows, cols), f32), pltpu.SemaphoreType.DMA((2,))],
         compiler_params=params(8 << 20),
         name="phi_all",
-    )(index, momentum_dist, order_dist, top, bottom)
+    )(momentum_dist, order_dist, top, bottom)
     to_north = jnp.concatenate([fall, to_north], 0)
     to_south = jnp.concatenate([rise, to_south], 0)
     south_msg, north_msg = hop_y(to_north, 1), hop_y(to_south, -1)
@@ -732,6 +734,9 @@
 
         cross = hop(cross, lambda x, y: (x, y + 1 if y % 2 == 1 else y - 1))
         mate = hop(mate, lambda x, y: (x, y ^ 1))
+        direct, direct_short, across, across_short, cross = lax.optimization_barrier(
+            (direct, direct_short, across, across_short, cross)
+        )
         direct = hop_some(direct, True, 0, False)
         direct_short = hop_some(direct_short, True, 0, True)
         across = hop_some(across, False, 1, True)
@@ -754,6 +759,17 @@
         )(after, momentum_dist, order_dist, *around, mate, cross)
 
         next_f, next_g = pl.pallas_call(
+            joint_fill_kernel,
+            out_shape=[whole, whole],
+            in_specs=[vmem, anywhere, anywhere],
+            out_specs=[anywhere, anywhere],
+            scratch_shapes=[pltpu.SemaphoreType.DMA((10,))],
+            input_output_aliases={1: 0, 2: 1},
+            compiler_params=params(24 << 20),
+            name="joint_fill",
+        )(joint, next_f, next_g)
+
+        return pl.pallas_call(
             functools.partial(merge_fill_kernel, (count_x, count_y)),
             out_shape=[whole, whole],
             in_specs=[smem] + [vmem] * 4 + [anywhere, anywhere],
@@ -764,17 +780,6 @@
             name="merge_fill",
         )(offsets, direct, direct_short, across, across_short, next_f, next_g)
 
-        return pl.pallas_call(
-            joint_fill_kernel,
-            out_shape=[whole, whole],
-            in_specs=[vmem, anywhere, anywhere],
-            out_specs=[anywhere, anywhere],
-            scratch_shapes=[pltpu.SemaphoreType.DMA((10,))],
-            input_output_aliases={1: 0, 2: 1},
-            compiler_params=params(24 << 20),
-            name="joint_fill",
-        )(joint, next_f, next_g)
-
     branches = [
         functools.partial(finish, {3} | ({1} if k & 2 else set()) | ({2} if k & 1 else set()))
         for k in range(4)

time: 61.8 us -> 62.9 us (1.018)
  the two profiles are of different devices: /device:TPU:7 before, /device:TPU:0 now
where the time goes in v11:
time: 62.9 us; the launch traced here: 62.6 us
  waiting for transfers between devices  23.1 us (37%)
  starting transfers between devices  21.2 us (34%)
  Pallas kernels  16.8 us (27%)
  between operations  1.35 us (2%)
    ppermute x7, waiting for transfers between devices, hop(): return lax.ppermute(value, ('gx', 'gy'), perm)  15.1 us
    ppermute x7, starting transfers between devices, hop(): return lax.ppermute(value, ('gx', 'gy'), perm)  10.8 us
    ppermute x4, starting transfers between devices, hop_some(): return lax.ppermute(value, ('gx', 'gy'), pairs)  10.4 us
    pallas_call x1, Pallas kernels, finish(): pl.pallas_call(bulk_kernel, out_shape=[whole, whole], in_specs=[anywhere]...  8.9 us
    ppermute x4, waiting for transfers between devices, hop_some(): return lax.ppermute(value, ('gx', 'gy'), pairs)  8.01 us
    pallas_call x1, Pallas kernels, on_device(): pl.pallas_call(functools.partial(phi_faces_kernel, part, half * rows), ou...  2.98 us
    pallas_call x1, Pallas kernels, on_device(): pl.pallas_call(functools.partial(face_kernel, (count_x, count_y)), out_sh...  2.05 us
    pallas_call x1, Pallas kernels, finish(): pl.pallas_call(functools.partial(merge_fill_kernel, (count_x, count_y)),...  1.42 us
  transfers between devices with their start and end apart: 11, of which 8 were waited for; matrix products, arithmetic and copies ran while one was open for 0% of the time, Pallas kernels for 17%

profile of v11, /device:TPU:0, one launch (start us, length us, event | category | flops | bytes accessed | tf_op | source)
XLA Modules:
  0.0 62.6 jit_solution(8820028417001338382)
XLA Ops:
  0.6 0.0 copy-start
  0.6 0.0 copy-start.1
  0.6 3.0 %phi_faces.1 = (f32[16,512]{1,0:T(8,128)S(1)}, f32[16,512]{1,0:T(8,128)S(1)}, s32[1]{0:T(128)}) custom-call(f32[19,8,16,512]{3,2,1,0:T(8,128)} %f_ref.7, f32[19,8,16,512]{3,2,1,0:T(8,128)} %g_ref.7, s32[4]{0:T(128)} %offsets.3), custom_call_target="tpu_custom_call" | custom-call | tf_op jit(solution)/shard_map/phi_faces/pallas_call | solution.py:641
  3.6 5.0 %collective-permute-start.29 = (f32[16,512]{1,0:T(8,128)S(1)}, f32[16,512]{1,0:T(8,128)S(1)}, u32[]{:S(2)}, u32[]{:S(2)}) collective-permute-start(f32[16,512]{1,0:T(8,128)S(1)} %get-tuple-element.237.top), channel_id=1, source_target_pairs={{0,12},{1,13},{2,14},{3,15},{4,8},{5,9},{6,10},{7,11},{8,20},{9,21... | collective-permute-start | bytes 98312 | tf_op jit(solution)/shard_map/ppermute | solution.py:619
  8.7 1.0 %collective-permute-start.28 = (f32[16,512]{1,0:T(8,128)S(1)}, f32[16,512]{1,0:T(8,128)S(1)}, u32[]{:S(2)}, u32[]{:S(2)}) collective-permute-start(f32[16,512]{1,0:T(8,128)S(1)} %get-tuple-element.236.bottom), channel_id=1, source_target_pairs={{0,28},{1,29},{2,30},{3,31},{4,24},{5,25},{6,26},{7,27},{8,4},{9,5... | collective-permute-start | bytes 98312 | tf_op jit(solution)/shard_map/ppermute | solution.py:619
  9.7 0.0 copy-done
  9.7 0.0 copy-done.1
  9.7 0.2 phi_all.1
  9.9 1.9 %collective-permute-done.29.rise = f32[16,512]{1,0:T(8,128)S(1)} collective-permute-done((f32[16,512]{1,0:T(8,128)S(1)}, f32[16,512]{1,0:T(8,128)S(1)}, u32[]{:S(2)}, u32[]{:S(2)}) %collective-permute-start.29) | collective-permute-done | bytes 32800 | tf_op jit(solution)/shard_map/ppermute | solution.py:619
  11.9 2.1 %collective-permute-start.31 = (f32[40,512]{1,0:T(8,128)S(1)}, f32[40,512]{1,0:T(8,128)S(1)}, u32[]{:S(2)}, u32[]{:S(2)}) collective-permute-start(f32[40,512]{1,0:T(8,128)S(1)} %constant_dynamic-update-slice_fusion.2.after_south), channel_id=1, source_target_pairs={{0,7},{1,0},{2,1},{3,2},{4,3},{5,4},{6,5},{7,6},{8,15},{9,8},{10,9... | collective-permute-start | bytes 245768 | tf_op jit(solution)/shard_map/ppermute | solution.py:619
  13.9 0.4 collective-permute-done.28.fall
  14.4 0.1 collective-permute-start.30
  15.1 0.0 copy-start.2
  15.1 0.4 moments.1
  15.5 0.5 collective-permute-done.31.north_msg
  16.0 4.1 %collective-permute-done.30.south_msg = f32[40,512]{1,0:T(8,128)S(1)} collective-permute-done((f32[40,512]{1,0:T(8,128)S(1)}, f32[40,512]{1,0:T(8,128)S(1)}, u32[]{:S(2)}, u32[]{:S(2)}) %collective-permute-start.30) | collective-permute-done | bytes 81952 | tf_op jit(solution)/shard_map/ppermute | solution.py:619
  20.1 0.0 copy-done.2
  20.1 2.1 %faces.1 = (f32[10,24,512]{2,1,0:T(8,128)S(1)}, f32[10,16,512]{2,1,0:T(8,128)S(1)}, f32[10,8,512]{2,1,0:T(8,128)S(1)}, f32[10,16,512]{2,1,0:T(8,128)S(1)}, f32[1...) custom-call(s32[4]{0:T(128)S(1)} %copy-done.2, ...), custom_call_target="tpu_custom_call" | custom-call | tf_op jit(solution)/shard_map/faces/pallas_call | solution.py:683
  22.2 40.5 %conditional.1 = ((f32[19,8,16,512]{3,2,1,0:T(8,128)}, f32[19,8,16,512]{3,2,1,0:T(8,128)})) conditional(s32[]{:T(128)} %bitcast, (f32[10,8,512]{2,1,0:T(8,128)S(1)}, f32[10,16,512]{2,1,0:T(8,128)S(1)}, f32[10,8,512]{2,1,0:T(8,128)S(1)}, f32[10,16,512]{2,1,0:T(8,128)S(1)}, f32[104,512]{1,0:T(8,128)S(1)}, ...), branch_computations={%region_0.0_spmd, %region_1.0_spmd, %region_2.0_spmd, %region_3.0_... | conditional | flops 81920 | bytes 9044256 | solution.py:787
  22.2 0.1 collective-permute-start.5
  22.3 1.2 %collective-permute-start = (f32[10,8,512]{2,1,0:T(8,128)S(1)}, f32[10,8,512]{2,1,0:T(8,128)S(1)}, u32[]{:S(2)}, u32[]{:S(2)}) collective-permute-start(f32[10,8,512]{2,1,0:T(8,128)S(1)} %get-tuple-element.125), channel_id=1, source_target_pairs={{0,7},{1,2},{2,1},{3,4},{4,3},{5,6},{6,5},{7,0},{8,15},{9,10},{10,... | collective-permute-start | bytes 491528 | tf_op jit(solution)/shard_map/cond/branch_0_fun/ppermute | solution.py:619
  23.4 0.7 %collective-permute-done.5.mate_rim = f32[10,24,512]{2,1,0:T(8,128)S(1)} collective-permute-done((f32[10,24,512]{2,1,0:T(8,128)S(1)}, f32[10,24,512]{2,1,0:T(8,128)S(1)}, u32[]{:S(2)}, u32[]{:S(2)}) %collective-permute-start.5) | collective-permute-done | bytes 491552 | tf_op jit(solution)/shard_map/cond/branch_0_fun/ppermute | solution.py:619
  24.2 1.4 %collective-permute-start.6 = (f32[10,16,512]{2,1,0:T(8,128)S(1)}, f32[10,16,512]{2,1,0:T(8,128)S(1)}, u32[]{:S(2)}, u32[]{:S(2)}) collective-permute-start(f32[10,16,512]{2,1,0:T(8,128)S(1)} %slice_add_fusion.after), channel_id=1, source_target_pairs={{0,12},{1,29},{2,14},{3,31},{4,8},{5,25},{6,10},{7,27},{8,20},{9,5... | collective-permute-start | bytes 983048 | tf_op jit(solution)/shard_map/cond/branch_0_fun/ppermute | solution.py:619
  25.5 3.4 %collective-permute-done.cross_rim = f32[10,8,512]{2,1,0:T(8,128)S(1)} collective-permute-done((f32[10,8,512]{2,1,0:T(8,128)S(1)}, f32[10,8,512]{2,1,0:T(8,128)S(1)}, u32[]{:S(2)}, u32[]{:S(2)}) %collective-permute-start) | collective-permute-done | bytes 163872 | tf_op jit(solution)/shard_map/cond/branch_0_fun/ppermute | solution.py:619
  29.0 1.9 %collective-permute-start.1 = (f32[10,16,512]{2,1,0:T(8,128)S(1)}, f32[10,16,512]{2,1,0:T(8,128)S(1)}, u32[]{:S(2)}, u32[]{:S(2)}) collective-permute-start(f32[10,16,512]{2,1,0:T(8,128)S(1)} %get-tuple-element.126), channel_id=1, source_target_pairs={{0,28},{1,13},{2,30},{3,15},{4,24},{5,9},{6,26},{7,11},{8,4},{9,21... | collective-permute-start | bytes 983048 | tf_op jit(solution)/shard_map/cond/branch_0_fun/ppermute | solution.py:733
  30.9 0.7 %collective-permute-start.3 = (f32[10,16,512]{2,1,0:T(8,128)S(1)}, f32[10,16,512]{2,1,0:T(8,128)S(1)}, u32[]{:S(2)}, u32[]{:S(2)}) collective-permute-start(f32[10,16,512]{2,1,0:T(8,128)S(1)} %get-tuple-element.128), channel_id=1, source_target_pairs={{16,27},{18,29},{20,31},{22,25},{25,22},{27,16},{29,18},{31,20}} | collective-permute-start | bytes 983048 | tf_op jit(solution)/shard_map/cond/branch_0_fun/ppermute | solution.py:733
  31.6 7.1 %collective-permute-start.4 = (f32[104,512]{1,0:T(8,128)S(1)}, f32[104,512]{1,0:T(8,128)S(1)}, u32[]{:S(2)}, u32[]{:S(2)}) collective-permute-start(f32[104,512]{1,0:T(8,128)S(1)} %get-tuple-element.129), channel_id=1, source_target_pairs={{0,11},{1,30},{2,13},{3,24},{4,15},{5,26},{6,9},{7,28},{8,19},{9,6... | collective-permute-start | bytes 638984 | tf_op jit(solution)/shard_map/cond/branch_0_fun/ppermute | solution.py:733
  38.7 0.7 %collective-permute-start.2 = (f32[10,8,512]{2,1,0:T(8,128)S(1)}, f32[10,8,512]{2,1,0:T(8,128)S(1)}, u32[]{:S(2)}, u32[]{:S(2)}) collective-permute-start(f32[10,8,512]{2,1,0:T(8,128)S(1)} %get-tuple-element.127), channel_id=1, source_target_pairs={{17,29},{19,31},{21,25},{23,27},{24,20},{26,22},{28,16},{30,18}} | collective-permute-start | bytes 491528 | tf_op jit(solution)/shard_map/cond/branch_0_fun/ppermute | solution.py:733
  39.4 8.9 %bulk.4 = (f32[19,8,16,512]{3,2,1,0:T(8,128)}, f32[19,8,16,512]{3,2,1,0:T(8,128)}) custom-call(f32[10,16,512]{2,1,0:T(8,128)S(1)} %slice_add_fusion.after, f32[19,8,16,512]{3,2,1,0:T(8,128)S(1)} %get-tuple-element.132.f_ref, f32[19,8,16,512]{3,2,1,0:T(8,128)S(1)} %get-tuple-element.133.g_ref, f32[8,16,512]{2,1,0:T(8,128)S(1)} %get-tuple-element.134.phi_ref, ...), custom_call_target="tpu_custom_call" | custom-call | tf_op jit(solution)/shard_map/cond/branch_0_fun/bulk/pallas_call | solution.py:748
  48.3 4.1 %collective-permute-done.6.joint = f32[10,16,512]{2,1,0:T(8,128)S(1)} collective-permute-done((f32[10,16,512]{2,1,0:T(8,128)S(1)}, f32[10,16,512]{2,1,0:T(8,128)S(1)}, u32[]{:S(2)}, u32[]{:S(2)}) %collective-permute-start.6) | collective-permute-done | bytes 327712 | tf_op jit(solution)/shard_map/cond/branch_0_fun/ppermute | solution.py:619
  52.4 0.8 %joint_fill.4 = (f32[19,8,16,512]{3,2,1,0:T(8,128)}, f32[19,8,16,512]{3,2,1,0:T(8,128)}) custom-call(f32[10,16,512]{2,1,0:T(8,128)S(1)} %collective-permute-done.6.joint, f32[19,8,16,512]{3,2,1,0:T(8,128)} %get-tuple-element.140.f_in, f32[19,8,16,512]{3,2,1,0:T(8,128)} %get-tuple-element.141.g_in), custom_call_target="tpu_custom_call", output_to_operand_aliasing={{0}: (1, {}), {1}: (2, {})} | custom-call | tf_op jit(solution)/shard_map/cond/branch_0_fun/joint_fill/pallas_call | solution.py:761
  53.2 0.0 collective-permute-done.2.direct_short
  53.2 0.0 collective-permute-done.4.across_short
  53.2 8.0 %collective-permute-done.1.direct = f32[10,16,512]{2,1,0:T(8,128)S(1)} collective-permute-done((f32[10,16,512]{2,1,0:T(8,128)S(1)}, f32[10,16,512]{2,1,0:T(8,128)S(1)}, u32[]{:S(2)}, u32[]{:S(2)}) %collective-permute-start.1) | collective-permute-done | bytes 327712 | tf_op jit(solution)/shard_map/cond/branch_0_fun/ppermute | solution.py:733
  61.2 0.0 collective-permute-done.3.across
  61.2 1.4 %merge_fill.4 = (f32[19,8,16,512]{3,2,1,0:T(8,128)}, f32[19,8,16,512]{3,2,1,0:T(8,128)}) custom-call(s32[4]{0:T(128)S(1)} %get-tuple-element.120.offsets, f32[10,16,512]{2,1,0:T(8,128)S(1)} %collective-permute-done.1.direct, f32[10,8,512]{2,1,0:T(8,128)S(1)} %collective-permute-done.2.direct_short, ...), custom_call_target="tpu_custom_call", output_to_operand_aliasing={{0}: (5, {}), {1}: (6, {})} | custom-call | tf_op jit(solution)/shard_map/cond/branch_0_fun/merge_fill/pallas_call | solution.py:772
  (5 shorter events, 0.1 us)
Async XLA Ops:
  0.6 9.1 %copy-start = (f32[19,8,16,512]{3,2,1,0:T(8,128)S(1)}, f32[19,8,16,512]{3,2,1,0:T(8,128)}, u32[]{:S(2)}) copy-start(f32[19,8,16,512]{3,2,1,0:T(8,128)} %f_ref.7) | copy-start | bytes 14942212
  0.6 9.0 %copy-start.1 = (f32[19,8,16,512]{3,2,1,0:T(8,128)S(1)}, f32[19,8,16,512]{3,2,1,0:T(8,128)}, u32[]{:S(2)}) copy-start(f32[19,8,16,512]{3,2,1,0:T(8,128)} %g_ref.7) | copy-start | bytes 14942212
  3.6 8.2 %collective-permute-start.29 = (f32[16,512]{1,0:T(8,128)S(1)}, f32[16,512]{1,0:T(8,128)S(1)}, u32[]{:S(2)}, u32[]{:S(2)}) collective-permute-start(f32[16,512]{1,0:T(8,128)S(1)} %get-tuple-element.237.top), channel_id=1, source_target_pairs={{0,12},{1,13},{2,14},{3,15},{4,8},{5,9},{6,10},{7,11},{8,20},{9,21... | collective-permute-start | bytes 98312 | tf_op jit(solution)/shard_map/ppermute | solution.py:619
  8.7 5.7 %collective-permute-start.28 = (f32[16,512]{1,0:T(8,128)S(1)}, f32[16,512]{1,0:T(8,128)S(1)}, u32[]{:S(2)}, u32[]{:S(2)}) collective-permute-start(f32[16,512]{1,0:T(8,128)S(1)} %get-tuple-element.236.bottom), channel_id=1, source_target_pairs={{0,28},{1,29},{2,30},{3,31},{4,24},{5,25},{6,26},{7,27},{8,4},{9,5... | collective-permute-start | bytes 98312 | tf_op jit(solution)/shard_map/ppermute | solution.py:619
  11.9 4.1 %collective-permute-start.31 = (f32[40,512]{1,0:T(8,128)S(1)}, f32[40,512]{1,0:T(8,128)S(1)}, u32[]{:S(2)}, u32[]{:S(2)}) collective-permute-start(f32[40,512]{1,0:T(8,128)S(1)} %constant_dynamic-update-slice_fusion.2.after_south), channel_id=1, source_target_pairs={{0,7},{1,0},{2,1},{3,2},{4,3},{5,4},{6,5},{7,6},{8,15},{9,8},{10,9... | collective-permute-start | bytes 245768 | tf_op jit(solution)/shard_map/ppermute | solution.py:619
  14.4 5.7 %collective-permute-start.30 = (f32[40,512]{1,0:T(8,128)S(1)}, f32[40,512]{1,0:T(8,128)S(1)}, u32[]{:S(2)}, u32[]{:S(2)}) collective-permute-start(f32[40,512]{1,0:T(8,128)S(1)} %constant_dynamic-update-slice_fusion.after_north), channel_id=1, source_target_pairs={{0,1},{1,2},{2,3},{3,4},{4,5},{5,6},{6,7},{7,0},{8,9},{9,10},{10,1... | collective-permute-start | bytes 245768 | tf_op jit(solution)/shard_map/ppermute | solution.py:619
  15.1 5.0 %copy-start.2 = (s32[4]{0:T(128)S(1)}, s32[4]{0:T(128)}, u32[]{:S(2)}) copy-start(s32[4]{0:T(128)} %offsets.3) | copy-start | bytes 52
  22.2 1.9 %collective-permute-start.5 = (f32[10,24,512]{2,1,0:T(8,128)S(1)}, f32[10,24,512]{2,1,0:T(8,128)S(1)}, u32[]{:S(2)}, u32[]{:S(2)}) collective-permute-start(f32[10,24,512]{2,1,0:T(8,128)S(1)} %get-tuple-element.131), channel_id=1, source_target_pairs={{0,1},{1,0},{2,3},{3,2},{4,5},{5,4},{6,7},{7,6},{8,9},{9,8},{10,11... | collective-permute-start | bytes 1474568 | tf_op jit(solution)/shard_map/cond/branch_0_fun/ppermute | solution.py:619
  22.3 6.7 %collective-permute-start = (f32[10,8,512]{2,1,0:T(8,128)S(1)}, f32[10,8,512]{2,1,0:T(8,128)S(1)}, u32[]{:S(2)}, u32[]{:S(2)}) collective-permute-start(f32[10,8,512]{2,1,0:T(8,128)S(1)} %get-tuple-element.125), channel_id=1, source_target_pairs={{0,7},{1,2},{2,1},{3,4},{4,3},{5,6},{6,5},{7,0},{8,15},{9,10},{10,... | collective-permute-start | bytes 491528 | tf_op jit(solution)/shard_map/cond/branch_0_fun/ppermute | solution.py:619
  24.2 28.2 %collective-permute-start.6 = (f32[10,16,512]{2,1,0:T(8,128)S(1)}, f32[10,16,512]{2,1,0:T(8,128)S(1)}, u32[]{:S(2)}, u32[]{:S(2)}) collective-permute-start(f32[10,16,512]{2,1,0:T(8,128)S(1)} %slice_add_fusion.after), channel_id=1, source_target_pairs={{0,12},{1,29},{2,14},{3,31},{4,8},{5,25},{6,10},{7,27},{8,20},{9,5... | collective-permute-start | bytes 983048 | tf_op jit(solution)/shard_map/cond/branch_0_fun/ppermute | solution.py:619
  29.0 32.2 %collective-permute-start.1 = (f32[10,16,512]{2,1,0:T(8,128)S(1)}, f32[10,16,512]{2,1,0:T(8,128)S(1)}, u32[]{:S(2)}, u32[]{:S(2)}) collective-permute-start(f32[10,16,512]{2,1,0:T(8,128)S(1)} %get-tuple-element.126), channel_id=1, source_target_pairs={{0,28},{1,13},{2,30},{3,15},{4,24},{5,9},{6,26},{7,11},{8,4},{9,21... | collective-permute-start | bytes 983048 | tf_op jit(solution)/shard_map/cond/branch_0_fun/ppermute | solution.py:733
  30.9 30.3 %collective-permute-start.3 = (f32[10,16,512]{2,1,0:T(8,128)S(1)}, f32[10,16,512]{2,1,0:T(8,128)S(1)}, u32[]{:S(2)}, u32[]{:S(2)}) collective-permute-start(f32[10,16,512]{2,1,0:T(8,128)S(1)} %get-tuple-element.128), channel_id=1, source_target_pairs={{16,27},{18,29},{20,31},{22,25},{25,22},{27,16},{29,18},{31,20}} | collective-permute-start | bytes 983048 | tf_op jit(solution)/shard_map/cond/branch_0_fun/ppermute | solution.py:733
  31.6 21.6 %collective-permute-start.4 = (f32[104,512]{1,0:T(8,128)S(1)}, f32[104,512]{1,0:T(8,128)S(1)}, u32[]{:S(2)}, u32[]{:S(2)}) collective-permute-start(f32[104,512]{1,0:T(8,128)S(1)} %get-tuple-element.129), channel_id=1, source_target_pairs={{0,11},{1,30},{2,13},{3,24},{4,15},{5,26},{6,9},{7,28},{8,19},{9,6... | collective-permute-start | bytes 638984 | tf_op jit(solution)/shard_map/cond/branch_0_fun/ppermute | solution.py:733
  38.7 14.5 %collective-permute-start.2 = (f32[10,8,512]{2,1,0:T(8,128)S(1)}, f32[10,8,512]{2,1,0:T(8,128)S(1)}, u32[]{:S(2)}, u32[]{:S(2)}) collective-permute-start(f32[10,8,512]{2,1,0:T(8,128)S(1)} %get-tuple-element.127), channel_id=1, source_target_pairs={{17,29},{19,31},{21,25},{23,27},{24,20},{26,22},{28,16},{30,18}} | collective-permute-start | bytes 491528 | tf_op jit(solution)/shard_map/cond/branch_0_fun/ppermute | solution.py:733

commit v12 on v10

--- a/solution.py
+++ b/solution.py
@@ -189,7 +189,9 @@
     return total
 
 
-def phi_kernel(f_ref, g_ref, top, bottom, phi_ref, to_north, to_south, gbuf, fbuf, sems):
+def phi_kernel(
+    base, offsets, f_ref, g_ref, top, bottom, phi_ref, to_north, to_south, gbuf, index, fbuf, sems
+):
     layers, rows = phi_ref.shape[0], phi_ref.shape[1]
     faces = (layers - 1, 0)
     f_copies = [
@@ -201,6 +203,8 @@
     ]
     for copy in f_copies + g_copies:
         copy.start()
+    is_long = [(offsets[k] - base > rows // 2).astype(jnp.int32) for k in (1, 2)]
+    index[0] = 2 * is_long[0] + is_long[1]
     phi_ref[layers - 1] = top[...]
     phi_ref[0] = bottom[...]
     edges = ((to_north, rows - 1, rows - 2, (7, 10)), (to_south, 0, 1, (9, 8)))
@@ -568,27 +572,34 @@
     seam = 10 * part
 
     def merge(rest, up):
+        near, other, between = half_rows(rows, up), half_rows(rows, not up), seam_rows(rows, up)
+        chosen, x = (rising, 0) if up else (falling, layers - 1)
+        copies = [
+            pltpu.make_async_copy(
+                buf.at[j], (f_out if j < 5 else g_out).at[chosen[j % 5], x], sems.at[j]
+            )
+            for j in range(10)
+        ]
+
+        def long():
+            for j in range(10):
+                buf[j, near] = across[j, near] + direct_short[j]
+                buf[j, other] = across[j, other]
+                copies[j].start()
+
+        def short():
+            for j in range(10):
+                at = seam + 2 * j
+                buf[j, near] = direct[j, near]
+                buf[j, between] = direct[j, between] + across_short[at : at + 2]
+                buf[j, other] = direct[j, other] + across_short[part * j : part * j + part]
+                copies[j].start()
+
         is_long = rest > part
-        near, other, between = half_rows(rows, up), half_rows(rows, not up), seam_rows(rows, up)
-
-        @pl.when(is_long)
-        def _():
-            buf[...] = across[...]
-            for j in range(10):
-                buf[j, near] = buf[j, near] + direct_short[j]
-
-        @pl.when(jnp.logical_not(is_long))
-        def _():
-            buf[...] = direct[...]
-            for j in range(10):
-                buf[j, other] = buf[j, other] + across_short[part * j : part * j + part]
-                at = seam + 2 * j
-                buf[j, between] = buf[j, between] + across_short[at : at + 2]
-
-        if up:
-            put_faces(buf, f_out, g_out, rising, 0, sems)
-        else:
-            put_faces(buf, f_out, g_out, falling, layers - 1, sems)
+        pl.when(is_long)(long)
+        pl.when(jnp.logical_not(is_long))(short)
+        for copy in copies:
+            copy.wait()
 
     pl.when(planes.odd)(lambda: merge(planes.low_rest, True))
     pl.when(jnp.logical_not(planes.odd))(lambda: merge(planes.up_rest, False))
@@ -639,20 +650,20 @@
     fall = hop(bottom, lambda x, y: (x - 1, y + base_low(x)))
 
     block = jax.ShapeDtypeStruct((layers + 16, cols), f32)
-    phi, to_north, to_south, order_near = pl.pallas_call(
-        phi_kernel,
+    phi, to_north, to_south, order_near, index = pl.pallas_call(
+        functools.partial(phi_kernel, half * rows),
         out_shape=[jax.ShapeDtypeStruct((layers, rows, cols), f32)]
         + [block] * 2
-        + [jax.ShapeDtypeStruct(order_dist.shape, f32)],
-        in_specs=[anywhere, anywhere, vmem, vmem],
-        out_specs=[vmem] * 4,
+        + [jax.ShapeDtypeStruct(order_dist.shape, f32), jax.ShapeDtypeStruct((1,), jnp.int32)],
+        in_specs=[smem, anywhere, anywhere, vmem, vmem],
+        out_specs=[vmem] * 4 + [smem],
         scratch_shapes=[
             VMEM((19, 2, rows, cols), f32),
             pltpu.SemaphoreType.DMA((layers + 2,)),
         ],
         compiler_params=params(52 << 20),
         name="phi_all",
-    )(momentum_dist, order_dist, top, bottom)
+    )(offsets, momentum_dist, order_dist, top, bottom)
     to_north = jnp.concatenate([fall, to_north], 0)
     to_south = jnp.concatenate([rise, to_south], 0)
     south_msg, north_msg = hop_y(to_north, 1), hop_y(to_south, -1)
@@ -775,12 +786,11 @@
             name="merge_fill",
         )(offsets, direct, direct_short, across, across_short, next_f, next_g)
 
-    is_long = [(offsets[k] - half * rows > part).astype(jnp.int32) for k in (1, 2)]
     branches = [
         functools.partial(finish, {3} | ({1} if k & 2 else set()) | ({2} if k & 1 else set()))
         for k in range(4)
     ]
-    return lax.switch(2 * is_long[0] + is_long[1], branches, *outgoing)
+    return lax.switch(index[0], branches, *outgoing)
 
 
 def solution(mesh):

time: 61.2 us -> 60.8 us (level)
  the two profiles are of different devices: /device:TPU:0 before, /device:TPU:1 now
where the time goes in v12:
time: 60.8 us; the launch traced here: 61.5 us
  waiting for transfers between devices  22.6 us (37%)
  starting transfers between devices  18.2 us (30%)
  Pallas kernels  17.8 us (29%)
  other arithmetic  1.41 us (2%)
  between operations  1.37 us (2%)
    ppermute x7, waiting for transfers between devices, hop(): return lax.ppermute(value, ('gx', 'gy'), perm)  15 us
    ppermute x7, starting transfers between devices, hop(): return lax.ppermute(value, ('gx', 'gy'), perm)  13 us
    pallas_call x1, Pallas kernels, finish(): pl.pallas_call(bulk_kernel, out_shape=[whole, whole], in_specs=[anywhere]...  9 us
    ppermute x4, waiting for transfers between devices, hop_some(): return lax.ppermute(value, ('gx', 'gy'), pairs)  7.58 us
    ppermute x4, starting transfers between devices, hop_some(): return lax.ppermute(value, ('gx', 'gy'), pairs)  5.18 us
    pallas_call x1, Pallas kernels, on_device(): pl.pallas_call(functools.partial(phi_kernel, half * rows), out_shape=[jax...  4.17 us
    pallas_call x1, Pallas kernels, on_device(): pl.pallas_call(functools.partial(face_kernel, (count_x, count_y)), out_sh...  2.07 us
    pallas_call x1, Pallas kernels, finish(): pl.pallas_call(functools.partial(merge_fill_kernel, (count_x, count_y)),...  1.37 us
  transfers between devices with their start and end apart: 11, of which 5 were waited for; matrix products, arithmetic and copies ran while one was open for 0% of the time, Pallas kernels for 23%

profile of v12, /device:TPU:1, one launch (start us, length us, event | category | flops | bytes accessed | tf_op | source)
XLA Modules:
  0.0 61.5 jit_solution(13031319293736945221)
XLA Ops:
  0.6 1.4 %slice_reduce_fusion = (f32[16,512]{1,0:T(8,128)S(1)}, f32[16,512]{1,0:T(8,128)S(1)}) fusion(f32[19,8,16,512]{3,2,1,0:T(8,128)} %g_ref.1), kind=kLoop, calls=%fused_computation.4 | loop fusion | flops 294912 | bytes 1310720 | tf_op jit(solution)/shard_map/reduce_sum | solution.py:648
  2.0 4.1 %collective-permute-start.29 = (f32[16,512]{1,0:T(8,128)S(1)}, f32[16,512]{1,0:T(8,128)S(1)}, u32[]{:S(2)}, u32[]{:S(2)}) collective-permute-start(f32[16,512]{1,0:T(8,128)S(1)} %get-tuple-element.261.top), channel_id=1, source_target_pairs={{0,12},{1,13},{2,14},{3,15},{4,8},{5,9},{6,10},{7,11},{8,20},{9,21... | collective-permute-start | bytes 98312 | tf_op jit(solution)/shard_map/ppermute | solution.py:627
  6.1 0.0 slice-start
  6.1 0.0 slice-start.1
  6.1 1.0 %collective-permute-start.28 = (f32[16,512]{1,0:T(8,128)S(1)}, f32[16,512]{1,0:T(8,128)S(1)}, u32[]{:S(2)}, u32[]{:S(2)}) collective-permute-start(f32[16,512]{1,0:T(8,128)S(1)} %get-tuple-element.260.bottom), channel_id=1, source_target_pairs={{0,28},{1,29},{2,30},{3,31},{4,24},{5,25},{6,26},{7,27},{8,4},{9,5... | collective-permute-start | bytes 98312 | tf_op jit(solution)/shard_map/ppermute | solution.py:627
  7.2 4.2 %phi_all.1 = (f32[8,16,512]{2,1,0:T(8,128)S(1)}, f32[24,512]{1,0:T(8,128)S(1)}, f32[24,512]{1,0:T(8,128)S(1)}, f32[19,8,16,512]{3,2,1,0:T(8,128)S(1)}, s32[1]{0:T(128)}) custom-call(s32[4]{0:T(128)} %offsets.3, f32[19,8,16,512]{3,2,1,0:T(8,128)} %f_ref.5, f32[19,8,16,512]{3,2,1,0:T(8,128)} %g_ref.1, f32[16,512]{1,0:T(8,128)S(1)} %get-tuple-element.261.top, ...), custom_call_target="tpu_custom_call" | custom-call | tf_op jit(solution)/shard_map/phi_all/pallas_call | solution.py:653
  11.3 0.0 collective-permute-done.29.rise
  11.4 1.0 %collective-permute-start.31 = (f32[40,512]{1,0:T(8,128)S(1)}, f32[40,512]{1,0:T(8,128)S(1)}, u32[]{:S(2)}, u32[]{:S(2)}) collective-permute-start(f32[40,512]{1,0:T(8,128)S(1)} %constant_dynamic-update-slice_fusion.2.after_south), channel_id=1, source_target_pairs={{0,7},{1,0},{2,1},{3,2},{4,3},{5,4},{6,5},{7,6},{8,15},{9,8},{10,9... | collective-permute-start | bytes 245768 | tf_op jit(solution)/shard_map/ppermute | solution.py:627
  12.4 0.0 collective-permute-done.28.fall
  12.4 1.6 %collective-permute-start.30 = (f32[40,512]{1,0:T(8,128)S(1)}, f32[40,512]{1,0:T(8,128)S(1)}, u32[]{:S(2)}, u32[]{:S(2)}) collective-permute-start(f32[40,512]{1,0:T(8,128)S(1)} %constant_dynamic-update-slice_fusion.after_north), channel_id=1, source_target_pairs={{0,1},{1,2},{2,3},{3,4},{4,5},{5,6},{6,7},{7,0},{8,9},{9,10},{10,1... | collective-permute-start | bytes 245768 | tf_op jit(solution)/shard_map/ppermute | solution.py:627
  14.7 0.0 slice-done
  14.7 0.0 slice-done.1
  14.7 0.0 copy-start
  14.7 0.4 moments.1
  15.1 0.7 %collective-permute-done.31.north_msg = f32[40,512]{1,0:T(8,128)S(1)} collective-permute-done((f32[40,512]{1,0:T(8,128)S(1)}, f32[40,512]{1,0:T(8,128)S(1)}, u32[]{:S(2)}, u32[]{:S(2)}) %collective-permute-start.31) | collective-permute-done | bytes 81952 | tf_op jit(solution)/shard_map/ppermute | solution.py:627
  15.9 0.0 collective-permute-done.30.south_msg
  15.9 0.0 copy-done
  15.9 2.1 %faces.1 = (f32[10,24,512]{2,1,0:T(8,128)S(1)}, f32[10,16,512]{2,1,0:T(8,128)S(1)}, f32[10,8,512]{2,1,0:T(8,128)S(1)}, f32[10,16,512]{2,1,0:T(8,128)S(1)}, f32[1...) custom-call(s32[4]{0:T(128)S(1)} %copy-done, ...), custom_call_target="tpu_custom_call" | custom-call | tf_op jit(solution)/shard_map/faces/pallas_call | solution.py:689
  17.9 43.6 %conditional.1 = ((f32[19,8,16,512]{3,2,1,0:T(8,128)}, f32[19,8,16,512]{3,2,1,0:T(8,128)})) conditional(s32[]{:T(128)} %bitcast, (f32[10,8,512]{2,1,0:T(8,128)S(1)}, f32[10,16,512]{2,1,0:T(8,128)S(1)}, f32[10,8,512]{2,1,0:T(8,128)S(1)}, f32[10,16,512]{2,1,0:T(8,128)S(1)}, f32[104,512]{1,0:T(8,128)S(1)}, ...), branch_computations={%region_2.0_spmd, %region_3.0_spmd, %region_4.0_spmd, %region_5.0_... | conditional | flops 81920 | bytes 9044256 | solution.py:793
  18.0 4.8 %collective-permute-start.12 = (f32[10,24,512]{2,1,0:T(8,128)S(1)}, f32[10,24,512]{2,1,0:T(8,128)S(1)}, u32[]{:S(2)}, u32[]{:S(2)}) collective-permute-start(f32[10,24,512]{2,1,0:T(8,128)S(1)} %get-tuple-element.155), channel_id=1, source_target_pairs={{0,1},{1,0},{2,3},{3,2},{4,5},{5,4},{6,7},{7,6},{8,9},{9,8},{10,11... | collective-permute-start | bytes 1474568 | tf_op jit(solution)/shard_map/cond/branch_1_fun/ppermute | solution.py:627
  22.8 0.0 collective-permute-start.7
  22.8 1.5 %collective-permute-done.12.mate_rim = f32[10,24,512]{2,1,0:T(8,128)S(1)} collective-permute-done((f32[10,24,512]{2,1,0:T(8,128)S(1)}, f32[10,24,512]{2,1,0:T(8,128)S(1)}, u32[]{:S(2)}, u32[]{:S(2)}) %collective-permute-start.12) | collective-permute-done | bytes 491552 | tf_op jit(solution)/shard_map/cond/branch_1_fun/ppermute | solution.py:627
  24.3 0.4 collective-permute-start.13
  24.7 4.7 %collective-permute-done.7.cross_rim = f32[10,8,512]{2,1,0:T(8,128)S(1)} collective-permute-done((f32[10,8,512]{2,1,0:T(8,128)S(1)}, f32[10,8,512]{2,1,0:T(8,128)S(1)}, u32[]{:S(2)}, u32[]{:S(2)}) %collective-permute-start.7) | collective-permute-done | bytes 163872 | tf_op jit(solution)/shard_map/cond/branch_1_fun/ppermute | solution.py:627
  29.4 0.7 %collective-permute-start.10 = (f32[10,16,512]{2,1,0:T(8,128)S(1)}, f32[10,16,512]{2,1,0:T(8,128)S(1)}, u32[]{:S(2)}, u32[]{:S(2)}) collective-permute-start(f32[10,16,512]{2,1,0:T(8,128)S(1)} %get-tuple-element.152), channel_id=1, source_target_pairs={{8,19},{10,21},{12,23},{14,17},{16,27},{17,14},{18,29},{19,8},{20,... | collective-permute-start | bytes 983048 | tf_op jit(solution)/shard_map/cond/branch_1_fun/ppermute | solution.py:739
  30.1 1.9 %collective-permute-start.8 = (f32[10,16,512]{2,1,0:T(8,128)S(1)}, f32[10,16,512]{2,1,0:T(8,128)S(1)}, u32[]{:S(2)}, u32[]{:S(2)}) collective-permute-start(f32[10,16,512]{2,1,0:T(8,128)S(1)} %get-tuple-element.150), channel_id=1, source_target_pairs={{0,28},{1,13},{2,30},{3,15},{4,24},{5,9},{6,26},{7,11},{8,4},{10,6... | collective-permute-start | bytes 983048 | tf_op jit(solution)/shard_map/cond/branch_1_fun/ppermute | solution.py:739
  32.0 1.9 %collective-permute-start.11 = (f32[104,512]{1,0:T(8,128)S(1)}, f32[104,512]{1,0:T(8,128)S(1)}, u32[]{:S(2)}, u32[]{:S(2)}) collective-permute-start(f32[104,512]{1,0:T(8,128)S(1)} %get-tuple-element.153), channel_id=1, source_target_pairs={{0,11},{1,30},{2,13},{3,24},{4,15},{5,26},{6,9},{7,28},{9,6},{11,0... | collective-permute-start | bytes 638984 | tf_op jit(solution)/shard_map/cond/branch_1_fun/ppermute | solution.py:739
  34.0 0.7 %collective-permute-start.9 = (f32[10,8,512]{2,1,0:T(8,128)S(1)}, f32[10,8,512]{2,1,0:T(8,128)S(1)}, u32[]{:S(2)}, u32[]{:S(2)}) collective-permute-start(f32[10,8,512]{2,1,0:T(8,128)S(1)} %get-tuple-element.151), channel_id=1, source_target_pairs={{9,21},{11,23},{13,17},{15,19},{16,12},{17,29},{18,14},{19,31},{20... | collective-permute-start | bytes 491528 | tf_op jit(solution)/shard_map/cond/branch_1_fun/ppermute | solution.py:739
  34.6 9.0 %bulk.5 = (f32[19,8,16,512]{3,2,1,0:T(8,128)}, f32[19,8,16,512]{3,2,1,0:T(8,128)}) custom-call(f32[10,16,512]{2,1,0:T(8,128)S(1)} %slice_add_fusion.1.after, f32[19,8,16,512]{3,2,1,0:T(8,128)S(1)} %get-tuple-element.156.f_ref, f32[19,8,16,512]{3,2,1,0:T(8,128)S(1)} %get-tuple-element.157.g_ref, f32[8,16,512]{2,1,0:T(8,128)S(1)} %get-tuple-element.158.phi_ref, ...), custom_call_target="tpu_custom_call" | custom-call | tf_op jit(solution)/shard_map/cond/branch_1_fun/bulk/pallas_call | solution.py:754
  43.6 8.1 %collective-permute-done.13.joint = f32[10,16,512]{2,1,0:T(8,128)S(1)} collective-permute-done((f32[10,16,512]{2,1,0:T(8,128)S(1)}, f32[10,16,512]{2,1,0:T(8,128)S(1)}, u32[]{:S(2)}, u32[]{:S(2)}) %collective-permute-start.13) | collective-permute-done | bytes 327712 | tf_op jit(solution)/shard_map/cond/branch_1_fun/ppermute | solution.py:627
  51.8 0.8 %joint_fill.5 = (f32[19,8,16,512]{3,2,1,0:T(8,128)}, f32[19,8,16,512]{3,2,1,0:T(8,128)}) custom-call(f32[10,16,512]{2,1,0:T(8,128)S(1)} %collective-permute-done.13.joint, f32[19,8,16,512]{3,2,1,0:T(8,128)} %get-tuple-element.164.f_in, f32[19,8,16,512]{3,2,1,0:T(8,128)} %get-tuple-element.165.g_in), custom_call_target="tpu_custom_call", output_to_operand_aliasing={{0}: (1, {}), {1}: (2, {})} | custom-call | tf_op jit(solution)/shard_map/cond/branch_1_fun/joint_fill/pallas_call | solution.py:767
  52.6 0.0 collective-permute-done.9.direct_short
  52.6 0.0 collective-permute-done.11.across_short
  52.6 0.0 collective-permute-done.10.across
  52.6 7.6 %collective-permute-done.8.direct = f32[10,16,512]{2,1,0:T(8,128)S(1)} collective-permute-done((f32[10,16,512]{2,1,0:T(8,128)S(1)}, f32[10,16,512]{2,1,0:T(8,128)S(1)}, u32[]{:S(2)}, u32[]{:S(2)}) %collective-permute-start.8) | collective-permute-done | bytes 327712 | tf_op jit(solution)/shard_map/cond/branch_1_fun/ppermute | solution.py:739
  60.2 1.4 %merge_fill.5 = (f32[19,8,16,512]{3,2,1,0:T(8,128)}, f32[19,8,16,512]{3,2,1,0:T(8,128)}) custom-call(s32[4]{0:T(128)S(1)} %get-tuple-element.144.offsets, f32[10,16,512]{2,1,0:T(8,128)S(1)} %collective-permute-done.8.direct, f32[10,8,512]{2,1,0:T(8,128)S(1)} %collective-permute-done.9.direct_short, ...), custom_call_target="tpu_custom_call", output_to_operand_aliasing={{0}: (5, {}), {1}: (6, {})} | custom-call | tf_op jit(solution)/shard_map/cond/branch_1_fun/merge_fill/pallas_call | solution.py:778
  (6 shorter events, 0.1 us)
Async XLA Ops:
  2.0 9.3 %collective-permute-start.29 = (f32[16,512]{1,0:T(8,128)S(1)}, f32[16,512]{1,0:T(8,128)S(1)}, u32[]{:S(2)}, u32[]{:S(2)}) collective-permute-start(f32[16,512]{1,0:T(8,128)S(1)} %get-tuple-element.261.top), channel_id=1, source_target_pairs={{0,12},{1,13},{2,14},{3,15},{4,8},{5,9},{6,10},{7,11},{8,20},{9,21... | collective-permute-start | bytes 98312 | tf_op jit(solution)/shard_map/ppermute | solution.py:627
  6.1 8.6 %slice-start = ((s8[4980736]{0:T(1024)(128)(4,1)}), s8[4194304]{0:T(1024)(128)(4,1)S(1)}, s32[]{:S(2)}) async-start(s8[4980736]{0:T(1024)(128)(4,1)} %bitcast.1), calls=%async_computation | async-start | bytes 8388608
  6.1 8.6 %slice-start.1 = ((s8[4980736]{0:T(1024)(128)(4,1)}), s8[786432]{0:T(1024)(128)(4,1)S(1)}, s32[]{:S(2)}) async-start(s8[4980736]{0:T(1024)(128)(4,1)} %bitcast.1), calls=%async_computation.1 | async-start | bytes 1572864
  6.1 6.3 %collective-permute-start.28 = (f32[16,512]{1,0:T(8,128)S(1)}, f32[16,512]{1,0:T(8,128)S(1)}, u32[]{:S(2)}, u32[]{:S(2)}) collective-permute-start(f32[16,512]{1,0:T(8,128)S(1)} %get-tuple-element.260.bottom), channel_id=1, source_target_pairs={{0,28},{1,29},{2,30},{3,31},{4,24},{5,25},{6,26},{7,27},{8,4},{9,5... | collective-permute-start | bytes 98312 | tf_op jit(solution)/shard_map/ppermute | solution.py:627
  11.4 4.5 %collective-permute-start.31 = (f32[40,512]{1,0:T(8,128)S(1)}, f32[40,512]{1,0:T(8,128)S(1)}, u32[]{:S(2)}, u32[]{:S(2)}) collective-permute-start(f32[40,512]{1,0:T(8,128)S(1)} %constant_dynamic-update-slice_fusion.2.after_south), channel_id=1, source_target_pairs={{0,7},{1,0},{2,1},{3,2},{4,3},{5,4},{6,5},{7,6},{8,15},{9,8},{10,9... | collective-permute-start | bytes 245768 | tf_op jit(solution)/shard_map/ppermute | solution.py:627
  12.4 3.5 %collective-permute-start.30 = (f32[40,512]{1,0:T(8,128)S(1)}, f32[40,512]{1,0:T(8,128)S(1)}, u32[]{:S(2)}, u32[]{:S(2)}) collective-permute-start(f32[40,512]{1,0:T(8,128)S(1)} %constant_dynamic-update-slice_fusion.after_north), channel_id=1, source_target_pairs={{0,1},{1,2},{2,3},{3,4},{4,5},{5,6},{6,7},{7,0},{8,9},{9,10},{10,1... | collective-permute-start | bytes 245768 | tf_op jit(solution)/shard_map/ppermute | solution.py:627
  14.7 1.1 %copy-start = (s32[4]{0:T(128)S(1)}, s32[4]{0:T(128)}, u32[]{:S(2)}) copy-start(s32[4]{0:T(128)} %offsets.3) | copy-start | bytes 52
  18.0 6.3 %collective-permute-start.12 = (f32[10,24,512]{2,1,0:T(8,128)S(1)}, f32[10,24,512]{2,1,0:T(8,128)S(1)}, u32[]{:S(2)}, u32[]{:S(2)}) collective-permute-start(f32[10,24,512]{2,1,0:T(8,128)S(1)} %get-tuple-element.155), channel_id=1, source_target_pairs={{0,1},{1,0},{2,3},{3,2},{4,5},{5,4},{6,7},{7,6},{8,9},{9,8},{10,11... | collective-permute-start | bytes 1474568 | tf_op jit(solution)/shard_map/cond/branch_1_fun/ppermute | solution.py:627
  22.8 6.6 %collective-permute-start.7 = (f32[10,8,512]{2,1,0:T(8,128)S(1)}, f32[10,8,512]{2,1,0:T(8,128)S(1)}, u32[]{:S(2)}, u32[]{:S(2)}) collective-permute-start(f32[10,8,512]{2,1,0:T(8,128)S(1)} %get-tuple-element.149), channel_id=1, source_target_pairs={{0,7},{1,2},{2,1},{3,4},{4,3},{5,6},{6,5},{7,0},{8,15},{9,10},{10,... | collective-permute-start | bytes 491528 | tf_op jit(solution)/shard_map/cond/branch_1_fun/ppermute | solution.py:627
  24.3 27.4 %collective-permute-start.13 = (f32[10,16,512]{2,1,0:T(8,128)S(1)}, f32[10,16,512]{2,1,0:T(8,128)S(1)}, u32[]{:S(2)}, u32[]{:S(2)}) collective-permute-start(f32[10,16,512]{2,1,0:T(8,128)S(1)} %slice_add_fusion.1.after), channel_id=1, source_target_pairs={{0,12},{1,29},{2,14},{3,31},{4,8},{5,25},{6,10},{7,27},{8,20},{9,5... | collective-permute-start | bytes 983048 | tf_op jit(solution)/shard_map/cond/branch_1_fun/ppermute | solution.py:627
  29.4 23.2 %collective-permute-start.10 = (f32[10,16,512]{2,1,0:T(8,128)S(1)}, f32[10,16,512]{2,1,0:T(8,128)S(1)}, u32[]{:S(2)}, u32[]{:S(2)}) collective-permute-start(f32[10,16,512]{2,1,0:T(8,128)S(1)} %get-tuple-element.152), channel_id=1, source_target_pairs={{8,19},{10,21},{12,23},{14,17},{16,27},{17,14},{18,29},{19,8},{20,... | collective-permute-start | bytes 983048 | tf_op jit(solution)/shard_map/cond/branch_1_fun/ppermute | solution.py:739
  30.1 30.1 %collective-permute-start.8 = (f32[10,16,512]{2,1,0:T(8,128)S(1)}, f32[10,16,512]{2,1,0:T(8,128)S(1)}, u32[]{:S(2)}, u32[]{:S(2)}) collective-permute-start(f32[10,16,512]{2,1,0:T(8,128)S(1)} %get-tuple-element.150), channel_id=1, source_target_pairs={{0,28},{1,13},{2,30},{3,15},{4,24},{5,9},{6,26},{7,11},{8,4},{10,6... | collective-permute-start | bytes 983048 | tf_op jit(solution)/shard_map/cond/branch_1_fun/ppermute | solution.py:739
  32.0 20.5 %collective-permute-start.11 = (f32[104,512]{1,0:T(8,128)S(1)}, f32[104,512]{1,0:T(8,128)S(1)}, u32[]{:S(2)}, u32[]{:S(2)}) collective-permute-start(f32[104,512]{1,0:T(8,128)S(1)} %get-tuple-element.153), channel_id=1, source_target_pairs={{0,11},{1,30},{2,13},{3,24},{4,15},{5,26},{6,9},{7,28},{9,6},{11,0... | collective-permute-start | bytes 638984 | tf_op jit(solution)/shard_map/cond/branch_1_fun/ppermute | solution.py:739
  34.0 18.6 %collective-permute-start.9 = (f32[10,8,512]{2,1,0:T(8,128)S(1)}, f32[10,8,512]{2,1,0:T(8,128)S(1)}, u32[]{:S(2)}, u32[]{:S(2)}) collective-permute-start(f32[10,8,512]{2,1,0:T(8,128)S(1)} %get-tuple-element.151), channel_id=1, source_target_pairs={{9,21},{11,23},{13,17},{15,19},{16,12},{17,29},{18,14},{19,31},{20... | collective-permute-start | bytes 491528 | tf_op jit(solution)/shard_map/cond/branch_1_fun/ppermute | solution.py:739
